TPU v7x, 32 devices: a whole 2x2x4 slice. The times are simulated.
32 devices in a mesh: dp: 8 (over z, y), blk: 4 (over x, core).
Axes of the slice: x: 2, y: 2, z: 4, core: 2. Of those that a mesh axis runs over, the one named last changes fastest.
Arguments:
- tokens: bfloat16 [8, 1024, 512], P('dp', 'blk'), may hold values from -6 to 6
- segments: int32 [8, 1024], P('dp', 'blk'), may hold values from 0 to 4, as said below
- memory_init: float32 [20, 512], P(None, ('dp', 'blk')), may hold values from -6 to 6
- attn_weights: float32 [2, 12, 512, 512], P(None, None, ('dp', 'blk'))
- ffn_in: float32 [2, 512, 2048], P(None, ('dp', 'blk')), may hold values from -0.25 to 0.25
- ffn_out: float32 [2, 2048, 512], P(None, ('dp', 'blk')), may hold values from -0.125 to 0.125
- ffn_bias: float32 [2, 2048], P(None, ('dp', 'blk')), may hold values from -3 to 3
- norm_gain: float32 [2, 4, 512], P(None, None, ('dp', 'blk')), may hold values from 0.5 to 1.5
- norm_shift: float32 [2, 5, 512], P(None, None, ('dp', 'blk')), may hold values from -1.8 to 1.8
- out_grad: bfloat16 [8, 1024, 512], P('dp', 'blk'), may hold values from -6 to 6
- memory_cot: bfloat16 [8, 20, 512], P('dp'), may hold values from -6 to 6
Outputs:
- result: bfloat16 [8, 1024, 512], P('dp', 'blk')
- memory_out: float32 [8, 20, 512], P('dp')
- tokens_grad: float32 [8, 1024, 512], P('dp', 'blk')
- memory_init_grad: float32 [20, 512], P(None, ('dp', 'blk'))
- attn_weights_grad: float32 [2, 12, 512, 512], P(None, None, ('dp', 'blk'))
- ffn_in_grad: float32 [2, 512, 2048], P(None, ('dp', 'blk'))
- ffn_out_grad: float32 [2, 2048, 512], P(None, ('dp', 'blk'))
- ffn_bias_grad: float32 [2, 2048], P(None, ('dp', 'blk'))
- norm_gain_grad: float32 [2, 4, 512], P(None, None, ('dp', 'blk'))
- norm_shift_grad: float32 [2, 5, 512], P(None, None, ('dp', 'blk'))
Inputs may be any that keep to these rules, and one draw needn't show every extreme that they name: `segments`: in each row the document numbers start at 0 at position 0 and rise by one at exactly four positions: one in 1 to 63, one in 64 to 127, one in 896 to 959, and one in 960 to 1023.
All inputs are finite; a program needn't handle non-finite values.
Results may differ from a plain program's by a relative error of at most 0.03.
Values may be sent and summed in bfloat16 or wider, within the bound.
No kernel may reach another device: no remote copies, remote signals or barrier semaphores. Data moves between devices by JAX's collectives and lax.ppermute only.
A program may use at most 192 MiB of HBM per device.

v0:
```python
import jax
import jax.numpy as jnp
from jax import lax
from jax.sharding import PartitionSpec as P

HEADS = 8
HEAD = 64
MEM = 20


NEG = -1000000000.0
EPS = 1e-05


def combined_all(array, axis, join):
    gathered = jax.tree.map(
        lambda a, kind: lax.all_gather(a.astype(kind), axis),
        array,
        jax.tree.map(lambda a: jnp.bfloat16 if a.dtype == jnp.float32 else a.dtype, array),
    )

    def take(source):
        return jax.tree.map(
            lambda a, own: lax.dynamic_index_in_dim(a, source, 0, False).astype(own.dtype),
            gathered,
            array,
        )

    return lax.fori_loop(
        1, lax.axis_size(axis), lambda source, state: join(state, take(source)), take(0)
    )


def for_sending(array):

    def short(part):
        return part.astype(jnp.bfloat16) if part.dtype == jnp.float32 else part

    return jax.tree.map(short, array)


def passed_along(value, axis, steps):
    count = lax.axis_size(axis)
    pairs = [(source, (source + steps) % count) for source in range(count)]
    return lax.ppermute(value, axis, pairs)


def split_heads(matrix):
    return matrix.reshape(matrix.shape[0], HEADS, HEAD).transpose(1, 0, 2)


def join_heads(tensor):
    return tensor.transpose(1, 0, 2).reshape(tensor.shape[1], HEADS * HEAD)


def normalize(values, gain, shift):
    center = values - jnp.mean(values, -1, keepdims=True)
    spread = jnp.mean(center * center, -1, keepdims=True)
    return center * lax.rsqrt(spread + EPS) * gain + shift


def norm_back(values, gain, shift, grad):
    output, pull = jax.vjp(normalize, values, gain, shift)
    return pull(grad)


def linear(inputs, weight):
    return jnp.dot(inputs, weight, preferred_element_type=jnp.float32)


def stacked_linear(inputs, weights):
    return jnp.einsum("nd,jde->jne", inputs, weights, preferred_element_type=jnp.float32).astype(
        jnp.bfloat16
    )


def weight_grad(inputs, grads):
    return jnp.einsum("nd,ne->de", inputs, grads, preferred_element_type=jnp.float32)


def input_grad(grads, weight):
    return jnp.einsum("ne,de->nd", grads, weight, preferred_element_type=jnp.float32)


def mixed_grad(inputs, grads, share):
    return share * weight_grad(inputs[:MEM], grads[:MEM]) + weight_grad(inputs[MEM:], grads[MEM:])


def row_total(grads, share):
    values = grads.astype(jnp.float32)
    return share * jnp.sum(values[:MEM], 0) + jnp.sum(values[MEM:], 0)


def scores_of(query, keys, allowed):
    raw = jnp.einsum("hqe,hke->hqk", query, keys, preferred_element_type=jnp.float32) * HEAD ** (
        -0.5
    )
    if allowed is None:
        return raw
    return jnp.where(allowed[None], raw, NEG)


def fresh(query):
    count, rows, width = query.shape
    return (
        jnp.full((count, rows), -1e30, jnp.float32),
        jnp.zeros((count, rows), jnp.float32),
        jnp.zeros((count, rows, width), jnp.float32),
    )


def absorb(state, query, keys, values, allowed):
    highest, total, accum = state
    scores = scores_of(query, keys, allowed)
    summit = jnp.maximum(highest, jnp.max(scores, -1))
    weights = jnp.exp(scores - summit[..., None])
    fade = jnp.exp(highest - summit)
    total = total * fade + jnp.sum(weights, -1)
    accum = accum * fade[..., None] + jnp.einsum(
        "hqk,hke->hqe", weights.astype(jnp.bfloat16), values, preferred_element_type=jnp.float32
    )
    return (summit, total, accum)


def combine_parts(first, second):
    summit = jnp.maximum(first[0], second[0])
    fade_one = jnp.exp(first[0] - summit)
    fade_two = jnp.exp(second[0] - summit)
    return (
        summit,
        first[1] * fade_one + second[1] * fade_two,
        first[2] * fade_one[..., None] + second[2] * fade_two[..., None],
    )


def finish(state):
    highest, total, accum = state
    return (accum / total[..., None], highest + jnp.log(total))


def memory_over_sequence(query, keys, values):
    part = absorb(fresh(query), query, keys, values, None)
    return combined_all(part, "blk", combine_parts)


def memory_total(parts):
    return jax.tree.map(lambda part: part.astype(jnp.float32), lax.psum(for_sending(parts), "blk"))


def attend_back(query, keys, values, allowed, log_total, out_low, delta):
    scores = scores_of(query, keys, allowed)
    probs = jnp.exp(scores - log_total[..., None])
    prob_grad = jnp.einsum("hqe,hke->hqk", out_low, values, preferred_element_type=jnp.float32)
    score_grad = (probs * (prob_grad - delta[..., None])).astype(jnp.bfloat16)
    query_grad = jnp.einsum(
        "hqk,hke->hqe", score_grad, keys, preferred_element_type=jnp.float32
    ) * HEAD ** (-0.5)
    key_grad = jnp.einsum(
        "hqk,hqe->hke", score_grad, query, preferred_element_type=jnp.float32
    ) * HEAD ** (-0.5)
    value_grad = jnp.einsum(
        "hqk,hqe->hke", probs.astype(jnp.bfloat16), out_low, preferred_element_type=jnp.float32
    )
    return (query_grad, key_grad, value_grad)


def layer_forward(seq_in, mem_in, seg_float, params):
    matrices, ffn_up, ffn_down, up_bias, gains, shifts = params
    gains = gains.astype(jnp.float32)
    shifts = shifts.astype(jnp.float32)
    seq_low = seq_in.astype(jnp.bfloat16)
    mem_low = mem_in.astype(jnp.bfloat16)
    seq_qkv = stacked_linear(seq_low, matrices[0:3])
    mem_qkv = stacked_linear(mem_low, matrices[0:3])
    seq_query, seq_keys, seq_values = (
        split_heads(seq_qkv[0]),
        split_heads(seq_qkv[1]),
        split_heads(seq_qkv[2]),
    )
    mem_query, mem_keys, mem_values = (
        split_heads(mem_qkv[0]),
        split_heads(mem_qkv[1]),
        split_heads(mem_qkv[2]),
    )
    state = absorb(fresh(seq_query), seq_query, mem_keys, mem_values, None)
    travel = (seq_keys, seq_values, seg_float)
    for step in range(lax.axis_size("blk")):
        allowed = seg_float[:, None] == travel[2][None, :]
        state = absorb(state, seq_query, travel[0], travel[1], allowed)
        if step + 1 < lax.axis_size("blk"):
            travel = passed_along((travel[0], travel[1], travel[2]), "blk", 1)
    seq_out, seq_lse = finish(state)
    mem_state = memory_over_sequence(mem_query, seq_keys, seq_values)
    mem_state = absorb(mem_state, mem_query, mem_keys, mem_values, None)
    mem_out, mem_lse = finish(mem_state)
    full_low = jnp.concatenate([join_heads(mem_out), join_heads(seq_out)], 0).astype(jnp.bfloat16)
    joint_pre = jnp.concatenate([mem_in, seq_in], 0) + linear(full_low, matrices[3])
    joint_one = normalize(joint_pre, gains[0], shifts[0])
    mem_one, seq_one = (joint_one[:MEM], joint_one[MEM:])
    mem_one_low = mem_one.astype(jnp.bfloat16)
    seq_one_low = seq_one.astype(jnp.bfloat16)
    read_query = split_heads(linear(mem_one_low, matrices[4]).astype(jnp.bfloat16))
    read_kv = stacked_linear(seq_one_low, matrices[5:7])
    read_keys, read_values = (split_heads(read_kv[0]), split_heads(read_kv[1]))
    read_out, read_lse = finish(memory_over_sequence(read_query, read_keys, read_values))
    read_low = join_heads(read_out).astype(jnp.bfloat16)
    mem_pre = mem_one + linear(read_low, matrices[7])
    mem_two = normalize(mem_pre, gains[1], shifts[1])
    mem_two_low = mem_two.astype(jnp.bfloat16)
    write_query = split_heads(linear(seq_one_low, matrices[8]).astype(jnp.bfloat16))
    write_kv = stacked_linear(mem_two_low, matrices[9:11])
    write_keys, write_values = (split_heads(write_kv[0]), split_heads(write_kv[1]))
    write_out, write_lse = finish(
        absorb(fresh(write_query), write_query, write_keys, write_values, None)
    )
    write_low = join_heads(write_out).astype(jnp.bfloat16)
    seq_pre = seq_one + linear(write_low, matrices[11])
    seq_two = normalize(seq_pre, gains[2], shifts[2])
    feed_low = jnp.concatenate([mem_two_low, seq_two.astype(jnp.bfloat16)], 0)
    hidden_pre = linear(feed_low, ffn_up) + up_bias.astype(jnp.float32)
    hidden_low = jax.nn.gelu(hidden_pre).astype(jnp.bfloat16)
    feed_pre = jnp.concatenate([mem_two, seq_two], 0) + linear(hidden_low, ffn_down) + shifts[4]
    joint_three = normalize(feed_pre, gains[3], shifts[3])
    saved = dict(
        seq_low=seq_low,
        mem_low=mem_low,
        seq_query=seq_query,
        seq_keys=seq_keys,
        seq_values=seq_values,
        mem_query=mem_query,
        mem_keys=mem_keys,
        mem_values=mem_values,
        seq_out=seq_out,
        seq_lse=seq_lse,
        mem_out=mem_out,
        mem_lse=mem_lse,
        full_low=full_low,
        joint_pre=joint_pre,
        mem_one_low=mem_one_low,
        seq_one_low=seq_one_low,
        read_query=read_query,
        read_keys=read_keys,
        read_values=read_values,
        read_out=read_out,
        read_lse=read_lse,
        read_low=read_low,
        mem_pre=mem_pre,
        mem_two_low=mem_two_low,
        write_query=write_query,
        write_keys=write_keys,
        write_values=write_values,
        write_out=write_out,
        write_lse=write_lse,
        write_low=write_low,
        seq_pre=seq_pre,
        feed_low=feed_low,
        hidden_pre=hidden_pre,
        hidden_low=hidden_low,
        feed_pre=feed_pre,
    )
    return (joint_three[MEM:], joint_three[:MEM], saved)


def layer_backward(seq_grad, mem_grad, seg_float, params, saved):
    matrices, ffn_up, ffn_down, up_bias, gains, shifts = params
    gains = gains.astype(jnp.float32)
    shifts = shifts.astype(jnp.float32)
    share = 1.0 / lax.axis_size("blk")
    matrix_grads = [None] * 12
    feed_pre = saved["feed_pre"]
    mem_feed, gain_three_mem, shift_three_mem = norm_back(
        feed_pre[:MEM], gains[3], shifts[3], mem_grad
    )
    seq_feed, gain_three_seq, shift_three_seq = norm_back(
        feed_pre[MEM:], gains[3], shifts[3], seq_grad
    )
    feed_grad_low = jnp.concatenate([mem_feed, seq_feed], 0).astype(jnp.bfloat16)
    down_bias_grad = row_total(feed_grad_low, share)
    down_grad = mixed_grad(saved["hidden_low"], feed_grad_low, share)
    hidden_grad = input_grad(feed_grad_low, ffn_down)
    gelu_out, gelu_pull = jax.vjp(jax.nn.gelu, saved["hidden_pre"])
    pre_grad_low = gelu_pull(hidden_grad)[0].astype(jnp.bfloat16)
    bias_grad = row_total(pre_grad_low, share)
    up_grad = mixed_grad(saved["feed_low"], pre_grad_low, share)
    feed_in_grad = input_grad(pre_grad_low, ffn_up)
    mem_two_grad = mem_feed + feed_in_grad[:MEM]
    seq_two_grad = seq_feed + feed_in_grad[MEM:]
    seq_pre_grad, gain_two, shift_two = norm_back(
        saved["seq_pre"], gains[2], shifts[2], seq_two_grad
    )
    write_grad_low = seq_pre_grad.astype(jnp.bfloat16)
    matrix_grads[11] = weight_grad(saved["write_low"], write_grad_low)
    write_out_low = split_heads(input_grad(write_grad_low, matrices[11]).astype(jnp.bfloat16))
    delta = jnp.sum(write_out_low.astype(jnp.float32) * saved["write_out"], -1)
    query_grad, key_grad, value_grad = attend_back(
        saved["write_query"],
        saved["write_keys"],
        saved["write_values"],
        None,
        saved["write_lse"],
        write_out_low,
        delta,
    )
    key_grad, value_grad = memory_total((key_grad, value_grad))
    query_low = join_heads(query_grad).astype(jnp.bfloat16)
    key_low = join_heads(key_grad).astype(jnp.bfloat16)
    value_low = join_heads(value_grad).astype(jnp.bfloat16)
    matrix_grads[8] = weight_grad(saved["seq_one_low"], query_low)
    matrix_grads[9] = share * weight_grad(saved["mem_two_low"], key_low)
    matrix_grads[10] = share * weight_grad(saved["mem_two_low"], value_low)
    seq_one_grad = seq_pre_grad + input_grad(query_low, matrices[8])
    mem_two_grad = (
        mem_two_grad + input_grad(key_low, matrices[9]) + input_grad(value_low, matrices[10])
    )
    mem_pre_grad, gain_one, shift_one = norm_back(
        saved["mem_pre"], gains[1], shifts[1], mem_two_grad
    )
    read_grad_low = mem_pre_grad.astype(jnp.bfloat16)
    matrix_grads[7] = share * weight_grad(saved["read_low"], read_grad_low)
    read_out_low = split_heads(input_grad(read_grad_low, matrices[7]).astype(jnp.bfloat16))
    delta = jnp.sum(read_out_low.astype(jnp.float32) * saved["read_out"], -1)
    query_grad, key_grad, value_grad = attend_back(
        saved["read_query"],
        saved["read_keys"],
        saved["read_values"],
        None,
        saved["read_lse"],
        read_out_low,
        delta,
    )
    query_grad = memory_total((query_grad,))[0]
    query_low = join_heads(query_grad).astype(jnp.bfloat16)
    key_low = join_heads(key_grad).astype(jnp.bfloat16)
    value_low = join_heads(value_grad).astype(jnp.bfloat16)
    matrix_grads[4] = share * weight_grad(saved["mem_one_low"], query_low)
    matrix_grads[5] = weight_grad(saved["seq_one_low"], key_low)
    matrix_grads[6] = weight_grad(saved["seq_one_low"], value_low)
    mem_one_grad = mem_pre_grad + input_grad(query_low, matrices[4])
    seq_one_grad = (
        seq_one_grad + input_grad(key_low, matrices[5]) + input_grad(value_low, matrices[6])
    )
    joint_pre = saved["joint_pre"]
    mem_joint, gain_zero_mem, shift_zero_mem = norm_back(
        joint_pre[:MEM], gains[0], shifts[0], mem_one_grad
    )
    seq_joint, gain_zero_seq, shift_zero_seq = norm_back(
        joint_pre[MEM:], gains[0], shifts[0], seq_one_grad
    )
    joint_grad_low = jnp.concatenate([mem_joint, seq_joint], 0).astype(jnp.bfloat16)
    matrix_grads[3] = mixed_grad(saved["full_low"], joint_grad_low, share)
    attn_grad = input_grad(joint_grad_low, matrices[3]).astype(jnp.bfloat16)
    mem_out_low = split_heads(attn_grad[:MEM])
    seq_out_low = split_heads(attn_grad[MEM:])
    mem_delta = jnp.sum(mem_out_low.astype(jnp.float32) * saved["mem_out"], -1)
    seq_delta = jnp.sum(seq_out_low.astype(jnp.float32) * saved["seq_out"], -1)
    seq_query, seq_keys, seq_values = (saved["seq_query"], saved["seq_keys"], saved["seq_values"])
    mem_query, mem_keys, mem_values = (saved["mem_query"], saved["mem_keys"], saved["mem_values"])
    seq_q_grad, mem_k_part, mem_v_part = attend_back(
        seq_query, mem_keys, mem_values, None, saved["seq_lse"], seq_out_low, seq_delta
    )
    travel = (seq_keys, seq_values, seg_float)
    moving = (jnp.zeros(seq_keys.shape, jnp.float32), jnp.zeros(seq_values.shape, jnp.float32))
    for step in range(lax.axis_size("blk")):
        allowed = seg_float[:, None] == travel[2][None, :]
        query_grad, key_grad, value_grad = attend_back(
            seq_query, travel[0], travel[1], allowed, saved["seq_lse"], seq_out_low, seq_delta
        )
        seq_q_grad = seq_q_grad + query_grad
        moving = (moving[0] + key_grad, moving[1] + value_grad)
        if step + 1 < lax.axis_size("blk"):
            travel = passed_along(
                (for_sending(travel[0]), for_sending(travel[1]), travel[2]), "blk", 1
            )
        moving = (
            passed_along(moving[0].astype(jnp.bfloat16), "blk", 1).astype(jnp.float32),
            passed_along(moving[1].astype(jnp.bfloat16), "blk", 1).astype(jnp.float32),
        )
    mem_q_part, key_grad, value_grad = attend_back(
        mem_query, seq_keys, seq_values, None, saved["mem_lse"], mem_out_low, mem_delta
    )
    seq_k_grad = moving[0] + key_grad
    seq_v_grad = moving[1] + value_grad
    mem_q_part, mem_k_part, mem_v_part = memory_total((mem_q_part, mem_k_part, mem_v_part))
    query_grad, key_grad, value_grad = attend_back(
        mem_query, mem_keys, mem_values, None, saved["mem_lse"], mem_out_low, mem_delta
    )
    mem_qkv_low = jnp.stack(
        [
            join_heads(mem_q_part + query_grad),
            join_heads(mem_k_part + key_grad),
            join_heads(mem_v_part + value_grad),
        ]
    ).astype(jnp.bfloat16)
    seq_qkv_low = jnp.stack(
        [join_heads(seq_q_grad), join_heads(seq_k_grad), join_heads(seq_v_grad)]
    ).astype(jnp.bfloat16)
    first_grads = share * jnp.einsum(
        "nd,jne->jde", saved["mem_low"], mem_qkv_low, preferred_element_type=jnp.float32
    )
    first_grads = first_grads + jnp.einsum(
        "nd,jne->jde", saved["seq_low"], seq_qkv_low, preferred_element_type=jnp.float32
    )
    matrix_grads[0], matrix_grads[1], matrix_grads[2] = (
        first_grads[0],
        first_grads[1],
        first_grads[2],
    )
    mem_in_grad = mem_joint + jnp.einsum(
        "jne,jde->nd", mem_qkv_low, matrices[0:3], preferred_element_type=jnp.float32
    )
    seq_in_grad = seq_joint + jnp.einsum(
        "jne,jde->nd", seq_qkv_low, matrices[0:3], preferred_element_type=jnp.float32
    )
    gain_grads = jnp.stack(
        [
            share * gain_zero_mem + gain_zero_seq,
            share * gain_one,
            gain_two,
            share * gain_three_mem + gain_three_seq,
        ]
    )
    shift_grads = jnp.stack(
        [
            share * shift_zero_mem + shift_zero_seq,
            share * shift_one,
            shift_two,
            share * shift_three_mem + shift_three_seq,
            down_bias_grad,
        ]
    )
    layer_grads = (jnp.stack(matrix_grads), up_grad, down_grad, bias_grad, gain_grads, shift_grads)
    return (seq_in_grad, mem_in_grad, layer_grads)


def local(
    tokens,
    segments,
    memory_init,
    attn_weights,
    ffn_in,
    ffn_out,
    ffn_bias,
    norm_gain,
    norm_shift,
    out_grad,
    memory_cot,
):
    shard_attn = attn_weights.astype(jnp.bfloat16)
    shard_up = ffn_in.astype(jnp.bfloat16)
    shard_down = ffn_out.astype(jnp.bfloat16)
    shard_bias = ffn_bias.astype(jnp.bfloat16)
    shard_gain = norm_gain.astype(jnp.bfloat16)
    shard_shift = norm_shift.astype(jnp.bfloat16)
    shard_memory = memory_init.astype(jnp.bfloat16)
    gathered = (
        lax.all_gather(shard_attn, ("dp", "blk"), axis=2, tiled=True),
        lax.all_gather(shard_up, ("dp", "blk"), axis=1, tiled=True),
        lax.all_gather(shard_down, ("dp", "blk"), axis=1, tiled=True),
        lax.all_gather(shard_bias, ("dp", "blk"), axis=1, tiled=True),
        lax.all_gather(shard_gain, ("dp", "blk"), axis=2, tiled=True),
        lax.all_gather(shard_shift, ("dp", "blk"), axis=2, tiled=True),
        lax.all_gather(shard_memory, ("dp", "blk"), axis=1, tiled=True),
    )
    seg_float = segments[0].astype(jnp.bfloat16)
    seq_state = tokens[0].astype(jnp.float32)
    mem_state = gathered[6].astype(jnp.float32)
    layers = attn_weights.shape[0]
    kept = []
    for index in range(layers):
        params = tuple((member[index] for member in gathered[:6]))
        seq_state, mem_state, saved = layer_forward(seq_state, mem_state, seg_float, params)
        kept.append(saved)
    seq_grad = out_grad[0].astype(jnp.float32)
    mem_grad = memory_cot[0].astype(jnp.float32)
    share = 1.0 / lax.axis_size("blk")
    grads_list = [None] * layers
    for index in reversed(range(layers)):
        params = tuple((member[index] for member in gathered[:6]))
        seq_grad, mem_grad, layer_grads = layer_backward(
            seq_grad, mem_grad, seg_float, params, kept[index]
        )
        grads_list[index] = layer_grads
    stacked = [
        jnp.stack([grads_list[index][member] for index in range(layers)]) for member in range(6)
    ]
    summed = (
        lax.psum_scatter(stacked[0], ("dp", "blk"), scatter_dimension=2, tiled=True),
        lax.psum_scatter(stacked[1], ("dp", "blk"), scatter_dimension=1, tiled=True),
        lax.psum_scatter(stacked[2], ("dp", "blk"), scatter_dimension=1, tiled=True),
        lax.psum_scatter(stacked[3], ("dp", "blk"), scatter_dimension=1, tiled=True),
        lax.psum_scatter(stacked[4], ("dp", "blk"), scatter_dimension=2, tiled=True),
        lax.psum_scatter(stacked[5], ("dp", "blk"), scatter_dimension=2, tiled=True),
        lax.psum_scatter(mem_grad * share, ("dp", "blk"), scatter_dimension=1, tiled=True),
    )
    return (
        seq_state.astype(jnp.bfloat16)[None],
        mem_state[None],
        seq_grad[None],
        summed[6],
        summed[0],
        summed[1],
        summed[2],
        summed[3],
        summed[4],
        summed[5],
    )


def solution(mesh):
    in_specs = (
        P("dp", "blk", None),
        P("dp", "blk"),
        P(None, ("dp", "blk")),
        P(None, None, ("dp", "blk"), None),
        P(None, ("dp", "blk"), None),
        P(None, ("dp", "blk"), None),
        P(None, ("dp", "blk")),
        P(None, None, ("dp", "blk")),
        P(None, None, ("dp", "blk")),
        P("dp", "blk", None),
        P("dp", None, None),
    )
    out_specs = (
        P("dp", "blk", None),
        P("dp", None, None),
        P("dp", "blk", None),
        P(None, ("dp", "blk")),
        P(None, None, ("dp", "blk"), None),
        P(None, ("dp", "blk"), None),
        P(None, ("dp", "blk"), None),
        P(None, ("dp", "blk")),
        P(None, None, ("dp", "blk")),
        P(None, None, ("dp", "blk")),
    )
    return jax.shard_map(local, mesh=mesh, in_specs=in_specs, out_specs=out_specs, check_vma=False)
```

profile of v0, /device:TPU:0, one launch (start us, length us, event | category | flops | bytes accessed | tf_op | source)
XLA Modules:
  0.0 2025.7 jit_solution(14898270402862703654)
XLA Ops:
  14.2 42.7 %all-gather.12 = bf16[32,64,2]{1,2,0:T(2,128)(2,1)S(1)} all-gather(bf16[1,64,2]{1,2,0:T(2,128)(2,1)S(1)} %convert_bitcast_fusion.6), channel_id=1, replica_groups=mesh['dp'=8,'blk'=4] {'dp','blk'}, dimensions={0}, use_global_device_ids=true | all-gather | bytes 8448 | tf_op jit(solution)/shard_map/all_gather | solution.py:459
  57.7 38.6 %all_gather.83 = bf16[2,4,512]{1,0,2:T(2,128)(2,1)S(1)} all-gather(bf16[2,4,16]{1,0,2:T(2,128)(2,1)S(1)} %copy.560), channel_id=1, replica_groups=mesh['dp'=8,'blk'=4] {'dp','blk'}, dimensions={2}, use_global_device_ids=true | all-gather | bytes 8448 | tf_op jit(solution)/shard_map/all_gather | solution.py:460
  96.3 39.1 %all_gather.84 = bf16[2,5,512]{1,0,2:T(2,128)(2,1)S(1)} all-gather(bf16[2,5,16]{1,0,2:T(2,128)(2,1)S(1)} %copy.561), channel_id=1, replica_groups=mesh['dp'=8,'blk'=4] {'dp','blk'}, dimensions={2}, use_global_device_ids=true | all-gather | bytes 10560 | tf_op jit(solution)/shard_map/all_gather | solution.py:461
  136.1 17.1 slice_reduce_fusion.8
  153.2 13.3 slice_reduce_fusion.9
  170.0 37.2 %all_gather.77 = bf16[20,512]{0,1:T(8,128)(2,1)S(1)} all-gather(bf16[20,16]{0,1:T(8,128)(2,1)S(1)} %convert_element_type.1051), channel_id=1, replica_groups=mesh['dp'=8,'blk'=4] {'dp','blk'}, dimensions={1}, use_global_device_ids=true | all-gather | bytes 21120 | tf_op jit(solution)/shard_map/all_gather | solution.py:462
  218.5 5.2 all-gather
  223.6 5.2 all-gather.1
  229.1 5.5 all-gather.2
  240.4 3.7 collective-permute-done.4
  244.1 2.8 collective-permute-done.5
  247.5 2.4 collective-permute-done.7
  269.4 5.5 all-gather.5
  275.0 5.2 all-gather.3
  280.2 5.3 all-gather.4
  285.5 2.9 while.77
  308.1 4.7 multiply_convert_fusion.1
  312.8 2.9 fusion.558
  332.4 3.4 fusion.562
  339.0 2.5 fusion.34
  350.7 5.4 all-gather.6
  356.7 5.1 all-gather.7
  363.6 5.5 all-gather.8
  369.9 11.2 while.78
  395.2 3.2 collective-permute-done.12
  398.4 2.8 collective-permute-done.11
  401.8 5.3 collective-permute-done.13
  428.3 2.2 convolution_convert_fusion.12
  436.0 5.4 all-gather.9
  441.9 5.1 all-gather.10
  449.0 5.9 all-gather.11
  455.6 11.2 while.79
  516.8 12.7 all-reduce.4
  551.9 11.6 psum.86
  586.2 2.8 convolution_convert_fusion.9
  600.6 13.4 all-reduce.3
  627.1 3.1 fusion.461
  630.3 2.6 multiply_reduce_fusion.30
  650.2 4.2 collective-permute-done.16
  654.8 2.5 collective-permute-done.20
  658.0 2.6 collective-permute-done.17
  675.3 3.3 multiply_reduce_fusion.6
  696.9 12.2 all-reduce.2
  727.8 11.4 psum.92
  754.6 2.8 convolution_convert_fusion.6
  768.9 13.4 all-reduce.1
  786.3 2.5 fusion.100
  798.1 2.3 multiply_convert_fusion.2
  802.8 2.2 fusion.296
  820.9 3.3 collective-permute-done.24
  824.3 2.7 collective-permute-done.28
  852.6 14.6 pad_maximum_fusion
  867.1 37.5 %copy.684 = f32[2,12,512,512]{3,0,1,2:T(2,128)} copy(f32[2,12,512,512]{2,3,1,0:T(8,128)} %pad_maximum_fusion) | data formatting | bytes 50331648 | tf_op jit(solution)/shard_map/stack | solution.py:484
  906.8 2.7 add_bitcast_fusion.2
  913.1 2.9 add_bitcast_fusion.3
  916.1 7.9 pad_maximum_fusion.1
  928.8 4.3 pad_maximum_fusion.2
  937.5 124.6 %reduce-scatter.21.cloned.1.call-done = f32[64,2]{1,0:T(8,128)} async-done(((f32[2048,2]{1,0:T(8,128)}), f32[64,2]{1,0:T(8,128)}) %reduce-scatter.21.cloned.1.call-update) | async-done | bytes 528
  1063.5 130.1 %reduce-scatter.25.cloned.1.call-done = f32[16,10]{1,0:T(8,128)} async-done(((f32[512,10]{1,0:T(8,128)}), f32[16,10]{1,0:T(8,128)}) %reduce-scatter.25.cloned.1.call-update) | async-done | bytes 656
  1195.0 2.8 fusion.98
  1197.8 389.3 %all-reduce.7.cloned.1.call-done = f32[2,12,512,512]{3,0,1,2:T(2,128)} async-done(((f32[2,12,512,512]{3,0,1,2:T(2,128)}), f32[2,12,512,512]{3,0,1,2:T(2,128)}) %all-reduce.7.cloned.1.call-update) | async-done | bytes 25165840
  1589.9 133.2 %reduce-scatter.19.cloned.1.call-done = f32[16,20]{1,0:T(8,128)} async-done(((f32[512,20]{1,0:T(8,128)}), f32[16,20]{1,0:T(8,128)}) %reduce-scatter.19.cloned.1.call-update) | async-done | bytes 1296
  1723.1 147.8 %reduce-scatter.15.cloned.1.call-done = f32[2,16,2048]{2,1,0:T(8,128)} async-done(((f32[2,512,2048]{2,1,0:T(8,128)}), f32[2,16,2048]{2,1,0:T(8,128)}) %reduce-scatter.15.cloned.1.call-update) | async-done | bytes 262160 | tf_op jit(solution)/shard_map/reduce_scatter | solution.py:488
  1870.9 147.6 %reduce-scatter.17.cloned.1.call-done = f32[2,64,512]{2,1,0:T(8,128)} async-done(((f32[2,2048,512]{2,1,0:T(8,128)}), f32[2,64,512]{2,1,0:T(8,128)}) %reduce-scatter.17.cloned.1.call-update) | async-done | bytes 262160 | tf_op jit(solution)/shard_map/reduce_scatter | solution.py:489
  (1512 shorter events, 460.5 us)
Async XLA Ops:
  7.2 201.5 %all-gather.17.cloned.1.call-start = ((), (), s32[]{:S(2)}) async-start(), calls=%async_computation.6 | async-start | bytes 12976128 | tf_op jit(solution)/shard_map/all_gather | solution.py:456
  9.3 298.9 %all-gather.19.cloned.1.call-start = ((), (), s32[]{:S(2)}) async-start(), calls=%async_computation.7 | async-start | bytes 4325376 | tf_op jit(solution)/shard_map/all_gather | solution.py:457
  11.0 301.8 %all-gather.21.cloned.1.call-start = ((), (), s32[]{:S(2)}) async-start(), calls=%async_computation.8 | async-start | bytes 4325376 | tf_op jit(solution)/shard_map/all_gather | solution.py:458
  11.7 154.9 %collective-permute-start = (bf16[256]{0:T(256)(128)(2,1)S(1)}, bf16[256]{0:T(256)(128)(2,1)S(1)}, u32[]{:S(2)}, u32[]{:S(2)}) collective-permute-start(bf16[256]{0:T(256)(128)(2,1)S(1)} %convert_reduce_fusion.2), channel_id=1, source_target_pairs={{0,1},{1,2},{2,3},{3,0},{4,5},{5,6},{6,7},{7,4},{8,9},{9,10},{10,1... | collective-permute-start | bytes 1544 | tf_op jit(solution)/shard_map/ppermute | solution.py:45
  13.8 922.2 %reduce-scatter.23.cloned.1.call-start = ((), (), s32[]{:S(2)}) async-start(), calls=%async_computation.13 | async-start | bytes 270336
  136.1 30.5 %copy-start.232 = (bf16[1,20,512]{2,1,0:T(8,128)(2,1)S(1)}, bf16[1,20,512]{2,1,0:T(8,128)(2,1)}, u32[]{:S(2)}) copy-start(bf16[1,20,512]{2,1,0:T(8,128)(2,1)} %param.29) | copy-start | bytes 61444
  136.1 31.9 %copy-start.378 = (f32[20,16]{0,1:T(8,128)S(1)}, f32[20,16]{0,1:T(8,128)}, u32[]{:S(2)}) copy-start(f32[20,16]{0,1:T(8,128)} %param.21) | copy-start | bytes 3844
  153.2 57.5 %copy-start.215 = (bf16[1,256,512]{2,1,0:T(8,128)(2,1)S(1)}, bf16[1,256,512]{2,1,0:T(8,128)(2,1)}, u32[]{:S(2)}) copy-start(bf16[1,256,512]{2,1,0:T(8,128)(2,1)} %param.19) | copy-start | bytes 786436
  166.6 3.4 collective-permute-start.3
  170.0 37.9 %collective-permute-start.6 = (bf16[256]{0:T(256)(128)(2,1)S(1)}, bf16[256]{0:T(256)(128)(2,1)S(1)}, u32[]{:S(2)}, u32[]{:S(2)}) collective-permute-start(bf16[256]{0:T(256)(128)(2,1)S(1)} %collective-permute-done.3), channel_id=1, source_target_pairs={{0,1},{1,2},{2,3},{3,0},{4,5},{5,6},{6,7},{7,4},{8,9},{9,10},{10,1... | collective-permute-start | bytes 1544 | tf_op jit(solution)/shard_map/ppermute | solution.py:45
  208.7 38.2 %copy-start.189 = (pred[256,256]{0,1:T(8,128)(4,1)}, pred[256,256]{0,1:T(8,128)(4,1)S(1)}, u32[]{:S(2)}) copy-start(pred[256,256]{0,1:T(8,128)(4,1)S(1)} %get-tuple-element.1121) | copy-start | bytes 196612
  208.7 41.2 %copy-start.187 = (pred[256,256]{0,1:T(8,128)(4,1)}, pred[256,256]{0,1:T(8,128)(4,1)S(1)}, u32[]{:S(2)}) copy-start(pred[256,256]{0,1:T(8,128)(4,1)S(1)} %get-tuple-element.1122) | copy-start | bytes 196612
  213.1 24.9 %collective-permute-start.1 = (bf16[8,256,64]{1,2,0:T(8,128)(2,1)S(1)}, bf16[8,256,64]{1,2,0:T(8,128)(2,1)}, u32[]{:S(2)}, u32[]{:S(2)}) collective-permute-start(bf16[8,256,64]{1,2,0:T(8,128)(2,1)S(1)} %bitcast.1263), channel_id=1, source_target_pairs={{0,1},{1,2},{2,3},{3,0},{4,5},{5,6},{6,7},{7,4},{8,9},{9,10},{10,1... | collective-permute-start | bytes 786440 | tf_op jit(solution)/shard_map/ppermute | solution.py:45
  213.8 22.1 %copy-start.111 = (f32[8,20,20]{1,2,0:T(8,128)}, f32[8,20,20]{1,2,0:T(8,128)S(1)}, u32[]{:S(2)}) copy-start(f32[8,20,20]{1,2,0:T(8,128)S(1)} %get-tuple-element.1139) | copy-start | bytes 38404
  214.0 23.8 %copy-start.48 = (f32[8,256,20]{1,2,0:T(8,128)}, f32[8,256,20]{1,2,0:T(8,128)S(1)}, u32[]{:S(2)}) copy-start(f32[8,256,20]{1,2,0:T(8,128)S(1)} %get-tuple-element.1129) | copy-start | bytes 491524
  214.0 39.8 %copy-start.247 = (f32[8,256]{1,0:T(8,128)}, f32[8,256]{1,0:T(8,128)S(1)}, u32[]{:S(2)}) copy-start(f32[8,256]{1,0:T(8,128)S(1)} %get-tuple-element.1128) | copy-start | bytes 24580
  214.0 24.4 %collective-permute-start.2 = (bf16[8,256,64]{1,2,0:T(8,128)(2,1)S(1)}, bf16[8,256,64]{1,2,0:T(8,128)(2,1)}, u32[]{:S(2)}, u32[]{:S(2)}) collective-permute-start(bf16[8,256,64]{1,2,0:T(8,128)(2,1)S(1)} %bitcast.1257), channel_id=1, source_target_pairs={{0,1},{1,2},{2,3},{3,0},{4,5},{5,6},{6,7},{7,4},{8,9},{9,10},{10,1... | collective-permute-start | bytes 786440 | tf_op jit(solution)/shard_map/ppermute | solution.py:45
  216.8 33.9 %copy-start.234 = (f32[8,256]{1,0:T(8,128)}, f32[8,256]{1,0:T(8,128)S(1)}, u32[]{:S(2)}) copy-start(f32[8,256]{1,0:T(8,128)S(1)} %get-tuple-element.1003) | copy-start | bytes 24580
  218.1 35.8 %copy-start.60 = (f32[8,256,64]{1,2,0:T(8,128)}, f32[8,256,64]{1,2,0:T(8,128)S(1)}, u32[]{:S(2)}) copy-start(f32[8,256,64]{1,2,0:T(8,128)S(1)} %fusion.198) | copy-start | bytes 1572868
  238.1 6.1 collective-permute-start.4
  238.5 8.5 collective-permute-start.5
  244.1 5.8 collective-permute-start.7
  246.9 6.9 collective-permute-start.8
  265.9 19.7 copy-start.88
  269.0 26.2 %copy-start.54 = (f32[8,20,256]{2,1,0:T(8,128)}, f32[8,20,256]{2,1,0:T(8,128)S(1)}, u32[]{:S(2)}) copy-start(f32[8,20,256]{2,1,0:T(8,128)S(1)} %get-tuple-element.1143) | copy-start | bytes 491524
  328.1 64.7 %collective-permute-start.9 = (bf16[8,256,64]{1,2,0:T(8,128)(2,1)}, bf16[8,256,64]{1,2,0:T(8,128)(2,1)}, u32[]{:S(2)}, u32[]{:S(2)}) collective-permute-start(bf16[8,256,64]{1,2,0:T(8,128)(2,1)} %bitcast.95), channel_id=1, source_target_pairs={{0,1},{1,2},{2,3},{3,0},{4,5},{5,6},{6,7},{7,4},{8,9},{9,10},{10,1... | collective-permute-start | bytes 786440 | tf_op jit(solution)/shard_map/ppermute | solution.py:45
  336.9 244.5 %copy-start.42 = (bf16[1,256,512]{1,2,0:T(8,128)(2,1)}, bf16[1,256,512]{1,2,0:T(8,128)(2,1)S(1)}, u32[]{:S(2)}) copy-start(bf16[1,256,512]{1,2,0:T(8,128)(2,1)S(1)} %copy.575) | copy-start | bytes 786436
  336.9 55.4 %collective-permute-start.10 = (bf16[8,256,64]{1,2,0:T(8,128)(2,1)S(1)}, bf16[8,256,64]{1,2,0:T(8,128)(2,1)}, u32[]{:S(2)}, u32[]{:S(2)}) collective-permute-start(bf16[8,256,64]{1,2,0:T(8,128)(2,1)S(1)} %bitcast.1252), channel_id=1, source_target_pairs={{0,1},{1,2},{2,3},{3,0},{4,5},{5,6},{6,7},{7,4},{8,9},{9,10},{10,1... | collective-permute-start | bytes 786440 | tf_op jit(solution)/shard_map/ppermute | solution.py:45
  392.3 6.1 collective-permute-start.12
  392.8 8.5 collective-permute-start.11
  398.4 13.1 collective-permute-start.14
  401.2 5.8 collective-permute-start.13
  634.6 13.5 collective-permute-start.15
  634.7 14.0 collective-permute-start.19
  648.6 5.8 collective-permute-start.16
  649.2 8.1 collective-permute-start.20
  654.5 6.1 collective-permute-start.17
  657.3 6.1 collective-permute-start.21
  661.4 6.5 collective-permute-start.18
  664.2 7.4 collective-permute-start.22
  689.1 21.4 %copy-start.126 = (f32[20,512]{1,0:T(8,128)S(1)}, f32[20,512]{1,0:T(8,128)}, u32[]{:S(2)}) copy-start(f32[20,512]{1,0:T(8,128)} %copy-done.125) | copy-start | bytes 122884
  712.4 30.4 %copy-start.40 = (f32[256,512]{1,0:T(8,128)S(1)}, f32[256,512]{1,0:T(8,128)}, u32[]{:S(2)}) copy-start(f32[256,512]{1,0:T(8,128)} %copy-done.39) | copy-start | bytes 1572868
  719.1 20.1 copy-start.201
  719.1 20.1 copy-start.317
  719.1 23.7 %copy-start.338 = (f32[256]{0:T(256)S(1)}, f32[256]{0:T(256)}, u32[]{:S(2)}) copy-start(f32[256]{0:T(256)} %copy-done.337) | copy-start | bytes 3076
  788.7 28.0 %collective-permute-start.23 = (bf16[8,256,64]{1,2,0:T(8,128)(2,1)}, bf16[8,256,64]{1,2,0:T(8,128)(2,1)}, u32[]{:S(2)}, u32[]{:S(2)}) collective-permute-start(bf16[8,256,64]{1,2,0:T(8,128)(2,1)} %fusion.100), channel_id=1, source_target_pairs={{0,1},{1,2},{2,3},{3,0},{4,5},{5,6},{6,7},{7,4},{8,9},{9,10},{10,1... | collective-permute-start | bytes 786440 | tf_op jit(solution)/shard_map/ppermute | solution.py:45
  788.7 29.5 %collective-permute-start.27 = (bf16[8,256,64]{1,2,0:T(8,128)(2,1)}, bf16[8,256,64]{1,2,0:T(8,128)(2,1)}, u32[]{:S(2)}, u32[]{:S(2)}) collective-permute-start(bf16[8,256,64]{1,2,0:T(8,128)(2,1)} %convolution_convert_fusion.6), channel_id=1, source_target_pairs={{0,1},{1,2},{2,3},{3,0},{4,5},{5,6},{6,7},{7,4},{8,9},{9,10},{10,1... | collective-permute-start | bytes 786440 | tf_op jit(solution)/shard_map/ppermute | solution.py:45
  797.8 264.3 %reduce-scatter.21.cloned.1.call-start = ((), (), s32[]{:S(2)}) async-start(), calls=%async_computation.12 | async-start | bytes 1081344
  818.2 6.0 collective-permute-start.24
  819.7 7.2 collective-permute-start.28
  824.2 5.9 collective-permute-start.25
  827.1 6.0 collective-permute-start.29
  828.5 365.0 %reduce-scatter.25.cloned.1.call-start = ((), (), s32[]{:S(2)}) async-start(), calls=%async_computation.14 | async-start | bytes 270336
  830.9 8.7 collective-permute-start.26
  833.9 9.4 collective-permute-start.30
  839.3 747.8 %all-reduce.7.cloned.1.call-start = ((), (), s32[]{:S(2)}) async-start(), calls=%async_computation.15 | async-start | bytes 50331648
  904.7 818.4 %reduce-scatter.19.cloned.1.call-start = ((), (), s32[]{:S(2)}) async-start(), calls=%async_computation.11 | async-start | bytes 270336
  916.0 954.9 %reduce-scatter.15.cloned.1.call-start = ((), (), s32[]{:S(2)}) async-start(), calls=%async_computation.9 | async-start | bytes 8650752 | tf_op jit(solution)/shard_map/reduce_scatter | solution.py:488
  924.0 1094.6 %reduce-scatter.17.cloned.1.call-start = ((), (), s32[]{:S(2)}) async-start(), calls=%async_computation.10 | async-start | bytes 8650752 | tf_op jit(solution)/shard_map/reduce_scatter | solution.py:489
  933.2 261.9 %copy-start.96 = (f32[256,512]{1,0:T(8,128)S(1)}, f32[256,512]{1,0:T(8,128)}, u32[]{:S(2)}) copy-start(f32[256,512]{1,0:T(8,128)} %copy-done.95) | copy-start | bytes 1572868
  933.2 261.9 %copy-start.145 = (bf16[1,256,512]{2,1,0:T(8,128)(2,1)S(1)}, bf16[1,256,512]{2,1,0:T(8,128)(2,1)}, u32[]{:S(2)}) copy-start(bf16[1,256,512]{2,1,0:T(8,128)(2,1)} %copy.653) | copy-start | bytes 786436
  933.2 261.8 %copy-start.146 = (bf16[1,256,512]{2,1,0:T(8,128)(2,1)S(1)}, bf16[1,256,512]{2,1,0:T(8,128)(2,1)}, u32[]{:S(2)}) copy-start(bf16[1,256,512]{2,1,0:T(8,128)(2,1)} %copy.654) | copy-start | bytes 786436
  933.2 261.8 %copy-start.147 = (bf16[1,256,512]{2,1,0:T(8,128)(2,1)S(1)}, bf16[1,256,512]{2,1,0:T(8,128)(2,1)}, u32[]{:S(2)}) copy-start(bf16[1,256,512]{2,1,0:T(8,128)(2,1)} %copy.655) | copy-start | bytes 786436
  933.2 261.8 %copy-start.387 = (f32[256]{0:T(256)S(1)}, f32[256]{0:T(256)}, u32[]{:S(2)}) copy-start(f32[256]{0:T(256)} %copy-done.386) | copy-start | bytes 3076
  (411 other events, 1625.8 us)
Sparse Core Ops, SparseCore 0:
  11.5 100.0 all-gather.16
  114.6 62.5 all-gather.18
  180.1 61.0 all-gather.20
  797.9 131.2 reduce-scatter.22
  931.4 130.6 reduce-scatter.20
  1064.2 129.3 reduce-scatter.24
  1201.1 385.9 all-reduce.6
  1590.0 133.0 reduce-scatter.18
  1726.0 144.8 reduce-scatter.14
  1873.6 144.8 reduce-scatter.16
where the time goes:
time: 2040 us; the launch traced here: 2030 us
  waiting for transfers between devices  1120 us (55%)
  blocking collectives  297 us (15%)
  matrix products  241 us (12%)
  local copies, waits for them, and re-layouts  196 us (10%)
  other arithmetic  143 us (7%)
  between operations  20.5 us (1%)
    unnamed x15, waiting for transfers between devices  777 us
    reduce_scatter x1, waiting for transfers between devices, local(): lax.psum_scatter(stacked[1], ('dp', 'blk'), scatter_dimension=1, tiled=True)  148 us
    reduce_scatter x1, waiting for transfers between devices, local(): lax.psum_scatter(stacked[2], ('dp', 'blk'), scatter_dimension=1, tiled=True)  148 us
    psum x6, blocking collectives, memory_total(): lax.psum(for_sending(parts), 'blk')  74.6 us
    all_gather x12, blocking collectives, combined_all(): lax.all_gather(a.astype(kind), axis)  64.4 us
    ppermute x31, waiting for transfers between devices, passed_along(): return lax.ppermute(value, axis, pairs)  43.2 us
    unnamed x887, local copies, waits for them, and re-layouts  43.2 us
    all_gather x1, blocking collectives, local(): lax.all_gather(shard_bias, ('dp', 'blk'), axis=1, tiled=True)  42.7 us
  transfers between devices with their start and end apart: 41, of which 21 were waited for; matrix products, arithmetic and copies ran while one was open for 15% of the time, Pallas kernels for 0%

commit v1 on v0

--- a/solution.py
+++ b/solution.py
@@ -13,22 +13,16 @@
 
 
 def combined_all(array, axis, join):
-    gathered = jax.tree.map(
-        lambda a, kind: lax.all_gather(a.astype(kind), axis),
-        array,
-        jax.tree.map(lambda a: jnp.bfloat16 if a.dtype == jnp.float32 else a.dtype, array),
-    )
-
-    def take(source):
-        return jax.tree.map(
-            lambda a, own: lax.dynamic_index_in_dim(a, source, 0, False).astype(own.dtype),
-            gathered,
-            array,
-        )
-
-    return lax.fori_loop(
-        1, lax.axis_size(axis), lambda source, state: join(state, take(source)), take(0)
-    )
+    highest, total, accum = array
+    packed = jnp.concatenate([accum, highest[..., None], total[..., None]], -1)
+    gathered = lax.all_gather(packed, axis)
+    width = accum.shape[-1]
+    state = None
+    for source in range(lax.axis_size(axis)):
+        part = gathered[source]
+        part = (part[..., width], part[..., width + 1], part[..., :width])
+        state = part if state is None else join(state, part)
+    return state
 
 
 def for_sending(array):
@@ -445,26 +439,40 @@
     out_grad,
     memory_cot,
 ):
-    shard_attn = attn_weights.astype(jnp.bfloat16)
-    shard_up = ffn_in.astype(jnp.bfloat16)
-    shard_down = ffn_out.astype(jnp.bfloat16)
-    shard_bias = ffn_bias.astype(jnp.bfloat16)
-    shard_gain = norm_gain.astype(jnp.bfloat16)
-    shard_shift = norm_shift.astype(jnp.bfloat16)
-    shard_memory = memory_init.astype(jnp.bfloat16)
+    layers, count, rows, width = attn_weights.shape
+    per = ffn_in.shape[2] // width
+    small = [ffn_bias, norm_gain, norm_shift, memory_init]
+    sizes = [part.size for part in small]
+    flat = jnp.concatenate([part.astype(jnp.bfloat16).reshape(-1) for part in small])
+    blocks = -(-flat.size // (rows * width))
+    flat = jnp.pad(flat, (0, blocks * rows * width - flat.size))
+    packed = jnp.concatenate(
+        [
+            attn_weights.astype(jnp.bfloat16).reshape(layers * count, rows, width),
+            ffn_in.astype(jnp.bfloat16).reshape(layers, rows, per, width).transpose(0, 2, 1, 3).reshape(-1, rows, width),
+            ffn_out.astype(jnp.bfloat16).reshape(-1, rows, width),
+            flat.reshape(blocks, rows, width),
+        ]
+    )
+    everyone = lax.axis_size("dp") * lax.axis_size("blk")
+    whole = lax.all_gather(packed, ("dp", "blk"), axis=1, tiled=True)
+    one, two, three = (layers * count, layers * (count + per), layers * (count + 2 * per))
+    full_small = whole[three:].reshape(blocks, everyone, rows * width).transpose(1, 0, 2).reshape(everyone, -1)
+    starts = [sum(sizes[:k]) for k in range(5)]
+    pieces = [full_small[:, starts[k] : starts[k + 1]].reshape((everyone,) + small[k].shape) for k in range(4)]
+    full_pieces = [jnp.moveaxis(piece, 0, -2).reshape(piece.shape[1:-1] + (-1,)) for piece in pieces]
     gathered = (
-        lax.all_gather(shard_attn, ("dp", "blk"), axis=2, tiled=True),
-        lax.all_gather(shard_up, ("dp", "blk"), axis=1, tiled=True),
-        lax.all_gather(shard_down, ("dp", "blk"), axis=1, tiled=True),
-        lax.all_gather(shard_bias, ("dp", "blk"), axis=1, tiled=True),
-        lax.all_gather(shard_gain, ("dp", "blk"), axis=2, tiled=True),
-        lax.all_gather(shard_shift, ("dp", "blk"), axis=2, tiled=True),
-        lax.all_gather(shard_memory, ("dp", "blk"), axis=1, tiled=True),
+        whole[:one].reshape(layers, count, width, width),
+        whole[one:two].reshape(layers, per, width, width).transpose(0, 2, 1, 3).reshape(layers, width, per * width),
+        whole[two:three].reshape(layers, per, everyone, rows, width).transpose(0, 2, 1, 3, 4).reshape(layers, per * width, width),
+        full_pieces[0],
+        full_pieces[1],
+        full_pieces[2],
+        full_pieces[3],
     )
     seg_float = segments[0].astype(jnp.bfloat16)
     seq_state = tokens[0].astype(jnp.float32)
     mem_state = gathered[6].astype(jnp.float32)
-    layers = attn_weights.shape[0]
     kept = []
     for index in range(layers):
         params = tuple((member[index] for member in gathered[:6]))
@@ -483,14 +491,31 @@
     stacked = [
         jnp.stack([grads_list[index][member] for index in range(layers)]) for member in range(6)
     ]
+    tiny = [stacked[3], stacked[4], stacked[5], mem_grad * share]
+    tiny = [
+        jnp.moveaxis(part.reshape(part.shape[:-1] + (everyone, -1)), -2, 0).reshape(everyone, -1) for part in tiny
+    ]
+    tiny = jnp.concatenate(tiny, 1)
+    tiny = jnp.pad(tiny, ((0, 0), (0, blocks * rows * width - tiny.shape[1])))
+    outgoing = jnp.concatenate(
+        [
+            stacked[0].reshape(layers * count, width, width),
+            stacked[1].reshape(layers, width, per, width).transpose(0, 2, 1, 3).reshape(-1, width, width),
+            stacked[2].reshape(layers, everyone, per, rows, width).transpose(0, 2, 1, 3, 4).reshape(-1, width, width),
+            tiny.reshape(everyone, blocks, rows, width).transpose(1, 0, 2, 3).reshape(blocks, width, width),
+        ]
+    ).astype(jnp.bfloat16)
+    mine = lax.psum_scatter(outgoing, ("dp", "blk"), scatter_dimension=1, tiled=True).astype(jnp.float32)
+    mine_small = mine[three:].reshape(-1)
+    back = [mine_small[starts[k] : starts[k + 1]].reshape(small[k].shape) for k in range(4)]
     summed = (
-        lax.psum_scatter(stacked[0], ("dp", "blk"), scatter_dimension=2, tiled=True),
-        lax.psum_scatter(stacked[1], ("dp", "blk"), scatter_dimension=1, tiled=True),
-        lax.psum_scatter(stacked[2], ("dp", "blk"), scatter_dimension=1, tiled=True),
-        lax.psum_scatter(stacked[3], ("dp", "blk"), scatter_dimension=1, tiled=True),
-        lax.psum_scatter(stacked[4], ("dp", "blk"), scatter_dimension=2, tiled=True),
-        lax.psum_scatter(stacked[5], ("dp", "blk"), scatter_dimension=2, tiled=True),
-        lax.psum_scatter(mem_grad * share, ("dp", "blk"), scatter_dimension=1, tiled=True),
+        mine[:one].reshape(layers, count, rows, width),
+        mine[one:two].reshape(layers, per, rows, width).transpose(0, 2, 1, 3).reshape(layers, rows, per * width),
+        mine[two:three].reshape(layers, per * rows, width),
+        back[0],
+        back[1],
+        back[2],
+        back[3],
     )
     return (
         seq_state.astype(jnp.bfloat16)[None],

time: 2040 us -> 1150 us (0.56)
  waiting for transfers between devices: 1120 us -> 401 us
  blocking collectives: 297 us -> 101 us
  local copies, waits for them, and re-layouts: 196 us -> 218 us
    unnamed x15 -> x2, waiting for transfers between devices: 777 us -> 0.03 us
    all_gather x16 -> x4, blocking collectives: 222 us -> 26.9 us  [combined_all(): gathered = lax.all_gather(packed, axis)]
    all_gather x3 -> x1, waiting for transfers between devices: 0.01 us -> 131 us  [local(): whole = lax.all_gather(packed, ('dp', 'blk'), axis=1, tiled=True)]
    reduce_scatter x2 -> x1, waiting for transfers between devices: 295 us -> 225 us  [local(): lax.psum_scatter(outgoing, ('dp', 'blk'), scatter_dimension=1, tiled=True)]
    reshape x0 -> x19, local copies, waits for them, and re-layouts: none -> 35.8 us  [the longest x1 16.7 us: local(): stacked[0].reshape(layers * count, width, width)]
    another operation x1, local copies, waits for them, and re-layouts: 37.5 us -> 4.79 us  [local(): jnp.stack([grads_list[index][member] for index in range(layers)])]
    slice x2 -> x6, local copies, waits for them, and re-layouts: 30.5 us -> 0.91 us  [layer_forward(): joint_three = normalize(feed_pre, gains[3], shifts[3])]
    add x37 -> x0, other arithmetic: 23 us -> none  [the longest x12 10.7 us: combine_parts(): first[2] * fade_one[..., None] + second[2] * fade_two[..., None]]
  transfers between devices with their start and end apart: 41 -> 33, of which waited for: 21 -> 19; matrix products, arithmetic and copies ran while one was open for 15% -> 16% of each run, Pallas kernels for 0% -> 0%
where the time goes in v1:
time: 1150 us; the launch traced here: 1130 us
  waiting for transfers between devices  401 us (35%)
  matrix products  250 us (22%)
  local copies, waits for them, and re-layouts  218 us (19%)
  other arithmetic  126 us (11%)
  blocking collectives  101 us (9%)
  between operations  20 us (2%)
  starting transfers between devices  12.9 us (1%)
    reduce_scatter x1, waiting for transfers between devices, local(): lax.psum_scatter(outgoing, ('dp', 'blk'), scatter_dimension=1, tiled=True)  225 us
    all_gather x1, waiting for transfers between devices, local(): whole = lax.all_gather(packed, ('dp', 'blk'), axis=1, tiled=True)  131 us
    psum x6, blocking collectives, memory_total(): lax.psum(for_sending(parts), 'blk')  73.9 us
    unnamed x858, local copies, waits for them, and re-layouts  56.8 us
    ppermute x31, waiting for transfers between devices, passed_along(): return lax.ppermute(value, axis, pairs)  44.9 us
    dot_general x28, matrix products, weight_grad(): jnp.einsum('nd,ne->de', inputs, grads, preferred_element_type=jnp.float32)  37.1 us
    dot_general x22, matrix products, input_grad(): jnp.einsum('ne,de->nd', grads, weight, preferred_element_type=jnp.float32)  35.9 us
    all_gather x4, blocking collectives, combined_all(): gathered = lax.all_gather(packed, axis)  26.9 us
  transfers between devices with their start and end apart: 33, of which 19 were waited for; matrix products, arithmetic and copies ran while one was open for 16% of the time, Pallas kernels for 0%

profile of v1, /device:TPU:0, one launch (start us, length us, event | category | flops | bytes accessed | tf_op | source)
XLA Modules:
  0.0 1128.5 jit_solution(5917451056075397382)
XLA Ops:
  15.4 3.1 collective-permute-done
  18.7 2.8 collective-permute-done.3
  22.3 2.1 collective-permute-done.6
  25.2 131.2 %all-gather.6.cloned.1.call-done = bf16[41,512,512]{2,1,0:T(8,128)(2,1)} async-done(((bf16[41,16,512]{2,1,0:T(8,128)(2,1)}), bf16[41,512,512]{2,1,0:T(8,128)(2,1)}) %all-gather.6.cloned.1.call-update) | async-done | bytes 21495824 | tf_op jit(solution)/shard_map/all_gather | solution.py:458
  166.5 8.0 all-gather
  182.2 5.3 fusion.628
  187.5 2.5 copy.1888
  190.0 7.3 copy.1342
  197.3 4.6 fusion.631
  202.0 2.5 fusion.630
  224.8 2.8 collective-permute-done.4
  227.6 2.8 collective-permute-done.5
  231.2 2.2 collective-permute-done.7
  244.1 2.2 convolution_convert_fusion.21
  254.5 6.1 all-gather.1
  283.3 2.5 multiply_convert_fusion.1
  292.1 2.1 fusion.59
  303.4 6.6 all-gather.2
  340.4 3.7 collective-permute-done.11
  344.1 2.8 collective-permute-done.12
  347.5 2.4 collective-permute-done.13
  361.1 2.1 convolution_convert_fusion.20
  370.2 6.1 all-gather.3
  413.0 2.1 convolution_convert_fusion.19
  428.0 12.2 %all-reduce.5 = (bf16[20,512]{1,0:T(8,128)(2,1)}, bf16[20,512]{1,0:T(8,128)(2,1)}) all-reduce(bf16[20,512]{1,0:T(8,128)(2,1)} %convert_element_type.832, bf16[20,512]{1,0:T(8,128)(2,1)} %convert_element_type.836), channel_id=1, replica_groups=mesh['dp'=8,'blk'=4] {'blk'}, use_global_device_ids=true, to_apply=%region_63.64 | all-reduce | flops 20480 | bytes 81920 | tf_op jit(solution)/shard_map/psum | solution.py:141
  459.6 10.5 psum.86
  476.9 2.2 multiply_reduce_fusion.5
  492.2 2.8 convolution_convert_fusion.17
  508.1 2.8 fusion.233
  510.9 2.8 fusion.237
  522.4 13.8 %all-reduce.4 = (bf16[8,20,64]{2,1,0:T(8,128)(2,1)}, bf16[8,20,64]{2,1,0:T(8,128)(2,1)}, bf16[8,20,64]{2,1,0:T(8,128)(2,1)}) all-reduce(bf16[8,20,64]{2,1,0:T(8,128)(2,1)} %fusion.161, bf16[8,20,64]{2,1,0:T(8,128)(2,1)} %fusion.162, bf16[8,20,64]{2,1,0:T(8,128)(2,1)} %convolution_convert_fusion.28), channel_id=1, replica_groups=mesh['dp'=8,'blk'=4] {'blk'}, use_global_device_ids=true, to_apply=%region_83.84 | all-reduce | flops 30720 | bytes 122880 | tf_op jit(solution)/shard_map/psum | solution.py:141
  546.6 3.1 fusion.520
  549.8 2.6 multiply_reduce_fusion.30
  560.6 3.1 add_convert_fusion
  563.8 3.1 add_bitcast_fusion
  577.4 3.3 collective-permute-done.16
  580.8 2.7 collective-permute-done.20
  601.1 3.4 multiply_reduce_fusion.6
  613.2 2.1 convolution_convert_fusion.16
  625.8 13.3 %all-reduce.3 = (bf16[20,512]{1,0:T(8,128)(2,1)}, bf16[20,512]{1,0:T(8,128)(2,1)}) all-reduce(bf16[20,512]{1,0:T(8,128)(2,1)} %convert_element_type.900, bf16[20,512]{1,0:T(8,128)(2,1)} %convert_element_type.904), channel_id=1, replica_groups=mesh['dp'=8,'blk'=4] {'blk'}, use_global_device_ids=true, to_apply=%region_93.94 | all-reduce | flops 20480 | bytes 81920 | tf_op jit(solution)/shard_map/psum | solution.py:141
  652.2 10.5 psum.92
  669.5 2.2 multiply_reduce_fusion.8
  681.9 2.8 convolution_convert_fusion.14
  693.7 2.8 fusion.235
  696.6 2.8 fusion.239
  729.9 13.7 %all-reduce.2 = (bf16[8,20,64]{2,1,0:T(8,128)(2,1)}, bf16[8,20,64]{2,1,0:T(8,128)(2,1)}, bf16[8,20,64]{2,1,0:T(8,128)(2,1)}) all-reduce(bf16[8,20,64]{2,1,0:T(8,128)(2,1)} %fusion.165, bf16[8,20,64]{2,1,0:T(8,128)(2,1)} %fusion.166, bf16[8,20,64]{2,1,0:T(8,128)(2,1)} %convolution_convert_fusion.26), channel_id=1, replica_groups=mesh['dp'=8,'blk'=4] {'blk'}, use_global_device_ids=true, to_apply=%region_109.110 | all-reduce | flops 30720 | bytes 122880 | tf_op jit(solution)/shard_map/psum | solution.py:141
  756.7 3.0 fusion.693
  759.7 2.5 fusion.196
  767.0 2.5 fusion.118
  770.7 2.5 convolution_add_fusion.9
  783.2 4.2 bitcast_dynamic-update-slice_fusion
  803.9 2.1 pad_maximum_fusion.2
  815.6 2.6 collective-permute-done.24
  818.4 2.7 collective-permute-done.28
  821.5 2.7 collective-permute-done.25
  824.3 2.7 collective-permute-done.29
  828.0 2.4 pad_maximum_fusion.3
  830.9 4.8 copy.1579
  837.2 2.6 bitcast_dynamic-update-slice_fusion.1
  843.3 8.3 pad_maximum_fusion.1
  851.6 16.7 %copy.1502 = bf16[24,512,512]{2,1,0:T(8,128)(2,1)} copy(bf16[24,512,512]{1,2,0:T(8,128)(2,1)} %bitcast.1219) | data formatting | bytes 25165824 | tf_op jit(solution)/shard_map/reshape | solution.py:502
  868.2 15.1 %pad_maximum_fusion = bf16[41,512,512]{2,1,0:T(8,128)(2,1)} fusion(bf16[1,512,512]{2,1,0:T(8,128)(2,1)S(1)} %reshape_transpose_reshape.8, bf16[8,512,512]{2,1,0:T(8,128)(2,1)} %bitcast.1265, bf16[8,512,512]{2,1,0:T(8,128)(2,1)} %bitcast.1264, bf16[24,512,512]{2,1,0:T(8,128)(2,1)} %copy.1502), kind=kLoop, calls=%fused_computation | loop fusion | flops 32243712 | bytes 42991616 | tf_op jit(solution)/shard_map/concatenate | solution.py:500
  886.1 2.8 fusion.111
  888.9 224.6 %reduce-scatter.2.cloned.1.call-done = bf16[41,16,512]{2,1,0:T(8,128)(2,1)} async-done(((bf16[41,512,512]{2,1,0:T(8,128)(2,1)}), bf16[41,16,512]{2,1,0:T(8,128)(2,1)}) %reduce-scatter.2.cloned.1.call-update) | async-done | bytes 671760 | tf_op jit(solution)/shard_map/reduce_scatter | solution.py:508
  (1527 shorter events, 469.2 us)
Async XLA Ops:
  7.2 149.3 %all-gather.6.cloned.1.call-start = ((), (), s32[]{:S(2)}) async-start(), calls=%async_computation.1 | async-start | bytes 22167552 | tf_op jit(solution)/shard_map/all_gather | solution.py:458
  14.7 1098.8 %reduce-scatter.2.cloned.1.call-start = ((), (), s32[]{:S(2)}) async-start(), calls=%async_computation.2 | async-start | bytes 22167552 | tf_op jit(solution)/shard_map/reduce_scatter | solution.py:508
  14.8 3.7 collective-permute-start
  18.5 3.0 collective-permute-start.3
  21.4 3.0 collective-permute-start.6
  25.2 150.8 %copy-start.192 = (pred[256,256]{0,1:T(8,128)(4,1)}, pred[256,256]{0,1:T(8,128)(4,1)S(1)}, u32[]{:S(2)}) copy-start(pred[256,256]{0,1:T(8,128)(4,1)S(1)} %get-tuple-element.375) | copy-start | bytes 196612
  25.2 205.4 %copy-start.190 = (pred[256,256]{0,1:T(8,128)(4,1)}, pred[256,256]{0,1:T(8,128)(4,1)S(1)}, u32[]{:S(2)}) copy-start(pred[256,256]{0,1:T(8,128)(4,1)S(1)} %get-tuple-element.373) | copy-start | bytes 196612
  25.2 208.2 %copy-start.188 = (pred[256,256]{0,1:T(8,128)(4,1)}, pred[256,256]{0,1:T(8,128)(4,1)S(1)}, u32[]{:S(2)}) copy-start(pred[256,256]{0,1:T(8,128)(4,1)S(1)} %get-tuple-element.374) | copy-start | bytes 196612
  163.6 58.1 %collective-permute-start.1 = (bf16[8,256,64]{1,2,0:T(8,128)(2,1)S(1)}, bf16[8,256,64]{1,2,0:T(8,128)(2,1)S(1)}, u32[]{:S(2)}, u32[]{:S(2)}) collective-permute-start(bf16[8,256,64]{1,2,0:T(8,128)(2,1)S(1)} %bitcast.1278), channel_id=1, source_target_pairs={{0,1},{1,2},{2,3},{3,0},{4,5},{5,6},{6,7},{7,4},{8,9},{9,10},{10,1... | collective-permute-start | bytes 786440 | tf_op jit(solution)/shard_map/ppermute | solution.py:39
  164.4 57.6 %collective-permute-start.2 = (bf16[8,256,64]{1,2,0:T(8,128)(2,1)S(1)}, bf16[8,256,64]{1,2,0:T(8,128)(2,1)S(1)}, u32[]{:S(2)}, u32[]{:S(2)}) collective-permute-start(bf16[8,256,64]{1,2,0:T(8,128)(2,1)S(1)} %bitcast.1268), channel_id=1, source_target_pairs={{0,1},{1,2},{2,3},{3,0},{4,5},{5,6},{6,7},{7,4},{8,9},{9,10},{10,1... | collective-permute-start | bytes 786440 | tf_op jit(solution)/shard_map/ppermute | solution.py:39
  176.0 45.5 %copy-start.56 = (f32[8,256,20]{1,2,0:T(8,128)}, f32[8,256,20]{1,2,0:T(8,128)S(1)}, u32[]{:S(2)}) copy-start(f32[8,256,20]{1,2,0:T(8,128)S(1)} %get-tuple-element.381) | copy-start | bytes 491524
  178.6 58.3 %copy-start.68 = (f32[8,256,64]{1,2,0:T(8,128)}, f32[8,256,64]{1,2,0:T(8,128)S(1)}, u32[]{:S(2)}) copy-start(f32[8,256,64]{1,2,0:T(8,128)S(1)} %fusion.227) | copy-start | bytes 1572868
  179.1 42.4 %copy-start.183 = (bf16[20,8,64]{2,1,0:T(8,128)(2,1)}, bf16[20,8,64]{2,1,0:T(8,128)(2,1)S(1)}, u32[]{:S(2)}) copy-start(bf16[20,8,64]{2,1,0:T(8,128)(2,1)S(1)} %reshape_squeeze.64) | copy-start | bytes 61444
  221.8 5.8 collective-permute-start.4
  222.0 8.4 collective-permute-start.5
  227.6 5.8 collective-permute-start.7
  230.4 6.4 collective-permute-start.8
  240.1 80.7 %copy-start.23 = (f32[276,512]{1,0:T(8,128)}, f32[276,512]{1,0:T(8,128)S(1)}, u32[]{:S(2)}) copy-start(f32[276,512]{1,0:T(8,128)S(1)} %get-tuple-element.393) | copy-start | bytes 1695748
  247.5 29.8 %copy-start.99 = (bf16[256,512]{0,1:T(8,128)(2,1)}, bf16[256,512]{0,1:T(8,128)(2,1)S(1)}, u32[]{:S(2)}) copy-start(bf16[256,512]{0,1:T(8,128)(2,1)S(1)} %copy.1337) | copy-start | bytes 786436
  251.1 21.6 %copy-start.58 = (f32[8,20,256]{2,1,0:T(8,128)}, f32[8,20,256]{2,1,0:T(8,128)S(1)}, u32[]{:S(2)}) copy-start(f32[8,20,256]{2,1,0:T(8,128)S(1)} %get-tuple-element.395) | copy-start | bytes 491524
  254.5 20.4 %copy-start.282 = (f32[512]{0:T(512)S(1)}, f32[512]{0:T(512)}, u32[]{:S(2)}) copy-start(f32[512]{0:T(512)} %mul.2022) | copy-start | bytes 6148
  254.5 20.4 %copy-start.342 = (f32[512]{0:T(512)S(1)}, f32[512]{0:T(512)}, u32[]{:S(2)}) copy-start(f32[512]{0:T(512)} %add.1191) | copy-start | bytes 6148
  294.9 192.5 %copy-start.47 = (bf16[1,256,512]{1,2,0:T(8,128)(2,1)}, bf16[1,256,512]{1,2,0:T(8,128)(2,1)S(1)}, u32[]{:S(2)}) copy-start(bf16[1,256,512]{1,2,0:T(8,128)(2,1)S(1)} %get-tuple-element.236) | copy-start | bytes 786436
  294.9 43.1 %collective-permute-start.9 = (bf16[8,256,64]{1,2,0:T(8,128)(2,1)}, bf16[8,256,64]{1,2,0:T(8,128)(2,1)}, u32[]{:S(2)}, u32[]{:S(2)}) collective-permute-start(bf16[8,256,64]{1,2,0:T(8,128)(2,1)} %bitcast.100), channel_id=1, source_target_pairs={{0,1},{1,2},{2,3},{3,0},{4,5},{5,6},{6,7},{7,4},{8,9},{9,10},{10,1... | collective-permute-start | bytes 786440 | tf_op jit(solution)/shard_map/ppermute | solution.py:39
  297.9 40.5 %collective-permute-start.10 = (bf16[8,256,64]{1,2,0:T(8,128)(2,1)S(1)}, bf16[8,256,64]{1,2,0:T(8,128)(2,1)}, u32[]{:S(2)}, u32[]{:S(2)}) collective-permute-start(bf16[8,256,64]{1,2,0:T(8,128)(2,1)S(1)} %bitcast.1273), channel_id=1, source_target_pairs={{0,1},{1,2},{2,3},{3,0},{4,5},{5,6},{6,7},{7,4},{8,9},{9,10},{10,1... | collective-permute-start | bytes 786440 | tf_op jit(solution)/shard_map/ppermute | solution.py:39
  314.0 20.1 %copy-start.128 = (f32[8,20,20]{1,2,0:T(8,128)}, f32[8,20,20]{1,2,0:T(8,128)S(1)}, u32[]{:S(2)}) copy-start(f32[8,20,20]{1,2,0:T(8,128)S(1)} %get-tuple-element.423) | copy-start | bytes 38404
  338.0 6.1 collective-permute-start.11
  338.5 8.5 collective-permute-start.12
  344.1 5.8 collective-permute-start.13
  346.9 7.4 collective-permute-start.14
  377.4 18.1 %copy-start.100 = (bf16[256,512]{0,1:T(8,128)(2,1)S(1)}, bf16[256,512]{0,1:T(8,128)(2,1)}, u32[]{:S(2)}) copy-start(bf16[256,512]{0,1:T(8,128)(2,1)} %copy.1397) | copy-start | bytes 786436
  415.1 26.4 %copy-start.287 = (f32[512]{0:T(512)S(1)}, f32[512]{0:T(512)}, u32[]{:S(2)}) copy-start(f32[512]{0:T(512)} %mul.2127) | copy-start | bytes 6148
  415.1 26.4 %copy-start.336 = (f32[20]{0:T(128)S(1)}, f32[20]{0:T(128)}, u32[]{:S(2)}) copy-start(f32[20]{0:T(128)} %copy-done.335) | copy-start | bytes 244
  445.5 28.3 %copy-start.319 = (f32[256]{0:T(256)S(1)}, f32[256]{0:T(256)}, u32[]{:S(2)}) copy-start(f32[256]{0:T(256)} %copy-done.318) | copy-start | bytes 3076
  457.3 19.6 %copy-start.327 = (f32[256]{0:T(256)}, f32[256]{0:T(256)S(1)}, u32[]{:S(2)}) copy-start(f32[256]{0:T(256)S(1)} %broadcast_multiply_fusion.6) | copy-start | bytes 3076
  554.0 20.4 %collective-permute-start.15 = (bf16[8,256,64]{1,2,0:T(8,128)(2,1)S(1)}, bf16[8,256,64]{1,2,0:T(8,128)(2,1)S(1)}, u32[]{:S(2)}, u32[]{:S(2)}) collective-permute-start(bf16[8,256,64]{1,2,0:T(8,128)(2,1)S(1)} %fusion.117), channel_id=1, source_target_pairs={{0,1},{1,2},{2,3},{3,0},{4,5},{5,6},{6,7},{7,4},{8,9},{9,10},{10,1... | collective-permute-start | bytes 786440 | tf_op jit(solution)/shard_map/ppermute | solution.py:39
  554.1 20.9 %collective-permute-start.19 = (bf16[8,256,64]{1,2,0:T(8,128)(2,1)S(1)}, bf16[8,256,64]{1,2,0:T(8,128)(2,1)S(1)}, u32[]{:S(2)}, u32[]{:S(2)}) collective-permute-start(bf16[8,256,64]{1,2,0:T(8,128)(2,1)S(1)} %copy-done.207), channel_id=1, source_target_pairs={{0,1},{1,2},{2,3},{3,0},{4,5},{5,6},{6,7},{7,4},{8,9},{9,10},{10,1... | collective-permute-start | bytes 786440 | tf_op jit(solution)/shard_map/ppermute | solution.py:39
  568.7 36.2 %copy-start.218 = (bf16[20,512]{1,0:T(8,128)(2,1)}, bf16[20,512]{1,0:T(8,128)(2,1)S(1)}, u32[]{:S(2)}) copy-start(bf16[20,512]{1,0:T(8,128)(2,1)S(1)} %add_convert_fusion.28) | copy-start | bytes 61444
  574.8 5.8 collective-permute-start.16
  575.5 17.9 %copy-start.369 = (bf16[512]{0:T(512)(128)(2,1)S(1)}, bf16[512]{0:T(512)(128)(2,1)}, u32[]{:S(2)}) copy-start(bf16[512]{0:T(512)(128)(2,1)} %add_convert_fusion.40) | copy-start | bytes 3076
  575.5 18.6 %copy-start.356 = (bf16[512]{0:T(512)(128)(2,1)S(1)}, bf16[512]{0:T(512)(128)(2,1)}, u32[]{:S(2)}) copy-start(bf16[512]{0:T(512)(128)(2,1)} %get-tuple-element.98) | copy-start | bytes 3076
  575.5 19.9 %copy-start.367 = (bf16[512]{0:T(512)(128)(2,1)S(1)}, bf16[512]{0:T(512)(128)(2,1)}, u32[]{:S(2)}) copy-start(bf16[512]{0:T(512)(128)(2,1)} %multiply_convert_fusion.12) | copy-start | bytes 3076
  575.5 20.6 %copy-start.368 = (bf16[512]{0:T(512)(128)(2,1)S(1)}, bf16[512]{0:T(512)(128)(2,1)}, u32[]{:S(2)}) copy-start(bf16[512]{0:T(512)(128)(2,1)} %add_convert_fusion.41) | copy-start | bytes 3076
  575.5 21.2 %copy-start.169 = (bf16[8,256,64]{1,2,0:T(8,128)(2,1)S(1)}, bf16[8,256,64]{1,2,0:T(8,128)(2,1)}, u32[]{:S(2)}) copy-start(bf16[8,256,64]{1,2,0:T(8,128)(2,1)} %fusion.124) | copy-start | bytes 786436
  575.5 8.0 collective-permute-start.20
  580.8 6.0 collective-permute-start.17
  584.3 6.1 collective-permute-start.21
  588.6 8.3 collective-permute-start.18
  592.3 6.8 collective-permute-start.22
  615.3 25.1 %copy-start.137 = (f32[20,512]{1,0:T(8,128)S(1)}, f32[20,512]{1,0:T(8,128)}, u32[]{:S(2)}) copy-start(f32[20,512]{1,0:T(8,128)} %copy-done.136) | copy-start | bytes 122884
  617.2 29.7 %copy-start.59 = (f32[8,20,256]{2,1,0:T(8,128)S(1)}, f32[8,20,256]{2,1,0:T(8,128)}, u32[]{:S(2)}) copy-start(f32[8,20,256]{2,1,0:T(8,128)} %copy-done.58) | copy-start | bytes 491524
  619.5 30.2 %copy-start.102 = (bf16[1,256,512]{1,2,0:T(8,128)(2,1)S(1)}, bf16[1,256,512]{1,2,0:T(8,128)(2,1)}, u32[]{:S(2)}) copy-start(bf16[1,256,512]{1,2,0:T(8,128)(2,1)} %copy-done.101) | copy-start | bytes 786436
  651.0 18.4 %copy-start.153 = (bf16[8,256,64]{1,2,0:T(8,128)(2,1)}, bf16[8,256,64]{1,2,0:T(8,128)(2,1)S(1)}, u32[]{:S(2)}) copy-start(bf16[8,256,64]{1,2,0:T(8,128)(2,1)S(1)} %fusion.122) | copy-start | bytes 786436
  652.1 17.4 %copy-start.151 = (bf16[8,256,64]{1,2,0:T(8,128)(2,1)}, bf16[8,256,64]{1,2,0:T(8,128)(2,1)S(1)}, u32[]{:S(2)}) copy-start(bf16[8,256,64]{1,2,0:T(8,128)(2,1)S(1)} %fusion.121) | copy-start | bytes 786436
  696.5 31.7 %copy-start.50 = (bf16[1,256,512]{1,2,0:T(8,128)(2,1)S(1)}, bf16[1,256,512]{1,2,0:T(8,128)(2,1)}, u32[]{:S(2)}) copy-start(bf16[1,256,512]{1,2,0:T(8,128)(2,1)} %copy-done.49) | copy-start | bytes 786436
  696.5 52.0 %copy-start.130 = (bf16[20,8,64]{2,1,0:T(8,128)(2,1)S(1)}, bf16[20,8,64]{2,1,0:T(8,128)(2,1)}, u32[]{:S(2)}) copy-start(bf16[20,8,64]{2,1,0:T(8,128)(2,1)} %copy-done.129) | copy-start | bytes 61444
  769.6 41.3 %collective-permute-start.23 = (bf16[8,256,64]{1,2,0:T(8,128)(2,1)}, bf16[8,256,64]{1,2,0:T(8,128)(2,1)}, u32[]{:S(2)}, u32[]{:S(2)}) collective-permute-start(bf16[8,256,64]{1,2,0:T(8,128)(2,1)} %fusion.118), channel_id=1, source_target_pairs={{0,1},{1,2},{2,3},{3,0},{4,5},{5,6},{6,7},{7,4},{8,9},{9,10},{10,1... | collective-permute-start | bytes 786440 | tf_op jit(solution)/shard_map/ppermute | solution.py:39
  769.6 42.9 %collective-permute-start.27 = (bf16[8,256,64]{1,2,0:T(8,128)(2,1)}, bf16[8,256,64]{1,2,0:T(8,128)(2,1)}, u32[]{:S(2)}, u32[]{:S(2)}) collective-permute-start(bf16[8,256,64]{1,2,0:T(8,128)(2,1)} %convolution_convert_fusion.14), channel_id=1, source_target_pairs={{0,1},{1,2},{2,3},{3,0},{4,5},{5,6},{6,7},{7,4},{8,9},{9,10},{10,1... | collective-permute-start | bytes 786440 | tf_op jit(solution)/shard_map/ppermute | solution.py:39
  812.4 5.8 collective-permute-start.24
  813.9 7.1 collective-permute-start.28
  818.3 5.8 collective-permute-start.25
  821.1 5.8 collective-permute-start.29
  824.2 11.5 %collective-permute-start.26 = (bf16[8,256,64]{1,2,0:T(8,128)(2,1)S(1)}, bf16[8,256,64]{1,2,0:T(8,128)(2,1)}, u32[]{:S(2)}, u32[]{:S(2)}) collective-permute-start(bf16[8,256,64]{1,2,0:T(8,128)(2,1)S(1)} %add_convert_fusion.9), channel_id=1, source_target_pairs={{0,1},{1,2},{2,3},{3,0},{4,5},{5,6},{6,7},{7,4},{8,9},{9,10},{10,1... | collective-permute-start | bytes 786440 | tf_op jit(solution)/shard_map/ppermute | solution.py:39
  827.8 9.1 collective-permute-start.30
  (373 other events, 1492.7 us)
Sparse Core Ops, SparseCore 0:
  14.9 141.5 all-gather.5
  883.5 229.9 reduce-scatter.1

commit v2 on v1

v2 whole, which is shorter than its diff:
```python
import functools

import jax
import jax.numpy as jnp
from jax import lax
from jax.experimental import pallas as pl
from jax.experimental.pallas import tpu as pltpu
from jax.sharding import PartitionSpec as P

HEADS = 8
HEAD = 64
MEM = 20
PAD = 32
NEG = -1000000000.0
BIG = 3.0e38
EPS = 1e-05
SCALE = HEAD**-0.5
ALL = ("dp", "blk")
LOW = jnp.bfloat16
F32 = jnp.float32
VMEM_LIMIT = 56 * 1024 * 1024


def dot(a, b):
    return jnp.dot(a, b, preferred_element_type=F32)


def dot_nt(a, b):
    return lax.dot_general(a, b, (((1,), (1,)), ((), ())), preferred_element_type=F32)


def dot_tn(a, b):
    return lax.dot_general(a, b, (((0,), (0,)), ((), ())), preferred_element_type=F32)


def hat(x):
    center = x - jnp.mean(x, -1, keepdims=True)
    spread = jnp.mean(center * center, -1, keepdims=True)
    inv = lax.rsqrt(spread + EPS)
    return center * inv, inv


def norm(x, gain, shift):
    return hat(x)[0] * gain + shift


def norm_back(x, gain, grad):
    unit, inv = hat(x)
    scaled = grad * gain
    mean_one = jnp.mean(scaled, -1, keepdims=True)
    mean_two = jnp.mean(scaled * unit, -1, keepdims=True)
    return inv * (scaled - mean_one - unit * mean_two), grad * unit


def total(x):
    return jnp.sum(x, 0, keepdims=True)


def gelu_parts(u):
    k = 0.7978845608028654
    t = jnp.tanh(k * (u + 0.044715 * u * u * u))
    half = 0.5 * (1.0 + t)
    slope = half + 0.5 * u * (1.0 - t * t) * (k * (1.0 + 0.134145 * u * u))
    return u * half, slope


def head_mask(width):
    lanes = lax.broadcasted_iota(jnp.int32, (HEADS, 1, width), 2) // HEAD
    return lanes == lax.broadcasted_iota(jnp.int32, (HEADS, 1, width), 0)


def spread_heads(x):
    rows, width = x.shape
    full = jnp.where(head_mask(width), x.astype(F32)[None], 0.0)
    return full.reshape(HEADS * rows, width).astype(x.dtype)


def fold_heads(x):
    rows, width = x.shape
    full = x.reshape(HEADS, rows // HEADS, width)
    return jnp.sum(jnp.where(head_mask(width), full, 0.0), 0)


def two_heads(x):
    first = lax.broadcasted_iota(jnp.int32, x.shape, 1) < HEAD
    zero = jnp.zeros_like(x)
    return jnp.concatenate([jnp.where(first, x, zero), jnp.where(first, zero, x)], 0)


def pick_heads(x):
    width, rows = x.shape
    mine = (lax.broadcasted_iota(jnp.int32, x.shape, 0) < HEAD) == (
        lax.broadcasted_iota(jnp.int32, x.shape, 1) < rows // 2
    )
    both = jnp.where(mine, x, 0.0).T
    return both[: rows // 2] + both[rows // 2 :]


def bound_of(seg_keys, seg_queries):
    same = seg_keys == seg_queries
    allowed = (same | (seg_keys == -2.0) | (seg_queries == -1.0)) & (seg_keys != -3.0)
    return jnp.where(allowed, BIG, NEG)


def place_keys(keys_ref, own_ref, core_ref, chip_ref, both_ref):
    rows = core_ref.shape[0]
    me = lax.axis_index("blk")
    pieces = ((me, own_ref), (me ^ 1, core_ref), (me ^ 2, chip_ref), (me ^ 3, both_ref))
    for place, piece in pieces:
        keys_ref[pl.ds(pl.multiple_of(place * rows, rows), rows), :] = piece[0:rows, :]
    keys_ref[4 * rows :, :] = own_ref[rows:, :]


def project(z, weight, q_ref, kv_ref):
    low = z.astype(LOW)
    width = low.shape[1]
    q_ref[...] = dot(low, weight(0)).astype(LOW)
    kv_ref[:, :width] = dot(low, weight(1)).astype(LOW)
    kv_ref[:, width:] = dot(low, weight(2)).astype(LOW)


def first_kernel(weight, tokens_ref, memory_ref, z_ref, q_ref, kv_ref):
    rows = tokens_ref.shape[0]
    z_ref[:rows, :] = tokens_ref[...].astype(F32)
    z_ref[rows:, :] = memory_ref[...]
    project(z_ref[...], weight, q_ref, kv_ref)


def attend_kernel(
    weight, z_ref, q_ref, own_ref, core_ref, chip_ref, both_ref, segk_ref, segq_ref, gain_ref, shift_ref,
    att_ref, pre_ref, one_ref, rq_ref, rkv_ref, wq_ref, part_ref,
    keys_ref, bound_ref,
):
    rows = core_ref.shape[0]
    width = z_ref.shape[1]
    place_keys(keys_ref, own_ref, core_ref, chip_ref, both_ref)
    bound_ref[...] = bound_of(segk_ref[...], segq_ref[...])

    def pair(step, carry):
        lanes = pl.ds(pl.multiple_of(step * 128, 128), 128)
        more = pl.ds(pl.multiple_of(width + step * 128, 128), 128)
        query = two_heads(q_ref[:, lanes]) * jnp.asarray(SCALE, LOW)
        keys = keys_ref[:, lanes]
        values = keys_ref[:, more]
        scores = jnp.minimum(dot_nt(keys, query), bound_ref[...])
        expo = jnp.exp(scores - jnp.max(scores, 0, keepdims=True))
        probs = expo * (1.0 / jnp.sum(expo, 0, keepdims=True))
        att_ref[:, lanes] = pick_heads(dot_tn(values, probs.astype(LOW))).astype(LOW)
        return carry

    lax.fori_loop(0, width // 128, pair, 0)
    pre = z_ref[...] + dot(att_ref[...], weight(3))
    pre_ref[...] = pre
    one = norm(pre, gain_ref[0:1, :], shift_ref[0:1, :])
    one_ref[...] = one
    low = one.astype(LOW)
    seq_low, mem_low = low[:rows], low[rows:]
    wq_ref[...] = dot(seq_low, weight(8)).astype(LOW)
    rq = dot(mem_low, weight(4)).astype(LOW)
    rk = dot(seq_low, weight(5)).astype(LOW)
    rv = dot(seq_low, weight(6)).astype(LOW)
    rq_ref[...] = rq
    rkv_ref[:, :width] = rk
    rkv_ref[:, width:] = rv
    scores = dot_nt(spread_heads(rq * jnp.asarray(SCALE, LOW)), rk)
    top = jnp.max(scores, -1, keepdims=True)
    expo = jnp.exp(scores - top)
    summed = jnp.sum(expo, -1, keepdims=True)
    part_ref[0:PAD, :] = fold_heads(dot(expo.astype(LOW), rv))
    wide = (HEADS * PAD, width)
    part_ref[PAD : 2 * PAD, :] = fold_heads(jnp.broadcast_to(top, wide))
    part_ref[2 * PAD :, :] = fold_heads(jnp.broadcast_to(summed, wide))


def write_probs(wk, wq):
    scores = dot_nt(spread_heads(wk * jnp.asarray(SCALE, LOW)), wq)
    scores = scores.reshape(HEADS, PAD, scores.shape[1])
    real = lax.broadcasted_iota(jnp.int32, scores.shape, 1) < MEM
    scores = jnp.where(real, scores, NEG)
    expo = jnp.exp(scores - jnp.max(scores, 1, keepdims=True))
    return expo * (1.0 / jnp.sum(expo, 1, keepdims=True))


def finish_kernel(
    last, weight, one_ref, parts_ref, wq_ref, bias_ref, gain_ref, shift_ref, *rest
):
    if last:
        (z_ref, rout_ref, rlse_ref, mempre_ref, two_ref, wkv_ref, wlow_ref, seqpre_ref, x_ref, feedpre_ref) = rest
    else:
        (z_ref, q_ref, kv_ref,
         rout_ref, rlse_ref, mempre_ref, two_ref, wkv_ref, wlow_ref, seqpre_ref, x_ref, feedpre_ref) = rest
    rows, width = wq_ref.shape
    count = parts_ref.shape[0]
    top = parts_ref[0, PAD : 2 * PAD, :]
    for source in range(1, count):
        top = jnp.maximum(top, parts_ref[source, PAD : 2 * PAD, :])
    accum = jnp.zeros((PAD, width), F32)
    summed = jnp.zeros((PAD, width), F32)
    for source in range(count):
        fade = jnp.exp(parts_ref[source, PAD : 2 * PAD, :] - top)
        accum = accum + fade * parts_ref[source, 0:PAD, :]
        summed = summed + fade * parts_ref[source, 2 * PAD :, :]
    rout = accum / summed
    rout_ref[...] = rout
    rlse_ref[...] = top + jnp.log(summed)
    mempre = one_ref[rows:, :] + dot(rout.astype(LOW), weight(7))
    mempre_ref[...] = mempre
    memtwo = norm(mempre, gain_ref[1:2, :], shift_ref[1:2, :])
    memlow = memtwo.astype(LOW)
    wk = dot(memlow, weight(9)).astype(LOW)
    wv = dot(memlow, weight(10)).astype(LOW)
    wkv_ref[:, :width] = wk
    wkv_ref[:, width:] = wv
    probs = write_probs(wk, wq_ref[...]).reshape(HEADS * PAD, rows)
    wlow = dot_tn(probs.astype(LOW), spread_heads(wv)).astype(LOW)
    wlow_ref[...] = wlow
    seqpre = one_ref[:rows, :] + dot(wlow, weight(11))
    seqpre_ref[...] = seqpre
    seqtwo = norm(seqpre, gain_ref[2:3, :], shift_ref[2:3, :])
    two_ref[:rows, :] = seqtwo
    two_ref[rows:, :] = memtwo
    two = two_ref[...]
    x = two.astype(LOW)
    x_ref[...] = x
    feed = two + shift_ref[4:5, :]
    for part in range(bias_ref.shape[0]):
        u = dot(x, weight(("up", part))) + bias_ref[part : part + 1, :]
        feed = feed + dot(gelu_parts(u)[0].astype(LOW), weight(("down", part)))
    feedpre_ref[...] = feed
    z_ref[...] = norm(feed, gain_ref[3:4, :], shift_ref[3:4, :])
    if not last:
        project(z_ref[...], weight, q_ref, kv_ref)


def feed_back_kernel(
    share, weight, grad_ref, feedpre_ref, x_ref, seqpre_ref, wlow_ref, wq_ref, wkv_ref, one_ref,
    bias_ref, gain_ref,
    gup_ref, gdown_ref, g11_ref, g8_ref, gbias_ref, gsmall_ref, mem_ref, seq_ref, part_ref,
):
    rows, width = wq_ref.shape
    full = grad_ref.shape[0]
    balance = jnp.where(lax.broadcasted_iota(jnp.int32, (full, 1), 0) < rows, 1.0, share)
    grad = grad_ref[...]
    feed, by_unit = norm_back(feedpre_ref[...], gain_ref[3:4, :], grad)
    gsmall_ref[0:1, :] = total(by_unit * balance)
    gsmall_ref[1:2, :] = total(grad * balance)
    low = feed.astype(LOW)
    low_share = (low.astype(F32) * balance).astype(LOW)
    gsmall_ref[2:3, :] = total(low_share.astype(F32))
    x = x_ref[...]
    two = feed
    for part in range(bias_ref.shape[0]):
        u = dot(x, weight(("up", part))) + bias_ref[part : part + 1, :]
        value, slope = gelu_parts(u)
        gdown_ref[part] = dot_tn(value.astype(LOW), low_share).astype(LOW)
        pre = (dot_nt(low, weight(("down", part))) * slope).astype(LOW)
        pre_share = (pre.astype(F32) * balance).astype(LOW)
        gbias_ref[part : part + 1, :] = total(pre_share.astype(F32))
        gup_ref[part] = dot_tn(x, pre_share).astype(LOW)
        two = two + dot_nt(pre, weight(("up", part)))
    mem_ref[...] = two[rows:]
    grad = two[:rows]
    seq, by_unit = norm_back(seqpre_ref[...], gain_ref[2:3, :], grad)
    gsmall_ref[3:4, :] = total(by_unit)
    gsmall_ref[4:5, :] = total(grad)
    low = seq.astype(LOW)
    g11_ref[...] = dot_tn(wlow_ref[...], low).astype(LOW)
    out_low = dot_nt(low, weight(11)).astype(LOW)
    wk, wv = wkv_ref[:, :width], wkv_ref[:, width:]
    wq = wq_ref[...]
    probs = write_probs(wk, wq)
    prob_grad = dot_nt(spread_heads(wv), out_low).reshape(probs.shape)
    delta = jnp.sum(probs * prob_grad, 1, keepdims=True)
    score_grad = (probs * (prob_grad - delta)).reshape(HEADS * PAD, rows).astype(LOW)
    wq_low = (dot_tn(score_grad, spread_heads(wk)) * SCALE).astype(LOW)
    part_ref[:PAD, :] = fold_heads(dot(score_grad, wq)) * SCALE
    part_ref[PAD:, :] = fold_heads(dot(probs.reshape(HEADS * PAD, rows).astype(LOW), out_low))
    g8_ref[...] = dot_tn(one_ref[:rows, :].astype(LOW), wq_low).astype(LOW)
    seq_ref[...] = seq + dot_nt(wq_low, weight(8))


def read_back_kernel(
    share, weight, parts_ref, mem_ref, seq_ref, two_ref, mempre_ref, rout_ref, rlse_ref, rq_ref, rkv_ref, one_ref,
    pre_ref, gain_ref,
    g5_ref, g6_ref, g7_ref, g9_ref, g10_ref, gsmall_ref, memgrad_ref, seqjoint_ref, part_ref,
):
    rows, width = seq_ref.shape
    both = parts_ref[0]
    for source in range(1, parts_ref.shape[0]):
        both = both + parts_ref[source]
    k_low = both[:PAD].astype(LOW)
    v_low = both[PAD:].astype(LOW)
    mem_low = two_ref[rows:, :].astype(LOW)
    g9_ref[...] = (dot_tn(mem_low, k_low) * share).astype(LOW)
    g10_ref[...] = (dot_tn(mem_low, v_low) * share).astype(LOW)
    grad = mem_ref[...] + dot_nt(k_low, weight(9)) + dot_nt(v_low, weight(10))
    mem, by_unit = norm_back(mempre_ref[...], gain_ref[1:2, :], grad)
    gsmall_ref[0:1, :] = total(by_unit) * share
    gsmall_ref[1:2, :] = total(grad) * share
    low = mem.astype(LOW)
    rout = rout_ref[...]
    g7_ref[...] = (dot_tn(rout.astype(LOW), low) * share).astype(LOW)
    out_low = dot_nt(low, weight(7)).astype(LOW)
    memgrad_ref[...] = mem
    rk, rv = rkv_ref[:, :width], rkv_ref[:, width:]
    rq = spread_heads(rq_ref[...] * jnp.asarray(SCALE, LOW))
    out_wide = spread_heads(out_low)
    delta = jnp.sum(spread_heads(out_low.astype(F32) * rout), -1, keepdims=True)
    mask = head_mask(width)
    lse = jnp.max(jnp.where(mask, rlse_ref[...][None], -BIG).reshape(HEADS * PAD, width), -1, keepdims=True)
    probs = jnp.exp(dot_nt(rq, rk) - lse)
    score_grad = (probs * (dot_nt(out_wide, rv) - delta)).astype(LOW)
    part_ref[...] = fold_heads(dot(score_grad, rk)) * SCALE
    key_low = dot_tn(score_grad, rq).astype(LOW)
    value_low = dot_tn(probs.astype(LOW), out_wide).astype(LOW)
    seq_low = one_ref[:rows, :].astype(LOW)
    g5_ref[...] = dot_tn(seq_low, key_low).astype(LOW)
    g6_ref[...] = dot_tn(seq_low, value_low).astype(LOW)
    grad = seq_ref[...] + dot_nt(key_low, weight(5)) + dot_nt(value_low, weight(6))
    joint, by_unit = norm_back(pre_ref[:rows, :], gain_ref[0:1, :], grad)
    gsmall_ref[2:3, :] = total(by_unit)
    gsmall_ref[3:4, :] = total(grad)
    seqjoint_ref[...] = joint


def attend_back_kernel(
    share, weight, parts_ref, memgrad_ref, seqjoint_ref, one_ref, pre_ref, att_ref,
    q_ref, own_ref, core_ref, chip_ref, both_ref, segk_ref, segq_ref, gain_ref,
    g3_ref, g4_ref, gsmall_ref, joint_ref, qgrad_ref, kvgrad_ref,
    keys_ref, bound_ref, out_ref,
):
    rows, width = seqjoint_ref.shape
    full = att_ref.shape[0]
    place_keys(keys_ref, own_ref, core_ref, chip_ref, both_ref)
    bound_ref[...] = bound_of(segk_ref[...], segq_ref[...])
    part = parts_ref[0]
    for source in range(1, parts_ref.shape[0]):
        part = part + parts_ref[source]
    q_low = part.astype(LOW)
    g4_ref[...] = (dot_tn(one_ref[rows:, :].astype(LOW), q_low) * share).astype(LOW)
    grad = memgrad_ref[...] + dot_nt(q_low, weight(4))
    mem, by_unit = norm_back(pre_ref[rows:, :], gain_ref[0:1, :], grad)
    gsmall_ref[0:1, :] = total(by_unit) * share
    gsmall_ref[1:2, :] = total(grad) * share
    joint_ref[:rows, :] = seqjoint_ref[...]
    joint_ref[rows:, :] = mem
    low = joint_ref[...].astype(LOW)
    balance = jnp.where(lax.broadcasted_iota(jnp.int32, (full, 1), 0) < rows, 1.0, share)
    g3_ref[...] = dot_tn(att_ref[...], (low.astype(F32) * balance).astype(LOW)).astype(LOW)
    out_ref[...] = dot_nt(low, weight(3)).astype(LOW)

    def pair(step, carry):
        lanes = pl.ds(pl.multiple_of(step * 128, 128), 128)
        more = pl.ds(pl.multiple_of(width + step * 128, 128), 128)
        query = q_ref[:, lanes] * jnp.asarray(SCALE, LOW)
        out = out_ref[:, lanes]
        low_balance = jnp.concatenate([balance, balance], 0)
        query = two_heads(query)
        out = two_heads(out)
        keys = keys_ref[:, lanes]
        values = keys_ref[:, more]
        scores = jnp.minimum(dot_nt(keys, query), bound_ref[...])
        expo = jnp.exp(scores - jnp.max(scores, 0, keepdims=True))
        probs = expo * (1.0 / jnp.sum(expo, 0, keepdims=True))
        prob_grad = dot_nt(values, out)
        delta = jnp.sum(probs * prob_grad, 0, keepdims=True)
        score_grad = (probs * (prob_grad - delta)).astype(LOW)
        qgrad_ref[:, lanes] = (pick_heads(dot_tn(keys, score_grad)) * SCALE).astype(LOW)
        query_share = (query.astype(F32) * low_balance).astype(LOW)
        out_share = (out.astype(F32) * low_balance).astype(LOW)
        kvgrad_ref[:, lanes] = dot(score_grad, query_share).astype(LOW)
        kvgrad_ref[:, more] = dot(probs.astype(LOW), out_share).astype(LOW)
        return carry

    lax.fori_loop(0, width // 128, pair, 0)


def input_back_kernel(share, weight, z_ref, joint_ref, qgrad_ref, kvgrad_ref, g0_ref, g1_ref, g2_ref, zgrad_ref):
    full, width = z_ref.shape
    rows = full - PAD
    balance = jnp.where(lax.broadcasted_iota(jnp.int32, (full, 1), 0) < rows, 1.0, share)
    low = z_ref[...].astype(LOW)
    grads = (qgrad_ref[...], kvgrad_ref[:, :width], kvgrad_ref[:, width:])
    grad = joint_ref[...]
    for part, (value, out_ref) in enumerate(zip(grads, (g0_ref, g1_ref, g2_ref))):
        out_ref[...] = dot_tn(low, (value.astype(F32) * balance).astype(LOW)).astype(LOW)
        grad = grad + dot_nt(value, weight(part))
    zgrad_ref[...] = grad


def call(kernel, name, ins, outs, weights, scratch=()):
    sources = []
    for array, _ in weights.values():
        if not any(array is source for source in sources):
            sources.append(array)
    places = {
        key: ([array is source for source in sources].index(True), index) for key, (array, index) in weights.items()
    }
    shape = sources[0].shape[1:]

    def body(*refs):
        in_refs, refs = refs[: len(ins)], refs[len(ins) :]
        source_refs, refs = refs[: len(sources)], refs[len(sources) :]
        *refs, buffer, sems = refs
        copies = {}
        for slot, (key, (source, index)) in enumerate(places.items()):
            copies[key] = pltpu.make_async_copy(source_refs[source].at[index], buffer.at[slot], sems.at[slot])
            copies[key].start()
        slots = {key: slot for slot, key in enumerate(places)}
        arrived = set()

        def weight(key):
            if key not in arrived:
                copies[key].wait()
                arrived.add(key)
            return buffer[slots[key]]

        kernel(weight, *in_refs, *refs)

    inside = pl.BlockSpec(memory_space=pltpu.VMEM)
    return pl.pallas_call(
        body,
        out_shape=[jax.ShapeDtypeStruct(shape, kind) for shape, kind in outs],
        in_specs=[inside] * len(ins) + [pl.BlockSpec(memory_space=pl.ANY)] * len(sources),
        out_specs=[inside] * len(outs),
        scratch_shapes=list(scratch)
        + [pltpu.VMEM((len(weights),) + shape, LOW), pltpu.SemaphoreType.DMA((len(weights),))],
        compiler_params=pltpu.CompilerParams(vmem_limit_bytes=VMEM_LIMIT),
        name=name,
    )(*ins, *sources)


def flipped(value, bit):
    size = lax.axis_size("blk")
    return lax.ppermute(value, "blk", [(source, source ^ bit) for source in range(size)])


def everyone_of(value):
    return lax.all_gather(value, "blk")


def local(
    tokens, segments, memory_init, attn_weights, ffn_in, ffn_out, ffn_bias, norm_gain, norm_shift, out_grad, memory_cot
):
    layers, count, rows, width = attn_weights.shape
    hidden = ffn_in.shape[2]
    per = hidden // width
    small = [ffn_bias, norm_gain, norm_shift, memory_init]
    sizes = [part.size for part in small]
    starts = [sum(sizes[:k]) for k in range(5)]
    flat = jnp.concatenate([part.astype(LOW).reshape(-1) for part in small])
    blocks = -(-flat.size // (rows * width))
    flat = jnp.pad(flat, (0, blocks * rows * width - flat.size))
    packed = jnp.concatenate(
        [
            attn_weights.astype(LOW).reshape(layers * count, rows, width),
            ffn_in.astype(LOW).reshape(layers, rows, per, width).transpose(0, 2, 1, 3).reshape(-1, rows, width),
            ffn_out.astype(LOW).reshape(-1, rows, width),
            flat.reshape(blocks, rows, width),
        ]
    )
    everyone = lax.axis_size("dp") * lax.axis_size("blk")
    whole = lax.all_gather(packed, ALL, axis=1, tiled=True)
    one, two, three = (layers * count, layers * (count + per), layers * (count + 2 * per))
    full_small = whole[three:].reshape(blocks, everyone, rows * width).transpose(1, 0, 2).reshape(everyone, -1)
    pieces = [full_small[:, starts[k] : starts[k + 1]].reshape((everyone,) + small[k].shape) for k in range(4)]
    bias, gains, shifts, memory = [
        jnp.moveaxis(piece, 0, -2).reshape(piece.shape[1:-1] + (-1,)).astype(F32) for piece in pieces
    ]
    down_all = (
        whole[two:three].reshape(layers, per, everyone, rows, width).transpose(0, 2, 1, 3, 4)
    ).reshape(layers * per, width, width)
    bias = bias.reshape(layers, per, width)

    def attn(index, *keys):
        return {key: (whole, index * count + key) for key in keys}

    def feed(index):
        pairs = {}
        for part in range(per):
            pairs["up", part] = (whole, one + index * per + part)
            pairs["down", part] = (down_all, index * per + part)
        return pairs

    length = tokens.shape[1]
    full = length + PAD
    size = lax.axis_size("blk")
    share = 1.0 / size
    seg = segments[0].astype(F32)
    seg_all = lax.all_gather(segments[0], "blk", tiled=True).astype(F32)
    seg_keys = jnp.concatenate(
        [seg_all, jnp.full((MEM,), -2.0, F32), jnp.full((PAD - MEM,), -3.0, F32)]
    ).reshape(-1, 1)
    seg_row = jnp.concatenate([seg, jnp.full((PAD,), -1.0, F32)])
    seg_queries = jnp.concatenate([seg_row, seg_row]).reshape(1, -1)
    every = size * length + PAD
    memory = jnp.pad(memory, ((0, PAD - MEM), (0, 0)))
    keys_scratch = pltpu.VMEM((every, 2 * width), LOW)
    bound_scratch = pltpu.VMEM((every, 2 * full), F32)

    z, q, kv = call(
        first_kernel,
        "first",
        [tokens[0], memory],
        [((full, width), F32), ((full, width), LOW), ((full, 2 * width), LOW)],
        attn(0, 0, 1, 2),
    )
    kept = []
    for index in range(layers):
        own = kv[:length]
        core = flipped(own, 1)
        chip = flipped(own, 2)
        both = flipped(chip, 1)
        att, pre, first, rq, rkv, wq, part = call(
            attend_kernel,
            f"attend_{index}",
            [z, q, kv, core, chip, both, seg_keys, seg_queries, gains[index], shifts[index]],
            [
                ((full, width), LOW), ((full, width), F32), ((full, width), F32), ((PAD, width), LOW),
                ((length, 2 * width), LOW), ((length, width), LOW), ((3 * PAD, width), F32),
            ],
            attn(index, 3, 8, 4, 5, 6),
            [keys_scratch, bound_scratch],
        )
        parts = everyone_of(part)
        last = index + 1 == layers
        results = call(
            functools.partial(finish_kernel, last),
            f"finish_{index}",
            [first, parts, wq, bias[index], gains[index], shifts[index]],
            [((full, width), F32)]
            + ([] if last else [((full, width), LOW), ((full, 2 * width), LOW)])
            + [
                ((PAD, width), F32), ((PAD, width), F32), ((PAD, width), F32), ((full, width), F32),
                ((PAD, 2 * width), LOW), ((length, width), LOW), ((length, width), F32), ((full, width), LOW),
                ((full, width), F32),
            ],
            attn(index, 7, 9, 10, 11) | feed(index) | ({} if last else attn(index + 1, 0, 1, 2)),
        )
        rout, rlse, mempre, second, wkv, wlow, seqpre, x, feedpre = results[-9:]
        kept.append(
            dict(
                z=z, q=q, kv=kv, core=core, chip=chip, both=both, att=att, pre=pre, first=first, rq=rq, rkv=rkv,
                wq=wq, rout=rout, rlse=rlse, mempre=mempre, second=second, wkv=wkv, wlow=wlow, seqpre=seqpre, x=x,
                feedpre=feedpre,
            )
        )
        z = results[0]
        if not last:
            q, kv = results[1:3]
    final = z
    grad = jnp.concatenate(
        [out_grad[0].astype(F32), jnp.pad(memory_cot[0].astype(F32), ((0, PAD - MEM), (0, 0)))]
    )
    square = ((width, width), LOW)
    square_f32 = [((full, width), F32)]
    made = [None] * layers
    for index in reversed(range(layers)):
        k = kept[index]
        gup, gdown, g11, g8, gbias, small_one, mem, seq, part = call(
            functools.partial(feed_back_kernel, share),
            f"feed_back_{index}",
            [grad, k["feedpre"], k["x"], k["seqpre"], k["wlow"], k["wq"], k["wkv"], k["first"], bias[index],
             gains[index]],
            [
                ((per, width, width), LOW), ((per, width, width), LOW), square, square, ((per, width), F32),
                ((5, width), F32), ((PAD, width), F32), ((length, width), F32), ((2 * PAD, width), F32),
            ],
            feed(index) | attn(index, 11, 8),
        )
        parts = everyone_of(part)
        g5, g6, g7, g9, g10, small_two, mem, seq, part = call(
            functools.partial(read_back_kernel, share),
            f"read_back_{index}",
            [parts, mem, seq, k["second"], k["mempre"], k["rout"], k["rlse"], k["rq"], k["rkv"], k["first"],
             k["pre"], gains[index]],
            [square] * 5
            + [((4, width), F32), ((PAD, width), F32), ((length, width), F32), ((PAD, width), F32)],
            attn(index, 9, 10, 7, 5, 6),
        )
        parts = everyone_of(part)
        g3, g4, small_three, joint, qgrad, kvgrad = call(
            functools.partial(attend_back_kernel, share),
            f"attend_back_{index}",
            [parts, mem, seq, k["first"], k["pre"], k["att"], k["q"], k["kv"], k["core"], k["chip"], k["both"],
             seg_keys, seg_queries, gains[index]],
            [square, square, ((2, width), F32), ((full, width), F32), ((full, width), LOW),
             ((every, 2 * width), LOW)],
            attn(index, 4, 3),
            [keys_scratch, bound_scratch, pltpu.VMEM((full, width), LOW)],
        )
        me = lax.axis_index("blk")
        chunks = kvgrad[: size * length].reshape(size // 2, 2, length, 2 * width)
        memory_part = kvgrad[size * length :]
        here = jnp.take(chunks, me % 2, axis=1)
        there = jnp.take(chunks, 1 - me % 2, axis=1)
        got, got_memory = flipped(there, 1), flipped(memory_part, 1)
        here = here.astype(F32) + got.astype(F32)
        memory_part = (memory_part.astype(F32) + got_memory.astype(F32)).astype(LOW)
        mine = jnp.take(here, me // 2, axis=0)
        theirs = jnp.take(here, 1 - me // 2, axis=0).astype(LOW)
        got, got_memory = flipped(theirs, 2), flipped(memory_part, 2)
        mine = (mine + got.astype(F32)).astype(LOW)
        memory_part = (memory_part.astype(F32) + got_memory.astype(F32)).astype(LOW)
        kvgrad = jnp.concatenate([mine, memory_part])
        g0, g1, g2, grad = call(
            functools.partial(input_back_kernel, share),
            f"input_back_{index}",
            [k["z"], joint, qgrad, kvgrad],
            [square, square, square] + square_f32,
            attn(index, 0, 1, 2),
        )
        made[index] = dict(
            attn=jnp.stack([g0, g1, g2, g3, g4, g5, g6, g7, g8, g9, g10, g11]),
            up=gup,
            down=gdown,
            bias=gbias.reshape(-1),
            gain=jnp.stack([small_two[2] + small_three[0], small_two[0], small_one[3], small_one[0]]),
            shift=jnp.stack([small_two[3] + small_three[1], small_two[1], small_one[4], small_one[1], small_one[2]]),
        )
    tiny = [jnp.stack([m[name] for m in made]) for name in ("bias", "gain", "shift")] + [grad[length : length + MEM] * share]
    tiny = [jnp.moveaxis(part.reshape(part.shape[:-1] + (everyone, -1)), -2, 0).reshape(everyone, -1) for part in tiny]
    tiny = jnp.concatenate(tiny, 1)
    tiny = jnp.pad(tiny, ((0, 0), (0, blocks * rows * width - tiny.shape[1]))).astype(LOW)
    outgoing = jnp.concatenate(
        [m["attn"] for m in made]
        + [m["up"] for m in made]
        + [
            m["down"].reshape(everyone, per, rows, width).transpose(1, 0, 2, 3).reshape(per, width, width)
            for m in made
        ]
        + [tiny.reshape(everyone, blocks, rows, width).transpose(1, 0, 2, 3).reshape(blocks, width, width)]
    )
    mine = lax.psum_scatter(outgoing, ALL, scatter_dimension=1, tiled=True).astype(F32)
    mine_small = mine[three:].reshape(-1)
    back = [mine_small[starts[k] : starts[k + 1]].reshape(small[k].shape) for k in range(4)]
    return (
        final[:length].astype(LOW)[None],
        final[length : length + MEM][None],
        grad[:length][None],
        back[3],
        mine[:one].reshape(layers, count, rows, width),
        mine[one:two].reshape(layers, per, rows, width).transpose(0, 2, 1, 3).reshape(layers, rows, hidden),
        mine[two:three].reshape(layers, per * rows, width),
        back[0],
        back[1],
        back[2],
    )


def solution(mesh):
    in_specs = (
        P("dp", "blk", None),
        P("dp", "blk"),
        P(None, ALL),
        P(None, None, ALL, None),
        P(None, ALL, None),
        P(None, ALL, None),
        P(None, ALL),
        P(None, None, ALL),
        P(None, None, ALL),
        P("dp", "blk", None),
        P("dp", None, None),
    )
    out_specs = (
        P("dp", "blk", None),
        P("dp", None, None),
        P("dp", "blk", None),
        P(None, ALL),
        P(None, None, ALL, None),
        P(None, ALL, None),
        P(None, ALL, None),
        P(None, ALL),
        P(None, None, ALL),
        P(None, None, ALL),
    )
    return jax.shard_map(local, mesh=mesh, in_specs=in_specs, out_specs=out_specs, check_vma=False)
```

time: 1150 us -> 755 us (0.66)
  matrix products: 250 us -> 0 us
  Pallas kernels: 0 us -> 138 us
  local copies, waits for them, and re-layouts: 218 us -> 94.3 us
  other arithmetic: 126 us -> 22.7 us
  blocking collectives: 101 us -> 59.3 us
    dot_general x188 -> x0, matrix products: 250 us -> none  [the longest x28 37.1 us: weight_grad(): jnp.einsum('nd,ne->de', inputs, grads, preferred_element_type=jnp.float32)]
    pallas_call x0 -> x13, Pallas kernels: none -> 138 us  [call(): pl.pallas_call(body, out_shape=[jax.ShapeDtypeStruct(shape, kind) for sha...]
    psum x6 -> x0, blocking collectives: 73.9 us -> none  [memory_total(): lax.psum(for_sending(parts), 'blk')]
    reduce_sum x75 -> x0, other arithmetic: 39.1 us -> none  [the longest x20 11.9 us: normalize(): center = values - jnp.mean(values, -1, keepdims=True)]
    all_gather x4 -> x7, blocking collectives: 26.9 us -> 59.3 us  [the longest x6 53 us: everyone_of(): return lax.all_gather(value, 'blk')]
    another operation x31 -> x14, other arithmetic: 30.5 us -> 2.48 us
    reshape x20 -> x7, local copies, waits for them, and re-layouts: 30.5 us -> 3.75 us  [the longest x1 1.81 us: local(): m['down'].reshape(everyone, per, rows, width).transpose(1, 0, 2, 3)]
    another operation x36 -> x8, local copies, waits for them, and re-layouts: 27.1 us -> 0.55 us  [the longest x6 0.55 us: local(): jnp.stack([m[name] for m in made])]
  transfers between devices with their start and end apart: 33 -> 16, of which waited for: 19 -> 7; matrix products, arithmetic and copies ran while one was open for 16% -> 4% of each run, Pallas kernels for 0% -> 0%
where the time goes in v2:
time: 755 us; the launch traced here: 744 us
  waiting for transfers between devices  407 us (54%)
  Pallas kernels  138 us (18%)
  local copies, waits for them, and re-layouts  94.3 us (12%)
  blocking collectives  59.3 us (8%)
  other arithmetic  22.7 us (3%)
  between operations  15 us (2%)
  starting transfers between devices  7.77 us (1%)
    reduce_scatter x1, waiting for transfers between devices, local(): lax.psum_scatter(outgoing, ALL, scatter_dimension=1, tiled=True).astype(F32)  226 us
    pallas_call x13, Pallas kernels, call(): pl.pallas_call(body, out_shape=[jax.ShapeDtypeStruct(shape, kind) for sha...  138 us
    all_gather x1, waiting for transfers between devices, local(): whole = lax.all_gather(packed, ALL, axis=1, tiled=True)  133 us
    unnamed x82, local copies, waits for them, and re-layouts  55.6 us
    all_gather x6, blocking collectives, everyone_of(): return lax.all_gather(value, 'blk')  53 us
    ppermute x14, waiting for transfers between devices, flipped(): lax.ppermute(value, 'blk', [(source, source ^ bit) for source in range(si...  48.5 us
  transfers between devices with their start and end apart: 16, of which 7 were waited for; matrix products, arithmetic and copies ran while one was open for 4% of the time, Pallas kernels for 0%

profile of v2, /device:TPU:0, one launch (start us, length us, event | category | flops | bytes accessed | tf_op | source)
XLA Modules:
  0.0 744.0 jit_solution(8370446515663856624)
XLA Ops:
  16.1 6.2 all-gather
  23.5 133.0 %all-gather.9.cloned.1.call-done.refs_2_.refs_10_.refs_6_.refs_12_.refs_14_.refs_4_ = bf16[41,512,512]{2,1,0:T(8,128)(2,1)} async-done(((bf16[41,16,512]{2,1,0:T(8,128)(2,1)}), bf16[41,512,512]{2,1,0:T(8,128)(2,1)}) %all-gather.9.cloned.1.call-update) | async-done | bytes 21495824 | tf_op jit(solution)/shard_map/all_gather | solution.py:463
  159.0 3.8 first.1
  163.9 1.5 collective-permute-start.1
  165.7 12.4 %collective-permute-done.1.refs_4_.refs_9_ = bf16[256,1024]{1,0:T(8,128)(2,1)S(1)} collective-permute-done((bf16[256,1024]{1,0:T(8,128)(2,1)S(1)}, bf16[256,1024]{1,0:T(8,128)(2,1)S(1)}, u32[]{:S(2)}, u32[]{:S(2)}) %collective-permute-start.1) | collective-permute-done | bytes 524320 | tf_op jit(solution)/shard_map/ppermute | solution.py:435
  180.4 2.6 slice.297
  183.1 2.5 copy.74
  186.5 13.0 %attend_0.1 = (bf16[288,512]{1,0:T(8,128)(2,1)}, f32[288,512]{1,0:T(8,128)}, f32[288,512]{1,0:T(8,128)}, bf16[32,512]{1,0:T(8,128)(2,1)}, bf16[256,1024]{1,0:T(8...) custom-call(f32[288,512]{1,0:T(8,128)} %get-tuple-element.107.refs_0_, ...), custom_call_target="tpu_custom_call" | custom-call | tf_op jit(solution)/shard_map/attend_0/pallas_call | solution.py:421
  199.5 11.0 %all-gather.1 = f32[384,512]{1,0:T(8,128)} all-gather(f32[96,512]{1,0:T(8,128)} %get-tuple-element.111), channel_id=3, replica_groups=mesh['dp'=8,'blk'=4] {'blk'}, dimensions={0}, use_global_device_ids=true | all-gather | bytes 983040 | tf_op jit(solution)/shard_map/all_gather | solution.py:439
  210.5 10.0 %finish_0.1 = (f32[288,512]{1,0:T(8,128)}, bf16[288,512]{1,0:T(8,128)(2,1)}, bf16[288,1024]{1,0:T(8,128)(2,1)}, f32[32,512]{1,0:T(8,128)}, f32[32,512]{1,0:T(8,1...) custom-call(f32[288,512]{1,0:T(8,128)} %get-tuple-element.110.refs_0, ...), custom_call_target="tpu_custom_call" | custom-call | tf_op jit(solution)/shard_map/finish_0/pallas_call | solution.py:421
  222.3 13.6 %collective-permute-done.4.refs_4_.refs_9_ = bf16[256,1024]{1,0:T(8,128)(2,1)S(1)} collective-permute-done((bf16[256,1024]{1,0:T(8,128)(2,1)S(1)}, bf16[256,1024]{1,0:T(8,128)(2,1)S(1)}, u32[]{:S(2)}, u32[]{:S(2)}) %collective-permute-start.4) | collective-permute-done | bytes 524320 | tf_op jit(solution)/shard_map/ppermute | solution.py:435
  240.1 12.9 %attend_1.1 = (bf16[288,512]{1,0:T(8,128)(2,1)}, f32[288,512]{1,0:T(8,128)}, f32[288,512]{1,0:T(8,128)}, bf16[32,512]{1,0:T(8,128)(2,1)}, bf16[256,1024]{1,0:T(8...) custom-call(f32[288,512]{1,0:T(8,128)} %get-tuple-element.113.refs_0_, ...), custom_call_target="tpu_custom_call" | custom-call | tf_op jit(solution)/shard_map/attend_1/pallas_call | solution.py:421
  253.0 10.1 %all-gather.2 = f32[384,512]{1,0:T(8,128)} all-gather(f32[96,512]{1,0:T(8,128)} %get-tuple-element.117), channel_id=4, replica_groups=mesh['dp'=8,'blk'=4] {'blk'}, dimensions={0}, use_global_device_ids=true | all-gather | bytes 983040 | tf_op jit(solution)/shard_map/all_gather | solution.py:439
  263.1 8.6 %finish_1.1 = (f32[288,512]{1,0:T(8,128)}, f32[32,512]{1,0:T(8,128)}, f32[32,512]{1,0:T(8,128)}, f32[32,512]{1,0:T(8,128)}, f32[288,512]{1,0:T(8,128)}, /*index=...) custom-call(f32[288,512]{1,0:T(8,128)} %get-tuple-element.116.refs_0, ...), custom_call_target="tpu_custom_call" | custom-call | tf_op jit(solution)/shard_map/finish_1/pallas_call | solution.py:421
  271.7 14.5 %feed_back_1.1 = (bf16[4,512,512]{2,1,0:T(8,128)(2,1)}, bf16[4,512,512]{2,1,0:T(8,128)(2,1)}, bf16[512,512]{1,0:T(8,128)(2,1)}, bf16[512,512]{1,0:T(8,128)(2,1)}...) custom-call(f32[288,512]{1,0:T(8,128)} %fusion.15.refs_0_, ...), custom_call_target="tpu_custom_call" | custom-call | tf_op jit(solution)/shard_map/feed_back_1/pallas_call | solution.py:421
  286.2 9.6 %all-gather.3 = f32[256,512]{1,0:T(8,128)} all-gather(f32[64,512]{1,0:T(8,128)} %get-tuple-element.125), channel_id=5, replica_groups=mesh['dp'=8,'blk'=4] {'blk'}, dimensions={0}, use_global_device_ids=true | all-gather | bytes 655360 | tf_op jit(solution)/shard_map/all_gather | solution.py:439
  295.8 7.1 read_back_1.1
  302.9 6.8 all-gather.4
  309.7 18.1 %attend_back_1.1 = (bf16[512,512]{1,0:T(8,128)(2,1)}, bf16[512,512]{1,0:T(8,128)(2,1)}, f32[2,512]{1,0:T(2,128)}, f32[288,512]{1,0:T(8,128)}, bf16[288,512]{1,0:T(8,128)(2,1)}, /*index=5*/bf16[1056,1024]{1,0:T(8,128)(2,1)}) custom-call(f32[4,32,512]{2,1,0:T(8,128)} %bitcast.187, f32[32,512]{1,0:T(8,128)} %get-tuple-element.136.refs_1_, ...), custom_call_target="tpu_custom_call" | custom-call | tf_op jit(solution)/shard_map/attend_back_1/pallas_call | solution.py:421
  327.8 1.8 slice.228
  334.1 1.5 collective-permute-start.7
  337.9 11.9 %collective-permute-done.9 = bf16[32,1024]{1,0:T(8,128)(2,1)S(1)} collective-permute-done((bf16[32,1024]{1,0:T(8,128)(2,1)S(1)}, bf16[32,1024]{1,0:T(8,128)(2,1)S(1)}, u32[]{:S(2)}, u32[]{:S(2)}) %collective-permute-start.9) | collective-permute-done | bytes 65568 | tf_op jit(solution)/shard_map/ppermute | solution.py:435
  350.8 5.2 input_back_1.1
  356.0 14.4 %feed_back_0.1 = (bf16[4,512,512]{2,1,0:T(8,128)(2,1)}, bf16[4,512,512]{2,1,0:T(8,128)(2,1)}, bf16[512,512]{1,0:T(8,128)(2,1)}, bf16[512,512]{1,0:T(8,128)(2,1)}...) custom-call(f32[288,512]{1,0:T(8,128)} %get-tuple-element.142.refs_0_,, ...), custom_call_target="tpu_custom_call" | custom-call | tf_op jit(solution)/shard_map/feed_back_0/pallas_call | solution.py:421
  370.4 8.4 %all-gather.5 = f32[256,512]{1,0:T(8,128)} all-gather(f32[64,512]{1,0:T(8,128)} %get-tuple-element.148), channel_id=7, replica_groups=mesh['dp'=8,'blk'=4] {'blk'}, dimensions={0}, use_global_device_ids=true | all-gather | bytes 655360 | tf_op jit(solution)/shard_map/all_gather | solution.py:439
  378.8 7.1 read_back_0.1
  385.9 7.1 all-gather.6
  393.1 17.9 %attend_back_0.1 = (bf16[512,512]{1,0:T(8,128)(2,1)}, bf16[512,512]{1,0:T(8,128)(2,1)}, f32[2,512]{1,0:T(2,128)}, f32[288,512]{1,0:T(8,128)}, bf16[288,512]{1,0:T(8,128)(2,1)}, /*index=5*/bf16[1056,1024]{1,0:T(8,128)(2,1)}) custom-call(f32[4,32,512]{2,1,0:T(8,128)} %bitcast.186, f32[32,512]{1,0:T(8,128)} %get-tuple-element.159.refs_1_, ...), custom_call_target="tpu_custom_call" | custom-call | tf_op jit(solution)/shard_map/attend_back_0/pallas_call | solution.py:421
  411.0 1.8 slice.230
  416.0 1.8 copy.85
  420.4 1.6 convert_add_fusion
  423.4 1.5 collective-permute-start.11
  426.6 3.2 copy.84
  429.8 9.3 %collective-permute-done.13 = bf16[32,1024]{1,0:T(8,128)(2,1)S(1)} collective-permute-done((bf16[32,1024]{1,0:T(8,128)(2,1)S(1)}, bf16[32,1024]{1,0:T(8,128)(2,1)S(1)}, u32[]{:S(2)}, u32[]{:S(2)}) %collective-permute-start.13) | collective-permute-done | bytes 65568 | tf_op jit(solution)/shard_map/ppermute | solution.py:435
  441.3 5.2 input_back_0.1
  448.2 2.0 bitcast_dynamic-update-slice_fusion.23
  450.2 2.4 bitcast_dynamic-update-slice_fusion.22
  452.6 1.9 bitcast_dynamic-update-slice_fusion.21
  454.5 1.9 bitcast_dynamic-update-slice_fusion.20
  456.4 1.9 bitcast_dynamic-update-slice_fusion.19
  458.3 1.9 bitcast_dynamic-update-slice_fusion.18
  460.2 1.9 bitcast_dynamic-update-slice_fusion.17
  462.0 1.9 bitcast_dynamic-update-slice_fusion.16
  463.9 1.9 bitcast_dynamic-update-slice_fusion.15
  465.8 1.9 bitcast_dynamic-update-slice_fusion.14
  467.7 1.9 bitcast_dynamic-update-slice_fusion.13
  469.6 1.9 bitcast_dynamic-update-slice_fusion.12
  471.5 1.9 bitcast_dynamic-update-slice_fusion.11
  473.3 1.9 bitcast_dynamic-update-slice_fusion.10
  475.2 1.9 bitcast_dynamic-update-slice_fusion.9
  477.1 1.9 bitcast_dynamic-update-slice_fusion.8
  479.1 1.9 bitcast_dynamic-update-slice_fusion.7
  480.9 1.9 bitcast_dynamic-update-slice_fusion.6
  482.8 1.9 bitcast_dynamic-update-slice_fusion.5
  484.7 1.9 bitcast_dynamic-update-slice_fusion.4
  486.6 1.9 bitcast_dynamic-update-slice_fusion.3
  491.1 1.4 constant_dynamic-update-slice_fusion.4
  492.5 1.4 constant_dynamic-update-slice_fusion.3
  493.9 1.5 constant_dynamic-update-slice_fusion.2
  495.4 1.5 constant_dynamic-update-slice_fusion.1
  499.3 1.8 fusion.16
  501.9 225.7 %reduce-scatter.2.cloned.1.call-done = bf16[41,16,512]{2,1,0:T(8,128)(2,1)} async-done(((bf16[41,512,512]{2,1,0:T(8,128)(2,1)}), bf16[41,16,512]{2,1,0:T(8,128)(2,1)}) %reduce-scatter.2.cloned.1.call-update) | async-done | bytes 671760 | tf_op jit(solution)/shard_map/reduce_scatter | solution.py:634
  730.6 1.7 fusion.24
  735.0 2.0 slice.316
  (202 shorter events, 54.8 us)
Async XLA Ops:
  7.2 149.3 %all-gather.9.cloned.1.call-start = ((), (), s32[]{:S(2)}) async-start(), calls=%async_computation.1 | async-start | bytes 22167552 | tf_op jit(solution)/shard_map/all_gather | solution.py:463
  14.7 712.8 %reduce-scatter.2.cloned.1.call-start = ((), (), s32[]{:S(2)}) async-start(), calls=%async_computation.2 | async-start | bytes 22167552 | tf_op jit(solution)/shard_map/reduce_scatter | solution.py:634
  163.9 14.2 %collective-permute-start.1 = (bf16[256,1024]{1,0:T(8,128)(2,1)S(1)}, bf16[256,1024]{1,0:T(8,128)(2,1)S(1)}, u32[]{:S(2)}, u32[]{:S(2)}) collective-permute-start(bf16[256,1024]{1,0:T(8,128)(2,1)S(1)} %slice.214), channel_id=1, source_target_pairs={{0,2},{1,3},{2,0},{3,1},{4,6},{5,7},{6,4},{7,5},{8,10},{9,11},{10,... | collective-permute-start | bytes 1572872 | tf_op jit(solution)/shard_map/ppermute | solution.py:435
  165.4 20.2 %collective-permute-start = (bf16[256,1024]{1,0:T(8,128)(2,1)S(1)}, bf16[256,1024]{1,0:T(8,128)(2,1)S(1)}, u32[]{:S(2)}, u32[]{:S(2)}) collective-permute-start(bf16[256,1024]{1,0:T(8,128)(2,1)S(1)} %slice.214), channel_id=1, source_target_pairs={{0,1},{1,0},{2,3},{3,2},{4,5},{5,4},{6,7},{7,6},{8,9},{9,8},{10,11... | collective-permute-start | bytes 1572872 | tf_op jit(solution)/shard_map/ppermute | solution.py:435
  178.0 7.6 %copy-start.3 = (bf16[256,1024]{1,0:T(8,128)(2,1)}, bf16[256,1024]{1,0:T(8,128)(2,1)S(1)}, u32[]{:S(2)}) copy-start(bf16[256,1024]{1,0:T(8,128)(2,1)S(1)} %collective-permute-done.1.refs_4_.refs_9_) | copy-start | bytes 1572868
  178.0 7.6 %collective-permute-start.2 = (bf16[256,1024]{1,0:T(8,128)(2,1)S(1)}, bf16[256,1024]{1,0:T(8,128)(2,1)S(1)}, u32[]{:S(2)}, u32[]{:S(2)}) collective-permute-start(bf16[256,1024]{1,0:T(8,128)(2,1)S(1)} %collective-permute-done.1.refs_4_.refs_9_), channel_id=1, source_target_pairs={{0,1},{1,0},{2,3},{3,2},{4,5},{5,4},{6,7},{7,6},{8,9},{9,8},{10,11... | collective-permute-start | bytes 1572872 | tf_op jit(solution)/shard_map/ppermute | solution.py:435
  185.6 0.8 copy-start.4
  185.6 1.0 copy-start.5
  186.5 49.3 %copy-start.15 = (bf16[1,256,512]{2,1,0:T(8,128)(2,1)S(1)}, bf16[1,256,512]{2,1,0:T(8,128)(2,1)}, u32[]{:S(2)}) copy-start(bf16[1,256,512]{2,1,0:T(8,128)(2,1)} %param.24) | copy-start | bytes 786436
  186.5 49.3 %copy-start.16 = (bf16[1,20,512]{2,1,0:T(8,128)(2,1)S(1)}, bf16[1,20,512]{2,1,0:T(8,128)(2,1)}, u32[]{:S(2)}) copy-start(bf16[1,20,512]{2,1,0:T(8,128)(2,1)} %param.25) | copy-start | bytes 61444
  221.6 14.2 %collective-permute-start.4 = (bf16[256,1024]{1,0:T(8,128)(2,1)S(1)}, bf16[256,1024]{1,0:T(8,128)(2,1)S(1)}, u32[]{:S(2)}, u32[]{:S(2)}) collective-permute-start(bf16[256,1024]{1,0:T(8,128)(2,1)S(1)} %slice.222), channel_id=1, source_target_pairs={{0,2},{1,3},{2,0},{3,1},{4,6},{5,7},{6,4},{7,5},{8,10},{9,11},{10,... | collective-permute-start | bytes 1572872 | tf_op jit(solution)/shard_map/ppermute | solution.py:435
  222.2 16.9 %collective-permute-start.3 = (bf16[256,1024]{1,0:T(8,128)(2,1)S(1)}, bf16[256,1024]{1,0:T(8,128)(2,1)S(1)}, u32[]{:S(2)}, u32[]{:S(2)}) collective-permute-start(bf16[256,1024]{1,0:T(8,128)(2,1)S(1)} %slice.222), channel_id=1, source_target_pairs={{0,1},{1,0},{2,3},{3,2},{4,5},{5,4},{6,7},{7,6},{8,9},{9,8},{10,11... | collective-permute-start | bytes 1572872 | tf_op jit(solution)/shard_map/ppermute | solution.py:435
  235.8 3.3 copy-start.6
  235.8 3.3 collective-permute-start.5
  239.1 0.8 copy-start.7
  239.1 1.0 copy-start.8
  302.9 29.0 %copy-start.19 = (f32[5,512]{1,0:T(8,128)S(1)}, f32[5,512]{1,0:T(8,128)}, u32[]{:S(2)}) copy-start(f32[5,512]{1,0:T(8,128)} %get-tuple-element.201) | copy-start | bytes 30724
  302.9 29.0 %copy-start.17 = (f32[4,512]{1,0:T(4,128)S(1)}, f32[4,512]{1,0:T(4,128)}, u32[]{:S(2)}) copy-start(f32[4,512]{1,0:T(4,128)} %get-tuple-element.199) | copy-start | bytes 24580
  330.7 2.9 collective-permute-start.6
  331.9 3.7 collective-permute-start.8
  334.1 15.7 %collective-permute-start.7 = (bf16[256,1024]{1,0:T(8,128)(2,1)S(1)}, bf16[256,1024]{1,0:T(8,128)(2,1)S(1)}, u32[]{:S(2)}, u32[]{:S(2)}) collective-permute-start(bf16[256,1024]{1,0:T(8,128)(2,1)S(1)} %bitcast_convert_fusion.1), channel_id=1, source_target_pairs={{0,2},{1,3},{2,0},{3,1},{4,6},{5,7},{6,4},{7,5},{8,10},{9,11},{10,... | collective-permute-start | bytes 1572872 | tf_op jit(solution)/shard_map/ppermute | solution.py:435
  336.4 13.3 %collective-permute-start.9 = (bf16[32,1024]{1,0:T(8,128)(2,1)S(1)}, bf16[32,1024]{1,0:T(8,128)(2,1)S(1)}, u32[]{:S(2)}, u32[]{:S(2)}) collective-permute-start(bf16[32,1024]{1,0:T(8,128)(2,1)S(1)} %add_convert_fusion.3), channel_id=1, source_target_pairs={{0,2},{1,3},{2,0},{3,1},{4,6},{5,7},{6,4},{7,5},{8,10},{9,11},{10,... | collective-permute-start | bytes 196616 | tf_op jit(solution)/shard_map/ppermute | solution.py:435
  385.9 29.8 %copy-start.21 = (f32[4,512]{1,0:T(4,128)S(1)}, f32[4,512]{1,0:T(4,128)}, u32[]{:S(2)}) copy-start(f32[4,512]{1,0:T(4,128)} %get-tuple-element.195) | copy-start | bytes 24580
  385.9 32.7 %copy-start.22 = (f32[4,512]{1,0:T(4,128)S(1)}, f32[4,512]{1,0:T(4,128)}, u32[]{:S(2)}) copy-start(f32[4,512]{1,0:T(4,128)} %get-tuple-element.194) | copy-start | bytes 24580
  385.9 32.7 %copy-start.20 = (f32[5,512]{1,0:T(8,128)S(1)}, f32[5,512]{1,0:T(8,128)}, u32[]{:S(2)}) copy-start(f32[5,512]{1,0:T(8,128)} %get-tuple-element.198) | copy-start | bytes 30724
  385.9 33.0 %copy-start.18 = (f32[4,512]{1,0:T(4,128)S(1)}, f32[4,512]{1,0:T(4,128)}, u32[]{:S(2)}) copy-start(f32[4,512]{1,0:T(4,128)} %get-tuple-element.196) | copy-start | bytes 24580
  412.8 1.3 copy-start.1
  415.2 5.1 collective-permute-start.10
  420.2 4.8 collective-permute-start.12
  422.0 1.3 copy-start.2
  423.4 15.7 %collective-permute-start.11 = (bf16[256,1024]{1,0:T(8,128)(2,1)S(1)}, bf16[256,1024]{1,0:T(8,128)(2,1)S(1)}, u32[]{:S(2)}, u32[]{:S(2)}) collective-permute-start(bf16[256,1024]{1,0:T(8,128)(2,1)S(1)} %bitcast_convert_fusion), channel_id=1, source_target_pairs={{0,2},{1,3},{2,0},{3,1},{4,6},{5,7},{6,4},{7,5},{8,10},{9,11},{10,... | collective-permute-start | bytes 1572872 | tf_op jit(solution)/shard_map/ppermute | solution.py:435
  425.8 13.3 %collective-permute-start.13 = (bf16[32,1024]{1,0:T(8,128)(2,1)S(1)}, bf16[32,1024]{1,0:T(8,128)(2,1)S(1)}, u32[]{:S(2)}, u32[]{:S(2)}) collective-permute-start(bf16[32,1024]{1,0:T(8,128)(2,1)S(1)} %add_convert_fusion.1), channel_id=1, source_target_pairs={{0,2},{1,3},{2,0},{3,1},{4,6},{5,7},{6,4},{7,5},{8,10},{9,11},{10,... | collective-permute-start | bytes 196616 | tf_op jit(solution)/shard_map/ppermute | solution.py:435
  448.1 40.4 %copy-start.14 = (bf16[512,512]{1,0:T(8,128)(2,1)S(1)}, bf16[512,512]{1,0:T(8,128)(2,1)}, u32[]{:S(2)}) copy-start(bf16[512,512]{1,0:T(8,128)(2,1)} %get-tuple-element.187) | copy-start | bytes 1572868
  448.1 41.2 %copy-start.13 = (bf16[512,512]{1,0:T(8,128)(2,1)S(1)}, bf16[512,512]{1,0:T(8,128)(2,1)}, u32[]{:S(2)}) copy-start(bf16[512,512]{1,0:T(8,128)(2,1)} %get-tuple-element.188) | copy-start | bytes 1572868
  448.1 42.0 %copy-start.12 = (bf16[512,512]{1,0:T(8,128)(2,1)S(1)}, bf16[512,512]{1,0:T(8,128)(2,1)}, u32[]{:S(2)}) copy-start(bf16[512,512]{1,0:T(8,128)(2,1)} %get-tuple-element.189) | copy-start | bytes 1572868
  448.1 42.9 %copy-start.10 = (bf16[4,512,512]{2,1,0:T(8,128)(2,1)S(1)}, bf16[4,512,512]{2,1,0:T(8,128)(2,1)}, u32[]{:S(2)}) copy-start(bf16[4,512,512]{2,1,0:T(8,128)(2,1)} %get-tuple-element.190) | copy-start | bytes 6291460
  448.1 44.3 %copy-start.9 = (bf16[4,512,512]{2,1,0:T(8,128)(2,1)S(1)}, bf16[4,512,512]{2,1,0:T(8,128)(2,1)}, u32[]{:S(2)}) copy-start(bf16[4,512,512]{2,1,0:T(8,128)(2,1)} %get-tuple-element.191) | copy-start | bytes 6291460
  448.1 45.8 %copy-start = (bf16[4,32,16,512]{3,2,1,0:T(8,128)(2,1)S(1)}, bf16[4,32,16,512]{3,2,1,0:T(8,128)(2,1)}, u32[]{:S(2)}) copy-start(bf16[4,32,16,512]{3,2,1,0:T(8,128)(2,1)} %copy.84) | copy-start | bytes 6291460
  488.5 12.6 %copy-start.11 = (f32[288,512]{1,0:T(8,128)S(1)}, f32[288,512]{1,0:T(8,128)}, u32[]{:S(2)}) copy-start(f32[288,512]{1,0:T(8,128)} %get-tuple-element.165) | copy-start | bytes 1769476
Sparse Core Ops, SparseCore 0:
  14.8 141.5 all-gather.8
  497.9 229.6 reduce-scatter.1

commit v3 on v2

v3 whole, which is shorter than its diff:
```python
import functools

import jax
import jax.numpy as jnp
from jax import lax
from jax.experimental import pallas as pl
from jax.experimental.pallas import tpu as pltpu
from jax.sharding import PartitionSpec as P

HEADS = 8
HEAD = 64
MEM = 20
PAD = 32
NEG = -1000000000.0
BIG = 3.0e38
EPS = 1e-05
SCALE = HEAD**-0.5
ALL = ("dp", "blk")
LOW = jnp.bfloat16
F32 = jnp.float32
VMEM_LIMIT = 56 * 1024 * 1024
GATHER_AT = 4
PLAN = {
    1: [("early_1",), ("early_1",), ("early_1",), ("early_1",)],
    0: [
        ("early_1", "middle_1", "early_0"),
        ("middle_1", "early_0", "middle_0"),
        ("middle_1", "early_0", "attend_0"),
        ("middle_1", "early_0", "middle_0", "attend_0"),
        ("last", "middle_1", "middle_0", "attend_0"),
        ("last", "early_0", "middle_0", "attend_0"),
        ("last", "middle_0", "attend_0"),
        ("last",),
        ("last",),
    ],
}


def dot(a, b):
    return jnp.dot(a, b, preferred_element_type=F32)


def dot_nt(a, b):
    return lax.dot_general(a, b, (((1,), (1,)), ((), ())), preferred_element_type=F32)


def dot_tn(a, b):
    return lax.dot_general(a, b, (((0,), (0,)), ((), ())), preferred_element_type=F32)


def hat(x):
    center = x - jnp.mean(x, -1, keepdims=True)
    spread = jnp.mean(center * center, -1, keepdims=True)
    inv = lax.rsqrt(spread + EPS)
    return center * inv, inv


def norm(x, gain, shift):
    return hat(x)[0] * gain + shift


def norm_back(x, gain, grad):
    unit, inv = hat(x)
    scaled = grad * gain
    mean_one = jnp.mean(scaled, -1, keepdims=True)
    mean_two = jnp.mean(scaled * unit, -1, keepdims=True)
    return inv * (scaled - mean_one - unit * mean_two), grad * unit


def row(small_ref, rows_of, name, which):
    place = rows_of[name] + which
    return small_ref[place : place + 1, :]


def total(x):
    return jnp.sum(x, 0, keepdims=True)


def gelu_parts(u):
    k = 0.7978845608028654
    t = jnp.tanh(k * (u + 0.044715 * u * u * u))
    half = 0.5 * (1.0 + t)
    slope = half + 0.5 * u * (1.0 - t * t) * (k * (1.0 + 0.134145 * u * u))
    return u * half, slope


def head_mask(width):
    lanes = lax.broadcasted_iota(jnp.int32, (HEADS, 1, width), 2) // HEAD
    return lanes == lax.broadcasted_iota(jnp.int32, (HEADS, 1, width), 0)


def spread_heads(x):
    rows, width = x.shape
    full = jnp.where(head_mask(width), x.astype(F32)[None], 0.0)
    return full.reshape(HEADS * rows, width).astype(x.dtype)


def fold_heads(x):
    rows, width = x.shape
    full = x.reshape(HEADS, rows // HEADS, width)
    return jnp.sum(jnp.where(head_mask(width), full, 0.0), 0)


def two_heads(x):
    first = lax.broadcasted_iota(jnp.int32, x.shape, 1) < HEAD
    zero = jnp.zeros_like(x)
    return jnp.concatenate([jnp.where(first, x, zero), jnp.where(first, zero, x)], 0)


def pick_heads(x):
    width, rows = x.shape
    mine = (lax.broadcasted_iota(jnp.int32, x.shape, 0) < HEAD) == (
        lax.broadcasted_iota(jnp.int32, x.shape, 1) < rows // 2
    )
    both = jnp.where(mine, x, 0.0).T
    return both[: rows // 2] + both[rows // 2 :]


def bound_of(seg_keys, seg_queries):
    same = seg_keys == seg_queries
    allowed = (same | (seg_keys == -2.0) | (seg_queries == -1.0)) & (seg_keys != -3.0)
    return jnp.where(allowed, BIG, NEG)


def place_keys(keys_ref, own_ref, core_ref, chip_ref, both_ref, memory_ref):
    rows = core_ref.shape[0]
    me = lax.axis_index("blk")
    pieces = ((me, own_ref), (me ^ 1, core_ref), (me ^ 2, chip_ref), (me ^ 3, both_ref))
    for place, piece in pieces:
        keys_ref[pl.ds(pl.multiple_of(place * rows, rows), rows), :] = piece[0:rows, :]
    keys_ref[4 * rows :, :] = memory_ref[...]


def project(z, weight, q_ref, kv_ref, kvmem_ref):
    low = z.astype(LOW)
    rows, width = kv_ref.shape[0], low.shape[1]
    for part in (1, 2):
        lanes = pl.ds((part - 1) * width, width)
        value = dot(low, weight(part)).astype(LOW)
        kv_ref[:, lanes] = value[:rows]
        kvmem_ref[:, lanes] = value[rows:]
    q_ref[...] = dot(low, weight(0)).astype(LOW)


def first_kernel(weight, put, rows_of, tokens_ref, small_ref, z_ref, q_ref, kv_ref, kvmem_ref):
    rows = tokens_ref.shape[0]
    small = weight("small")[:, :128].astype(F32).T
    small_ref[...] = small
    z_ref[:rows, :] = tokens_ref[...].astype(F32)
    start = rows_of["memory"]
    z_ref[rows : rows + MEM, :] = small[start : start + MEM]
    z_ref[rows + MEM :, :] = jnp.zeros((PAD - MEM, small.shape[1]), F32)
    project(z_ref[...], weight, q_ref, kv_ref, kvmem_ref)


def attend_kernel(
    weight, put, rows_of, z_ref, q_ref, own_ref, core_ref, chip_ref, both_ref, kvmem_ref, segk_ref, segq_ref, small_ref,
    att_ref, pre_ref, one_ref, rq_ref, rkv_ref, wq_ref, part_ref,
    keys_ref, bound_ref,
):
    rows = core_ref.shape[0]
    width = z_ref.shape[1]
    place_keys(keys_ref, own_ref, core_ref, chip_ref, both_ref, kvmem_ref)
    bound_ref[...] = bound_of(segk_ref[...], segq_ref[...])

    def pair(step, carry):
        lanes = pl.ds(pl.multiple_of(step * 128, 128), 128)
        more = pl.ds(pl.multiple_of(width + step * 128, 128), 128)
        query = two_heads(q_ref[:, lanes]) * jnp.asarray(SCALE, LOW)
        keys = keys_ref[:, lanes]
        values = keys_ref[:, more]
        scores = jnp.minimum(dot_nt(keys, query), bound_ref[...])
        expo = jnp.exp(scores - jnp.max(scores, 0, keepdims=True))
        probs = expo * (1.0 / jnp.sum(expo, 0, keepdims=True))
        att_ref[:, lanes] = pick_heads(dot_tn(values, probs.astype(LOW))).astype(LOW)
        return carry

    lax.fori_loop(0, width // 128, pair, 0)
    pre = z_ref[...] + dot(att_ref[...], weight(3))
    pre_ref[...] = pre
    one = norm(pre, row(small_ref, rows_of, "gain", 0), row(small_ref, rows_of, "shift", 0))
    one_ref[...] = one
    low = one.astype(LOW)
    seq_low, mem_low = low[:rows], low[rows:]
    wq_ref[...] = dot(seq_low, weight(8)).astype(LOW)
    rq = dot(mem_low, weight(4)).astype(LOW)
    rk = dot(seq_low, weight(5)).astype(LOW)
    rv = dot(seq_low, weight(6)).astype(LOW)
    rq_ref[...] = rq
    rkv_ref[:, :width] = rk
    rkv_ref[:, width:] = rv
    scores = dot_nt(spread_heads(rq * jnp.asarray(SCALE, LOW)), rk)
    top = jnp.max(scores, -1, keepdims=True)
    expo = jnp.exp(scores - top)
    summed = jnp.sum(expo, -1, keepdims=True)
    part_ref[:, :width] = fold_heads(dot(expo.astype(LOW), rv))
    lanes = lax.broadcasted_iota(jnp.int32, (HEADS, PAD, 128), 2)
    heads = lax.broadcasted_iota(jnp.int32, (HEADS, PAD, 128), 0)
    top = jnp.where(lanes == heads, top.reshape(HEADS, PAD, 1), 0.0)
    summed = jnp.where(lanes == heads + HEADS, summed.reshape(HEADS, PAD, 1), 0.0)
    part_ref[:, width:] = jnp.sum(top + summed, 0)


def in_pairs(values):
    own, core, chip, both = values
    return (own + core) + (chip + both)


def widened(stats, start, width):
    lanes = lax.broadcasted_iota(jnp.int32, (128, width), 0)
    heads = lax.broadcasted_iota(jnp.int32, (128, width), 1) // HEAD + start
    return jnp.dot(
        stats, (lanes == heads).astype(F32), precision=lax.Precision.HIGHEST, preferred_element_type=F32
    )


def write_probs(wk, wq):
    scores = dot_nt(spread_heads(wk * jnp.asarray(SCALE, LOW)), wq)
    scores = scores.reshape(HEADS, PAD, scores.shape[1])
    real = lax.broadcasted_iota(jnp.int32, scores.shape, 1) < MEM
    scores = jnp.where(real, scores, NEG)
    expo = jnp.exp(scores - jnp.max(scores, 1, keepdims=True))
    return expo * (1.0 / jnp.sum(expo, 1, keepdims=True))


def finish_kernel(
    last, weight, put, rows_of, one_ref, own_ref, core_ref, chip_ref, both_ref, wq_ref, bias_ref, small_ref, *rest
):
    if last:
        (z_ref, rout_ref, rlse_ref, mempre_ref, two_ref, wkv_ref, wlow_ref, seqpre_ref, x_ref, feedpre_ref) = rest
    else:
        (z_ref, q_ref, kv_ref, kvmem_ref,
         rout_ref, rlse_ref, mempre_ref, two_ref, wkv_ref, wlow_ref, seqpre_ref, x_ref, feedpre_ref) = rest
    rows, width = wq_ref.shape
    parts = (own_ref, core_ref, chip_ref, both_ref)
    tops = [widened(part[:, width:], 0, width) for part in parts]
    sums = [widened(part[:, width:], HEADS, width) for part in parts]
    top = jnp.maximum(jnp.maximum(tops[0], tops[1]), jnp.maximum(tops[2], tops[3]))
    fades = [jnp.exp(value - top) for value in tops]
    accum = in_pairs([fade * part[:, :width] for fade, part in zip(fades, parts)])
    summed = in_pairs([fade * value for fade, value in zip(fades, sums)])
    rout = accum / summed
    rout_ref[...] = rout
    rlse_ref[...] = top + jnp.log(summed)
    mempre = one_ref[rows:, :] + dot(rout.astype(LOW), weight(7))
    mempre_ref[...] = mempre
    memtwo = norm(mempre, row(small_ref, rows_of, "gain", 1), row(small_ref, rows_of, "shift", 1))
    memlow = memtwo.astype(LOW)
    wk = dot(memlow, weight(9)).astype(LOW)
    wv = dot(memlow, weight(10)).astype(LOW)
    wkv_ref[:, :width] = wk
    wkv_ref[:, width:] = wv
    probs = write_probs(wk, wq_ref[...]).reshape(HEADS * PAD, rows)
    wlow = dot_tn(probs.astype(LOW), spread_heads(wv)).astype(LOW)
    wlow_ref[...] = wlow
    seqpre = one_ref[:rows, :] + dot(wlow, weight(11))
    seqpre_ref[...] = seqpre
    seqtwo = norm(seqpre, row(small_ref, rows_of, "gain", 2), row(small_ref, rows_of, "shift", 2))
    two_ref[:rows, :] = seqtwo
    two_ref[rows:, :] = memtwo
    two = two_ref[...]
    x = two.astype(LOW)
    x_ref[...] = x
    feed = two + row(small_ref, rows_of, "shift", 4)
    for part in range(bias_ref.shape[0]):
        u = dot(x, weight(("up", part))) + bias_ref[part : part + 1, :]
        feed = feed + dot(gelu_parts(u)[0].astype(LOW), weight("down", part))
    feedpre_ref[...] = feed
    z_ref[...] = norm(feed, row(small_ref, rows_of, "gain", 3), row(small_ref, rows_of, "shift", 3))
    if not last:
        project(z_ref[...], weight, q_ref, kv_ref, kvmem_ref)


def feed_back_kernel(
    share, weight, put, rows_of, grad_ref, feedpre_ref, x_ref, seqpre_ref, wlow_ref, wq_ref, wkv_ref, one_ref,
    bias_ref, small_ref,
    gbias_ref, gsmall_ref, mem_ref, seq_ref, part_ref,
):
    rows, width = wq_ref.shape
    full = grad_ref.shape[0]
    balance = jnp.where(lax.broadcasted_iota(jnp.int32, (full, 1), 0) < rows, 1.0, share)
    grad = grad_ref[...]
    feed, by_unit = norm_back(feedpre_ref[...], row(small_ref, rows_of, "gain", 3), grad)
    gsmall_ref[0:1, :] = total(by_unit * balance)
    gsmall_ref[1:2, :] = total(grad * balance)
    low = feed.astype(LOW)
    low_share = (low.astype(F32) * balance).astype(LOW)
    gsmall_ref[2:3, :] = total(low_share.astype(F32))
    x = x_ref[...]
    two = feed
    parts = bias_ref.shape[0]
    for part in range(parts):
        u = dot(x, weight(("up", part))) + bias_ref[part : part + 1, :]
        value, slope = gelu_parts(u)
        put(("down", part), dot_tn(value.astype(LOW), low_share))
        pre = (dot_nt(low, weight("down", part)) * slope).astype(LOW)
        pre_share = (pre.astype(F32) * balance).astype(LOW)
        gbias_ref[part : part + 1, :] = total(pre_share.astype(F32))
        put(("up", part), dot_tn(x, pre_share))
        two = two + dot_nt(pre, weight(("up", part)))
    mem_ref[...] = two[rows:]
    grad = two[:rows]
    seq, by_unit = norm_back(seqpre_ref[...], row(small_ref, rows_of, "gain", 2), grad)
    gsmall_ref[3:4, :] = total(by_unit)
    gsmall_ref[4:5, :] = total(grad)
    low = seq.astype(LOW)
    put(11, dot_tn(wlow_ref[...], low))
    out_low = dot_nt(low, weight(11)).astype(LOW)
    wk, wv = wkv_ref[:, :width], wkv_ref[:, width:]
    wq = wq_ref[...]
    probs = write_probs(wk, wq)
    prob_grad = dot_nt(spread_heads(wv), out_low).reshape(probs.shape)
    delta = jnp.sum(probs * prob_grad, 1, keepdims=True)
    score_grad = (probs * (prob_grad - delta)).reshape(HEADS * PAD, rows).astype(LOW)
    wq_low = (dot_tn(score_grad, spread_heads(wk)) * SCALE).astype(LOW)
    part_ref[:PAD, :] = (fold_heads(dot(score_grad, wq)) * SCALE).astype(LOW)
    part_ref[PAD:, :] = fold_heads(dot(probs.reshape(HEADS * PAD, rows).astype(LOW), out_low)).astype(LOW)
    put(8, dot_tn(one_ref[:rows, :].astype(LOW), wq_low))
    seq_ref[...] = seq + dot_nt(wq_low, weight(8))


def read_back_kernel(
    share, weight, put, rows_of, own_ref, core_ref, chip_ref, both_ref, mem_ref, seq_ref, two_ref, mempre_ref, rout_ref, rlse_ref, rq_ref, rkv_ref, one_ref,
    pre_ref, small_ref,
    gsmall_ref, memgrad_ref, seqjoint_ref, part_ref,
):
    rows, width = seq_ref.shape
    summed = in_pairs([part[...].astype(F32) for part in (own_ref, core_ref, chip_ref, both_ref)])
    k_low = summed[:PAD].astype(LOW)
    v_low = summed[PAD:].astype(LOW)
    mem_low = two_ref[rows:, :].astype(LOW)
    put(9, dot_tn(mem_low, k_low) * share)
    put(10, dot_tn(mem_low, v_low) * share)
    grad = mem_ref[...] + dot_nt(k_low, weight(9)) + dot_nt(v_low, weight(10))
    mem, by_unit = norm_back(mempre_ref[...], row(small_ref, rows_of, "gain", 1), grad)
    gsmall_ref[0:1, :] = total(by_unit) * share
    gsmall_ref[1:2, :] = total(grad) * share
    low = mem.astype(LOW)
    rout = rout_ref[...]
    put(7, dot_tn(rout.astype(LOW), low) * share)
    out_low = dot_nt(low, weight(7)).astype(LOW)
    memgrad_ref[...] = mem
    rk, rv = rkv_ref[:, :width], rkv_ref[:, width:]
    rq = spread_heads(rq_ref[...] * jnp.asarray(SCALE, LOW))
    out_wide = spread_heads(out_low)
    delta = jnp.sum(spread_heads(out_low.astype(F32) * rout), -1, keepdims=True)
    mask = head_mask(width)
    lse = jnp.max(jnp.where(mask, rlse_ref[...][None], -BIG).reshape(HEADS * PAD, width), -1, keepdims=True)
    probs = jnp.exp(dot_nt(rq, rk) - lse)
    score_grad = (probs * (dot_nt(out_wide, rv) - delta)).astype(LOW)
    part_ref[...] = (fold_heads(dot(score_grad, rk)) * SCALE).astype(LOW)
    key_low = dot_tn(score_grad, rq).astype(LOW)
    value_low = dot_tn(probs.astype(LOW), out_wide).astype(LOW)
    seq_low = one_ref[:rows, :].astype(LOW)
    put(5, dot_tn(seq_low, key_low))
    put(6, dot_tn(seq_low, value_low))
    grad = seq_ref[...] + dot_nt(key_low, weight(5)) + dot_nt(value_low, weight(6))
    joint, by_unit = norm_back(pre_ref[:rows, :], row(small_ref, rows_of, "gain", 0), grad)
    gsmall_ref[2:3, :] = total(by_unit)
    gsmall_ref[3:4, :] = total(grad)
    seqjoint_ref[...] = joint


def attend_back_kernel(
    share, weight, put, rows_of, z_ref, part_ref, corepart_ref, chippart_ref, bothpart_ref, memgrad_ref, seqjoint_ref, one_ref, pre_ref, att_ref,
    q_ref, own_ref, core_ref, chip_ref, both_ref, kvmem_ref, segk_ref, segq_ref, small_ref,
    gsmall_ref, joint_ref, qgrad_ref, keep_ref, send_ref,
    keys_ref, bound_ref, out_ref, kvgrad_ref,
):
    rows, width = seqjoint_ref.shape
    full = att_ref.shape[0]
    place_keys(keys_ref, own_ref, core_ref, chip_ref, both_ref, kvmem_ref)
    bound_ref[...] = bound_of(segk_ref[...], segq_ref[...])
    parts = (part_ref, corepart_ref, chippart_ref, bothpart_ref)
    q_low = in_pairs([part[...].astype(F32) for part in parts]).astype(LOW)
    put(4, dot_tn(one_ref[rows:, :].astype(LOW), q_low) * share)
    grad = memgrad_ref[...] + dot_nt(q_low, weight(4))
    mem, by_unit = norm_back(pre_ref[rows:, :], row(small_ref, rows_of, "gain", 0), grad)
    gsmall_ref[0:1, :] = total(by_unit) * share
    gsmall_ref[1:2, :] = total(grad) * share
    joint_ref[:rows, :] = seqjoint_ref[...]
    joint_ref[rows:, :] = mem
    low = joint_ref[...].astype(LOW)
    balance = jnp.where(lax.broadcasted_iota(jnp.int32, (full, 1), 0) < rows, 1.0, share)
    put(3, dot_tn(att_ref[...], (low.astype(F32) * balance).astype(LOW)))
    out_ref[...] = dot_nt(low, weight(3)).astype(LOW)

    def pair(step, carry):
        lanes = pl.ds(pl.multiple_of(step * 128, 128), 128)
        more = pl.ds(pl.multiple_of(width + step * 128, 128), 128)
        query = q_ref[:, lanes] * jnp.asarray(SCALE, LOW)
        out = out_ref[:, lanes]
        low_balance = jnp.concatenate([balance, balance], 0)
        query = two_heads(query)
        out = two_heads(out)
        keys = keys_ref[:, lanes]
        values = keys_ref[:, more]
        scores = jnp.minimum(dot_nt(keys, query), bound_ref[...])
        expo = jnp.exp(scores - jnp.max(scores, 0, keepdims=True))
        probs = expo * (1.0 / jnp.sum(expo, 0, keepdims=True))
        prob_grad = dot_nt(values, out)
        delta = jnp.sum(probs * prob_grad, 0, keepdims=True)
        score_grad = (probs * (prob_grad - delta)).astype(LOW)
        qgrad_ref[:, lanes] = (pick_heads(dot_tn(keys, score_grad)) * SCALE).astype(LOW)
        query_share = (query.astype(F32) * low_balance).astype(LOW)
        out_share = (out.astype(F32) * low_balance).astype(LOW)
        kvgrad_ref[:, lanes] = dot(score_grad, query_share).astype(LOW)
        kvgrad_ref[:, more] = dot(probs.astype(LOW), out_share).astype(LOW)
        return carry

    lax.fori_loop(0, width // 128, pair, 0)
    z_low = z_ref[...].astype(LOW)
    put(0, dot_tn(z_low, (qgrad_ref[...].astype(F32) * balance).astype(LOW)))
    me = lax.axis_index("blk")
    for place, (goal, other) in enumerate(((keep_ref, 0), (keep_ref, 2), (send_ref, 1), (send_ref, 3))):
        rest = pl.ds(pl.multiple_of((me ^ other) * rows, rows), rows)
        goal[place % 2 * rows : (place % 2 + 1) * rows, :] = kvgrad_ref[rest, :]
    for goal in (keep_ref, send_ref):
        goal[2 * rows :, :] = kvgrad_ref[4 * rows :, :]


def input_back_kernel(
    share, weight, put, rows_of, z_ref, joint_ref, qgrad_ref, mine_ref, sent_ref, got_ref, *rest
):
    *small_refs, zgrad_ref, kvgrad_ref = rest
    full, width = z_ref.shape
    rows = full - PAD
    balance = jnp.where(lax.broadcasted_iota(jnp.int32, (full, 1), 0) < rows, 1.0, share)
    low = z_ref[...].astype(LOW)
    kvgrad_ref[:rows, :] = (mine_ref[...] + got_ref[:rows, :].astype(F32)).astype(LOW)
    kvgrad_ref[rows:, :] = (sent_ref[rows:, :].astype(F32) + got_ref[rows:, :].astype(F32)).astype(LOW)
    grads = (qgrad_ref[...], kvgrad_ref[:, :width], kvgrad_ref[:, width:])
    grad = joint_ref[...]
    for part, value in enumerate(grads):
        if part > 0:
            put(part, dot_tn(low, (value.astype(F32) * balance).astype(LOW)))
        grad = grad + dot_nt(value, weight(part))
    zgrad_ref[...] = grad
    if small_refs:
        layers = [[ref[...] for ref in small_refs[k : k + 4]] for k in range(0, len(small_refs), 4)]
        lines = []
        for one, two, three, _ in layers:
            lines.extend([two[2:3] + three[0:1], two[0:1], one[3:4], one[0:1]])
        for one, two, three, _ in layers:
            lines.extend([two[3:4] + three[1:2], two[1:2], one[4:5], one[1:2], one[2:3]])
        lines.extend(bias for _, _, _, bias in layers)
        lines.append(grad[rows:] * share)
        small = jnp.concatenate(lines, 0)
        small = jnp.concatenate([small, jnp.zeros((width - small.shape[0], width), F32)], 0)
        put("small", small.T)


class Order:
    def __init__(self, stages):
        self.stages = stages

    def place(self, number):
        result = 0
        for stage in self.stages:
            result = 2 * result + ((number >> bit_place(stage)) & 1)
        return result

    def mine(self):
        result = 0
        for axis, bit in self.stages:
            result = 2 * result + ((lax.axis_index(axis) >> bit) & 1)
        return result


def call(kernel, name, cost, ins, outs, weights, scratch=(), grads=None, after=(), rows_of=None):
    sources, operands, begins = [], [], []
    for source, _, _ in weights.values():
        if not any(source is other for other in sources):
            sources.append(source)
            begins.append(len(operands))
            operands.extend(source[0])
    places, slots = {}, 0
    for key, (source, slot, count) in weights.items():
        which = [source is other for other in sources].index(True)
        places[key] = (which, slot, slots, count)
        slots = slots + count
    high, width = operands[0].shape[2:]
    shards = width // high
    grad_slots, number = {}, 0
    if grads is not None:
        for key in grads[0]:
            if key in ("down",):
                grad_slots[key] = number
                number += grads[2]
            else:
                grad_slots[key] = number
                number += 1
    halves = 0 if grads is None else (1 if grads[1] is None else 2)

    def body(*refs):
        in_refs, refs = refs[: len(ins)], refs[len(ins) :]
        operand_refs, refs = refs[: len(operands)], refs[len(operands) + len(after) :]
        grad_refs, refs = refs[:halves], refs[halves:]
        if halves:
            *refs, buffer, sems, made, made_sems = refs
        else:
            *refs, buffer, sems = refs
        core = lax.axis_index("blk") % 2
        copies = {}
        for turn, (key, (which, slot, place, count)) in enumerate(places.items()):
            copies[key] = []
            arrays = len(sources[which][0])
            piece = shards // arrays
            for part in range(arrays):
                copy = pltpu.make_async_copy(
                    operand_refs[begins[which] + part].at[:, pl.ds(slot, count)],
                    buffer.at[pl.ds(part * piece, piece), pl.ds(place, count)],
                    sems.at[turn, part],
                )
                copy.start()
                copies[key].append(copy)
        arrived = set()
        offsets = [None if order is None else order.mine() for _, order in sources]

        def weight(key, part=None):
            if key not in arrived:
                for copy in copies[key]:
                    copy.wait()
                arrived.add(key)
            which, _, place, count = places[key]
            order = sources[which][1]
            span = range(shards) if part is None else range(part * (shards // count), (part + 1) * (shards // count))
            pieces = []
            for shard in span:
                if order is None:
                    at = shard
                else:
                    at = ((shard % 2) ^ core) * (shards // 2) + (order.place(shard) ^ offsets[which])
                pieces.extend(buffer[at, place + slot] for slot in range(count))
            return jnp.concatenate(pieces, 0)

        out = []
        if halves:
            offset = None if grads[1] is None else grads[1].mine()

        def put(key, grad):
            low = grad.astype(LOW)
            if isinstance(key, tuple) and key[0] == "down":
                count, slot, first = grads[2], grad_slots["down"], key[1] * (shards // grads[2])
            else:
                count, slot, first = 1, grad_slots[key], 0
            for block in range(low.shape[0] // high):
                shard, inner = first + block // count, block % count
                value = low[block * high : (block + 1) * high]
                if halves == 1:
                    made[shard, slot + inner] = value
                else:
                    at = ((shard % 2) ^ core) * (shards // 2) + (grads[1].place(shard) ^ offset)
                    made[at, slot + inner] = value
            if count == 1 or key[1] == count - 1:
                piece = shards // halves
                for half in range(halves):
                    copy = pltpu.make_async_copy(
                        made.at[pl.ds(half * piece, piece), pl.ds(slot, count)],
                        grad_refs[half].at[:, pl.ds(slot, count)],
                        made_sems.at[slot, half],
                    )
                    copy.start()
                    out.append(copy)

        kernel(weight, put, rows_of, *in_refs, *refs)
        for copy in out:
            copy.wait()

    inside, anywhere = pl.BlockSpec(memory_space=pltpu.VMEM), pl.BlockSpec(memory_space=pl.ANY)
    shapes = [jax.ShapeDtypeStruct((shards // max(halves, 1), number, high, width), LOW)] * halves
    scratch = list(scratch) + [
        pltpu.VMEM((shards, slots, high, width), LOW),
        pltpu.SemaphoreType.DMA((len(weights), 2)),
    ]
    if halves:
        scratch += [pltpu.VMEM((shards, number, high, width), LOW), pltpu.SemaphoreType.DMA((number, 2))]
    results = pl.pallas_call(
        body,
        out_shape=shapes + [jax.ShapeDtypeStruct(shape, kind) for shape, kind in outs],
        in_specs=[inside] * len(ins) + [anywhere] * (len(operands) + len(after)),
        out_specs=[anywhere] * halves + [inside] * len(outs),
        scratch_shapes=scratch,
        compiler_params=pltpu.CompilerParams(vmem_limit_bytes=VMEM_LIMIT),
        cost_estimate=pl.CostEstimate(flops=int(cost * 1.1e8), bytes_accessed=0, transcendentals=0),
        name=name,
    )(*ins, *operands, *after)
    return ([results[:halves]] if halves else []) + list(results[halves:])


def flipped(value, bit):
    size = lax.axis_size("blk")
    return lax.ppermute(value, "blk", [(source, source ^ bit) for source in range(size)])


def quartet(value):
    return [value] + [flipped(value, bit) for bit in (1, 2, 3)]


def bits_of(axis):
    return lax.axis_size(axis).bit_length() - 1


def bit_place(stage):
    axis, bit = stage
    return bit if axis == "blk" else bits_of("blk") + bit


def swapped(value, stage):
    axis, bit = stage
    return lax.ppermute(value, axis, [(source, source ^ (1 << bit)) for source in range(lax.axis_size(axis))])


def fence(*arrays):
    return list(lax.optimization_barrier(tuple(arrays)))


class Gathering:
    def __init__(self, groups):
        self.groups = groups
        self.held = [shard[None] for shard, _, _ in groups]
        self.got, self.turn = {}, 0

    def begin(self):
        done = {}
        for number, (_, stages, first) in enumerate(self.groups):
            if first <= self.turn < first + len(stages):
                self.got[number] = swapped(self.held[number], stages[self.turn - first])
                if self.turn - first + 1 == len(stages):
                    done[number] = ((self.held[number], self.got.pop(number)), Order(stages[-2::-1]))
        return done

    def end(self, *others):
        for number, value in self.got.items():
            self.held[number] = jnp.concatenate([self.held[number], value])
        self.turn += 1
        waiting = [n for n, (_, stages, first) in enumerate(self.groups) if self.turn < first + len(stages)]
        bundle = fence(*[self.held[n] for n in waiting], *others)
        for number, value in zip(waiting, bundle):
            self.held[number] = value
        self.got = {}
        return bundle[len(waiting) :]


def joined(values):
    return values[0] if len(values) == 1 else jnp.concatenate(values, 1)


class Scattering:
    def __init__(self, arrays, stages):
        self.keeps = [keep for keep, _ in arrays]
        self.sends = [send for _, send in arrays]
        self.stages = list(stages)
        self.gots, self.result = None, None

    def begin(self):
        stage = self.stages.pop(0)
        self.gots = [swapped(send, stage) for send in self.sends]

    def end(self):
        sums = [keep.astype(F32) + got.astype(F32) for keep, got in zip(self.keeps, self.gots)]
        self.gots = None
        if not self.stages:
            self.result = joined(sums)[0]
            return
        half = sums[0].shape[0] // 2
        self.keeps = [joined([value[:half] for value in sums]).astype(LOW)]
        self.sends = [joined([value[half:] for value in sums]).astype(LOW)]


class Background:
    def __init__(self):
        self.sums, self.running = {}, []

    def add(self, name, arrays, stages):
        self.sums[name] = Scattering(arrays, stages)

    def begin(self, *names):
        for name in names:
            if name in self.sums:
                self.sums[name].begin()
                self.running.append(self.sums[name])

    def end(self, *others):
        if not self.running:
            return list(others)
        gots = [got for run in self.running for got in run.gots]
        gots = fence(*gots, *others)
        for run in self.running:
            run.gots, gots = gots[: len(run.gots)], gots[len(run.gots) :]
            run.end()
        self.running = []
        return gots


def local(
    tokens, segments, memory_init, attn_weights, ffn_in, ffn_out, ffn_bias, norm_gain, norm_shift, out_grad, memory_cot
):
    layers, count, rows, width = attn_weights.shape
    hidden = ffn_in.shape[2]
    per = hidden // width
    everyone = lax.axis_size("dp") * lax.axis_size("blk")
    direct = rows == 16
    core_bit, chip_bits = ("blk", 0), [("blk", bit) for bit in range(1, bits_of("blk"))]
    line_bits, near_bit = [("dp", bit) for bit in reversed(range(1, bits_of("dp")))], [("dp", 0)]

    small = [
        norm_gain.reshape(-1, rows), norm_shift.reshape(-1, rows), ffn_bias.reshape(-1, rows), memory_init
    ]
    starts = [sum(part.shape[0] for part in small[:k]) for k in range(5)]
    gain_rows, shift_rows = norm_gain.shape[1], norm_shift.shape[1]
    small = jnp.concatenate(small, 0).T.astype(LOW)
    small = jnp.pad(small, ((0, 0), (0, width - small.shape[1])))[None]

    def rows_of(index):
        return dict(gain=starts[0] + index * gain_rows, shift=starts[1] + index * shift_rows, memory=starts[3])

    attn_low, up_low, down_low = attn_weights.astype(LOW), ffn_in.astype(LOW), ffn_out.astype(LOW)
    up_low = up_low.reshape(layers, rows, per, width).transpose(0, 2, 1, 3)
    down_low = down_low.reshape(layers, per, rows, width)
    early, middle, late = (0, 1, 2), (3, 8, 4, 5, 6), (7, 9, 10, 11)
    table = {}

    def listed(source, index, keys):
        place = 0
        for key in keys:
            size = per if key == "down" else 1
            table[index, key] = (source, place, size)
            place += size

    ups = tuple(("up", part) for part in range(per))
    if direct:

        def picked(index, keys):
            return [attn_low[index, key][None] for key in keys]

        y_last = line_bits + chip_bits + near_bit + [core_bit]
        x_last = near_bit + line_bits + chip_bits + [core_bit]
        x_early = chip_bits + line_bits + near_bit + [core_bit]
        gathering = Gathering(
            [
                (jnp.concatenate(picked(0, early) + [small]), y_last, 0),
                (jnp.concatenate(picked(0, middle)), y_last, 1),
                (jnp.concatenate(picked(0, late) + [up_low[0]]), y_last, 2),
                (jnp.concatenate([down_low[0]] + picked(1, early)), x_last, 2),
                (jnp.concatenate(picked(1, middle)), x_early, 4),
            ]
        )
        rest = jnp.concatenate(picked(1, late) + [up_low[1], down_low[1]])
        for turn in range(4):
            if turn == GATHER_AT:
                whole = lax.all_gather(rest, ALL)
            gathering.begin()
            (rest,) = gathering.end(rest)
        if GATHER_AT == 4:
            whole = lax.all_gather(rest, ALL)
        listed(gathering.begin()[0], 0, early + ("small",))
        listed(((whole,), None), 1, late + ups + ("down",))
    else:
        packed = jnp.concatenate(
            [attn_low.reshape(-1, rows, width), up_low.reshape(-1, rows, width), small, down_low.reshape(-1, rows, width)]
        )
        whole = lax.all_gather(packed, ALL)
        split = layers * (count + per) + 1
        square = whole[:, :split].transpose(1, 0, 2, 3).reshape(split, -1, 16, width)
        downs = whole[:, split:].reshape(everyone, layers, per * rows, width).transpose(1, 0, 2, 3)
        downs = downs.reshape(layers, -1, per, 16, width).transpose(0, 2, 1, 3, 4).reshape(layers * per, -1, 16, width)
        source = ((jnp.concatenate([square, downs]).transpose(1, 0, 2, 3),), None)
        for index in range(layers):
            for key in range(count):
                table[index, key] = (source, index * count + key, 1)
            for part in range(per):
                table[index, ("up", part)] = (source, layers * count + index * per + part, 1)
            table[index, "down"] = (source, split + index * per, per)
        table[0, "small"] = (source, split - 1, 1)

    def attn(index, *keys):
        return {key: table[index, key] for key in keys}

    def feed(index):
        return attn(index, *ups, "down")

    length = tokens.shape[1]
    full = length + PAD
    size = lax.axis_size("blk")
    share = 1.0 / size
    me = lax.axis_index("blk")
    seg = segments[0].astype(F32)
    seg_parts = jnp.zeros((size, length), F32)
    for other, part in enumerate(quartet(segments)):
        seg_parts = lax.dynamic_update_slice(seg_parts, part.astype(F32), (me ^ other, 0))
    seg_keys = jnp.concatenate(
        [seg_parts.reshape(-1), jnp.full((MEM,), -2.0, F32), jnp.full((PAD - MEM,), -3.0, F32)]
    ).reshape(-1, 1)
    seg_row = jnp.concatenate([seg, jnp.full((PAD,), -1.0, F32)])
    seg_queries = jnp.concatenate([seg_row, seg_row]).reshape(1, -1)
    every = size * length + PAD
    keys_scratch = pltpu.VMEM((every, 2 * width), LOW)
    bound_scratch = pltpu.VMEM((every, 2 * full), F32)
    projected = [((full, width), LOW), ((length, 2 * width), LOW), ((PAD, 2 * width), LOW)]

    smalls, z, q, own, kvmem = call(
        first_kernel,
        "first",
        4,
        [tokens[0]],
        [((128, width), F32), ((full, width), F32)] + projected,
        attn(0, *early, "small"),
        rows_of=rows_of(0),
    )
    bias = smalls[starts[2] : starts[3]].reshape(layers, per, everyone, rows).transpose(0, 2, 1, 3)
    bias = bias.reshape(layers, per, width)
    kept = []
    for index in range(layers):
        core = flipped(own, 1)
        chip = flipped(own, 2)
        both = flipped(chip, 1)
        if direct:
            core, chip, both, seg_keys = gathering.end(core, chip, both, seg_keys)
            listed(gathering.begin()[1 if index == 0 else 4], index, middle)
        att, pre, first, rq, rkv, wq, part = call(
            attend_kernel,
            f"attend_{index}",
            13,
            [z, q, own, core, chip, both, kvmem, seg_keys, seg_queries, smalls],
            [
                ((full, width), LOW), ((full, width), F32), ((full, width), F32), ((PAD, width), LOW),
                ((length, 2 * width), LOW), ((length, width), LOW), ((PAD, width + 128), F32),
            ],
            attn(index, 3, 8, 4, 5, 6),
            [keys_scratch, bound_scratch],
            rows_of=rows_of(index),
        )
        parts = quartet(part)
        if direct and index == 0:
            parts = gathering.end(*parts)
            found = gathering.begin()
            listed(found[2], 0, late + ups)
            listed(found[3], 0, ("down",))
            for key in early:
                table[1, key] = (found[3], per + key, 1)
        last = index + 1 == layers
        results = call(
            functools.partial(finish_kernel, last),
            f"finish_{index}",
            10,
            [first, *parts, wq, bias[index], smalls],
            [((full, width), F32)]
            + ([] if last else projected)
            + [
                ((PAD, width), F32), ((PAD, width), F32), ((PAD, width), F32), ((full, width), F32),
                ((PAD, 2 * width), LOW), ((length, width), LOW), ((length, width), F32), ((full, width), LOW),
                ((full, width), F32),
            ],
            attn(index, 7, 9, 10, 11) | feed(index) | ({} if last else attn(index + 1, *early)),
            rows_of=rows_of(index),
        )
        rout, rlse, mempre, second, wkv, wlow, seqpre, x, feedpre = results[-9:]
        kept.append(
            dict(
                z=z, q=q, own=own, kvmem=kvmem, core=core, chip=chip, both=both, att=att, pre=pre, first=first,
                rq=rq, rkv=rkv, wq=wq, rout=rout, rlse=rlse, mempre=mempre, second=second, wkv=wkv, wlow=wlow,
                seqpre=seqpre, x=x, feedpre=feedpre,
            )
        )
        z = results[0]
        if not last:
            q, own, kvmem = results[1:4]
            if direct:
                q, own, kvmem = gathering.end(q, own, kvmem)
                gathering.begin()
    final = z
    grad = jnp.concatenate(
        [out_grad[0].astype(F32), jnp.pad(memory_cot[0].astype(F32), ((0, PAD - MEM), (0, 0)))]
    )
    background = Background()
    upward = line_bits[::-1]
    x_late = near_bit + upward + chip_bits
    y_first = near_bit + chip_bits + upward
    x_first = chip_bits + near_bit + upward
    z_first = upward[:1] + near_bit + chip_bits + upward[1:]
    orders = {"early": (z_first, x_late), "middle": (y_first, x_late), "attend": (x_first, x_late), "last": (y_first, x_late)}

    def given(keys, order):
        return (keys, Order(order) if direct else None, per)

    group_keys = [ups + ("down", 11, 8), (9, 10, 7, 5, 6), (4, 3, 0), (1, 2)]
    made = [None] * layers
    for index in reversed(range(layers)):
        k = kept[index]
        grads_one, gbias, small_one, mem, seq, part = call(
            functools.partial(feed_back_kernel, share),
            f"feed_back_{index}",
            14,
            [grad, k["feedpre"], k["x"], k["seqpre"], k["wlow"], k["wq"], k["wkv"], k["first"], bias[index], smalls],
            [
                ((per, width), F32),
                ((5, width), F32), ((PAD, width), F32), ((length, width), F32), ((2 * PAD, width), LOW),
            ],
            feed(index) | attn(index, 11, 8),
            grads=given(group_keys[0], orders["early"][min(index, 1)]),
            rows_of=rows_of(index),
        )
        part, mem, seq = background.end(part, mem, seq)
        if direct:
            background.add(f"early_{index}", [grads_one], [core_bit] + orders["early"][min(index, 1)])
        background.begin(*PLAN[index][0])
        grads_two, small_two, mem, seq, part = call(
            functools.partial(read_back_kernel, share),
            f"read_back_{index}",
            7,
            [*quartet(part), mem, seq, k["second"], k["mempre"], k["rout"], k["rlse"], k["rq"], k["rkv"],
             k["first"], k["pre"], smalls],
            [((4, width), F32), ((PAD, width), F32), ((length, width), F32), ((PAD, width), LOW)],
            attn(index, 9, 10, 7, 5, 6),
            grads=given(group_keys[1], orders["middle"][min(index, 1)]),
            rows_of=rows_of(index),
        )
        part, mem, seq = background.end(part, mem, seq)
        if direct and index == 0:
            background.add("middle_0", [grads_two], [core_bit] + orders["middle"][0])
        background.begin(*PLAN[index][1])
        grads_three, small_three, joint, qgrad, keep, send = call(
            functools.partial(attend_back_kernel, share),
            f"attend_back_{index}",
            18,
            [k["z"], *quartet(part), mem, seq, k["first"], k["pre"], k["att"], k["q"], k["own"], k["core"], k["chip"],
             k["both"], k["kvmem"], seg_keys, seg_queries, smalls],
            [((2, width), F32), ((full, width), F32), ((full, width), LOW),
             ((2 * length + PAD, 2 * width), LOW), ((2 * length + PAD, 2 * width), LOW)],
            attn(index, 4, 3),
            [keys_scratch, bound_scratch, pltpu.VMEM((full, width), LOW), keys_scratch],
            grads=given(group_keys[2], orders["attend"][min(index, 1)]),
            rows_of=rows_of(index),
        )
        keep, send = background.end(keep, send)
        if direct and index == 0:
            background.add("attend_0", [grads_three], [core_bit] + orders["attend"][0])
        background.begin(*PLAN[index][2])
        pair_sum = keep.astype(F32) + flipped(send, 1).astype(F32)
        mine_part, theirs = pair_sum[:length], pair_sum[length:].astype(LOW)
        got = flipped(theirs, 2)
        got, mine_part, theirs = background.end(got, mine_part, theirs)
        background.begin(*PLAN[index][3])
        made[index] = dict(
            small=[small_one, small_two, small_three],
            bias=gbias.reshape(everyone, per, rows).transpose(1, 0, 2).reshape(per, width),
        )
        tiny = sum([m["small"] + [m["bias"]] for m in made], []) if index == 0 else []
        grads_four, grad = call(
            functools.partial(input_back_kernel, share),
            f"input_back_{index}",
            5,
            [k["z"], joint, qgrad, mine_part, theirs, got] + tiny,
            [((full, width), F32)],
            attn(index, 0, 1, 2),
            [pltpu.VMEM((full, 2 * width), LOW)],
            grads=given(group_keys[3] + (("small",) if tiny else ()), orders["last"][min(index, 1)]),
        )
        if direct and index > 0:
            background.add(f"middle_{index}", [grads_two, grads_three, grads_four], [core_bit] + x_late)
        made[index]["grads"] = (grads_one, grads_two, grads_three, grads_four)

    mine = [{} for _ in range(layers)]
    if direct:
        (kept_four,) = background.end(grads_four[0])
        background.add("last", [(kept_four, grads_four[1])], [core_bit] + orders["last"][0])
        for names in PLAN[0][4:]:
            background.begin(*names)
            background.end()
        for index in range(layers):
            wanted = (f"early_{index}", f"middle_{index}") + (("attend_0", "last") if index == 0 else ())
            results = [background.sums[name].result for name in wanted]
            keys = list(group_keys)
            if index > 0:
                keys = [keys[0], keys[1] + keys[2] + keys[3]]
            else:
                keys[3] = keys[3] + ("small",)
            for result, held in zip(results, keys):
                place = 0
                for key in held:
                    number = per if key == "down" else 1
                    mine[index][key] = result[place : place + number].reshape(number * rows, width)
                    place += number
    else:
        outgoing, order = [], []
        for index, m in enumerate(made):
            held = sum(group_keys, ()) + (("small",) if index == 0 else ())
            stack = jnp.concatenate([part[0] for part in m["grads"]], 1).transpose(1, 0, 2, 3)
            place = 0
            for key in held:
                if key == "down":
                    downs = stack[place : place + per].transpose(1, 0, 2, 3).reshape(everyone, per, rows, width)
                    outgoing.append(downs.transpose(1, 0, 2, 3).reshape(per, width, width))
                    order.extend((index, ("down", part)) for part in range(per))
                    place += per
                else:
                    outgoing.append(stack[place].reshape(1, width, width))
                    order.append((index, key))
                    place += 1
        result = lax.psum_scatter(jnp.concatenate(outgoing), ALL, scatter_dimension=1, tiled=True).astype(F32)
        for place, (index, key) in enumerate(order):
            mine[index][key] = result[place]
        for m in mine:
            m["down"] = jnp.concatenate([m["down", part] for part in range(per)])
    back = mine[0]["small"].T
    return (
        final[:length].astype(LOW)[None],
        final[length : length + MEM][None],
        grad[:length][None],
        back[starts[3] : starts[4]],
        jnp.stack([jnp.stack([m[key] for key in range(count)]) for m in mine]),
        jnp.stack([jnp.concatenate([m["up", part] for part in range(per)], -1) for m in mine]),
        jnp.stack([m["down"] for m in mine]),
        back[starts[2] : starts[3]].reshape(ffn_bias.shape),
        back[starts[0] : starts[1]].reshape(norm_gain.shape),
        back[starts[1] : starts[2]].reshape(norm_shift.shape),
    )


def solution(mesh):
    in_specs = (
        P("dp", "blk", None),
        P("dp", "blk"),
        P(None, ALL),
        P(None, None, ALL, None),
        P(None, ALL, None),
        P(None, ALL, None),
        P(None, ALL),
        P(None, None, ALL),
        P(None, None, ALL),
        P("dp", "blk", None),
        P("dp", None, None),
    )
    out_specs = (
        P("dp", "blk", None),
        P("dp", None, None),
        P("dp", "blk", None),
        P(None, ALL),
        P(None, None, ALL, None),
        P(None, ALL, None),
        P(None, ALL, None),
        P(None, ALL),
        P(None, None, ALL),
        P(None, None, ALL),
    )
    return jax.shard_map(local, mesh=mesh, in_specs=in_specs, out_specs=out_specs, check_vma=False)
```

time: 755 us -> 517 us (0.68)
  waiting for transfers between devices: 407 us -> 182 us
  starting transfers between devices: 7.77 us -> 84.1 us
  blocking collectives: 59.3 us -> 0 us
  local copies, waits for them, and re-layouts: 94.3 us -> 43 us
  other arithmetic: 22.7 us -> 40.4 us
    reduce_scatter x1 -> x0, waiting for transfers between devices: 226 us -> none  [local(): lax.psum_scatter(outgoing, ALL, scatter_dimension=1, tiled=True).astype(F32)]
    all_gather x1, waiting for transfers between devices: 133 us -> 0.02 us  [local(): whole = lax.all_gather(rest, ALL)]
    ppermute x0 -> x57, waiting for transfers between devices: none -> 119 us  [swapped(): lax.ppermute(value, axis, [(source, source ^ 1 << bit) for source in rang...]
    ppermute x0 -> x57, starting transfers between devices: none -> 65.8 us  [swapped(): lax.ppermute(value, axis, [(source, source ^ 1 << bit) for source in rang...]
    all_gather x7 -> x0, blocking collectives: 59.3 us -> none  [the longest x6 53 us: everyone_of(): return lax.all_gather(value, 'blk')]
    unnamed x82 -> x155, local copies, waits for them, and re-layouts: 55.6 us -> 14.8 us
    another operation x14 -> x34, other arithmetic: 2.48 us -> 23.1 us
    ppermute x14 -> x31, waiting for transfers between devices: 48.5 us -> 63.4 us  [flipped(): lax.ppermute(value, 'blk', [(source, source ^ bit) for source in range(si...]
  transfers between devices with their start and end apart: 16 -> 89, of which waited for: 7 -> 49; matrix products, arithmetic and copies ran while one was open for 4% -> 12% of each run, Pallas kernels for 0% -> 20%
where the time goes in v3:
time: 517 us; the launch traced here: 510 us
  waiting for transfers between devices  182 us (35%)
  Pallas kernels  144 us (28%)
  starting transfers between devices  84.1 us (16%)
  local copies, waits for them, and re-layouts  43 us (8%)
  other arithmetic  40.4 us (8%)
  between operations  16 us (3%)
    pallas_call x13, Pallas kernels, call(): pl.pallas_call(body, out_shape=shapes + [jax.ShapeDtypeStruct(shape, kind...  144 us
    ppermute x57, waiting for transfers between devices, swapped(): lax.ppermute(value, axis, [(source, source ^ 1 << bit) for source in rang...  119 us
    ppermute x57, starting transfers between devices, swapped(): lax.ppermute(value, axis, [(source, source ^ 1 << bit) for source in rang...  65.8 us
    ppermute x31, waiting for transfers between devices, flipped(): lax.ppermute(value, 'blk', [(source, source ^ bit) for source in range(si...  63.4 us
    another operation x30, other arithmetic  20.7 us
    ppermute x31, starting transfers between devices, flipped(): lax.ppermute(value, 'blk', [(source, source ^ bit) for source in range(si...  18.3 us
    unnamed x155, local copies, waits for them, and re-layouts  14.8 us
    concatenate x20, other arithmetic, end(): self.held[number] = jnp.concatenate([self.held[number], value])  12.8 us
  transfers between devices with their start and end apart: 89, of which 49 were waited for; matrix products, arithmetic and copies ran while one was open for 12% of the time, Pallas kernels for 20%

profile of v3, /device:TPU:0, one launch (start us, length us, event | category | flops | bytes accessed | tf_op | source)
XLA Modules:
  0.0 510.3 jit_solution(5239155718108186318)
XLA Ops:
  11.8 4.1 collective-permute-start
  16.2 3.4 collective-permute-done
  21.2 2.4 collective-permute-start.1
  23.6 2.4 collective-permute-done.2
  30.3 1.8 collective-permute-start.4
  33.7 3.4 collective-permute-done.5
  42.8 6.7 %collective-permute-done.10 = bf16[2,7,16,512]{3,2,1,0:T(8,128)(2,1)S(1)} collective-permute-done((bf16[2,7,16,512]{3,2,1,0:T(8,128)(2,1)S(1)}, bf16[2,7,16,512]{3,2,1,0:T(8,128)(2,1)S(1)}, u32[]{:S(2)}, u32[]{:S(2)}) %collective-permute-start.10) | collective-permute-done | bytes 229408 | tf_op jit(solution)/shard_map/ppermute | solution.py:611
  50.5 2.6 collective-permute-done.11.refs_2_.refs_15_
  54.1 4.6 first.1
  60.3 2.1 collective-permute-start.14
  65.8 24.6 %collective-permute-done.21 = s32[1,256]{1,0:T(1,128)S(1)} collective-permute-done((s32[1,256]{1,0:T(1,128)S(1)}, s32[1,256]{1,0:T(1,128)S(1)}, u32[]{:S(2)}, u32[]{:S(2)}) %collective-permute-start.21) | collective-permute-done | bytes 1056 | tf_op jit(solution)/shard_map/ppermute | solution.py:593
  90.4 3.5 collective-permute-done.20
  94.3 4.1 collective-permute-done.15
  99.6 2.0 pad_maximum_fusion.7
  107.5 2.9 collective-permute-start.25
  112.1 10.5 %collective-permute-done.25 = bf16[2,5,16,512]{3,2,1,0:T(8,128)(2,1)S(1)} collective-permute-done((bf16[2,5,16,512]{3,2,1,0:T(8,128)(2,1)}, bf16[2,5,16,512]{3,2,1,0:T(8,128)(2,1)S(1)}, u32[]{:S(2)}, u32[]{:S(2)}) %collective-permute-start.25) | collective-permute-done | bytes 163872 | tf_op jit(solution)/shard_map/ppermute | solution.py:611
  124.3 10.2 %collective-permute-done.24 = bf16[8,7,16,512]{3,2,1,0:T(8,128)(2,1)} collective-permute-done((bf16[8,7,16,512]{3,2,1,0:T(8,128)(2,1)}, bf16[8,7,16,512]{3,2,1,0:T(8,128)(2,1)}, u32[]{:S(2)}, u32[]{:S(2)}) %collective-permute-start.24) | collective-permute-done | bytes 917536 | tf_op jit(solution)/shard_map/ppermute | solution.py:611
  134.5 2.9 pad_maximum_fusion.1.refs_10_.refs_6_.refs_12_
  138.4 12.9 %attend_0.1 = (bf16[288,512]{1,0:T(8,128)(2,1)}, f32[288,512]{1,0:T(8,128)}, f32[288,512]{1,0:T(8,128)}, bf16[32,512]{1,0:T(8,128)(2,1)}, bf16[256,1024]{1,0:T(8...) custom-call(f32[288,512]{1,0:T(8,128)} %get-tuple-element.215.refs_0_, ...), custom_call_target="tpu_custom_call" | custom-call | flops 1430000000 | tf_op jit(solution)/shard_map/attend_0/pallas_call | solution.py:578
  156.2 1.8 collective-permute-done.27.refs_3_
  161.8 6.8 %collective-permute-done.31 = bf16[4,5,16,512]{3,2,1,0:T(8,128)(2,1)S(1)} collective-permute-done((bf16[4,5,16,512]{3,2,1,0:T(8,128)(2,1)}, bf16[4,5,16,512]{3,2,1,0:T(8,128)(2,1)S(1)}, u32[]{:S(2)}, u32[]{:S(2)}) %collective-permute-start.31) | collective-permute-done | bytes 327712 | tf_op jit(solution)/shard_map/ppermute | solution.py:611
  169.6 9.7 %finish_0.1 = (f32[288,512]{1,0:T(8,128)}, bf16[288,512]{1,0:T(8,128)(2,1)}, bf16[256,1024]{1,0:T(8,128)(2,1)}, bf16[32,1024]{1,0:T(8,128)(2,1)}, f32[32,512]{1,...) custom-call(f32[288,512]{1,0:T(8,128)} %get-tuple-element.229.refs_0, ...), custom_call_target="tpu_custom_call" | custom-call | flops 1100000000 | tf_op jit(solution)/shard_map/finish_0/pallas_call | solution.py:578
  181.4 11.2 %collective-permute-done.34.refs_4_.refs_13_ = bf16[256,1024]{1,0:T(8,128)(2,1)S(1)} collective-permute-done((bf16[256,1024]{1,0:T(8,128)(2,1)}, bf16[256,1024]{1,0:T(8,128)(2,1)S(1)}, u32[]{:S(2)}, u32[]{:S(2)}) %collective-permute-start.34) | collective-permute-done | bytes 524320 | tf_op jit(solution)/shard_map/ppermute | solution.py:593
  192.7 2.7 collective-permute-done.32
  197.5 2.0 collective-permute-done.36.refs_11_.refs_12_.refs_17_.refs_20_
  200.6 13.0 %attend_1.1 = (bf16[288,512]{1,0:T(8,128)(2,1)}, f32[288,512]{1,0:T(8,128)}, f32[288,512]{1,0:T(8,128)}, bf16[32,512]{1,0:T(8,128)(2,1)}, bf16[256,1024]{1,0:T(8...) custom-call(f32[288,512]{1,0:T(8,128)} %get-tuple-element.241.refs_0_, ...), custom_call_target="tpu_custom_call" | custom-call | flops 1430000000 | tf_op jit(solution)/shard_map/attend_1/pallas_call | solution.py:578
  218.2 2.1 collective-permute-done.38.refs_3_
  221.0 7.9 %finish_1.1 = (f32[288,512]{1,0:T(8,128)}, f32[32,512]{1,0:T(8,128)}, f32[32,512]{1,0:T(8,128)}, f32[32,512]{1,0:T(8,128)}, f32[288,512]{1,0:T(8,128)}, /*index=...) custom-call(f32[288,512]{1,0:T(8,128)} %get-tuple-element.255.refs_0, ...), custom_call_target="tpu_custom_call" | custom-call | flops 1100000000 | tf_op jit(solution)/shard_map/finish_1/pallas_call | solution.py:578
  228.9 12.9 %feed_back_1.1 = (bf16[16,10,16,512]{3,2,1,0:T(8,128)(2,1)}, bf16[16,10,16,512]{3,2,1,0:T(8,128)(2,1)}, f32[4,512]{1,0:T(4,128)}, f32[5,512]{1,0:T(8,128)}, f32[...) custom-call(f32[288,512]{1,0:T(8,128)} %fusion.2.refs_0_, f32[288,512]{1,0:T(8,128)} %get-tuple-element.260.refs_1_, ...), custom_call_target="tpu_custom_call" | custom-call | flops 1540000000 | tf_op jit(solution)/shard_map/feed_back_1/pallas_call | solution.py:578
  241.9 2.2 collective-permute-start.43
  244.4 2.4 collective-permute-done.43.refs_3_
  249.2 7.9 %read_back_1.1 = (bf16[16,5,16,512]{3,2,1,0:T(8,128)(2,1)}, bf16[16,5,16,512]{3,2,1,0:T(8,128)(2,1)}, f32[4,512]{1,0:T(4,128)}, f32[32,512]{1,0:T(8,128)}, f32[256,512]{1,0:T(8,128)}, /*index=5*/bf16[32,512]{1,0:T(8,128)(2,1)}) custom-call(bf16[64,512]{1,0:T(8,128)(2,1)} %get-tuple-element.267.refs_0_, bf16[64,512]{1,0:T(8,128)(2,1)} %copy-done.49, ...), custom_call_target="tpu_custom_call" | custom-call | flops 770000000 | tf_op jit(solution)/shard_map/read_back_1/pallas_call | solution.py:578
  262.0 1.8 collective-permute-done.47.refs_4_
  265.1 20.9 %attend_back_1.1 = (bf16[16,3,16,512]{3,2,1,0:T(8,128)(2,1)}, bf16[16,3,16,512]{3,2,1,0:T(8,128)(2,1)}, f32[2,512]{1,0:T(2,128)}, f32[288,512]{1,0:T(8,128)}, bf...) custom-call(f32[288,512]{1,0:T(8,128)} %get-tuple-element.241.refs_0_, ...), custom_call_target="tpu_custom_call" | custom-call | flops 1980000000 | tf_op jit(solution)/shard_map/attend_back_1/pallas_call | solution.py:578
  286.0 2.5 collective-permute-done.44
  289.1 1.8 collective-permute-start.48
  292.0 1.9 collective-permute-start.50
  295.0 11.4 %collective-permute-done.48 = bf16[4,10,16,512]{3,2,1,0:T(8,128)(2,1)S(1)} collective-permute-done((bf16[4,10,16,512]{3,2,1,0:T(8,128)(2,1)S(1)}, bf16[4,10,16,512]{3,2,1,0:T(8,128)(2,1)S(1)}, u32[]{:S(2)}, u32[]{:S(2)}) %collective-permute-start.48) | collective-permute-done | bytes 655392 | tf_op jit(solution)/shard_map/ppermute | solution.py:611
  308.4 6.0 %input_back_1.1 = (bf16[16,2,16,512]{3,2,1,0:T(8,128)(2,1)}, bf16[16,2,16,512]{3,2,1,0:T(8,128)(2,1)}, f32[288,512]{1,0:T(8,128)}) custom-call(f32[288,512]{1,0:T(8,128)} %get-tuple-element.241.refs_0_, f32[288,512]{1,0:T(8,128)} %get-tuple-element.291.refs_1_, bf16[288,512]{1,0:T(8,128)(2,1)} %get-tuple-element.292.refs_2_, f32[256,1024]{1,0:T(8,128)} %slice.720.refs_3_, ...), custom_call_target="tpu_custom_call" | custom-call | flops 550000000 | tf_op jit(solution)/shard_map/input_back_1/pallas_call | solution.py:578
  314.4 12.9 %feed_back_0.1 = (bf16[16,10,16,512]{3,2,1,0:T(8,128)(2,1)}, bf16[16,10,16,512]{3,2,1,0:T(8,128)(2,1)}, f32[4,512]{1,0:T(4,128)}, f32[5,512]{1,0:T(8,128)}, f32[...) custom-call(f32[288,512]{1,0:T(8,128)} %get-tuple-element.296.refs_0_, ...), custom_call_target="tpu_custom_call" | custom-call | flops 1540000000 | tf_op jit(solution)/shard_map/feed_back_0/pallas_call | solution.py:578
  328.1 2.6 collective-permute-start.51
  330.8 15.0 %collective-permute-done.51 = bf16[2,10,16,512]{3,2,1,0:T(8,128)(2,1)S(1)} collective-permute-done((bf16[2,10,16,512]{3,2,1,0:T(8,128)(2,1)S(1)}, bf16[2,10,16,512]{3,2,1,0:T(8,128)(2,1)S(1)}, u32[]{:S(2)}, u32[]{:S(2)}) %collective-permute-start.51) | collective-permute-done | bytes 327712 | tf_op jit(solution)/shard_map/ppermute | solution.py:611
  347.7 2.2 collective-permute-done.59.refs_3_
  351.4 2.8 collective-permute-done.58.refs_2_
  357.5 8.0 %read_back_0.1 = (bf16[16,5,16,512]{3,2,1,0:T(8,128)(2,1)}, bf16[16,5,16,512]{3,2,1,0:T(8,128)(2,1)}, f32[4,512]{1,0:T(4,128)}, f32[32,512]{1,0:T(8,128)}, f32[256,512]{1,0:T(8,128)}, /*index=5*/bf16[32,512]{1,0:T(8,128)(2,1)}) custom-call(bf16[64,512]{1,0:T(8,128)(2,1)} %get-tuple-element.310.refs_0_, bf16[64,512]{1,0:T(8,128)(2,1)} %copy-done.47, ...), custom_call_target="tpu_custom_call" | custom-call | flops 770000000 | tf_op jit(solution)/shard_map/read_back_0/pallas_call | solution.py:578
  377.4 2.2 collective-permute-done.62.refs_4_
  381.4 21.0 %attend_back_0.1 = (bf16[16,3,16,512]{3,2,1,0:T(8,128)(2,1)}, bf16[16,3,16,512]{3,2,1,0:T(8,128)(2,1)}, f32[2,512]{1,0:T(2,128)}, f32[288,512]{1,0:T(8,128)}, bf...) custom-call(f32[288,512]{1,0:T(8,128)} %get-tuple-element.215.refs_0_, ...), custom_call_target="tpu_custom_call" | custom-call | flops 1980000000 | tf_op jit(solution)/shard_map/attend_back_0/pallas_call | solution.py:578
  402.5 2.1 collective-permute-done.64
  407.6 1.9 add_convert_fusion.3
  410.5 1.9 add_convert_fusion.4
  428.2 2.4 add_convert_fusion.2
  437.2 2.7 collective-permute-start.71
  442.0 6.6 %input_back_0.1 = (bf16[16,3,16,512]{3,2,1,0:T(8,128)(2,1)}, bf16[16,3,16,512]{3,2,1,0:T(8,128)(2,1)}, f32[288,512]{1,0:T(8,128)}) custom-call(f32[288,512]{1,0:T(8,128)} %get-tuple-element.215.refs_0_, f32[288,512]{1,0:T(8,128)} %get-tuple-element.327.refs_1_, bf16[288,512]{1,0:T(8,128)(2,1)} %get-tuple-element.328.refs_2_, f32[256,1024]{1,0:T(8,128)} %slice.735.refs_3_, ...), custom_call_target="tpu_custom_call" | custom-call | flops 550000000 | tf_op jit(solution)/shard_map/input_back_0/pallas_call | solution.py:578
  448.7 1.9 slice_bitcast_fusion
  450.6 3.4 collective-permute-done.71
  458.9 1.9 collective-permute-start.80
  460.7 7.3 %collective-permute-done.76 = bf16[1,10,16,512]{3,2,1,0:T(8,128)(2,1)S(1)} collective-permute-done((bf16[1,10,16,512]{3,2,1,0:T(8,128)(2,1)S(1)}, bf16[1,10,16,512]{3,2,1,0:T(8,128)(2,1)S(1)}, u32[]{:S(2)}, u32[]{:S(2)}) %collective-permute-start.76) | collective-permute-done | bytes 163872 | tf_op jit(solution)/shard_map/ppermute | solution.py:611
  468.6 1.8 collective-permute-start.81
  471.3 2.0 collective-permute-done.82
  475.1 4.9 collective-permute-done.79
  480.3 2.6 collective-permute-start.85
  490.6 3.2 collective-permute-done.86
  493.9 2.6 collective-permute-start.87
  496.5 2.4 collective-permute-done.87
  (442 shorter events, 139.8 us)
Async XLA Ops:
  7.2 213.2 %all-gather.3.cloned.1.call-start = ((), (), s32[]{:S(2)}) async-start(), calls=%async_computation | async-start | bytes 6488064 | tf_op jit(solution)/shard_map/all_gather | solution.py:756
  11.8 7.8 %collective-permute-start = (bf16[1,4,16,512]{3,2,1,0:T(8,128)(2,1)S(1)}, bf16[1,4,16,512]{3,2,1,0:T(8,128)(2,1)S(1)}, u32[]{:S(2)}, u32[]{:S(2)}) collective-permute-start(bf16[1,4,16,512]{3,2,1,0:T(8,128)(2,1)S(1)} %maximum_bitcast_fusion.3), channel_id=1, source_target_pairs={{0,16},{4,20},{8,24},{12,28},{16,0},{20,4},{24,8},{28,12},{1,17},{... | collective-permute-start | bytes 196616 | tf_op jit(solution)/shard_map/ppermute | solution.py:611
  19.6 6.5 %collective-permute-start.2 = (bf16[1,5,16,512]{3,2,1,0:T(8,128)(2,1)S(1)}, bf16[1,5,16,512]{3,2,1,0:T(8,128)(2,1)S(1)}, u32[]{:S(2)}, u32[]{:S(2)}) collective-permute-start(bf16[1,5,16,512]{3,2,1,0:T(8,128)(2,1)S(1)} %bitcast.278), channel_id=1, source_target_pairs={{0,16},{4,20},{8,24},{12,28},{16,0},{20,4},{24,8},{28,12},{1,17},{... | collective-permute-start | bytes 245768 | tf_op jit(solution)/shard_map/ppermute | solution.py:611
  21.2 6.4 %collective-permute-start.1 = (bf16[2,4,16,512]{3,2,1,0:T(8,128)(2,1)S(1)}, bf16[2,4,16,512]{3,2,1,0:T(8,128)(2,1)S(1)}, u32[]{:S(2)}, u32[]{:S(2)}) collective-permute-start(bf16[2,4,16,512]{3,2,1,0:T(8,128)(2,1)S(1)} %pad_maximum_fusion.23), channel_id=1, source_target_pairs={{0,8},{4,12},{8,0},{12,4},{16,24},{20,28},{24,16},{28,20},{1,9},{5... | collective-permute-start | bytes 393224 | tf_op jit(solution)/shard_map/ppermute | solution.py:611
  27.6 6.1 %collective-permute-start.6 = (bf16[1,7,16,512]{3,2,1,0:T(8,128)(2,1)S(1)}, bf16[1,7,16,512]{3,2,1,0:T(8,128)(2,1)S(1)}, u32[]{:S(2)}, u32[]{:S(2)}) collective-permute-start(bf16[1,7,16,512]{3,2,1,0:T(8,128)(2,1)S(1)} %maximum_bitcast_fusion.2), channel_id=1, source_target_pairs={{0,4},{4,0},{8,12},{12,8},{16,20},{20,16},{24,28},{28,24},{1,5},{5... | collective-permute-start | bytes 344072 | tf_op jit(solution)/shard_map/ppermute | solution.py:611
  29.2 7.9 %collective-permute-start.5 = (bf16[1,8,16,512]{3,2,1,0:T(8,128)(2,1)S(1)}, bf16[1,8,16,512]{3,2,1,0:T(8,128)(2,1)S(1)}, u32[]{:S(2)}, u32[]{:S(2)}) collective-permute-start(bf16[1,8,16,512]{3,2,1,0:T(8,128)(2,1)S(1)} %bitcast.274), channel_id=1, source_target_pairs={{0,16},{4,20},{8,24},{12,28},{16,0},{20,4},{24,8},{28,12},{1,17},{... | collective-permute-start | bytes 393224 | tf_op jit(solution)/shard_map/ppermute | solution.py:611
  30.3 7.6 %collective-permute-start.4 = (bf16[2,5,16,512]{3,2,1,0:T(8,128)(2,1)S(1)}, bf16[2,5,16,512]{3,2,1,0:T(8,128)(2,1)S(1)}, u32[]{:S(2)}, u32[]{:S(2)}) collective-permute-start(bf16[2,5,16,512]{3,2,1,0:T(8,128)(2,1)S(1)} %pad_maximum_fusion.21), channel_id=1, source_target_pairs={{0,8},{4,12},{8,0},{12,4},{16,24},{20,28},{24,16},{28,20},{1,9},{5... | collective-permute-start | bytes 491528 | tf_op jit(solution)/shard_map/ppermute | solution.py:611
  32.1 6.5 %collective-permute-start.3 = (bf16[4,4,16,512]{3,2,1,0:T(8,128)(2,1)S(1)}, bf16[4,4,16,512]{3,2,1,0:T(8,128)(2,1)S(1)}, u32[]{:S(2)}, u32[]{:S(2)}) collective-permute-start(bf16[4,4,16,512]{3,2,1,0:T(8,128)(2,1)S(1)} %pad_maximum_fusion.16), channel_id=1, source_target_pairs={{0,2},{1,3},{2,0},{3,1},{4,6},{5,7},{6,4},{7,5},{8,10},{9,11},{10,... | collective-permute-start | bytes 786440 | tf_op jit(solution)/shard_map/ppermute | solution.py:611
  38.7 10.8 %collective-permute-start.10 = (bf16[2,7,16,512]{3,2,1,0:T(8,128)(2,1)S(1)}, bf16[2,7,16,512]{3,2,1,0:T(8,128)(2,1)S(1)}, u32[]{:S(2)}, u32[]{:S(2)}) collective-permute-start(bf16[2,7,16,512]{3,2,1,0:T(8,128)(2,1)S(1)} %pad_maximum_fusion.20), channel_id=1, source_target_pairs={{0,16},{4,20},{8,24},{12,28},{16,0},{20,4},{24,8},{28,12},{1,17},{... | collective-permute-start | bytes 688136 | tf_op jit(solution)/shard_map/ppermute | solution.py:611
  39.6 10.7 %collective-permute-start.7 = (bf16[8,4,16,512]{3,2,1,0:T(8,128)(2,1)S(1)}, bf16[8,4,16,512]{3,2,1,0:T(8,128)(2,1)S(1)}, u32[]{:S(2)}, u32[]{:S(2)}) collective-permute-start(bf16[8,4,16,512]{3,2,1,0:T(8,128)(2,1)S(1)} %pad_maximum_fusion.11), channel_id=1, source_target_pairs={{0,4},{4,0},{8,12},{12,8},{16,20},{20,16},{24,28},{28,24},{1,5},{5... | collective-permute-start | bytes 1572872 | tf_op jit(solution)/shard_map/ppermute | solution.py:611
  40.1 10.0 %collective-permute-start.9 = (bf16[2,8,16,512]{3,2,1,0:T(8,128)(2,1)S(1)}, bf16[2,8,16,512]{3,2,1,0:T(8,128)(2,1)S(1)}, u32[]{:S(2)}, u32[]{:S(2)}) collective-permute-start(bf16[2,8,16,512]{3,2,1,0:T(8,128)(2,1)S(1)} %pad_maximum_fusion.17), channel_id=1, source_target_pairs={{0,8},{4,12},{8,0},{12,4},{16,24},{20,28},{24,16},{28,20},{1,9},{5... | collective-permute-start | bytes 786440 | tf_op jit(solution)/shard_map/ppermute | solution.py:611
  41.3 8.9 %collective-permute-start.8 = (bf16[4,5,16,512]{3,2,1,0:T(8,128)(2,1)S(1)}, bf16[4,5,16,512]{3,2,1,0:T(8,128)(2,1)S(1)}, u32[]{:S(2)}, u32[]{:S(2)}) collective-permute-start(bf16[4,5,16,512]{3,2,1,0:T(8,128)(2,1)S(1)} %pad_maximum_fusion.14), channel_id=1, source_target_pairs={{0,2},{1,3},{2,0},{3,1},{4,6},{5,7},{6,4},{7,5},{8,10},{9,11},{10,... | collective-permute-start | bytes 983048 | tf_op jit(solution)/shard_map/ppermute | solution.py:611
  58.7 39.7 %collective-permute-start.17 = (bf16[256,1024]{1,0:T(8,128)(2,1)}, bf16[256,1024]{1,0:T(8,128)(2,1)S(1)}, u32[]{:S(2)}, u32[]{:S(2)}) collective-permute-start(bf16[256,1024]{1,0:T(8,128)(2,1)} %get-tuple-element.217.refs_2_.refs_11_), channel_id=1, source_target_pairs={{0,2},{1,3},{2,0},{3,1},{4,6},{5,7},{6,4},{7,5},{8,10},{9,11},{10,... | collective-permute-start | bytes 1572872 | tf_op jit(solution)/shard_map/ppermute | solution.py:593
  60.3 39.3 %collective-permute-start.14 = (bf16[4,7,16,512]{3,2,1,0:T(8,128)(2,1)S(1)}, bf16[4,7,16,512]{3,2,1,0:T(8,128)(2,1)}, u32[]{:S(2)}, u32[]{:S(2)}) collective-permute-start(bf16[4,7,16,512]{3,2,1,0:T(8,128)(2,1)S(1)} %pad_maximum_fusion.13), channel_id=1, source_target_pairs={{0,8},{4,12},{8,0},{12,4},{16,24},{20,28},{24,16},{28,20},{1,9},{5... | collective-permute-start | bytes 1376264 | tf_op jit(solution)/shard_map/ppermute | solution.py:611
  62.4 39.3 %collective-permute-start.13 = (bf16[4,8,16,512]{3,2,1,0:T(8,128)(2,1)S(1)}, bf16[4,8,16,512]{3,2,1,0:T(8,128)(2,1)S(1)}, u32[]{:S(2)}, u32[]{:S(2)}) collective-permute-start(bf16[4,8,16,512]{3,2,1,0:T(8,128)(2,1)S(1)} %pad_maximum_fusion.12), channel_id=1, source_target_pairs={{0,2},{1,3},{2,0},{3,1},{4,6},{5,7},{6,4},{7,5},{8,10},{9,11},{10,... | collective-permute-start | bytes 1572872 | tf_op jit(solution)/shard_map/ppermute | solution.py:611
  62.9 39.9 %collective-permute-start.12 = (bf16[8,5,16,512]{3,2,1,0:T(8,128)(2,1)S(1)}, bf16[8,5,16,512]{3,2,1,0:T(8,128)(2,1)}, u32[]{:S(2)}, u32[]{:S(2)}) collective-permute-start(bf16[8,5,16,512]{3,2,1,0:T(8,128)(2,1)S(1)} %pad_maximum_fusion.9), channel_id=1, source_target_pairs={{0,4},{4,0},{8,12},{12,8},{16,20},{20,16},{24,28},{28,24},{1,5},{5... | collective-permute-start | bytes 1966088 | tf_op jit(solution)/shard_map/ppermute | solution.py:611
  64.5 25.9 %collective-permute-start.21 = (s32[1,256]{1,0:T(1,128)S(1)}, s32[1,256]{1,0:T(1,128)S(1)}, u32[]{:S(2)}, u32[]{:S(2)}) collective-permute-start(s32[1,256]{1,0:T(1,128)S(1)} %copy-done.61), channel_id=1, source_target_pairs={{0,3},{1,2},{2,1},{3,0},{4,7},{5,6},{6,5},{7,4},{8,11},{9,10},{10,... | collective-permute-start | bytes 3080 | tf_op jit(solution)/shard_map/ppermute | solution.py:593
  98.4 5.5 %collective-permute-start.16 = (bf16[256,1024]{1,0:T(8,128)(2,1)}, bf16[256,1024]{1,0:T(8,128)(2,1)S(1)}, u32[]{:S(2)}, u32[]{:S(2)}) collective-permute-start(bf16[256,1024]{1,0:T(8,128)(2,1)} %get-tuple-element.217.refs_2_.refs_11_), channel_id=1, source_target_pairs={{0,1},{1,0},{2,3},{3,2},{4,5},{5,4},{6,7},{7,6},{8,9},{9,8},{10,11... | collective-permute-start | bytes 1572872 | tf_op jit(solution)/shard_map/ppermute | solution.py:593
  98.4 6.4 %collective-permute-start.18 = (bf16[256,1024]{1,0:T(8,128)(2,1)S(1)}, bf16[256,1024]{1,0:T(8,128)(2,1)S(1)}, u32[]{:S(2)}, u32[]{:S(2)}) collective-permute-start(bf16[256,1024]{1,0:T(8,128)(2,1)S(1)} %collective-permute-done.17.refs_4_.refs_13_), channel_id=1, source_target_pairs={{0,1},{1,0},{2,3},{3,2},{4,5},{5,4},{6,7},{7,6},{8,9},{9,8},{10,11... | collective-permute-start | bytes 1572872 | tf_op jit(solution)/shard_map/ppermute | solution.py:593
  105.6 31.7 %collective-permute-start.22 = (bf16[16,5,16,512]{3,2,1,0:T(8,128)(2,1)S(1)}, bf16[16,5,16,512]{3,2,1,0:T(8,128)(2,1)S(1)}, u32[]{:S(2)}, u32[]{:S(2)}) collective-permute-start(bf16[16,5,16,512]{3,2,1,0:T(8,128)(2,1)S(1)} %pad_maximum_fusion.2.refs_10_.refs_14_.refs_17_.refs_19_), channel_id=1, source_target_pairs={{0,1},{1,0},{2,3},{3,2},{4,5},{5,4},{6,7},{7,6},{8,9},{9,8},{10,11... | collective-permute-start | bytes 3932168 | tf_op jit(solution)/shard_map/ppermute | solution.py:611
  105.7 28.7 %collective-permute-start.24 = (bf16[8,7,16,512]{3,2,1,0:T(8,128)(2,1)}, bf16[8,7,16,512]{3,2,1,0:T(8,128)(2,1)}, u32[]{:S(2)}, u32[]{:S(2)}) collective-permute-start(bf16[8,7,16,512]{3,2,1,0:T(8,128)(2,1)} %pad_maximum_fusion.7), channel_id=1, source_target_pairs={{0,2},{1,3},{2,0},{3,1},{4,6},{5,7},{6,4},{7,5},{8,10},{9,11},{10,... | collective-permute-start | bytes 2752520 | tf_op jit(solution)/shard_map/ppermute | solution.py:611
  106.0 47.2 %collective-permute-start.23 = (bf16[8,8,16,512]{3,2,1,0:T(8,128)(2,1)}, bf16[8,8,16,512]{3,2,1,0:T(8,128)(2,1)}, u32[]{:S(2)}, u32[]{:S(2)}) collective-permute-start(bf16[8,8,16,512]{3,2,1,0:T(8,128)(2,1)} %pad_maximum_fusion.6), channel_id=1, source_target_pairs={{0,4},{4,0},{8,12},{12,8},{16,20},{20,16},{24,28},{28,24},{1,5},{5... | collective-permute-start | bytes 3145736 | tf_op jit(solution)/shard_map/ppermute | solution.py:611
  107.5 15.1 %collective-permute-start.25 = (bf16[2,5,16,512]{3,2,1,0:T(8,128)(2,1)}, bf16[2,5,16,512]{3,2,1,0:T(8,128)(2,1)S(1)}, u32[]{:S(2)}, u32[]{:S(2)}) collective-permute-start(bf16[2,5,16,512]{3,2,1,0:T(8,128)(2,1)} %pad_maximum_fusion.22), channel_id=1, source_target_pairs={{0,16},{4,20},{8,24},{12,28},{16,0},{20,4},{24,8},{28,12},{1,17},{... | collective-permute-start | bytes 491528 | tf_op jit(solution)/shard_map/ppermute | solution.py:611
  151.4 6.7 %collective-permute-start.27 = (f32[32,640]{1,0:T(8,128)}, f32[32,640]{1,0:T(8,128)S(1)}, u32[]{:S(2)}, u32[]{:S(2)}) collective-permute-start(f32[32,640]{1,0:T(8,128)} %get-tuple-element.234.refs_1_), channel_id=1, source_target_pairs={{0,2},{1,3},{2,0},{3,1},{4,6},{5,7},{6,4},{7,5},{8,10},{9,11},{10,... | collective-permute-start | bytes 245768 | tf_op jit(solution)/shard_map/ppermute | solution.py:593
  152.9 5.2 %collective-permute-start.26 = (f32[32,640]{1,0:T(8,128)}, f32[32,640]{1,0:T(8,128)S(1)}, u32[]{:S(2)}, u32[]{:S(2)}) collective-permute-start(f32[32,640]{1,0:T(8,128)} %get-tuple-element.234.refs_1_), channel_id=1, source_target_pairs={{0,1},{1,0},{2,3},{3,2},{4,5},{5,4},{6,7},{7,6},{8,9},{9,8},{10,11... | collective-permute-start | bytes 245768 | tf_op jit(solution)/shard_map/ppermute | solution.py:593
  158.1 11.5 %collective-permute-start.29 = (bf16[16,8,16,512]{3,2,1,0:T(8,128)(2,1)S(1)}, bf16[16,8,16,512]{3,2,1,0:T(8,128)(2,1)}, u32[]{:S(2)}, u32[]{:S(2)}) collective-permute-start(bf16[16,8,16,512]{3,2,1,0:T(8,128)(2,1)S(1)} %pad_maximum_fusion.refs_8_.refs_10_.refs_15_), channel_id=1, source_target_pairs={{0,1},{1,0},{2,3},{3,2},{4,5},{5,4},{6,7},{7,6},{8,9},{9,8},{10,11... | collective-permute-start | bytes 6291464 | tf_op jit(solution)/shard_map/ppermute | solution.py:611
  158.2 11.4 %collective-permute-start.30 = (bf16[16,7,16,512]{3,2,1,0:T(8,128)(2,1)}, bf16[16,7,16,512]{3,2,1,0:T(8,128)(2,1)}, u32[]{:S(2)}, u32[]{:S(2)}) collective-permute-start(bf16[16,7,16,512]{3,2,1,0:T(8,128)(2,1)} %pad_maximum_fusion.1.refs_10_.refs_6_.refs_12_), channel_id=1, source_target_pairs={{0,1},{1,0},{2,3},{3,2},{4,5},{5,4},{6,7},{7,6},{8,9},{9,8},{10,11... | collective-permute-start | bytes 5505032 | tf_op jit(solution)/shard_map/ppermute | solution.py:611
  158.6 9.9 %collective-permute-start.31 = (bf16[4,5,16,512]{3,2,1,0:T(8,128)(2,1)}, bf16[4,5,16,512]{3,2,1,0:T(8,128)(2,1)S(1)}, u32[]{:S(2)}, u32[]{:S(2)}) collective-permute-start(bf16[4,5,16,512]{3,2,1,0:T(8,128)(2,1)} %pad_maximum_fusion.15), channel_id=1, source_target_pairs={{0,8},{4,12},{8,0},{12,4},{16,24},{20,28},{24,16},{28,20},{1,9},{5... | collective-permute-start | bytes 983048 | tf_op jit(solution)/shard_map/ppermute | solution.py:611
  179.4 13.3 %collective-permute-start.34 = (bf16[256,1024]{1,0:T(8,128)(2,1)}, bf16[256,1024]{1,0:T(8,128)(2,1)S(1)}, u32[]{:S(2)}, u32[]{:S(2)}) collective-permute-start(bf16[256,1024]{1,0:T(8,128)(2,1)} %get-tuple-element.247.refs_2_.refs_11_), channel_id=1, source_target_pairs={{0,2},{1,3},{2,0},{3,1},{4,6},{5,7},{6,4},{7,5},{8,10},{9,11},{10,... | collective-permute-start | bytes 1572872 | tf_op jit(solution)/shard_map/ppermute | solution.py:593
  179.7 15.6 %collective-permute-start.32 = (bf16[8,5,16,512]{3,2,1,0:T(8,128)(2,1)S(1)}, bf16[8,5,16,512]{3,2,1,0:T(8,128)(2,1)S(1)}, u32[]{:S(2)}, u32[]{:S(2)}) collective-permute-start(bf16[8,5,16,512]{3,2,1,0:T(8,128)(2,1)S(1)} %pad_maximum_fusion.10), channel_id=1, source_target_pairs={{0,4},{4,0},{8,12},{12,8},{16,20},{20,16},{24,28},{28,24},{1,5},{5... | collective-permute-start | bytes 1966088 | tf_op jit(solution)/shard_map/ppermute | solution.py:611
  181.4 14.1 %collective-permute-start.33 = (bf16[256,1024]{1,0:T(8,128)(2,1)}, bf16[256,1024]{1,0:T(8,128)(2,1)S(1)}, u32[]{:S(2)}, u32[]{:S(2)}) collective-permute-start(bf16[256,1024]{1,0:T(8,128)(2,1)} %get-tuple-element.247.refs_2_.refs_11_), channel_id=1, source_target_pairs={{0,1},{1,0},{2,3},{3,2},{4,5},{5,4},{6,7},{7,6},{8,9},{9,8},{10,11... | collective-permute-start | bytes 1572872 | tf_op jit(solution)/shard_map/ppermute | solution.py:593
  215.0 5.3 %collective-permute-start.38 = (f32[32,640]{1,0:T(8,128)}, f32[32,640]{1,0:T(8,128)S(1)}, u32[]{:S(2)}, u32[]{:S(2)}) collective-permute-start(f32[32,640]{1,0:T(8,128)} %get-tuple-element.256.refs_1_), channel_id=1, source_target_pairs={{0,2},{1,3},{2,0},{3,1},{4,6},{5,7},{6,4},{7,5},{8,10},{9,11},{10,... | collective-permute-start | bytes 245768 | tf_op jit(solution)/shard_map/ppermute | solution.py:593
  241.8 15.3 %collective-permute-start.40 = (bf16[16,10,16,512]{3,2,1,0:T(8,128)(2,1)}, bf16[16,10,16,512]{3,2,1,0:T(8,128)(2,1)S(1)}, u32[]{:S(2)}, u32[]{:S(2)}) collective-permute-start(bf16[16,10,16,512]{3,2,1,0:T(8,128)(2,1)} %get-tuple-element.266), channel_id=1, source_target_pairs={{0,1},{1,0},{2,3},{3,2},{4,5},{5,4},{6,7},{7,6},{8,9},{9,8},{10,11... | collective-permute-start | bytes 7864328 | tf_op jit(solution)/shard_map/ppermute | solution.py:611
  258.6 29.9 %collective-permute-start.44 = (bf16[8,10,16,512]{3,2,1,0:T(8,128)(2,1)S(1)}, bf16[8,10,16,512]{3,2,1,0:T(8,128)(2,1)S(1)}, u32[]{:S(2)}, u32[]{:S(2)}) collective-permute-start(bf16[8,10,16,512]{3,2,1,0:T(8,128)(2,1)S(1)} %slice.716), channel_id=1, source_target_pairs={{0,4},{4,0},{8,12},{12,8},{16,20},{20,16},{24,28},{28,24},{1,5},{5... | collective-permute-start | bytes 3932168 | tf_op jit(solution)/shard_map/ppermute | solution.py:611
  289.1 17.2 %collective-permute-start.48 = (bf16[4,10,16,512]{3,2,1,0:T(8,128)(2,1)S(1)}, bf16[4,10,16,512]{3,2,1,0:T(8,128)(2,1)S(1)}, u32[]{:S(2)}, u32[]{:S(2)}) collective-permute-start(bf16[4,10,16,512]{3,2,1,0:T(8,128)(2,1)S(1)} %slice.718), channel_id=1, source_target_pairs={{0,8},{4,12},{8,0},{12,4},{16,24},{20,28},{24,16},{28,20},{1,9},{5... | collective-permute-start | bytes 1966088 | tf_op jit(solution)/shard_map/ppermute | solution.py:611
  292.0 15.6 %collective-permute-start.50 = (bf16[288,1024]{1,0:T(8,128)(2,1)S(1)}, bf16[288,1024]{1,0:T(8,128)(2,1)S(1)}, u32[]{:S(2)}, u32[]{:S(2)}) collective-permute-start(bf16[288,1024]{1,0:T(8,128)(2,1)S(1)} %slice.988.refs_4_), channel_id=1, source_target_pairs={{0,2},{1,3},{2,0},{3,1},{4,6},{5,7},{6,4},{7,5},{8,10},{9,11},{10,... | collective-permute-start | bytes 1769480 | tf_op jit(solution)/shard_map/ppermute | solution.py:593
  327.3 38.6 %collective-permute-start.56 = (bf16[16,10,16,512]{3,2,1,0:T(8,128)(2,1)}, bf16[16,10,16,512]{3,2,1,0:T(8,128)(2,1)S(1)}, u32[]{:S(2)}, u32[]{:S(2)}) collective-permute-start(bf16[16,10,16,512]{3,2,1,0:T(8,128)(2,1)} %get-tuple-element.309), channel_id=1, source_target_pairs={{0,1},{1,0},{2,3},{3,2},{4,5},{5,4},{6,7},{7,6},{8,9},{9,8},{10,11... | collective-permute-start | bytes 7864328 | tf_op jit(solution)/shard_map/ppermute | solution.py:611
  327.4 38.2 %collective-permute-start.53 = (bf16[16,5,16,512]{3,2,1,0:T(8,128)(2,1)}, bf16[16,5,16,512]{3,2,1,0:T(8,128)(2,1)S(1)}, u32[]{:S(2)}, u32[]{:S(2)}) collective-permute-start(bf16[16,5,16,512]{3,2,1,0:T(8,128)(2,1)} %get-tuple-element.306), channel_id=1, source_target_pairs={{0,1},{1,0},{2,3},{3,2},{4,5},{5,4},{6,7},{7,6},{8,9},{9,8},{10,11... | collective-permute-start | bytes 3932168 | tf_op jit(solution)/shard_map/ppermute | solution.py:611
  328.1 17.7 %collective-permute-start.51 = (bf16[2,10,16,512]{3,2,1,0:T(8,128)(2,1)S(1)}, bf16[2,10,16,512]{3,2,1,0:T(8,128)(2,1)S(1)}, u32[]{:S(2)}, u32[]{:S(2)}) collective-permute-start(bf16[2,10,16,512]{3,2,1,0:T(8,128)(2,1)S(1)} %slice.722), channel_id=1, source_target_pairs={{0,16},{4,20},{8,24},{12,28},{16,0},{20,4},{24,8},{28,12},{1,17},{... | collective-permute-start | bytes 983048 | tf_op jit(solution)/shard_map/ppermute | solution.py:611
  330.8 35.1 %collective-permute-start.54 = (bf16[16,3,16,512]{3,2,1,0:T(8,128)(2,1)}, bf16[16,3,16,512]{3,2,1,0:T(8,128)(2,1)S(1)}, u32[]{:S(2)}, u32[]{:S(2)}) collective-permute-start(bf16[16,3,16,512]{3,2,1,0:T(8,128)(2,1)} %get-tuple-element.307), channel_id=1, source_target_pairs={{0,1},{1,0},{2,3},{3,2},{4,5},{5,4},{6,7},{7,6},{8,9},{9,8},{10,11... | collective-permute-start | bytes 2359304 | tf_op jit(solution)/shard_map/ppermute | solution.py:611
  346.4 19.5 %collective-permute-start.55 = (bf16[16,2,16,512]{3,2,1,0:T(8,128)(2,1)}, bf16[16,2,16,512]{3,2,1,0:T(8,128)(2,1)S(1)}, u32[]{:S(2)}, u32[]{:S(2)}) collective-permute-start(bf16[16,2,16,512]{3,2,1,0:T(8,128)(2,1)} %get-tuple-element.308), channel_id=1, source_target_pairs={{0,1},{1,0},{2,3},{3,2},{4,5},{5,4},{6,7},{7,6},{8,9},{9,8},{10,11... | collective-permute-start | bytes 1572872 | tf_op jit(solution)/shard_map/ppermute | solution.py:611
  356.0 9.9 %collective-permute-start.52 = (bf16[1,10,16,512]{3,2,1,0:T(8,128)(2,1)S(1)}, bf16[1,10,16,512]{3,2,1,0:T(8,128)(2,1)S(1)}, u32[]{:S(2)}, u32[]{:S(2)}) collective-permute-start(bf16[1,10,16,512]{3,2,1,0:T(8,128)(2,1)S(1)} %slice.723), channel_id=1, source_target_pairs={{0,2},{1,3},{2,0},{3,1},{4,6},{5,7},{6,4},{7,5},{8,10},{9,11},{10,... | collective-permute-start | bytes 491528 | tf_op jit(solution)/shard_map/ppermute | solution.py:611
  365.6 36.9 %collective-permute-start.65 = (bf16[16,5,16,512]{3,2,1,0:T(8,128)(2,1)}, bf16[16,5,16,512]{3,2,1,0:T(8,128)(2,1)S(1)}, u32[]{:S(2)}, u32[]{:S(2)}) collective-permute-start(bf16[16,5,16,512]{3,2,1,0:T(8,128)(2,1)} %get-tuple-element.337), channel_id=1, source_target_pairs={{0,1},{1,0},{2,3},{3,2},{4,5},{5,4},{6,7},{7,6},{8,9},{9,8},{10,11... | collective-permute-start | bytes 3932168 | tf_op jit(solution)/shard_map/ppermute | solution.py:611
  373.4 31.1 %collective-permute-start.64 = (bf16[8,10,16,512]{3,2,1,0:T(8,128)(2,1)S(1)}, bf16[8,10,16,512]{3,2,1,0:T(8,128)(2,1)}, u32[]{:S(2)}, u32[]{:S(2)}) collective-permute-start(bf16[8,10,16,512]{3,2,1,0:T(8,128)(2,1)S(1)} %slice.730), channel_id=1, source_target_pairs={{0,8},{4,12},{8,0},{12,4},{16,24},{20,28},{24,16},{28,20},{1,9},{5... | collective-permute-start | bytes 3932168 | tf_op jit(solution)/shard_map/ppermute | solution.py:611
  374.5 30.9 %collective-permute-start.63 = (bf16[8,10,16,512]{3,2,1,0:T(8,128)(2,1)S(1)}, bf16[8,10,16,512]{3,2,1,0:T(8,128)(2,1)}, u32[]{:S(2)}, u32[]{:S(2)}) collective-permute-start(bf16[8,10,16,512]{3,2,1,0:T(8,128)(2,1)S(1)} %pad_maximum_fusion.4), channel_id=1, source_target_pairs={{0,4},{4,0},{8,12},{12,8},{16,20},{20,16},{24,28},{28,24},{1,5},{5... | collective-permute-start | bytes 3932168 | tf_op jit(solution)/shard_map/ppermute | solution.py:611
  405.3 10.6 %collective-permute-start.69 = (bf16[544,1024]{1,0:T(8,128)(2,1)}, bf16[544,1024]{1,0:T(8,128)(2,1)S(1)}, u32[]{:S(2)}, u32[]{:S(2)}) collective-permute-start(bf16[544,1024]{1,0:T(8,128)(2,1)} %get-tuple-element.344), channel_id=1, source_target_pairs={{0,1},{1,0},{2,3},{3,2},{4,5},{5,4},{6,7},{7,6},{8,9},{9,8},{10,11... | collective-permute-start | bytes 3342344 | tf_op jit(solution)/shard_map/ppermute | solution.py:593
  407.1 25.6 %collective-permute-start.68 = (bf16[16,3,16,512]{3,2,1,0:T(8,128)(2,1)}, bf16[16,3,16,512]{3,2,1,0:T(8,128)(2,1)}, u32[]{:S(2)}, u32[]{:S(2)}) collective-permute-start(bf16[16,3,16,512]{3,2,1,0:T(8,128)(2,1)} %get-tuple-element.342), channel_id=1, source_target_pairs={{0,1},{1,0},{2,3},{3,2},{4,5},{5,4},{6,7},{7,6},{8,9},{9,8},{10,11... | collective-permute-start | bytes 2359304 | tf_op jit(solution)/shard_map/ppermute | solution.py:611
  413.3 19.5 %collective-permute-start.66 = (bf16[4,10,16,512]{3,2,1,0:T(8,128)(2,1)}, bf16[4,10,16,512]{3,2,1,0:T(8,128)(2,1)}, u32[]{:S(2)}, u32[]{:S(2)}) collective-permute-start(bf16[4,10,16,512]{3,2,1,0:T(8,128)(2,1)} %slice.731), channel_id=1, source_target_pairs={{0,8},{4,12},{8,0},{12,4},{16,24},{20,28},{24,16},{28,20},{1,9},{5... | collective-permute-start | bytes 1966088 | tf_op jit(solution)/shard_map/ppermute | solution.py:611
  414.5 18.3 %collective-permute-start.67 = (bf16[4,10,16,512]{3,2,1,0:T(8,128)(2,1)}, bf16[4,10,16,512]{3,2,1,0:T(8,128)(2,1)}, u32[]{:S(2)}, u32[]{:S(2)}) collective-permute-start(bf16[4,10,16,512]{3,2,1,0:T(8,128)(2,1)} %slice.733), channel_id=1, source_target_pairs={{0,4},{4,0},{8,12},{12,8},{16,20},{20,16},{24,28},{28,24},{1,5},{5... | collective-permute-start | bytes 1966088 | tf_op jit(solution)/shard_map/ppermute | solution.py:611
  417.3 15.5 %collective-permute-start.70 = (bf16[288,1024]{1,0:T(8,128)(2,1)}, bf16[288,1024]{1,0:T(8,128)(2,1)}, u32[]{:S(2)}, u32[]{:S(2)}) collective-permute-start(bf16[288,1024]{1,0:T(8,128)(2,1)} %slice.987.refs_4_), channel_id=1, source_target_pairs={{0,2},{1,3},{2,0},{3,1},{4,6},{5,7},{6,4},{7,5},{8,10},{9,11},{10,... | collective-permute-start | bytes 1769480 | tf_op jit(solution)/shard_map/ppermute | solution.py:593
  431.4 19.1 %collective-permute-start.73 = (bf16[8,5,16,512]{3,2,1,0:T(8,128)(2,1)}, bf16[8,5,16,512]{3,2,1,0:T(8,128)(2,1)}, u32[]{:S(2)}, u32[]{:S(2)}) collective-permute-start(bf16[8,5,16,512]{3,2,1,0:T(8,128)(2,1)} %slice.740), channel_id=1, source_target_pairs={{0,4},{4,0},{8,12},{12,8},{16,20},{20,16},{24,28},{28,24},{1,5},{5... | collective-permute-start | bytes 1966088 | tf_op jit(solution)/shard_map/ppermute | solution.py:611
  435.7 14.8 %collective-permute-start.72 = (bf16[2,10,16,512]{3,2,1,0:T(8,128)(2,1)S(1)}, bf16[2,10,16,512]{3,2,1,0:T(8,128)(2,1)S(1)}, u32[]{:S(2)}, u32[]{:S(2)}) collective-permute-start(bf16[2,10,16,512]{3,2,1,0:T(8,128)(2,1)S(1)} %slice.739), channel_id=1, source_target_pairs={{0,2},{1,3},{2,0},{3,1},{4,6},{5,7},{6,4},{7,5},{8,10},{9,11},{10,... | collective-permute-start | bytes 983048 | tf_op jit(solution)/shard_map/ppermute | solution.py:611
  437.2 16.7 %collective-permute-start.71 = (bf16[2,10,16,512]{3,2,1,0:T(8,128)(2,1)S(1)}, bf16[2,10,16,512]{3,2,1,0:T(8,128)(2,1)S(1)}, u32[]{:S(2)}, u32[]{:S(2)}) collective-permute-start(bf16[2,10,16,512]{3,2,1,0:T(8,128)(2,1)S(1)} %slice.737), channel_id=1, source_target_pairs={{0,16},{4,20},{8,24},{12,28},{16,0},{20,4},{24,8},{28,12},{1,17},{... | collective-permute-start | bytes 983048 | tf_op jit(solution)/shard_map/ppermute | solution.py:611
  441.4 12.6 %collective-permute-start.74 = (bf16[8,3,16,512]{3,2,1,0:T(8,128)(2,1)S(1)}, bf16[8,3,16,512]{3,2,1,0:T(8,128)(2,1)S(1)}, u32[]{:S(2)}, u32[]{:S(2)}) collective-permute-start(bf16[8,3,16,512]{3,2,1,0:T(8,128)(2,1)S(1)} %slice.741), channel_id=1, source_target_pairs={{0,2},{1,3},{2,0},{3,1},{4,6},{5,7},{6,4},{7,5},{8,10},{9,11},{10,... | collective-permute-start | bytes 1179656 | tf_op jit(solution)/shard_map/ppermute | solution.py:611
  448.6 19.4 %collective-permute-start.75 = (bf16[16,3,16,512]{3,2,1,0:T(8,128)(2,1)}, bf16[16,3,16,512]{3,2,1,0:T(8,128)(2,1)S(1)}, u32[]{:S(2)}, u32[]{:S(2)}) collective-permute-start(bf16[16,3,16,512]{3,2,1,0:T(8,128)(2,1)} %get-tuple-element.365), channel_id=1, source_target_pairs={{0,1},{1,0},{2,3},{3,2},{4,5},{5,4},{6,7},{7,6},{8,9},{9,8},{10,11... | collective-permute-start | bytes 2359304 | tf_op jit(solution)/shard_map/ppermute | solution.py:611
  455.3 12.7 %collective-permute-start.77 = (bf16[4,5,16,512]{3,2,1,0:T(8,128)(2,1)S(1)}, bf16[4,5,16,512]{3,2,1,0:T(8,128)(2,1)S(1)}, u32[]{:S(2)}, u32[]{:S(2)}) collective-permute-start(bf16[4,5,16,512]{3,2,1,0:T(8,128)(2,1)S(1)} %slice.745), channel_id=1, source_target_pairs={{0,2},{1,3},{2,0},{3,1},{4,6},{5,7},{6,4},{7,5},{8,10},{9,11},{10,... | collective-permute-start | bytes 983048 | tf_op jit(solution)/shard_map/ppermute | solution.py:611
  456.2 11.8 %collective-permute-start.76 = (bf16[1,10,16,512]{3,2,1,0:T(8,128)(2,1)S(1)}, bf16[1,10,16,512]{3,2,1,0:T(8,128)(2,1)S(1)}, u32[]{:S(2)}, u32[]{:S(2)}) collective-permute-start(bf16[1,10,16,512]{3,2,1,0:T(8,128)(2,1)S(1)} %slice.743), channel_id=1, source_target_pairs={{0,2},{1,3},{2,0},{3,1},{4,6},{5,7},{6,4},{7,5},{8,10},{9,11},{10,... | collective-permute-start | bytes 491528 | tf_op jit(solution)/shard_map/ppermute | solution.py:611
  457.8 10.2 %collective-permute-start.78 = (bf16[4,3,16,512]{3,2,1,0:T(8,128)(2,1)S(1)}, bf16[4,3,16,512]{3,2,1,0:T(8,128)(2,1)S(1)}, u32[]{:S(2)}, u32[]{:S(2)}) collective-permute-start(bf16[4,3,16,512]{3,2,1,0:T(8,128)(2,1)S(1)} %slice.747), channel_id=1, source_target_pairs={{0,4},{4,0},{8,12},{12,8},{16,20},{20,16},{24,28},{28,24},{1,5},{5... | collective-permute-start | bytes 589832 | tf_op jit(solution)/shard_map/ppermute | solution.py:611
  458.9 12.4 %collective-permute-start.80 = (bf16[1,10,16,512]{3,2,1,0:T(8,128)(2,1)S(1)}, bf16[1,10,16,512]{3,2,1,0:T(8,128)(2,1)S(1)}, u32[]{:S(2)}, u32[]{:S(2)}) collective-permute-start(bf16[1,10,16,512]{3,2,1,0:T(8,128)(2,1)S(1)} %slice.751), channel_id=1, source_target_pairs={{0,16},{4,20},{8,24},{12,28},{16,0},{20,4},{24,8},{28,12},{1,17},{... | collective-permute-start | bytes 491528 | tf_op jit(solution)/shard_map/ppermute | solution.py:611
  468.6 6.5 %collective-permute-start.81 = (bf16[2,5,16,512]{3,2,1,0:T(8,128)(2,1)S(1)}, bf16[2,5,16,512]{3,2,1,0:T(8,128)(2,1)S(1)}, u32[]{:S(2)}, u32[]{:S(2)}) collective-permute-start(bf16[2,5,16,512]{3,2,1,0:T(8,128)(2,1)S(1)} %slice.753), channel_id=1, source_target_pairs={{0,8},{4,12},{8,0},{12,4},{16,24},{20,28},{24,16},{28,20},{1,9},{5... | collective-permute-start | bytes 491528 | tf_op jit(solution)/shard_map/ppermute | solution.py:611
  470.9 9.1 %collective-permute-start.79 = (bf16[8,3,16,512]{3,2,1,0:T(8,128)(2,1)S(1)}, bf16[8,3,16,512]{3,2,1,0:T(8,128)(2,1)S(1)}, u32[]{:S(2)}, u32[]{:S(2)}) collective-permute-start(bf16[8,3,16,512]{3,2,1,0:T(8,128)(2,1)S(1)} %slice.749), channel_id=1, source_target_pairs={{0,4},{4,0},{8,12},{12,8},{16,20},{20,16},{24,28},{28,24},{1,5},{5... | collective-permute-start | bytes 1179656 | tf_op jit(solution)/shard_map/ppermute | solution.py:611
  480.3 6.6 %collective-permute-start.85 = (bf16[1,3,16,512]{3,2,1,0:T(8,128)(2,1)S(1)}, bf16[1,3,16,512]{3,2,1,0:T(8,128)(2,1)S(1)}, u32[]{:S(2)}, u32[]{:S(2)}) collective-permute-start(bf16[1,3,16,512]{3,2,1,0:T(8,128)(2,1)S(1)} %slice.761), channel_id=1, source_target_pairs={{0,16},{4,20},{8,24},{12,28},{16,0},{20,4},{24,8},{28,12},{1,17},{... | collective-permute-start | bytes 147464 | tf_op jit(solution)/shard_map/ppermute | solution.py:611
  482.9 5.3 %collective-permute-start.84 = (bf16[1,5,16,512]{3,2,1,0:T(8,128)(2,1)S(1)}, bf16[1,5,16,512]{3,2,1,0:T(8,128)(2,1)S(1)}, u32[]{:S(2)}, u32[]{:S(2)}) collective-permute-start(bf16[1,5,16,512]{3,2,1,0:T(8,128)(2,1)S(1)} %slice.759), channel_id=1, source_target_pairs={{0,16},{4,20},{8,24},{12,28},{16,0},{20,4},{24,8},{28,12},{1,17},{... | collective-permute-start | bytes 245768 | tf_op jit(solution)/shard_map/ppermute | solution.py:611
  483.3 5.7 %collective-permute-start.83 = (bf16[4,3,16,512]{3,2,1,0:T(8,128)(2,1)S(1)}, bf16[4,3,16,512]{3,2,1,0:T(8,128)(2,1)S(1)}, u32[]{:S(2)}, u32[]{:S(2)}) collective-permute-start(bf16[4,3,16,512]{3,2,1,0:T(8,128)(2,1)S(1)} %slice.757), channel_id=1, source_target_pairs={{0,2},{1,3},{2,0},{3,1},{4,6},{5,7},{6,4},{7,5},{8,10},{9,11},{10,... | collective-permute-start | bytes 589832 | tf_op jit(solution)/shard_map/ppermute | solution.py:611
  (88 other events, 461.5 us)
Sparse Core Ops, SparseCore 0:
  50.5 80.1 all-gather.2

commit v4 on v3

--- a/solution.py
+++ b/solution.py
@@ -18,20 +18,26 @@
 ALL = ("dp", "blk")
 LOW = jnp.bfloat16
 F32 = jnp.float32
-VMEM_LIMIT = 56 * 1024 * 1024
-GATHER_AT = 4
+VMEM_LIMIT = 24 * 1024 * 1024
 PLAN = {
-    1: [("early_1",), ("early_1",), ("early_1",), ("early_1",)],
+    1: [
+        ("up_1", "down_1"),
+        ("up_1", "down_1"),
+        ("up_1", "down_1", "first_1"),
+        ("up_1", "down_1", "first_1"),
+        ("up_1", "down_1", "first_1"),
+    ],
     0: [
-        ("early_1", "middle_1", "early_0"),
-        ("middle_1", "early_0", "middle_0"),
-        ("middle_1", "early_0", "attend_0"),
-        ("middle_1", "early_0", "middle_0", "attend_0"),
-        ("last", "middle_1", "middle_0", "attend_0"),
-        ("last", "early_0", "middle_0", "attend_0"),
-        ("last", "middle_0", "attend_0"),
-        ("last",),
-        ("last",),
+        ("up_0", "down_0", "second_1", "first_1"),
+        ("up_0", "down_0"),
+        ("up_0", "down_0", "first_0", "second_1"),
+        ("up_0", "down_0", "first_0", "second_1"),
+        ("up_0", "first_1", "first_0", "second_1"),
+        ("last", "second_0", "down_0"),
+        ("last", "second_0", "first_0", "second_1"),
+        ("last", "second_0", "first_0"),
+        ("last", "second_0"),
+        ("last", "second_0"),
     ],
 }
 
@@ -116,10 +122,16 @@
     return both[: rows // 2] + both[rows // 2 :]
 
 
-def bound_of(seg_keys, seg_queries):
-    same = seg_keys == seg_queries
-    allowed = (same | (seg_keys == -2.0) | (seg_queries == -1.0)) & (seg_keys != -3.0)
-    return jnp.where(allowed, BIG, NEG)
+def place_bounds(bound_ref, seg_refs, seg_queries):
+    rows = seg_refs[0].shape[1]
+    me = lax.axis_index("blk")
+    for other, seg_ref in enumerate(seg_refs):
+        numbers = jnp.broadcast_to(seg_ref[...].astype(F32), (128, rows)).T[:, 0:1]
+        allowed = (numbers == seg_queries) | (seg_queries == -1.0)
+        place = pl.ds(pl.multiple_of((me ^ other) * rows, rows), rows)
+        bound_ref[place, :] = jnp.where(allowed, BIG, NEG)
+    memory = lax.broadcasted_iota(jnp.int32, (PAD, seg_queries.shape[1]), 0) < MEM
+    bound_ref[4 * rows :, :] = jnp.where(memory, BIG, NEG)
 
 
 def place_keys(keys_ref, own_ref, core_ref, chip_ref, both_ref, memory_ref):
@@ -142,10 +154,28 @@
     q_ref[...] = dot(low, weight(0)).astype(LOW)
 
 
+def bias_order(width, high, per):
+    lanes = lax.broadcasted_iota(jnp.int32, (width, width), 0)
+    shard, inner = lanes // (per * high), lanes % (per * high)
+    goal = inner // high * (width // per) + shard * high + inner % high
+    return (goal == lax.broadcasted_iota(jnp.int32, (width, width), 1)).astype(LOW)
+
+
 def first_kernel(weight, put, rows_of, tokens_ref, small_ref, z_ref, q_ref, kv_ref, kvmem_ref):
     rows = tokens_ref.shape[0]
-    small = weight("small")[:, :128].astype(F32).T
+    columns = weight("small")[:, :128]
+    small = columns.astype(F32).T
+    width = small.shape[1]
     small_ref[...] = small
+    high, per, start = rows_of["sizes"]
+    order = bias_order(width, high, per)
+    for layer in range((rows_of["memory"] - start) // per):
+        lines = small[start + layer * per : start + (layer + 1) * per].astype(LOW)
+        piece = width // per
+        for part in range(per):
+            line = jnp.concatenate([lines[j : j + 1, part * piece : (part + 1) * piece] for j in range(per)], 1)
+            place = 64 + layer * per + part
+            small_ref[place : place + 1, :] = dot_nt(line, order)
     z_ref[:rows, :] = tokens_ref[...].astype(F32)
     start = rows_of["memory"]
     z_ref[rows : rows + MEM, :] = small[start : start + MEM]
@@ -154,14 +184,14 @@
 
 
 def attend_kernel(
-    weight, put, rows_of, z_ref, q_ref, own_ref, core_ref, chip_ref, both_ref, kvmem_ref, segk_ref, segq_ref, small_ref,
-    att_ref, pre_ref, one_ref, rq_ref, rkv_ref, wq_ref, part_ref,
+    weight, put, rows_of, z_ref, q_ref, own_ref, core_ref, chip_ref, both_ref, kvmem_ref, sega_ref, segb_ref, segc_ref, segd_ref, segq_ref, small_ref,
+    att_ref, lse_ref, pre_ref, one_ref, rq_ref, rkv_ref, wq_ref, part_ref,
     keys_ref, bound_ref,
 ):
     rows = core_ref.shape[0]
     width = z_ref.shape[1]
     place_keys(keys_ref, own_ref, core_ref, chip_ref, both_ref, kvmem_ref)
-    bound_ref[...] = bound_of(segk_ref[...], segq_ref[...])
+    place_bounds(bound_ref, (sega_ref, segb_ref, segc_ref, segd_ref), segq_ref[...])
 
     def pair(step, carry):
         lanes = pl.ds(pl.multiple_of(step * 128, 128), 128)
@@ -170,9 +200,11 @@
         keys = keys_ref[:, lanes]
         values = keys_ref[:, more]
         scores = jnp.minimum(dot_nt(keys, query), bound_ref[...])
-        expo = jnp.exp(scores - jnp.max(scores, 0, keepdims=True))
-        probs = expo * (1.0 / jnp.sum(expo, 0, keepdims=True))
-        att_ref[:, lanes] = pick_heads(dot_tn(values, probs.astype(LOW))).astype(LOW)
+        top = jnp.max(scores, 0, keepdims=True)
+        expo = jnp.exp(scores - top)
+        summed = jnp.sum(expo, 0, keepdims=True)
+        att_ref[:, lanes] = pick_heads(dot_tn(values, expo.astype(LOW)) * (1.0 / summed)).astype(LOW)
+        lse_ref[pl.ds(step, 1), :] = top + jnp.log(summed)
         return carry
 
     lax.fori_loop(0, width // 128, pair, 0)
@@ -224,7 +256,7 @@
 
 
 def finish_kernel(
-    last, weight, put, rows_of, one_ref, own_ref, core_ref, chip_ref, both_ref, wq_ref, bias_ref, small_ref, *rest
+    last, weight, put, rows_of, one_ref, own_ref, core_ref, chip_ref, both_ref, wq_ref, small_ref, *rest
 ):
     if last:
         (z_ref, rout_ref, rlse_ref, mempre_ref, two_ref, wkv_ref, wlow_ref, seqpre_ref, x_ref, feedpre_ref) = rest
@@ -262,8 +294,8 @@
     x = two.astype(LOW)
     x_ref[...] = x
     feed = two + row(small_ref, rows_of, "shift", 4)
-    for part in range(bias_ref.shape[0]):
-        u = dot(x, weight(("up", part))) + bias_ref[part : part + 1, :]
+    for part in range(rows_of["sizes"][1]):
+        u = dot(x, weight(("up", part))) + row(small_ref, rows_of, "bias", part)
         feed = feed + dot(gelu_parts(u)[0].astype(LOW), weight("down", part))
     feedpre_ref[...] = feed
     z_ref[...] = norm(feed, row(small_ref, rows_of, "gain", 3), row(small_ref, rows_of, "shift", 3))
@@ -273,7 +305,7 @@
 
 def feed_back_kernel(
     share, weight, put, rows_of, grad_ref, feedpre_ref, x_ref, seqpre_ref, wlow_ref, wq_ref, wkv_ref, one_ref,
-    bias_ref, small_ref,
+    small_ref,
     gbias_ref, gsmall_ref, mem_ref, seq_ref, part_ref,
 ):
     rows, width = wq_ref.shape
@@ -288,14 +320,18 @@
     gsmall_ref[2:3, :] = total(low_share.astype(F32))
     x = x_ref[...]
     two = feed
-    parts = bias_ref.shape[0]
+    high, parts, _ = rows_of["sizes"]
+    order = bias_order(width, high, parts)
+    piece = width // parts
     for part in range(parts):
-        u = dot(x, weight(("up", part))) + bias_ref[part : part + 1, :]
+        u = dot(x, weight(("up", part))) + row(small_ref, rows_of, "bias", part)
         value, slope = gelu_parts(u)
         put(("down", part), dot_tn(value.astype(LOW), low_share))
         pre = (dot_nt(low, weight("down", part)) * slope).astype(LOW)
         pre_share = (pre.astype(F32) * balance).astype(LOW)
-        gbias_ref[part : part + 1, :] = total(pre_share.astype(F32))
+        line = dot(total(pre_share.astype(F32)).astype(LOW), order)
+        for j in range(parts):
+            gbias_ref[j : j + 1, part * piece : (part + 1) * piece] = line[:, j * piece : (j + 1) * piece]
         put(("up", part), dot_tn(x, pre_share))
         two = two + dot_nt(pre, weight(("up", part)))
     mem_ref[...] = two[rows:]
@@ -362,15 +398,15 @@
 
 
 def attend_back_kernel(
-    share, weight, put, rows_of, z_ref, part_ref, corepart_ref, chippart_ref, bothpart_ref, memgrad_ref, seqjoint_ref, one_ref, pre_ref, att_ref,
-    q_ref, own_ref, core_ref, chip_ref, both_ref, kvmem_ref, segk_ref, segq_ref, small_ref,
-    gsmall_ref, joint_ref, qgrad_ref, keep_ref, send_ref,
+    share, weight, put, rows_of, z_ref, part_ref, corepart_ref, chippart_ref, bothpart_ref, memgrad_ref, seqjoint_ref, one_ref, pre_ref, att_ref, lse_ref,
+    q_ref, own_ref, core_ref, chip_ref, both_ref, kvmem_ref, sega_ref, segb_ref, segc_ref, segd_ref, segq_ref, small_ref,
+    gsmall_ref, joint_ref, qgrad_ref, keep_ref, pass_ref, send_ref,
     keys_ref, bound_ref, out_ref, kvgrad_ref,
 ):
     rows, width = seqjoint_ref.shape
     full = att_ref.shape[0]
     place_keys(keys_ref, own_ref, core_ref, chip_ref, both_ref, kvmem_ref)
-    bound_ref[...] = bound_of(segk_ref[...], segq_ref[...])
+    place_bounds(bound_ref, (sega_ref, segb_ref, segc_ref, segd_ref), segq_ref[...])
     parts = (part_ref, corepart_ref, chippart_ref, bothpart_ref)
     q_low = in_pairs([part[...].astype(F32) for part in parts]).astype(LOW)
     put(4, dot_tn(one_ref[rows:, :].astype(LOW), q_low) * share)
@@ -391,15 +427,15 @@
         query = q_ref[:, lanes] * jnp.asarray(SCALE, LOW)
         out = out_ref[:, lanes]
         low_balance = jnp.concatenate([balance, balance], 0)
+        product = (out.astype(F32) * att_ref[:, lanes].astype(F32)).T
+        delta = jnp.concatenate([total(product[:HEAD]), total(product[HEAD:])], 1)
         query = two_heads(query)
         out = two_heads(out)
         keys = keys_ref[:, lanes]
         values = keys_ref[:, more]
         scores = jnp.minimum(dot_nt(keys, query), bound_ref[...])
-        expo = jnp.exp(scores - jnp.max(scores, 0, keepdims=True))
-        probs = expo * (1.0 / jnp.sum(expo, 0, keepdims=True))
+        probs = jnp.exp(scores - lse_ref[pl.ds(step, 1), :])
         prob_grad = dot_nt(values, out)
-        delta = jnp.sum(probs * prob_grad, 0, keepdims=True)
         score_grad = (probs * (prob_grad - delta)).astype(LOW)
         qgrad_ref[:, lanes] = (pick_heads(dot_tn(keys, score_grad)) * SCALE).astype(LOW)
         query_share = (query.astype(F32) * low_balance).astype(LOW)
@@ -412,22 +448,23 @@
     z_low = z_ref[...].astype(LOW)
     put(0, dot_tn(z_low, (qgrad_ref[...].astype(F32) * balance).astype(LOW)))
     me = lax.axis_index("blk")
-    for place, (goal, other) in enumerate(((keep_ref, 0), (keep_ref, 2), (send_ref, 1), (send_ref, 3))):
+    for goal, place, other in ((keep_ref, 0, 0), (pass_ref, 0, 2), (send_ref, 0, 1), (send_ref, rows, 3)):
         rest = pl.ds(pl.multiple_of((me ^ other) * rows, rows), rows)
-        goal[place % 2 * rows : (place % 2 + 1) * rows, :] = kvgrad_ref[rest, :]
-    for goal in (keep_ref, send_ref):
-        goal[2 * rows :, :] = kvgrad_ref[4 * rows :, :]
+        goal[place : place + rows, :] = kvgrad_ref[rest, :]
+    pass_ref[rows:, :] = kvgrad_ref[4 * rows :, :]
+    send_ref[2 * rows :, :] = kvgrad_ref[4 * rows :, :]
 
 
 def input_back_kernel(
-    share, weight, put, rows_of, z_ref, joint_ref, qgrad_ref, mine_ref, sent_ref, got_ref, *rest
+    share, weight, put, rows_of, z_ref, joint_ref, qgrad_ref, keep_ref, near_ref, sent_ref, got_ref, *rest
 ):
     *small_refs, zgrad_ref, kvgrad_ref = rest
     full, width = z_ref.shape
     rows = full - PAD
     balance = jnp.where(lax.broadcasted_iota(jnp.int32, (full, 1), 0) < rows, 1.0, share)
     low = z_ref[...].astype(LOW)
-    kvgrad_ref[:rows, :] = (mine_ref[...] + got_ref[:rows, :].astype(F32)).astype(LOW)
+    mine = keep_ref[...].astype(F32) + near_ref[:rows, :].astype(F32)
+    kvgrad_ref[:rows, :] = (mine + got_ref[:rows, :].astype(F32)).astype(LOW)
     kvgrad_ref[rows:, :] = (sent_ref[rows:, :].astype(F32) + got_ref[rows:, :].astype(F32)).astype(LOW)
     grads = (qgrad_ref[...], kvgrad_ref[:, :width], kvgrad_ref[:, width:])
     grad = joint_ref[...]
@@ -467,7 +504,7 @@
         return result
 
 
-def call(kernel, name, cost, ins, outs, weights, scratch=(), grads=None, after=(), rows_of=None):
+def call(kernel, name, cost, ins, outs, weights, scratch=(), grads=(), rows_of=None):
     sources, operands, begins = [], [], []
     for source, _, _ in weights.values():
         if not any(source is other for other in sources):
@@ -481,25 +518,27 @@
         slots = slots + count
     high, width = operands[0].shape[2:]
     shards = width // high
-    grad_slots, number = {}, 0
-    if grads is not None:
-        for key in grads[0]:
-            if key in ("down",):
-                grad_slots[key] = number
-                number += grads[2]
-            else:
-                grad_slots[key] = number
-                number += 1
-    halves = 0 if grads is None else (1 if grads[1] is None else 2)
+    groups, goals, aliases, shapes, made_shapes, grad_places = [], [], {}, [], [], {}
+    for number, (keys, order, count, total_slots, into) in enumerate(grads):
+        place = 0
+        for key in keys:
+            grad_places[key] = (number, place, count if key == "down" else 1)
+            place += grad_places[key][2]
+        halves = 1 if order is None else 2
+        arrays, start = into or ((), 0)
+        for half, array in enumerate(arrays):
+            aliases[len(ins) + len(operands) + len(goals)] = len(shapes) + half
+            goals.append(array)
+        groups.append((order, halves, len(shapes), start))
+        shapes += [jax.ShapeDtypeStruct((shards // halves, total_slots or place, high, width), LOW)] * halves
+        made_shapes += [pltpu.VMEM((shards, place, high, width), LOW), pltpu.SemaphoreType.DMA((place, 2))]
 
     def body(*refs):
         in_refs, refs = refs[: len(ins)], refs[len(ins) :]
-        operand_refs, refs = refs[: len(operands)], refs[len(operands) + len(after) :]
-        grad_refs, refs = refs[:halves], refs[halves:]
-        if halves:
-            *refs, buffer, sems, made, made_sems = refs
-        else:
-            *refs, buffer, sems = refs
+        operand_refs, refs = refs[: len(operands)], refs[len(operands) + len(goals) :]
+        grad_refs, refs = refs[: len(shapes)], refs[len(shapes) :]
+        refs, made_refs = refs[: len(refs) - len(made_shapes)], refs[len(refs) - len(made_shapes) :]
+        *refs, buffer, sems = refs
         core = lax.axis_index("blk") % 2
         copies = {}
         for turn, (key, (which, slot, place, count)) in enumerate(places.items()):
@@ -516,6 +555,7 @@
                 copies[key].append(copy)
         arrived = set()
         offsets = [None if order is None else order.mine() for _, order in sources]
+        goal_offsets = [None if order is None else order.mine() for order, _, _, _ in groups]
 
         def weight(key, part=None):
             if key not in arrived:
@@ -535,29 +575,26 @@
             return jnp.concatenate(pieces, 0)
 
         out = []
-        if halves:
-            offset = None if grads[1] is None else grads[1].mine()
 
         def put(key, grad):
             low = grad.astype(LOW)
-            if isinstance(key, tuple) and key[0] == "down":
-                count, slot, first = grads[2], grad_slots["down"], key[1] * (shards // grads[2])
-            else:
-                count, slot, first = 1, grad_slots[key], 0
+            down = isinstance(key, tuple) and key[0] == "down"
+            number, slot, count = grad_places["down" if down else key]
+            order, halves, begin, start = groups[number]
+            made, made_sems = made_refs[2 * number], made_refs[2 * number + 1]
+            first = key[1] * (shards // count) if down else 0
             for block in range(low.shape[0] // high):
                 shard, inner = first + block // count, block % count
-                value = low[block * high : (block + 1) * high]
-                if halves == 1:
-                    made[shard, slot + inner] = value
-                else:
-                    at = ((shard % 2) ^ core) * (shards // 2) + (grads[1].place(shard) ^ offset)
-                    made[at, slot + inner] = value
-            if count == 1 or key[1] == count - 1:
+                at = shard
+                if order is not None:
+                    at = ((shard % 2) ^ core) * (shards // 2) + (order.place(shard) ^ goal_offsets[number])
+                made[at, slot + inner] = low[block * high : (block + 1) * high]
+            if not down or key[1] == count - 1:
                 piece = shards // halves
                 for half in range(halves):
                     copy = pltpu.make_async_copy(
                         made.at[pl.ds(half * piece, piece), pl.ds(slot, count)],
-                        grad_refs[half].at[:, pl.ds(slot, count)],
+                        grad_refs[begin + half].at[:, pl.ds(start + slot, count)],
                         made_sems.at[slot, half],
                     )
                     copy.start()
@@ -568,24 +605,21 @@
             copy.wait()
 
     inside, anywhere = pl.BlockSpec(memory_space=pltpu.VMEM), pl.BlockSpec(memory_space=pl.ANY)
-    shapes = [jax.ShapeDtypeStruct((shards // max(halves, 1), number, high, width), LOW)] * halves
-    scratch = list(scratch) + [
-        pltpu.VMEM((shards, slots, high, width), LOW),
-        pltpu.SemaphoreType.DMA((len(weights), 2)),
-    ]
-    if halves:
-        scratch += [pltpu.VMEM((shards, number, high, width), LOW), pltpu.SemaphoreType.DMA((number, 2))]
     results = pl.pallas_call(
         body,
         out_shape=shapes + [jax.ShapeDtypeStruct(shape, kind) for shape, kind in outs],
-        in_specs=[inside] * len(ins) + [anywhere] * (len(operands) + len(after)),
-        out_specs=[anywhere] * halves + [inside] * len(outs),
-        scratch_shapes=scratch,
+        in_specs=[inside] * len(ins) + [anywhere] * (len(operands) + len(goals)),
+        out_specs=[anywhere] * len(shapes) + [inside] * len(outs),
+        scratch_shapes=list(scratch)
+        + [pltpu.VMEM((shards, slots, high, width), LOW), pltpu.SemaphoreType.DMA((len(weights), 2))]
+        + made_shapes,
+        input_output_aliases=aliases,
         compiler_params=pltpu.CompilerParams(vmem_limit_bytes=VMEM_LIMIT),
-        cost_estimate=pl.CostEstimate(flops=int(cost * 1.1e8), bytes_accessed=0, transcendentals=0),
+        cost_estimate=pl.CostEstimate(flops=int(cost * 3.3e8), bytes_accessed=0, transcendentals=0),
         name=name,
-    )(*ins, *operands, *after)
-    return ([results[:halves]] if halves else []) + list(results[halves:])
+    )(*ins, *operands, *goals)
+    made = [results[begin : begin + halves] for _, halves, begin, _ in groups]
+    return made + list(results[len(shapes) :])
 
 
 def flipped(value, bit):
@@ -594,7 +628,8 @@
 
 
 def quartet(value):
-    return [value] + [flipped(value, bit) for bit in (1, 2, 3)]
+    chip = flipped(value, 2)
+    return [value, flipped(value, 1), chip, flipped(chip, 1)]
 
 
 def bits_of(axis):
@@ -624,22 +659,27 @@
     def begin(self):
         done = {}
         for number, (_, stages, first) in enumerate(self.groups):
-            if first <= self.turn < first + len(stages):
+            if first <= self.turn < first + len(stages) and stages[self.turn - first] is not None:
                 self.got[number] = swapped(self.held[number], stages[self.turn - first])
-                if self.turn - first + 1 == len(stages):
-                    done[number] = ((self.held[number], self.got.pop(number)), Order(stages[-2::-1]))
+                if self.turn - first + 1 == len(stages) and stages[-1] == ("blk", 0):
+                    done[number] = ((self.held[number], self.got.pop(number)), Order([s for s in stages[-2::-1] if s]))
         return done
 
+    def split(self, number, slots, stages):
+        held, (shard, done, _) = self.held[number], self.groups[number]
+        parts = (held[:, :slots], held[:, slots:])
+        for place, part, more in zip((number, len(self.groups)), parts, stages):
+            self.groups[place : place + 1] = [(shard, done + more, self.turn - len(done))]
+            self.held[place : place + 1] = [part]
+
     def end(self, *others):
-        for number, value in self.got.items():
+        numbers = list(self.got)
+        bundle = fence(*self.got.values(), *others)
+        for number, value in zip(numbers, bundle):
             self.held[number] = jnp.concatenate([self.held[number], value])
+        self.got = {}
         self.turn += 1
-        waiting = [n for n, (_, stages, first) in enumerate(self.groups) if self.turn < first + len(stages)]
-        bundle = fence(*[self.held[n] for n in waiting], *others)
-        for number, value in zip(waiting, bundle):
-            self.held[number] = value
-        self.got = {}
-        return bundle[len(waiting) :]
+        return bundle[len(numbers) :]
 
 
 def joined(values):
@@ -670,26 +710,29 @@
 
 class Background:
     def __init__(self):
-        self.sums, self.running = {}, []
+        self.sums, self.running, self.staying = {}, [], set()
 
     def add(self, name, arrays, stages):
         self.sums[name] = Scattering(arrays, stages)
 
     def begin(self, *names):
+        self.staying = {name[1:] for name in names if name[0] == "~"}
         for name in names:
-            if name in self.sums:
-                self.sums[name].begin()
-                self.running.append(self.sums[name])
+            short = name.rstrip("+")
+            if short in self.sums:
+                self.sums[short].begin()
+                self.running.append(short)
+                if short != name:
+                    self.staying.add(short)
 
     def end(self, *others):
-        if not self.running:
-            return list(others)
-        gots = [got for run in self.running for got in run.gots]
-        gots = fence(*gots, *others)
-        for run in self.running:
+        ending = [self.sums[name] for name in self.running if name not in self.staying]
+        self.running = [name for name in self.running if name in self.staying]
+        self.staying = set()
+        gots = fence(*[got for run in ending for got in run.gots], *others)
+        for run in ending:
             run.gots, gots = gots[: len(run.gots)], gots[len(run.gots) :]
             run.end()
-        self.running = []
         return gots
 
 
@@ -713,11 +756,21 @@
     small = jnp.pad(small, ((0, 0), (0, width - small.shape[1])))[None]
 
     def rows_of(index):
-        return dict(gain=starts[0] + index * gain_rows, shift=starts[1] + index * shift_rows, memory=starts[3])
-
-    attn_low, up_low, down_low = attn_weights.astype(LOW), ffn_in.astype(LOW), ffn_out.astype(LOW)
-    up_low = up_low.reshape(layers, rows, per, width).transpose(0, 2, 1, 3)
-    down_low = down_low.reshape(layers, per, rows, width)
+        return dict(
+            gain=starts[0] + index * gain_rows,
+            shift=starts[1] + index * shift_rows,
+            bias=64 + index * per,
+            memory=starts[3],
+            sizes=(rows, per, starts[2]),
+        )
+
+    seg_low = segments.astype(LOW)
+
+    def lowered(attn, up, down):
+        up = up.astype(LOW).reshape(layers, rows, per, width).transpose(0, 2, 1, 3)
+        return attn, up, down.astype(LOW).reshape(layers, per, rows, width)
+
+    attn_low, up_low, down_low = lowered(attn_weights, ffn_in, ffn_out)
     early, middle, late = (0, 1, 2), (3, 8, 4, 5, 6), (7, 9, 10, 11)
     table = {}
 
@@ -732,33 +785,51 @@
     if direct:
 
         def picked(index, keys):
-            return [attn_low[index, key][None] for key in keys]
-
-        y_last = line_bits + chip_bits + near_bit + [core_bit]
-        x_last = near_bit + line_bits + chip_bits + [core_bit]
-        x_early = chip_bits + line_bits + near_bit + [core_bit]
+            return [attn_low[index, key][None].astype(LOW) for key in keys]
+
+        far, line = line_bits[:1], line_bits[1:]
+        last = [core_bit]
+        pause = [None]
         gathering = Gathering(
             [
-                (jnp.concatenate(picked(0, early) + [small]), y_last, 0),
-                (jnp.concatenate(picked(0, middle)), y_last, 1),
-                (jnp.concatenate(picked(0, late) + [up_low[0]]), y_last, 2),
-                (jnp.concatenate([down_low[0]] + picked(1, early)), x_last, 2),
-                (jnp.concatenate(picked(1, middle)), x_early, 4),
+                (jnp.concatenate(picked(0, early) + [small]), far + line + chip_bits + near_bit + last, 0),
+                (jnp.concatenate(picked(0, middle)), far + line + near_bit + chip_bits + last, 0),
             ]
         )
-        rest = jnp.concatenate(picked(1, late) + [up_low[1], down_low[1]])
-        for turn in range(4):
-            if turn == GATHER_AT:
-                whole = lax.all_gather(rest, ALL)
+        gathering.begin()
+        attn_weights, ffn_in, ffn_out, seg_low = gathering.end(attn_weights, ffn_in, ffn_out, seg_low)
+        attn_low, up_low, down_low = lowered(attn_weights, ffn_in, ffn_out)
+        gathering.groups += [
+            (
+                jnp.concatenate(picked(0, late) + [up_low[0, :1]]),
+                far + line + near_bit + chip_bits + last,
+                2,
+            ),
+            (
+                jnp.concatenate([down_low[0], up_low[0, 1:2]]),
+                chip_bits + far + line + pause + near_bit + last,
+                1,
+            ),
+            (
+                jnp.concatenate([up_low[0, 2:]] + picked(1, early)),
+                near_bit + chip_bits + pause + far + line + last,
+                1,
+            ),
+            (jnp.concatenate(picked(1, middle)), far + line + chip_bits + near_bit + last, 4),
+            (jnp.concatenate(picked(1, late) + [up_low[1], down_low[1]]), far + line, 6),
+        ]
+        gathering.held += [shard[None] for shard, _, _ in gathering.groups[2:]]
+        gathering.begin()
+        seg_all = gathering.end(*quartet(seg_low))
+        for turn in range(2, 4):
             gathering.begin()
-            (rest,) = gathering.end(rest)
-        if GATHER_AT == 4:
-            whole = lax.all_gather(rest, ALL)
-        listed(gathering.begin()[0], 0, early + ("small",))
-        listed(((whole,), None), 1, late + ups + ("down",))
+            gathering.end()
+        found = gathering.begin()
+        listed(found[0], 0, early + ("small",))
+        listed(found[1], 0, middle)
     else:
         packed = jnp.concatenate(
-            [attn_low.reshape(-1, rows, width), up_low.reshape(-1, rows, width), small, down_low.reshape(-1, rows, width)]
+            [attn_low.astype(LOW).reshape(-1, rows, width), up_low.reshape(-1, rows, width), small, down_low.reshape(-1, rows, width)]
         )
         whole = lax.all_gather(packed, ALL)
         split = layers * (count + per) + 1
@@ -786,12 +857,7 @@
     share = 1.0 / size
     me = lax.axis_index("blk")
     seg = segments[0].astype(F32)
-    seg_parts = jnp.zeros((size, length), F32)
-    for other, part in enumerate(quartet(segments)):
-        seg_parts = lax.dynamic_update_slice(seg_parts, part.astype(F32), (me ^ other, 0))
-    seg_keys = jnp.concatenate(
-        [seg_parts.reshape(-1), jnp.full((MEM,), -2.0, F32), jnp.full((PAD - MEM,), -3.0, F32)]
-    ).reshape(-1, 1)
+    seg_all = seg_all if direct else quartet(seg_low)
     seg_row = jnp.concatenate([seg, jnp.full((PAD,), -1.0, F32)])
     seg_queries = jnp.concatenate([seg_row, seg_row]).reshape(1, -1)
     every = size * length + PAD
@@ -808,43 +874,55 @@
         attn(0, *early, "small"),
         rows_of=rows_of(0),
     )
-    bias = smalls[starts[2] : starts[3]].reshape(layers, per, everyone, rows).transpose(0, 2, 1, 3)
-    bias = bias.reshape(layers, per, width)
     kept = []
     for index in range(layers):
         core = flipped(own, 1)
         chip = flipped(own, 2)
         both = flipped(chip, 1)
         if direct:
-            core, chip, both, seg_keys = gathering.end(core, chip, both, seg_keys)
-            listed(gathering.begin()[1 if index == 0 else 4], index, middle)
-        att, pre, first, rq, rkv, wq, part = call(
+            core, chip, both = gathering.end(core, chip, both)
+            if index > 0:
+                gathering.split(6, len(late) + 2, [chip_bits + near_bit + [core_bit], near_bit + chip_bits + [core_bit]])
+            found = gathering.begin()
+            if index > 0:
+                listed(found[5], index, middle)
+        att, lse, pre, first, rq, rkv, wq, part = call(
             attend_kernel,
             f"attend_{index}",
             13,
-            [z, q, own, core, chip, both, kvmem, seg_keys, seg_queries, smalls],
+            [z, q, own, core, chip, both, kvmem, *seg_all, seg_queries, smalls],
             [
-                ((full, width), LOW), ((full, width), F32), ((full, width), F32), ((PAD, width), LOW),
+                ((full, width), LOW), ((width // 128, 2 * full), F32), ((full, width), F32), ((full, width), F32),
+                ((PAD, width), LOW),
                 ((length, 2 * width), LOW), ((length, width), LOW), ((PAD, width + 128), F32),
             ],
             attn(index, 3, 8, 4, 5, 6),
             [keys_scratch, bound_scratch],
             rows_of=rows_of(index),
         )
+        if direct and index > 0:
+            (part,) = gathering.end(part)
+            gathering.begin()
         parts = quartet(part)
+        if direct and index > 0:
+            parts = gathering.end(*parts)
+            found = gathering.begin()
+            listed(found[6], 1, late + ups[:2])
+            listed(found[7], 1, ups[2:] + ("down",))
         if direct and index == 0:
             parts = gathering.end(*parts)
             found = gathering.begin()
-            listed(found[2], 0, late + ups)
-            listed(found[3], 0, ("down",))
+            listed(found[2], 0, late + ups[:1])
+            listed(found[3], 0, ("down",) + ups[1:2])
+            listed(found[4], 0, ups[2:])
             for key in early:
-                table[1, key] = (found[3], per + key, 1)
+                table[1, key] = (found[4], per - 2 + key, 1)
         last = index + 1 == layers
         results = call(
             functools.partial(finish_kernel, last),
             f"finish_{index}",
             10,
-            [first, *parts, wq, bias[index], smalls],
+            [first, *parts, wq, smalls],
             [((full, width), F32)]
             + ([] if last else projected)
             + [
@@ -858,7 +936,7 @@
         rout, rlse, mempre, second, wkv, wlow, seqpre, x, feedpre = results[-9:]
         kept.append(
             dict(
-                z=z, q=q, own=own, kvmem=kvmem, core=core, chip=chip, both=both, att=att, pre=pre, first=first,
+                z=z, q=q, own=own, kvmem=kvmem, core=core, chip=chip, both=both, att=att, lse=lse, pre=pre, first=first,
                 rq=rq, rkv=rkv, wq=wq, rout=rout, rlse=rlse, mempre=mempre, second=second, wkv=wkv, wlow=wlow,
                 seqpre=seqpre, x=x, feedpre=feedpre,
             )
@@ -874,108 +952,139 @@
         [out_grad[0].astype(F32), jnp.pad(memory_cot[0].astype(F32), ((0, PAD - MEM), (0, 0)))]
     )
     background = Background()
-    upward = line_bits[::-1]
-    x_late = near_bit + upward + chip_bits
-    y_first = near_bit + chip_bits + upward
-    x_first = chip_bits + near_bit + upward
-    z_first = upward[:1] + near_bit + chip_bits + upward[1:]
-    orders = {"early": (z_first, x_late), "middle": (y_first, x_late), "attend": (x_first, x_late), "last": (y_first, x_late)}
-
-    def given(keys, order):
-        return (keys, Order(order) if direct else None, per)
-
-    group_keys = [ups + ("down", 11, 8), (9, 10, 7, 5, 6), (4, 3, 0), (1, 2)]
+    y, x, upward = near_bit, chip_bits, line_bits[::-1]
+    orders = {
+        "up_1": y + upward + x,
+        "up_0": y + upward + x,
+        "down_1": upward[:1] + y + upward[1:] + x,
+        "down_0": upward[:1] + y + upward[1:] + x,
+        "first_1": y + upward + x,
+        "second_1": x + upward[:1] + y + upward[1:],
+        "second_0": upward[:1] + y + x + upward[1:],
+    }
+
+    def order_of(name):
+        return orders.get(name, y + x + upward)
+
+    def group(name, keys, slots=None, into=None):
+        if not direct:
+            return (keys, None, per, None, None)
+        return (keys, Order(order_of(name)), per, slots, into)
+
+    group_keys = [ups, ("down",), (11, 8), (9, 10, 7, 5, 6), (4, 3, 0), (1, 2)]
     made = [None] * layers
     for index in reversed(range(layers)):
         k = kept[index]
-        grads_one, gbias, small_one, mem, seq, part = call(
+        names = {name: f"{name}_{index}" for name in ("up", "down", "first", "second")}
+        end_name = names["second"] if index > 0 else "last"
+        plan = iter(PLAN[index])
+
+        def start(name, arrays):
+            if direct:
+                background.add(name, [arrays], [core_bit] + order_of(name))
+
+        grads_up, grads_down, grads_first, gbias, small_one, mem, seq, part = call(
             functools.partial(feed_back_kernel, share),
             f"feed_back_{index}",
-            14,
-            [grad, k["feedpre"], k["x"], k["seqpre"], k["wlow"], k["wq"], k["wkv"], k["first"], bias[index], smalls],
+            11,
+            [grad, k["feedpre"], k["x"], k["seqpre"], k["wlow"], k["wq"], k["wkv"], k["first"], smalls],
             [
                 ((per, width), F32),
                 ((5, width), F32), ((PAD, width), F32), ((length, width), F32), ((2 * PAD, width), LOW),
             ],
             feed(index) | attn(index, 11, 8),
-            grads=given(group_keys[0], orders["early"][min(index, 1)]),
+            grads=[
+                group(names["up"], group_keys[0]),
+                group(names["down"], group_keys[1]),
+                group(names["first"], group_keys[2], 7),
+            ],
             rows_of=rows_of(index),
         )
-        part, mem, seq = background.end(part, mem, seq)
-        if direct:
-            background.add(f"early_{index}", [grads_one], [core_bit] + orders["early"][min(index, 1)])
-        background.begin(*PLAN[index][0])
-        grads_two, small_two, mem, seq, part = call(
+        halves = len(grads_up)
+        part, mem, seq, *both = background.end(part, mem, seq, *grads_up, *grads_down)
+        grads_up, grads_down = both[:halves], both[halves:]
+        start(names["up"], grads_up)
+        start(names["down"], grads_down)
+        if index + 1 < layers:
+            start(*waiting)
+        background.begin(*next(plan))
+        parts = background.end(*quartet(part))
+        background.begin(*next(plan))
+        grads_read, small_two, mem, seq, part = call(
             functools.partial(read_back_kernel, share),
             f"read_back_{index}",
-            7,
-            [*quartet(part), mem, seq, k["second"], k["mempre"], k["rout"], k["rlse"], k["rq"], k["rkv"],
+            4,
+            [*parts, mem, seq, k["second"], k["mempre"], k["rout"], k["rlse"], k["rq"], k["rkv"],
              k["first"], k["pre"], smalls],
             [((4, width), F32), ((PAD, width), F32), ((length, width), F32), ((PAD, width), LOW)],
             attn(index, 9, 10, 7, 5, 6),
-            grads=given(group_keys[1], orders["middle"][min(index, 1)]),
+            grads=[group(names["first"], group_keys[3], 7, (grads_first, 2))],
             rows_of=rows_of(index),
         )
-        part, mem, seq = background.end(part, mem, seq)
-        if direct and index == 0:
-            background.add("middle_0", [grads_two], [core_bit] + orders["middle"][0])
-        background.begin(*PLAN[index][1])
-        grads_three, small_three, joint, qgrad, keep, send = call(
+        count_read = len(grads_read)
+        mem, seq, *rest = background.end(mem, seq, *grads_read, *quartet(part))
+        grads_read, parts = rest[:count_read], rest[count_read:]
+        start(names["first"], grads_read)
+        background.begin(*next(plan))
+        grads_attend, small_three, joint, qgrad, keep, pass_on, send = call(
             functools.partial(attend_back_kernel, share),
             f"attend_back_{index}",
-            18,
-            [k["z"], *quartet(part), mem, seq, k["first"], k["pre"], k["att"], k["q"], k["own"], k["core"], k["chip"],
-             k["both"], k["kvmem"], seg_keys, seg_queries, smalls],
+            14,
+            [k["z"], *parts, mem, seq, k["first"], k["pre"], k["att"], k["lse"], k["q"], k["own"], k["core"], k["chip"],
+             k["both"], k["kvmem"], *seg_all, seg_queries, smalls],
             [((2, width), F32), ((full, width), F32), ((full, width), LOW),
-             ((2 * length + PAD, 2 * width), LOW), ((2 * length + PAD, 2 * width), LOW)],
+             ((length, 2 * width), LOW), ((length + PAD, 2 * width), LOW), ((2 * length + PAD, 2 * width), LOW)],
             attn(index, 4, 3),
             [keys_scratch, bound_scratch, pltpu.VMEM((full, width), LOW), keys_scratch],
-            grads=given(group_keys[2], orders["attend"][min(index, 1)]),
+            grads=[group(names["second"], group_keys[4], 5 if index > 0 else 3)],
             rows_of=rows_of(index),
         )
-        keep, send = background.end(keep, send)
-        if direct and index == 0:
-            background.add("attend_0", [grads_three], [core_bit] + orders["attend"][0])
-        background.begin(*PLAN[index][2])
-        pair_sum = keep.astype(F32) + flipped(send, 1).astype(F32)
-        mine_part, theirs = pair_sum[:length], pair_sum[length:].astype(LOW)
+        pass_on, send, *grads_attend = background.end(pass_on, send, *grads_attend)
+        background.begin(*next(plan))
+        near = flipped(send, 1)
+        theirs = (pass_on.astype(F32) + near[length:].astype(F32)).astype(LOW)
         got = flipped(theirs, 2)
-        got, mine_part, theirs = background.end(got, mine_part, theirs)
-        background.begin(*PLAN[index][3])
-        made[index] = dict(
-            small=[small_one, small_two, small_three],
-            bias=gbias.reshape(everyone, per, rows).transpose(1, 0, 2).reshape(per, width),
-        )
+        got, theirs = background.end(got, theirs)
+        background.begin(*next(plan))
+        made[index] = dict(small=[small_one, small_two, small_three], bias=gbias)
         tiny = sum([m["small"] + [m["bias"]] for m in made], []) if index == 0 else []
-        grads_four, grad = call(
+        grads_last, grad = call(
             functools.partial(input_back_kernel, share),
             f"input_back_{index}",
-            5,
-            [k["z"], joint, qgrad, mine_part, theirs, got] + tiny,
+            3,
+            [k["z"], joint, qgrad, keep, near, theirs, got] + tiny,
             [((full, width), F32)],
             attn(index, 0, 1, 2),
             [pltpu.VMEM((full, 2 * width), LOW)],
-            grads=given(group_keys[3] + (("small",) if tiny else ()), orders["last"][min(index, 1)]),
+            grads=[
+                group(
+                    end_name,
+                    group_keys[5] + (("small",) if tiny else ()),
+                    *((5, (grads_attend, 3)) if index > 0 else ()),
+                )
+            ],
+            rows_of=rows_of(index),
         )
-        if direct and index > 0:
-            background.add(f"middle_{index}", [grads_two, grads_three, grads_four], [core_bit] + x_late)
-        made[index]["grads"] = (grads_one, grads_two, grads_three, grads_four)
+        waiting = (end_name, grads_last)
+        made[index]["grads"] = (grads_up, grads_down, grads_first, grads_read, grads_attend, grads_last)
 
     mine = [{} for _ in range(layers)]
     if direct:
-        (kept_four,) = background.end(grads_four[0])
-        background.add("last", [(kept_four, grads_four[1])], [core_bit] + orders["last"][0])
-        for names in PLAN[0][4:]:
-            background.begin(*names)
+        start("last", grads_last)
+        start("second_0", grads_attend)
+        background.begin(*next(plan))
+        background.end()
+        for moves in plan:
+            background.begin(*moves)
             background.end()
         for index in range(layers):
-            wanted = (f"early_{index}", f"middle_{index}") + (("attend_0", "last") if index == 0 else ())
+            wanted = [f"{name}_{index}" for name in ("up", "down", "first", "second")] + (["last"] if index == 0 else [])
             results = [background.sums[name].result for name in wanted]
-            keys = list(group_keys)
+            keys = [group_keys[0], group_keys[1], group_keys[2] + group_keys[3], group_keys[4]]
             if index > 0:
-                keys = [keys[0], keys[1] + keys[2] + keys[3]]
+                keys[3] = keys[3] + group_keys[5]
             else:
-                keys[3] = keys[3] + ("small",)
+                keys.append(group_keys[5] + ("small",))
             for result, held in zip(results, keys):
                 place = 0
                 for key in held:

time: 517 us -> 424 us (0.82)
  Pallas kernels: 144 us -> 92.5 us
  local copies, waits for them, and re-layouts: 43 us -> 8.61 us
  other arithmetic: 40.4 us -> 16.2 us
  waiting for transfers between devices: 182 us -> 205 us
  between operations: 16 us -> 3.33 us
  starting transfers between devices: 84.1 us -> 90.8 us
    pallas_call x13, Pallas kernels: 144 us -> 92.5 us  [call(): pl.pallas_call(body, out_shape=shapes + [jax.ShapeDtypeStruct(shape, kind...]
    ppermute x57 -> x83, waiting for transfers between devices: 119 us -> 136 us  [swapped(): lax.ppermute(value, axis, [(source, source ^ 1 << bit) for source in rang...]
    unnamed x155 -> x172, local copies, waits for them, and re-layouts: 14.8 us -> 3.17 us
    concatenate x20 -> x24, other arithmetic: 12.8 us -> 1.27 us  [end(): self.held[number] = jnp.concatenate([self.held[number], value])]
    ppermute x57 -> x83, starting transfers between devices: 65.8 us -> 76.4 us  [swapped(): lax.ppermute(value, axis, [(source, source ^ 1 << bit) for source in rang...]
    another operation x30 -> x42, other arithmetic: 20.7 us -> 11.6 us
  transfers between devices with their start and end apart: 89 -> 114, of which waited for: 49 -> 59; matrix products, arithmetic and copies ran while one was open for 12% -> 3% of each run, Pallas kernels for 20% -> 18%
where the time goes in v4:
time: 424 us; the launch traced here: 416 us
  waiting for transfers between devices  205 us (48%)
  Pallas kernels  92.5 us (22%)
  starting transfers between devices  90.8 us (21%)
  other arithmetic  16.2 us (4%)
  local copies, waits for them, and re-layouts  8.61 us (2%)
    ppermute x83, waiting for transfers between devices, swapped(): lax.ppermute(value, axis, [(source, source ^ 1 << bit) for source in rang...  136 us
    pallas_call x13, Pallas kernels, call(): pl.pallas_call(body, out_shape=shapes + [jax.ShapeDtypeStruct(shape, kind...  92.5 us
    ppermute x83, starting transfers between devices, swapped(): lax.ppermute(value, axis, [(source, source ^ 1 << bit) for source in rang...  76.4 us
    ppermute x31, waiting for transfers between devices, flipped(): lax.ppermute(value, 'blk', [(source, source ^ bit) for source in range(si...  68.3 us
    ppermute x31, starting transfers between devices, flipped(): lax.ppermute(value, 'blk', [(source, source ^ bit) for source in range(si...  14.5 us
    another operation x42, other arithmetic  11.6 us
  transfers between devices with their start and end apart: 114, of which 59 were waited for; matrix products, arithmetic and copies ran while one was open for 3% of the time, Pallas kernels for 18%

profile of v4, /device:TPU:0, one launch (start us, length us, event | category | flops | bytes accessed | tf_op | source)
XLA Modules:
  0.0 416.3 jit_solution(13340871571178266707)
XLA Ops:
  5.3 4.1 collective-permute-start
  9.6 3.5 collective-permute-done
  13.1 3.5 collective-permute-done.1
  21.2 1.8 collective-permute-start.5
  25.7 2.5 collective-permute-done.3
  28.2 1.8 collective-permute-start.13
  29.9 2.0 collective-permute-start.12
  35.1 7.9 %collective-permute-done.11 = bf16[1,5,16,512]{3,2,1,0:T(8,128)(2,1)S(1)} collective-permute-done((bf16[1,5,16,512]{3,2,1,0:T(8,128)(2,1)S(1)}, bf16[1,5,16,512]{3,2,1,0:T(8,128)(2,1)S(1)}, u32[]{:S(2)}, u32[]{:S(2)}) %collective-permute-start.11) | collective-permute-done | bytes 81952 | tf_op jit(solution)/shard_map/ppermute | solution.py:646
  47.7 9.8 %collective-permute-done.16 = bf16[2,5,16,512]{3,2,1,0:T(8,128)(2,1)S(1)} collective-permute-done((bf16[2,5,16,512]{3,2,1,0:T(8,128)(2,1)S(1)}, bf16[2,5,16,512]{3,2,1,0:T(8,128)(2,1)S(1)}, u32[]{:S(2)}, u32[]{:S(2)}) %collective-permute-start.16) | collective-permute-done | bytes 163872 | tf_op jit(solution)/shard_map/ppermute | solution.py:646
  57.5 1.8 collective-permute-done.15
  62.0 2.5 first.1
  65.1 2.1 collective-permute-start.20
  67.6 11.0 %collective-permute-done.23.refs_4_.refs_14_ = bf16[256,1024]{1,0:T(8,128)(2,1)S(1)} collective-permute-done((bf16[256,1024]{1,0:T(8,128)(2,1)S(1)}, bf16[256,1024]{1,0:T(8,128)(2,1)S(1)}, u32[]{:S(2)}, u32[]{:S(2)}) %collective-permute-start.23) | collective-permute-done | bytes 524320 | tf_op jit(solution)/shard_map/ppermute | solution.py:627
  80.4 2.8 collective-permute-done.20
  83.2 1.8 collective-permute-start.27
  85.0 4.3 %collective-permute-done.19 = bf16[4,5,16,512]{3,2,1,0:T(8,128)(2,1)S(1)} collective-permute-done((bf16[4,5,16,512]{3,2,1,0:T(8,128)(2,1)S(1)}, bf16[4,5,16,512]{3,2,1,0:T(8,128)(2,1)S(1)}, u32[]{:S(2)}, u32[]{:S(2)}) %collective-permute-start.19) | collective-permute-done | bytes 327712 | tf_op jit(solution)/shard_map/ppermute | solution.py:646
  89.4 2.2 collective-permute-start.28
  92.3 9.1 %attend_0.1 = (bf16[288,512]{1,0:T(8,128)(2,1)S(1)}, f32[4,576]{1,0:T(4,128)S(1)}, f32[288,512]{1,0:T(8,128)S(1)}, f32[288,512]{1,0:T(8,128)S(1)}, bf16[32,512]{...) custom-call(f32[288,512]{1,0:T(8,128)S(1)} %get-tuple-element.276.refs_0_,, ...), custom_call_target="tpu_custom_call" | custom-call | flops 4289999872 | tf_op jit(solution)/shard_map/attend_0/pallas_call | solution.py:608
  103.1 5.9 %collective-permute-done.31.refs_3_ = f32[32,640]{1,0:T(8,128)S(1)} collective-permute-done((f32[32,640]{1,0:T(8,128)S(1)}, f32[32,640]{1,0:T(8,128)S(1)}, u32[]{:S(2)}, u32[]{:S(2)}) %collective-permute-start.31) | collective-permute-done | bytes 81952 | tf_op jit(solution)/shard_map/ppermute | solution.py:627
  112.0 2.3 collective-permute-start.37
  115.4 1.9 collective-permute-done.35.refs_12_.refs_8_.refs_14_
  117.3 7.1 %finish_0.1 = (f32[288,512]{1,0:T(8,128)S(1)}, bf16[288,512]{1,0:T(8,128)(2,1)S(1)}, bf16[256,1024]{1,0:T(8,128)(2,1)S(1)}, bf16[32,1024]{1,0:T(8,128)(2,1)S(1)}...) custom-call(f32[288,512]{1,0:T(8,128)S(1)} %get-tuple-element.291.re, ...), custom_call_target="tpu_custom_call" | custom-call | flops 3300000000 | tf_op jit(solution)/shard_map/finish_0/pallas_call | solution.py:608
  127.6 10.9 %collective-permute-done.41.refs_4_.refs_14_ = bf16[256,1024]{1,0:T(8,128)(2,1)S(1)} collective-permute-done((bf16[256,1024]{1,0:T(8,128)(2,1)S(1)}, bf16[256,1024]{1,0:T(8,128)(2,1)S(1)}, u32[]{:S(2)}, u32[]{:S(2)}) %collective-permute-start.41) | collective-permute-done | bytes 524320 | tf_op jit(solution)/shard_map/ppermute | solution.py:627
  138.7 4.1 collective-permute-done.38
  146.0 9.1 %attend_1.1 = (bf16[288,512]{1,0:T(8,128)(2,1)S(1)}, f32[4,576]{1,0:T(4,128)S(1)}, f32[288,512]{1,0:T(8,128)S(1)}, f32[288,512]{1,0:T(8,128)S(1)}, bf16[32,512]{...) custom-call(f32[288,512]{1,0:T(8,128)S(1)} %get-tuple-element.305.refs_0_,, ...), custom_call_target="tpu_custom_call" | custom-call | flops 4289999872 | tf_op jit(solution)/shard_map/attend_1/pallas_call | solution.py:608
  158.9 17.8 %collective-permute-done.49.refs_3_ = f32[32,640]{1,0:T(8,128)S(1)} collective-permute-done((f32[32,640]{1,0:T(8,128)S(1)}, f32[32,640]{1,0:T(8,128)S(1)}, u32[]{:S(2)}, u32[]{:S(2)}) %collective-permute-start.49) | collective-permute-done | bytes 81952 | tf_op jit(solution)/shard_map/ppermute | solution.py:627
  179.2 2.6 collective-permute-done.52.refs_10_.refs_12_
  181.8 2.2 collective-permute-done.51.refs_8_.refs_10_.refs_16_
  184.1 6.0 %finish_1.1 = (f32[288,512]{1,0:T(8,128)S(1)}, f32[32,512]{1,0:T(8,128)S(1)}, f32[32,512]{1,0:T(8,128)S(1)}, f32[32,512]{1,0:T(8,128)S(1)}, f32[288,512]{1,0:T(8...) custom-call(f32[288,512]{1,0:T(8,128)S(1)} %get-tuple-element.319.re, ...), custom_call_target="tpu_custom_call" | custom-call | flops 3300000000 | tf_op jit(solution)/shard_map/finish_1/pallas_call | solution.py:608
  190.1 11.8 %feed_back_1.1 = (bf16[16,4,16,512]{3,2,1,0:T(8,128)(2,1)S(1)}, bf16[16,4,16,512]{3,2,1,0:T(8,128)(2,1)S(1)}, bf16[16,4,16,512]{3,2,1,0:T(8,128)(2,1)S(1)}, bf16...) custom-call(f32[288,512]{1,0:T(8,128)S(1)} %fusion.2.refs_0_, ...), custom_call_target="tpu_custom_call" | custom-call | flops 3630000128 | tf_op jit(solution)/shard_map/feed_back_1/pallas_call | solution.py:608
  203.5 3.2 collective-permute-done.56.refs_2_
  210.8 4.1 read_back_1.1
  216.4 2.4 collective-permute-done.61.refs_3_
  220.1 2.9 collective-permute-done.58
  226.3 11.1 %attend_back_1.1 = (bf16[16,5,16,512]{3,2,1,0:T(8,128)(2,1)S(1)}, bf16[16,5,16,512]{3,2,1,0:T(8,128)(2,1)S(1)}, f32[2,512]{1,0:T(2,128)S(1)}, f32[288,512]{1,0:T...) custom-call(f32[288,512]{1,0:T(8,128)S(1)} %copy-done.9, ...), custom_call_target="tpu_custom_call" | custom-call | flops 4620000256 | tf_op jit(solution)/shard_map/attend_back_1/pallas_call | solution.py:608
  242.0 2.3 collective-permute-start.66
  245.0 9.4 %collective-permute-done.66 = bf16[2,4,16,512]{3,2,1,0:T(8,128)(2,1)S(1)} collective-permute-done((bf16[2,4,16,512]{3,2,1,0:T(8,128)(2,1)S(1)}, bf16[2,4,16,512]{3,2,1,0:T(8,128)(2,1)S(1)}, u32[]{:S(2)}, u32[]{:S(2)}) %collective-permute-start.66) | collective-permute-done | bytes 131104 | tf_op jit(solution)/shard_map/ppermute | solution.py:646
  254.4 2.5 collective-permute-done.67
  256.8 4.4 %collective-permute-done.68 = bf16[8,7,16,512]{3,2,1,0:T(8,128)(2,1)S(1)} collective-permute-done((bf16[8,7,16,512]{3,2,1,0:T(8,128)(2,1)S(1)}, bf16[8,7,16,512]{3,2,1,0:T(8,128)(2,1)S(1)}, u32[]{:S(2)}, u32[]{:S(2)}) %collective-permute-start.68) | collective-permute-done | bytes 917536 | tf_op jit(solution)/shard_map/ppermute | solution.py:646
  265.0 2.4 input_back_1.1
  267.5 11.6 %feed_back_0.1 = (bf16[16,4,16,512]{3,2,1,0:T(8,128)(2,1)S(1)}, bf16[16,4,16,512]{3,2,1,0:T(8,128)(2,1)S(1)}, bf16[16,4,16,512]{3,2,1,0:T(8,128)(2,1)S(1)}, bf16...) custom-call(f32[288,512]{1,0:T(8,128)S(1)} %get-tuple-element.403.re, ...), custom_call_target="tpu_custom_call" | custom-call | flops 3630000128 | tf_op jit(solution)/shard_map/feed_back_0/pallas_call | solution.py:608
  280.0 1.9 collective-permute-start.77
  283.4 2.8 collective-permute-done.79.refs_2_
  288.7 5.1 %collective-permute-done.77 = bf16[2,7,16,512]{3,2,1,0:T(8,128)(2,1)S(1)} collective-permute-done((bf16[2,7,16,512]{3,2,1,0:T(8,128)(2,1)S(1)}, bf16[2,7,16,512]{3,2,1,0:T(8,128)(2,1)S(1)}, u32[]{:S(2)}, u32[]{:S(2)}) %collective-permute-start.77) | collective-permute-done | bytes 229408 | tf_op jit(solution)/shard_map/ppermute | solution.py:646
  296.2 4.1 read_back_0.1
  301.6 2.7 collective-permute-done.84.refs_3_
  305.5 2.9 collective-permute-done.81
  314.6 11.2 %attend_back_0.1 = (bf16[16,3,16,512]{3,2,1,0:T(8,128)(2,1)S(1)}, bf16[16,3,16,512]{3,2,1,0:T(8,128)(2,1)S(1)}, f32[2,512]{1,0:T(2,128)S(1)}, f32[288,512]{1,0:T...) custom-call(f32[288,512]{1,0:T(8,128)S(1)} %get-tuple-element.276.re, ...), custom_call_target="tpu_custom_call" | custom-call | flops 4620000256 | tf_op jit(solution)/shard_map/attend_back_0/pallas_call | solution.py:608
  325.8 3.2 collective-permute-done.89
  333.7 2.6 collective-permute-start.92
  336.8 7.7 %collective-permute-done.92 = bf16[2,4,16,512]{3,2,1,0:T(8,128)(2,1)S(1)} collective-permute-done((bf16[2,4,16,512]{3,2,1,0:T(8,128)(2,1)S(1)}, bf16[2,4,16,512]{3,2,1,0:T(8,128)(2,1)S(1)}, u32[]{:S(2)}, u32[]{:S(2)}) %collective-permute-start.92) | collective-permute-done | bytes 131104 | tf_op jit(solution)/shard_map/ppermute | solution.py:646
  346.2 2.2 collective-permute-done.94
  348.4 4.4 %collective-permute-done.93 = bf16[8,7,16,512]{3,2,1,0:T(8,128)(2,1)S(1)} collective-permute-done((bf16[8,7,16,512]{3,2,1,0:T(8,128)(2,1)S(1)}, bf16[8,7,16,512]{3,2,1,0:T(8,128)(2,1)S(1)}, u32[]{:S(2)}, u32[]{:S(2)}) %collective-permute-start.93) | collective-permute-done | bytes 917536 | tf_op jit(solution)/shard_map/ppermute | solution.py:646
  353.2 2.5 input_back_0.1
  360.7 10.0 %collective-permute-done.102 = bf16[1,4,16,512]{3,2,1,0:T(8,128)(2,1)S(1)} collective-permute-done((bf16[1,4,16,512]{3,2,1,0:T(8,128)(2,1)S(1)}, bf16[1,4,16,512]{3,2,1,0:T(8,128)(2,1)S(1)}, u32[]{:S(2)}, u32[]{:S(2)}) %collective-permute-start.102) | collective-permute-done | bytes 65568 | tf_op jit(solution)/shard_map/ppermute | solution.py:646
  373.3 1.8 collective-permute-start.105
  378.6 4.5 %collective-permute-done.105 = bf16[2,7,16,512]{3,2,1,0:T(8,128)(2,1)S(1)} collective-permute-done((bf16[2,7,16,512]{3,2,1,0:T(8,128)(2,1)S(1)}, bf16[2,7,16,512]{3,2,1,0:T(8,128)(2,1)S(1)}, u32[]{:S(2)}, u32[]{:S(2)}) %collective-permute-start.105) | collective-permute-done | bytes 229408 | tf_op jit(solution)/shard_map/ppermute | solution.py:646
  383.1 2.9 collective-permute-done.103
  386.0 4.5 %collective-permute-done.104 = bf16[8,3,16,512]{3,2,1,0:T(8,128)(2,1)S(1)} collective-permute-done((bf16[8,3,16,512]{3,2,1,0:T(8,128)(2,1)S(1)}, bf16[8,3,16,512]{3,2,1,0:T(8,128)(2,1)S(1)}, u32[]{:S(2)}, u32[]{:S(2)}) %collective-permute-start.104) | collective-permute-done | bytes 393248 | tf_op jit(solution)/shard_map/ppermute | solution.py:646
  393.3 5.1 %collective-permute-done.109 = bf16[1,7,16,512]{3,2,1,0:T(8,128)(2,1)S(1)} collective-permute-done((bf16[1,7,16,512]{3,2,1,0:T(8,128)(2,1)S(1)}, bf16[1,7,16,512]{3,2,1,0:T(8,128)(2,1)S(1)}, u32[]{:S(2)}, u32[]{:S(2)}) %collective-permute-start.109) | collective-permute-done | bytes 114720 | tf_op jit(solution)/shard_map/ppermute | solution.py:646
  400.6 2.6 collective-permute-done.111
  404.3 2.0 collective-permute-start.113
  407.3 2.0 collective-permute-done.113
  409.4 2.4 collective-permute-done.112
  (518 shorter events, 109.3 us)
Async XLA Ops:
  28.2 14.9 %collective-permute-start.13 = (bf16[2,5,16,512]{3,2,1,0:T(8,128)(2,1)S(1)}, bf16[2,5,16,512]{3,2,1,0:T(8,128)(2,1)S(1)}, u32[]{:S(2)}, u32[]{:S(2)}) collective-permute-start(bf16[2,5,16,512]{3,2,1,0:T(8,128)(2,1)S(1)} %pad_maximum_fusion.23), channel_id=1, source_target_pairs={{0,2},{1,3},{2,0},{3,1},{4,6},{5,7},{6,4},{7,5},{8,10},{9,11},{10,... | collective-permute-start | bytes 491528 | tf_op jit(solution)/shard_map/ppermute | solution.py:646
  29.9 13.1 %collective-permute-start.12 = (bf16[2,5,16,512]{3,2,1,0:T(8,128)(2,1)S(1)}, bf16[2,5,16,512]{3,2,1,0:T(8,128)(2,1)S(1)}, u32[]{:S(2)}, u32[]{:S(2)}) collective-permute-start(bf16[2,5,16,512]{3,2,1,0:T(8,128)(2,1)S(1)} %pad_maximum_fusion.22), channel_id=1, source_target_pairs={{0,16},{4,20},{8,24},{12,28},{16,0},{20,4},{24,8},{28,12},{1,17},{... | collective-permute-start | bytes 491528 | tf_op jit(solution)/shard_map/ppermute | solution.py:646
  32.0 11.1 %collective-permute-start.9 = (bf16[4,4,16,512]{3,2,1,0:T(8,128)(2,1)S(1)}, bf16[4,4,16,512]{3,2,1,0:T(8,128)(2,1)S(1)}, u32[]{:S(2)}, u32[]{:S(2)}) collective-permute-start(bf16[4,4,16,512]{3,2,1,0:T(8,128)(2,1)S(1)} %pad_maximum_fusion.18), channel_id=1, source_target_pairs={{0,2},{1,3},{2,0},{3,1},{4,6},{5,7},{6,4},{7,5},{8,10},{9,11},{10,... | collective-permute-start | bytes 786440 | tf_op jit(solution)/shard_map/ppermute | solution.py:646
  43.2 16.1 %collective-permute-start.15 = (bf16[8,5,16,512]{3,2,1,0:T(8,128)(2,1)S(1)}, bf16[8,5,16,512]{3,2,1,0:T(8,128)(2,1)S(1)}, u32[]{:S(2)}, u32[]{:S(2)}) collective-permute-start(bf16[8,5,16,512]{3,2,1,0:T(8,128)(2,1)S(1)} %pad_maximum_fusion.6), channel_id=1, source_target_pairs={{0,2},{1,3},{2,0},{3,1},{4,6},{5,7},{6,4},{7,5},{8,10},{9,11},{10,... | collective-permute-start | bytes 1966088 | tf_op jit(solution)/shard_map/ppermute | solution.py:646
  43.6 13.8 %collective-permute-start.14 = (bf16[8,4,16,512]{3,2,1,0:T(8,128)(2,1)S(1)}, bf16[8,4,16,512]{3,2,1,0:T(8,128)(2,1)S(1)}, u32[]{:S(2)}, u32[]{:S(2)}) collective-permute-start(bf16[8,4,16,512]{3,2,1,0:T(8,128)(2,1)S(1)} %pad_maximum_fusion.11), channel_id=1, source_target_pairs={{0,4},{4,0},{8,12},{12,8},{16,20},{20,16},{24,28},{28,24},{1,5},{5... | collective-permute-start | bytes 1572872 | tf_op jit(solution)/shard_map/ppermute | solution.py:646
  45.4 12.0 %collective-permute-start.17 = (bf16[4,5,16,512]{3,2,1,0:T(8,128)(2,1)S(1)}, bf16[4,5,16,512]{3,2,1,0:T(8,128)(2,1)S(1)}, u32[]{:S(2)}, u32[]{:S(2)}) collective-permute-start(bf16[4,5,16,512]{3,2,1,0:T(8,128)(2,1)S(1)} %pad_maximum_fusion.14), channel_id=1, source_target_pairs={{0,8},{4,12},{8,0},{12,4},{16,24},{20,28},{24,16},{28,20},{1,9},{5... | collective-permute-start | bytes 983048 | tf_op jit(solution)/shard_map/ppermute | solution.py:646
  46.0 11.4 %collective-permute-start.16 = (bf16[2,5,16,512]{3,2,1,0:T(8,128)(2,1)S(1)}, bf16[2,5,16,512]{3,2,1,0:T(8,128)(2,1)S(1)}, u32[]{:S(2)}, u32[]{:S(2)}) collective-permute-start(bf16[2,5,16,512]{3,2,1,0:T(8,128)(2,1)S(1)} %pad_maximum_fusion.24), channel_id=1, source_target_pairs={{0,8},{4,12},{8,0},{12,4},{16,24},{20,28},{24,16},{28,20},{1,9},{5... | collective-permute-start | bytes 491528 | tf_op jit(solution)/shard_map/ppermute | solution.py:646
  59.5 19.2 %collective-permute-start.21 = (bf16[1,5,16,512]{3,2,1,0:T(8,128)(2,1)S(1)}, bf16[1,5,16,512]{3,2,1,0:T(8,128)(2,1)S(1)}, u32[]{:S(2)}, u32[]{:S(2)}) collective-permute-start(bf16[1,5,16,512]{3,2,1,0:T(8,128)(2,1)S(1)} %bitcast.269), channel_id=1, source_target_pairs={{0,16},{4,20},{8,24},{12,28},{16,0},{20,4},{24,8},{28,12},{1,17},{... | collective-permute-start | bytes 245768 | tf_op jit(solution)/shard_map/ppermute | solution.py:646
  64.6 14.0 %collective-permute-start.23 = (bf16[256,1024]{1,0:T(8,128)(2,1)S(1)}, bf16[256,1024]{1,0:T(8,128)(2,1)S(1)}, u32[]{:S(2)}, u32[]{:S(2)}) collective-permute-start(bf16[256,1024]{1,0:T(8,128)(2,1)S(1)} %get-tuple-element.278.refs_2_.refs_12_), channel_id=1, source_target_pairs={{0,2},{1,3},{2,0},{3,1},{4,6},{5,7},{6,4},{7,5},{8,10},{9,11},{10,... | collective-permute-start | bytes 1572872 | tf_op jit(solution)/shard_map/ppermute | solution.py:627
  65.0 27.3 %collective-permute-start.25 = (bf16[16,5,16,512]{3,2,1,0:T(8,128)(2,1)S(1)}, bf16[16,5,16,512]{3,2,1,0:T(8,128)(2,1)S(1)}, u32[]{:S(2)}, u32[]{:S(2)}) collective-permute-start(bf16[16,5,16,512]{3,2,1,0:T(8,128)(2,1)S(1)} %constant_dynamic-update-slice_fusion.20.refs_13_.refs_15_.refs_17_.refs_23_), channel_id=1, source_target_pairs={{0,1},{1,0},{2,3},{3,2},{4,5},{5,4},{6,7},{7,6},{8,9},{9,8},{10,11... | collective-permute-start | bytes 3932168 | tf_op jit(solution)/shard_map/ppermute | solution.py:646
  65.1 18.1 %collective-permute-start.20 = (bf16[4,5,16,512]{3,2,1,0:T(8,128)(2,1)S(1)}, bf16[4,5,16,512]{3,2,1,0:T(8,128)(2,1)S(1)}, u32[]{:S(2)}, u32[]{:S(2)}) collective-permute-start(bf16[4,5,16,512]{3,2,1,0:T(8,128)(2,1)S(1)} %pad_maximum_fusion.16), channel_id=1, source_target_pairs={{0,16},{4,20},{8,24},{12,28},{16,0},{20,4},{24,8},{28,12},{1,17},{... | collective-permute-start | bytes 983048 | tf_op jit(solution)/shard_map/ppermute | solution.py:646
  67.3 21.9 %collective-permute-start.22 = (bf16[256,1024]{1,0:T(8,128)(2,1)S(1)}, bf16[256,1024]{1,0:T(8,128)(2,1)S(1)}, u32[]{:S(2)}, u32[]{:S(2)}) collective-permute-start(bf16[256,1024]{1,0:T(8,128)(2,1)S(1)} %get-tuple-element.278.refs_2_.refs_12_), channel_id=1, source_target_pairs={{0,1},{1,0},{2,3},{3,2},{4,5},{5,4},{6,7},{7,6},{8,9},{9,8},{10,11... | collective-permute-start | bytes 1572872 | tf_op jit(solution)/shard_map/ppermute | solution.py:627
  78.6 10.6 %collective-permute-start.24 = (bf16[256,1024]{1,0:T(8,128)(2,1)S(1)}, bf16[256,1024]{1,0:T(8,128)(2,1)S(1)}, u32[]{:S(2)}, u32[]{:S(2)}) collective-permute-start(bf16[256,1024]{1,0:T(8,128)(2,1)S(1)} %collective-permute-done.23.refs_4_.refs_14_), channel_id=1, source_target_pairs={{0,1},{1,0},{2,3},{3,2},{4,5},{5,4},{6,7},{7,6},{8,9},{9,8},{10,11... | collective-permute-start | bytes 1572872 | tf_op jit(solution)/shard_map/ppermute | solution.py:627
  78.7 10.6 %collective-permute-start.19 = (bf16[4,5,16,512]{3,2,1,0:T(8,128)(2,1)S(1)}, bf16[4,5,16,512]{3,2,1,0:T(8,128)(2,1)S(1)}, u32[]{:S(2)}, u32[]{:S(2)}) collective-permute-start(bf16[4,5,16,512]{3,2,1,0:T(8,128)(2,1)S(1)} %pad_maximum_fusion.15), channel_id=1, source_target_pairs={{0,4},{4,0},{8,12},{12,8},{16,20},{20,16},{24,28},{28,24},{1,5},{5... | collective-permute-start | bytes 983048 | tf_op jit(solution)/shard_map/ppermute | solution.py:646
  83.2 19.8 %collective-permute-start.27 = (bf16[8,5,16,512]{3,2,1,0:T(8,128)(2,1)S(1)}, bf16[8,5,16,512]{3,2,1,0:T(8,128)(2,1)S(1)}, u32[]{:S(2)}, u32[]{:S(2)}) collective-permute-start(bf16[8,5,16,512]{3,2,1,0:T(8,128)(2,1)S(1)} %pad_maximum_fusion.8), channel_id=1, source_target_pairs={{0,4},{4,0},{8,12},{12,8},{16,20},{20,16},{24,28},{28,24},{1,5},{5... | collective-permute-start | bytes 1966088 | tf_op jit(solution)/shard_map/ppermute | solution.py:646
  89.4 20.9 %collective-permute-start.28 = (bf16[8,5,16,512]{3,2,1,0:T(8,128)(2,1)S(1)}, bf16[8,5,16,512]{3,2,1,0:T(8,128)(2,1)S(1)}, u32[]{:S(2)}, u32[]{:S(2)}) collective-permute-start(bf16[8,5,16,512]{3,2,1,0:T(8,128)(2,1)S(1)} %pad_maximum_fusion.9), channel_id=1, source_target_pairs={{0,8},{4,12},{8,0},{12,4},{16,24},{20,28},{24,16},{28,20},{1,9},{5... | collective-permute-start | bytes 1966088 | tf_op jit(solution)/shard_map/ppermute | solution.py:646
  91.6 18.7 %collective-permute-start.26 = (bf16[8,5,16,512]{3,2,1,0:T(8,128)(2,1)S(1)}, bf16[8,5,16,512]{3,2,1,0:T(8,128)(2,1)S(1)}, u32[]{:S(2)}, u32[]{:S(2)}) collective-permute-start(bf16[8,5,16,512]{3,2,1,0:T(8,128)(2,1)S(1)} %pad_maximum_fusion.7), channel_id=1, source_target_pairs={{0,2},{1,3},{2,0},{3,1},{4,6},{5,7},{6,4},{7,5},{8,10},{9,11},{10,... | collective-permute-start | bytes 1966088 | tf_op jit(solution)/shard_map/ppermute | solution.py:646
  92.2 18.2 %collective-permute-start.29 = (bf16[2,5,16,512]{3,2,1,0:T(8,128)(2,1)S(1)}, bf16[2,5,16,512]{3,2,1,0:T(8,128)(2,1)S(1)}, u32[]{:S(2)}, u32[]{:S(2)}) collective-permute-start(bf16[2,5,16,512]{3,2,1,0:T(8,128)(2,1)S(1)} %pad_maximum_fusion.25), channel_id=1, source_target_pairs={{0,8},{4,12},{8,0},{12,4},{16,24},{20,28},{24,16},{28,20},{1,9},{5... | collective-permute-start | bytes 491528 | tf_op jit(solution)/shard_map/ppermute | solution.py:646
  111.4 13.1 %collective-permute-start.36 = (bf16[4,5,16,512]{3,2,1,0:T(8,128)(2,1)S(1)}, bf16[4,5,16,512]{3,2,1,0:T(8,128)(2,1)S(1)}, u32[]{:S(2)}, u32[]{:S(2)}) collective-permute-start(bf16[4,5,16,512]{3,2,1,0:T(8,128)(2,1)S(1)} %pad_maximum_fusion.17), channel_id=1, source_target_pairs={{0,2},{1,3},{2,0},{3,1},{4,6},{5,7},{6,4},{7,5},{8,10},{9,11},{10,... | collective-permute-start | bytes 983048 | tf_op jit(solution)/shard_map/ppermute | solution.py:646
  112.0 12.5 %collective-permute-start.37 = (bf16[1,12,16,512]{3,2,1,0:T(8,128)(2,1)S(1)}, bf16[1,12,16,512]{3,2,1,0:T(8,128)(2,1)S(1)}, u32[]{:S(2)}, u32[]{:S(2)}) collective-permute-start(bf16[1,12,16,512]{3,2,1,0:T(8,128)(2,1)S(1)} %bitcast.281), channel_id=1, source_target_pairs={{0,16},{4,20},{8,24},{12,28},{16,0},{20,4},{24,8},{28,12},{1,17},{... | collective-permute-start | bytes 589832 | tf_op jit(solution)/shard_map/ppermute | solution.py:646
  124.5 14.0 %collective-permute-start.41 = (bf16[256,1024]{1,0:T(8,128)(2,1)S(1)}, bf16[256,1024]{1,0:T(8,128)(2,1)S(1)}, u32[]{:S(2)}, u32[]{:S(2)}) collective-permute-start(bf16[256,1024]{1,0:T(8,128)(2,1)S(1)} %get-tuple-element.311.refs_2_.refs_12_), channel_id=1, source_target_pairs={{0,2},{1,3},{2,0},{3,1},{4,6},{5,7},{6,4},{7,5},{8,10},{9,11},{10,... | collective-permute-start | bytes 1572872 | tf_op jit(solution)/shard_map/ppermute | solution.py:627
  125.5 13.2 %collective-permute-start.40 = (bf16[256,1024]{1,0:T(8,128)(2,1)S(1)}, bf16[256,1024]{1,0:T(8,128)(2,1)S(1)}, u32[]{:S(2)}, u32[]{:S(2)}) collective-permute-start(bf16[256,1024]{1,0:T(8,128)(2,1)S(1)} %get-tuple-element.311.refs_2_.refs_12_), channel_id=1, source_target_pairs={{0,1},{1,0},{2,3},{3,2},{4,5},{5,4},{6,7},{7,6},{8,9},{9,8},{10,11... | collective-permute-start | bytes 1572872 | tf_op jit(solution)/shard_map/ppermute | solution.py:627
  125.6 17.2 %collective-permute-start.38 = (bf16[8,5,16,512]{3,2,1,0:T(8,128)(2,1)S(1)}, bf16[8,5,16,512]{3,2,1,0:T(8,128)(2,1)S(1)}, u32[]{:S(2)}, u32[]{:S(2)}) collective-permute-start(bf16[8,5,16,512]{3,2,1,0:T(8,128)(2,1)S(1)} %pad_maximum_fusion.10), channel_id=1, source_target_pairs={{0,4},{4,0},{8,12},{12,8},{16,20},{20,16},{24,28},{28,24},{1,5},{5... | collective-permute-start | bytes 1966088 | tf_op jit(solution)/shard_map/ppermute | solution.py:646
  127.2 11.5 %collective-permute-start.39 = (bf16[2,12,16,512]{3,2,1,0:T(8,128)(2,1)S(1)}, bf16[2,12,16,512]{3,2,1,0:T(8,128)(2,1)S(1)}, u32[]{:S(2)}, u32[]{:S(2)}) collective-permute-start(bf16[2,12,16,512]{3,2,1,0:T(8,128)(2,1)S(1)} %pad_maximum_fusion.12), channel_id=1, source_target_pairs={{0,8},{4,12},{8,0},{12,4},{16,24},{20,28},{24,16},{28,20},{1,9},{5... | collective-permute-start | bytes 1179656 | tf_op jit(solution)/shard_map/ppermute | solution.py:646
  143.1 12.0 %collective-permute-start.45 = (bf16[4,6,16,512]{3,2,1,0:T(8,128)(2,1)S(1)}, bf16[4,6,16,512]{3,2,1,0:T(8,128)(2,1)S(1)}, u32[]{:S(2)}, u32[]{:S(2)}) collective-permute-start(bf16[4,6,16,512]{3,2,1,0:T(8,128)(2,1)S(1)} %get-tuple-element.532), channel_id=1, source_target_pairs={{0,4},{4,0},{8,12},{12,8},{16,20},{20,16},{24,28},{28,24},{1,5},{5... | collective-permute-start | bytes 1179656 | tf_op jit(solution)/shard_map/ppermute | solution.py:646
  144.7 11.2 %collective-permute-start.44 = (bf16[4,6,16,512]{3,2,1,0:T(8,128)(2,1)S(1)}, bf16[4,6,16,512]{3,2,1,0:T(8,128)(2,1)S(1)}, u32[]{:S(2)}, u32[]{:S(2)}) collective-permute-start(bf16[4,6,16,512]{3,2,1,0:T(8,128)(2,1)S(1)} %get-tuple-element.533), channel_id=1, source_target_pairs={{0,2},{1,3},{2,0},{3,1},{4,6},{5,7},{6,4},{7,5},{8,10},{9,11},{10,... | collective-permute-start | bytes 1179656 | tf_op jit(solution)/shard_map/ppermute | solution.py:646
  156.0 21.9 %collective-permute-start.47 = (bf16[8,6,16,512]{3,2,1,0:T(8,128)(2,1)S(1)}, bf16[8,6,16,512]{3,2,1,0:T(8,128)(2,1)S(1)}, u32[]{:S(2)}, u32[]{:S(2)}) collective-permute-start(bf16[8,6,16,512]{3,2,1,0:T(8,128)(2,1)S(1)} %pad_maximum_fusion.4), channel_id=1, source_target_pairs={{0,2},{1,3},{2,0},{3,1},{4,6},{5,7},{6,4},{7,5},{8,10},{9,11},{10,... | collective-permute-start | bytes 2359304 | tf_op jit(solution)/shard_map/ppermute | solution.py:646
  157.2 20.8 %collective-permute-start.46 = (bf16[8,6,16,512]{3,2,1,0:T(8,128)(2,1)S(1)}, bf16[8,6,16,512]{3,2,1,0:T(8,128)(2,1)S(1)}, u32[]{:S(2)}, u32[]{:S(2)}) collective-permute-start(bf16[8,6,16,512]{3,2,1,0:T(8,128)(2,1)S(1)} %pad_maximum_fusion.3), channel_id=1, source_target_pairs={{0,4},{4,0},{8,12},{12,8},{16,20},{20,16},{24,28},{28,24},{1,5},{5... | collective-permute-start | bytes 2359304 | tf_op jit(solution)/shard_map/ppermute | solution.py:646
  157.9 18.8 %collective-permute-start.49 = (f32[32,640]{1,0:T(8,128)S(1)}, f32[32,640]{1,0:T(8,128)S(1)}, u32[]{:S(2)}, u32[]{:S(2)}) collective-permute-start(f32[32,640]{1,0:T(8,128)S(1)} %get-tuple-element.325.refs_1_), channel_id=1, source_target_pairs={{0,2},{1,3},{2,0},{3,1},{4,6},{5,7},{6,4},{7,5},{8,10},{9,11},{10,... | collective-permute-start | bytes 245768 | tf_op jit(solution)/shard_map/ppermute | solution.py:627
  158.9 17.9 %collective-permute-start.48 = (f32[32,640]{1,0:T(8,128)S(1)}, f32[32,640]{1,0:T(8,128)S(1)}, u32[]{:S(2)}, u32[]{:S(2)}) collective-permute-start(f32[32,640]{1,0:T(8,128)S(1)} %get-tuple-element.325.refs_1_), channel_id=1, source_target_pairs={{0,1},{1,0},{2,3},{3,2},{4,5},{5,4},{6,7},{7,6},{8,9},{9,8},{10,11... | collective-permute-start | bytes 245768 | tf_op jit(solution)/shard_map/ppermute | solution.py:627
  208.9 14.1 %collective-permute-start.58 = (bf16[8,4,16,512]{3,2,1,0:T(8,128)(2,1)S(1)}, bf16[8,4,16,512]{3,2,1,0:T(8,128)(2,1)S(1)}, u32[]{:S(2)}, u32[]{:S(2)}) collective-permute-start(bf16[8,4,16,512]{3,2,1,0:T(8,128)(2,1)S(1)} %slice.822), channel_id=1, source_target_pairs={{0,4},{4,0},{8,12},{12,8},{16,20},{20,16},{24,28},{28,24},{1,5},{5... | collective-permute-start | bytes 1572872 | tf_op jit(solution)/shard_map/ppermute | solution.py:646
  210.4 13.7 %collective-permute-start.59 = (bf16[8,4,16,512]{3,2,1,0:T(8,128)(2,1)S(1)}, bf16[8,4,16,512]{3,2,1,0:T(8,128)(2,1)S(1)}, u32[]{:S(2)}, u32[]{:S(2)}) collective-permute-start(bf16[8,4,16,512]{3,2,1,0:T(8,128)(2,1)S(1)} %slice.823), channel_id=1, source_target_pairs={{0,8},{4,12},{8,0},{12,4},{16,24},{20,28},{24,16},{28,20},{1,9},{5... | collective-permute-start | bytes 1572872 | tf_op jit(solution)/shard_map/ppermute | solution.py:646
  224.1 13.3 %collective-permute-start.65 = (bf16[16,7,16,512]{3,2,1,0:T(8,128)(2,1)S(1)}, bf16[16,7,16,512]{3,2,1,0:T(8,128)(2,1)S(1)}, u32[]{:S(2)}, u32[]{:S(2)}) collective-permute-start(bf16[16,7,16,512]{3,2,1,0:T(8,128)(2,1)S(1)} %get-tuple-element.374), channel_id=1, source_target_pairs={{0,1},{1,0},{2,3},{3,2},{4,5},{5,4},{6,7},{7,6},{8,9},{9,8},{10,11... | collective-permute-start | bytes 5505032 | tf_op jit(solution)/shard_map/ppermute | solution.py:646
  224.7 12.7 %collective-permute-start.63 = (bf16[4,4,16,512]{3,2,1,0:T(8,128)(2,1)S(1)}, bf16[4,4,16,512]{3,2,1,0:T(8,128)(2,1)S(1)}, u32[]{:S(2)}, u32[]{:S(2)}) collective-permute-start(bf16[4,4,16,512]{3,2,1,0:T(8,128)(2,1)S(1)} %slice.825), channel_id=1, source_target_pairs={{0,8},{4,12},{8,0},{12,4},{16,24},{20,28},{24,16},{28,20},{1,9},{5... | collective-permute-start | bytes 786440 | tf_op jit(solution)/shard_map/ppermute | solution.py:646
  225.0 12.3 %collective-permute-start.64 = (bf16[4,4,16,512]{3,2,1,0:T(8,128)(2,1)S(1)}, bf16[4,4,16,512]{3,2,1,0:T(8,128)(2,1)S(1)}, u32[]{:S(2)}, u32[]{:S(2)}) collective-permute-start(bf16[4,4,16,512]{3,2,1,0:T(8,128)(2,1)S(1)} %slice.827), channel_id=1, source_target_pairs={{0,4},{4,0},{8,12},{12,8},{16,20},{20,16},{24,28},{28,24},{1,5},{5... | collective-permute-start | bytes 786440 | tf_op jit(solution)/shard_map/ppermute | solution.py:646
  238.9 22.3 %collective-permute-start.68 = (bf16[8,7,16,512]{3,2,1,0:T(8,128)(2,1)S(1)}, bf16[8,7,16,512]{3,2,1,0:T(8,128)(2,1)S(1)}, u32[]{:S(2)}, u32[]{:S(2)}) collective-permute-start(bf16[8,7,16,512]{3,2,1,0:T(8,128)(2,1)S(1)} %slice.832), channel_id=1, source_target_pairs={{0,4},{4,0},{8,12},{12,8},{16,20},{20,16},{24,28},{28,24},{1,5},{5... | collective-permute-start | bytes 2752520 | tf_op jit(solution)/shard_map/ppermute | solution.py:646
  240.6 20.6 %collective-permute-start.70 = (bf16[288,1024]{1,0:T(8,128)(2,1)S(1)}, bf16[288,1024]{1,0:T(8,128)(2,1)S(1)}, u32[]{:S(2)}, u32[]{:S(2)}) collective-permute-start(bf16[288,1024]{1,0:T(8,128)(2,1)S(1)} %add_convert_fusion.13.refs_5_), channel_id=1, source_target_pairs={{0,2},{1,3},{2,0},{3,1},{4,6},{5,7},{6,4},{7,5},{8,10},{9,11},{10,... | collective-permute-start | bytes 1769480 | tf_op jit(solution)/shard_map/ppermute | solution.py:627
  242.0 12.4 %collective-permute-start.66 = (bf16[2,4,16,512]{3,2,1,0:T(8,128)(2,1)S(1)}, bf16[2,4,16,512]{3,2,1,0:T(8,128)(2,1)S(1)}, u32[]{:S(2)}, u32[]{:S(2)}) collective-permute-start(bf16[2,4,16,512]{3,2,1,0:T(8,128)(2,1)S(1)} %slice.829), channel_id=1, source_target_pairs={{0,16},{4,20},{8,24},{12,28},{16,0},{20,4},{24,8},{28,12},{1,17},{... | collective-permute-start | bytes 393224 | tf_op jit(solution)/shard_map/ppermute | solution.py:646
  244.3 12.5 %collective-permute-start.67 = (bf16[2,4,16,512]{3,2,1,0:T(8,128)(2,1)S(1)}, bf16[2,4,16,512]{3,2,1,0:T(8,128)(2,1)S(1)}, u32[]{:S(2)}, u32[]{:S(2)}) collective-permute-start(bf16[2,4,16,512]{3,2,1,0:T(8,128)(2,1)S(1)} %slice.831), channel_id=1, source_target_pairs={{0,16},{4,20},{8,24},{12,28},{16,0},{20,4},{24,8},{28,12},{1,17},{... | collective-permute-start | bytes 393224 | tf_op jit(solution)/shard_map/ppermute | solution.py:646
  261.6 17.5 %collective-permute-start.73 = (bf16[4,7,16,512]{3,2,1,0:T(8,128)(2,1)S(1)}, bf16[4,7,16,512]{3,2,1,0:T(8,128)(2,1)S(1)}, u32[]{:S(2)}, u32[]{:S(2)}) collective-permute-start(bf16[4,7,16,512]{3,2,1,0:T(8,128)(2,1)S(1)} %slice.838), channel_id=1, source_target_pairs={{0,8},{4,12},{8,0},{12,4},{16,24},{20,28},{24,16},{28,20},{1,9},{5... | collective-permute-start | bytes 1376264 | tf_op jit(solution)/shard_map/ppermute | solution.py:646
  262.9 16.2 %collective-permute-start.71 = (bf16[1,4,16,512]{3,2,1,0:T(8,128)(2,1)S(1)}, bf16[1,4,16,512]{3,2,1,0:T(8,128)(2,1)S(1)}, u32[]{:S(2)}, u32[]{:S(2)}) collective-permute-start(bf16[1,4,16,512]{3,2,1,0:T(8,128)(2,1)S(1)} %slice.834), channel_id=1, source_target_pairs={{0,2},{1,3},{2,0},{3,1},{4,6},{5,7},{6,4},{7,5},{8,10},{9,11},{10,... | collective-permute-start | bytes 196616 | tf_op jit(solution)/shard_map/ppermute | solution.py:646
  264.1 15.1 %collective-permute-start.72 = (bf16[1,4,16,512]{3,2,1,0:T(8,128)(2,1)S(1)}, bf16[1,4,16,512]{3,2,1,0:T(8,128)(2,1)S(1)}, u32[]{:S(2)}, u32[]{:S(2)}) collective-permute-start(bf16[1,4,16,512]{3,2,1,0:T(8,128)(2,1)S(1)} %slice.836), channel_id=1, source_target_pairs={{0,2},{1,3},{2,0},{3,1},{4,6},{5,7},{6,4},{7,5},{8,10},{9,11},{10,... | collective-permute-start | bytes 196616 | tf_op jit(solution)/shard_map/ppermute | solution.py:646
  267.4 26.4 %collective-permute-start.76 = (bf16[16,5,16,512]{3,2,1,0:T(8,128)(2,1)S(1)}, bf16[16,5,16,512]{3,2,1,0:T(8,128)(2,1)S(1)}, u32[]{:S(2)}, u32[]{:S(2)}) collective-permute-start(bf16[16,5,16,512]{3,2,1,0:T(8,128)(2,1)S(1)} %get-tuple-element.419), channel_id=1, source_target_pairs={{0,1},{1,0},{2,3},{3,2},{4,5},{5,4},{6,7},{7,6},{8,9},{9,8},{10,11... | collective-permute-start | bytes 3932168 | tf_op jit(solution)/shard_map/ppermute | solution.py:646
  279.2 14.6 %collective-permute-start.74 = (bf16[16,4,16,512]{3,2,1,0:T(8,128)(2,1)S(1)}, bf16[16,4,16,512]{3,2,1,0:T(8,128)(2,1)S(1)}, u32[]{:S(2)}, u32[]{:S(2)}) collective-permute-start(bf16[16,4,16,512]{3,2,1,0:T(8,128)(2,1)S(1)} %get-tuple-element.417), channel_id=1, source_target_pairs={{0,1},{1,0},{2,3},{3,2},{4,5},{5,4},{6,7},{7,6},{8,9},{9,8},{10,11... | collective-permute-start | bytes 3145736 | tf_op jit(solution)/shard_map/ppermute | solution.py:646
  279.7 14.1 %collective-permute-start.75 = (bf16[16,4,16,512]{3,2,1,0:T(8,128)(2,1)S(1)}, bf16[16,4,16,512]{3,2,1,0:T(8,128)(2,1)S(1)}, u32[]{:S(2)}, u32[]{:S(2)}) collective-permute-start(bf16[16,4,16,512]{3,2,1,0:T(8,128)(2,1)S(1)} %get-tuple-element.418), channel_id=1, source_target_pairs={{0,1},{1,0},{2,3},{3,2},{4,5},{5,4},{6,7},{7,6},{8,9},{9,8},{10,11... | collective-permute-start | bytes 3145736 | tf_op jit(solution)/shard_map/ppermute | solution.py:646
  280.0 13.8 %collective-permute-start.77 = (bf16[2,7,16,512]{3,2,1,0:T(8,128)(2,1)S(1)}, bf16[2,7,16,512]{3,2,1,0:T(8,128)(2,1)S(1)}, u32[]{:S(2)}, u32[]{:S(2)}) collective-permute-start(bf16[2,7,16,512]{3,2,1,0:T(8,128)(2,1)S(1)} %slice.840), channel_id=1, source_target_pairs={{0,16},{4,20},{8,24},{12,28},{16,0},{20,4},{24,8},{28,12},{1,17},{... | collective-permute-start | bytes 688136 | tf_op jit(solution)/shard_map/ppermute | solution.py:646
  294.8 13.7 %collective-permute-start.81 = (bf16[8,4,16,512]{3,2,1,0:T(8,128)(2,1)S(1)}, bf16[8,4,16,512]{3,2,1,0:T(8,128)(2,1)S(1)}, u32[]{:S(2)}, u32[]{:S(2)}) collective-permute-start(bf16[8,4,16,512]{3,2,1,0:T(8,128)(2,1)S(1)} %slice.841), channel_id=1, source_target_pairs={{0,4},{4,0},{8,12},{12,8},{16,20},{20,16},{24,28},{28,24},{1,5},{5... | collective-permute-start | bytes 1572872 | tf_op jit(solution)/shard_map/ppermute | solution.py:646
  296.1 13.6 %collective-permute-start.82 = (bf16[8,4,16,512]{3,2,1,0:T(8,128)(2,1)S(1)}, bf16[8,4,16,512]{3,2,1,0:T(8,128)(2,1)S(1)}, u32[]{:S(2)}, u32[]{:S(2)}) collective-permute-start(bf16[8,4,16,512]{3,2,1,0:T(8,128)(2,1)S(1)} %slice.842), channel_id=1, source_target_pairs={{0,8},{4,12},{8,0},{12,4},{16,24},{20,28},{24,16},{28,20},{1,9},{5... | collective-permute-start | bytes 1572872 | tf_op jit(solution)/shard_map/ppermute | solution.py:646
  309.7 19.2 %collective-permute-start.88 = (bf16[16,7,16,512]{3,2,1,0:T(8,128)(2,1)S(1)}, bf16[16,7,16,512]{3,2,1,0:T(8,128)(2,1)S(1)}, u32[]{:S(2)}, u32[]{:S(2)}) collective-permute-start(bf16[16,7,16,512]{3,2,1,0:T(8,128)(2,1)S(1)} %get-tuple-element.458), channel_id=1, source_target_pairs={{0,1},{1,0},{2,3},{3,2},{4,5},{5,4},{6,7},{7,6},{8,9},{9,8},{10,11... | collective-permute-start | bytes 5505032 | tf_op jit(solution)/shard_map/ppermute | solution.py:646
  311.7 17.2 %collective-permute-start.89 = (bf16[8,5,16,512]{3,2,1,0:T(8,128)(2,1)S(1)}, bf16[8,5,16,512]{3,2,1,0:T(8,128)(2,1)S(1)}, u32[]{:S(2)}, u32[]{:S(2)}) collective-permute-start(bf16[8,5,16,512]{3,2,1,0:T(8,128)(2,1)S(1)} %slice.847), channel_id=1, source_target_pairs={{0,2},{1,3},{2,0},{3,1},{4,6},{5,7},{6,4},{7,5},{8,10},{9,11},{10,... | collective-permute-start | bytes 1966088 | tf_op jit(solution)/shard_map/ppermute | solution.py:646
  313.4 15.6 %collective-permute-start.87 = (bf16[4,4,16,512]{3,2,1,0:T(8,128)(2,1)S(1)}, bf16[4,4,16,512]{3,2,1,0:T(8,128)(2,1)S(1)}, u32[]{:S(2)}, u32[]{:S(2)}) collective-permute-start(bf16[4,4,16,512]{3,2,1,0:T(8,128)(2,1)S(1)} %slice.846), channel_id=1, source_target_pairs={{0,4},{4,0},{8,12},{12,8},{16,20},{20,16},{24,28},{28,24},{1,5},{5... | collective-permute-start | bytes 786440 | tf_op jit(solution)/shard_map/ppermute | solution.py:646
  314.0 15.0 %collective-permute-start.86 = (bf16[4,4,16,512]{3,2,1,0:T(8,128)(2,1)S(1)}, bf16[4,4,16,512]{3,2,1,0:T(8,128)(2,1)S(1)}, u32[]{:S(2)}, u32[]{:S(2)}) collective-permute-start(bf16[4,4,16,512]{3,2,1,0:T(8,128)(2,1)S(1)} %slice.844), channel_id=1, source_target_pairs={{0,8},{4,12},{8,0},{12,4},{16,24},{20,28},{24,16},{28,20},{1,9},{5... | collective-permute-start | bytes 786440 | tf_op jit(solution)/shard_map/ppermute | solution.py:646
  330.0 22.8 %collective-permute-start.93 = (bf16[8,7,16,512]{3,2,1,0:T(8,128)(2,1)S(1)}, bf16[8,7,16,512]{3,2,1,0:T(8,128)(2,1)S(1)}, u32[]{:S(2)}, u32[]{:S(2)}) collective-permute-start(bf16[8,7,16,512]{3,2,1,0:T(8,128)(2,1)S(1)} %slice.852), channel_id=1, source_target_pairs={{0,4},{4,0},{8,12},{12,8},{16,20},{20,16},{24,28},{28,24},{1,5},{5... | collective-permute-start | bytes 2752520 | tf_op jit(solution)/shard_map/ppermute | solution.py:646
  332.0 20.8 %collective-permute-start.95 = (bf16[288,1024]{1,0:T(8,128)(2,1)S(1)}, bf16[288,1024]{1,0:T(8,128)(2,1)S(1)}, u32[]{:S(2)}, u32[]{:S(2)}) collective-permute-start(bf16[288,1024]{1,0:T(8,128)(2,1)S(1)} %add_convert_fusion.12.refs_5_), channel_id=1, source_target_pairs={{0,2},{1,3},{2,0},{3,1},{4,6},{5,7},{6,4},{7,5},{8,10},{9,11},{10,... | collective-permute-start | bytes 1769480 | tf_op jit(solution)/shard_map/ppermute | solution.py:627
  333.2 15.2 %collective-permute-start.94 = (bf16[4,5,16,512]{3,2,1,0:T(8,128)(2,1)S(1)}, bf16[4,5,16,512]{3,2,1,0:T(8,128)(2,1)S(1)}, u32[]{:S(2)}, u32[]{:S(2)}) collective-permute-start(bf16[4,5,16,512]{3,2,1,0:T(8,128)(2,1)S(1)} %slice.854), channel_id=1, source_target_pairs={{0,8},{4,12},{8,0},{12,4},{16,24},{20,28},{24,16},{28,20},{1,9},{5... | collective-permute-start | bytes 983048 | tf_op jit(solution)/shard_map/ppermute | solution.py:646
  333.7 10.8 %collective-permute-start.92 = (bf16[2,4,16,512]{3,2,1,0:T(8,128)(2,1)S(1)}, bf16[2,4,16,512]{3,2,1,0:T(8,128)(2,1)S(1)}, u32[]{:S(2)}, u32[]{:S(2)}) collective-permute-start(bf16[2,4,16,512]{3,2,1,0:T(8,128)(2,1)S(1)} %slice.851), channel_id=1, source_target_pairs={{0,16},{4,20},{8,24},{12,28},{16,0},{20,4},{24,8},{28,12},{1,17},{... | collective-permute-start | bytes 393224 | tf_op jit(solution)/shard_map/ppermute | solution.py:646
  344.5 13.7 %collective-permute-start.97 = (bf16[1,7,16,512]{3,2,1,0:T(8,128)(2,1)S(1)}, bf16[1,7,16,512]{3,2,1,0:T(8,128)(2,1)S(1)}, u32[]{:S(2)}, u32[]{:S(2)}) collective-permute-start(bf16[1,7,16,512]{3,2,1,0:T(8,128)(2,1)S(1)} %slice.859), channel_id=1, source_target_pairs={{0,2},{1,3},{2,0},{3,1},{4,6},{5,7},{6,4},{7,5},{8,10},{9,11},{10,... | collective-permute-start | bytes 344072 | tf_op jit(solution)/shard_map/ppermute | solution.py:646
  346.2 13.1 %collective-permute-start.101 = (bf16[16,3,16,512]{3,2,1,0:T(8,128)(2,1)S(1)}, bf16[16,3,16,512]{3,2,1,0:T(8,128)(2,1)S(1)}, u32[]{:S(2)}, u32[]{:S(2)}) collective-permute-start(bf16[16,3,16,512]{3,2,1,0:T(8,128)(2,1)S(1)} %get-tuple-element.489), channel_id=1, source_target_pairs={{0,1},{1,0},{2,3},{3,2},{4,5},{5,4},{6,7},{7,6},{8,9},{9,8},{10,11... | collective-permute-start | bytes 2359304 | tf_op jit(solution)/shard_map/ppermute | solution.py:646
  355.7 16.0 %collective-permute-start.100 = (bf16[16,3,16,512]{3,2,1,0:T(8,128)(2,1)S(1)}, bf16[16,3,16,512]{3,2,1,0:T(8,128)(2,1)S(1)}, u32[]{:S(2)}, u32[]{:S(2)}) collective-permute-start(bf16[16,3,16,512]{3,2,1,0:T(8,128)(2,1)S(1)} %get-tuple-element.488), channel_id=1, source_target_pairs={{0,1},{1,0},{2,3},{3,2},{4,5},{5,4},{6,7},{7,6},{8,9},{9,8},{10,11... | collective-permute-start | bytes 2359304 | tf_op jit(solution)/shard_map/ppermute | solution.py:646
  355.9 15.8 %collective-permute-start.98 = (bf16[4,7,16,512]{3,2,1,0:T(8,128)(2,1)S(1)}, bf16[4,7,16,512]{3,2,1,0:T(8,128)(2,1)S(1)}, u32[]{:S(2)}, u32[]{:S(2)}) collective-permute-start(bf16[4,7,16,512]{3,2,1,0:T(8,128)(2,1)S(1)} %slice.861), channel_id=1, source_target_pairs={{0,2},{1,3},{2,0},{3,1},{4,6},{5,7},{6,4},{7,5},{8,10},{9,11},{10,... | collective-permute-start | bytes 1376264 | tf_op jit(solution)/shard_map/ppermute | solution.py:646
  357.2 13.5 %collective-permute-start.102 = (bf16[1,4,16,512]{3,2,1,0:T(8,128)(2,1)S(1)}, bf16[1,4,16,512]{3,2,1,0:T(8,128)(2,1)S(1)}, u32[]{:S(2)}, u32[]{:S(2)}) collective-permute-start(bf16[1,4,16,512]{3,2,1,0:T(8,128)(2,1)S(1)} %slice.865), channel_id=1, source_target_pairs={{0,2},{1,3},{2,0},{3,1},{4,6},{5,7},{6,4},{7,5},{8,10},{9,11},{10,... | collective-permute-start | bytes 196616 | tf_op jit(solution)/shard_map/ppermute | solution.py:646
  358.2 13.4 %collective-permute-start.96 = (bf16[1,4,16,512]{3,2,1,0:T(8,128)(2,1)S(1)}, bf16[1,4,16,512]{3,2,1,0:T(8,128)(2,1)S(1)}, u32[]{:S(2)}, u32[]{:S(2)}) collective-permute-start(bf16[1,4,16,512]{3,2,1,0:T(8,128)(2,1)S(1)} %slice.857), channel_id=1, source_target_pairs={{0,2},{1,3},{2,0},{3,1},{4,6},{5,7},{6,4},{7,5},{8,10},{9,11},{10,... | collective-permute-start | bytes 196616 | tf_op jit(solution)/shard_map/ppermute | solution.py:646
  359.3 12.3 %collective-permute-start.99 = (bf16[2,5,16,512]{3,2,1,0:T(8,128)(2,1)S(1)}, bf16[2,5,16,512]{3,2,1,0:T(8,128)(2,1)S(1)}, u32[]{:S(2)}, u32[]{:S(2)}) collective-permute-start(bf16[2,5,16,512]{3,2,1,0:T(8,128)(2,1)S(1)} %slice.863), channel_id=1, source_target_pairs={{0,4},{4,0},{8,12},{12,8},{16,20},{20,16},{24,28},{28,24},{1,5},{5... | collective-permute-start | bytes 491528 | tf_op jit(solution)/shard_map/ppermute | solution.py:646
  376.4 14.1 %collective-permute-start.104 = (bf16[8,3,16,512]{3,2,1,0:T(8,128)(2,1)S(1)}, bf16[8,3,16,512]{3,2,1,0:T(8,128)(2,1)S(1)}, u32[]{:S(2)}, u32[]{:S(2)}) collective-permute-start(bf16[8,3,16,512]{3,2,1,0:T(8,128)(2,1)S(1)} %slice.868), channel_id=1, source_target_pairs={{0,8},{4,12},{8,0},{12,4},{16,24},{20,28},{24,16},{28,20},{1,9},{5... | collective-permute-start | bytes 1179656 | tf_op jit(solution)/shard_map/ppermute | solution.py:646
  (109 other events, 1147.3 us)

commit v5 on v4

--- a/solution.py
+++ b/solution.py
@@ -18,7 +18,7 @@
 ALL = ("dp", "blk")
 LOW = jnp.bfloat16
 F32 = jnp.float32
-VMEM_LIMIT = 24 * 1024 * 1024
+VMEM_LIMIT = 20 * 1024 * 1024
 PLAN = {
     1: [
         ("up_1", "down_1"),
@@ -28,16 +28,14 @@
         ("up_1", "down_1", "first_1"),
     ],
     0: [
-        ("up_0", "down_0", "second_1", "first_1"),
+        ("up_0", "down_0", "second_1"),
         ("up_0", "down_0"),
         ("up_0", "down_0", "first_0", "second_1"),
-        ("up_0", "down_0", "first_0", "second_1"),
-        ("up_0", "first_1", "first_0", "second_1"),
-        ("last", "second_0", "down_0"),
-        ("last", "second_0", "first_0", "second_1"),
-        ("last", "second_0", "first_0"),
-        ("last", "second_0"),
-        ("last", "second_0"),
+        ("up_0", "down_0", "first_0", "second_1", "second_0"),
+        ("first_0", "second_0", "up_0", "first_1", "second_1"),
+        ("last", "down_0"),
+        ("last", "second_0", "first_0", "second_1", "first_1"),
+        ("last", "first_0"),
     ],
 }
 
@@ -122,11 +120,11 @@
     return both[: rows // 2] + both[rows // 2 :]
 
 
-def place_bounds(bound_ref, seg_refs, seg_queries):
-    rows = seg_refs[0].shape[1]
+def place_bounds(bound_ref, seg_ref, seg_queries):
+    parts, rows = seg_ref.shape
     me = lax.axis_index("blk")
-    for other, seg_ref in enumerate(seg_refs):
-        numbers = jnp.broadcast_to(seg_ref[...].astype(F32), (128, rows)).T[:, 0:1]
+    for other in range(parts):
+        numbers = jnp.broadcast_to(seg_ref[other : other + 1, :], (128, rows)).T[:, 0:1]
         allowed = (numbers == seg_queries) | (seg_queries == -1.0)
         place = pl.ds(pl.multiple_of((me ^ other) * rows, rows), rows)
         bound_ref[place, :] = jnp.where(allowed, BIG, NEG)
@@ -161,9 +159,19 @@
     return (goal == lax.broadcasted_iota(jnp.int32, (width, width), 1)).astype(LOW)
 
 
-def first_kernel(weight, put, rows_of, tokens_ref, small_ref, z_ref, q_ref, kv_ref, kvmem_ref):
+def first_kernel(weight, put, rows_of, tokens_ref, small_ref, z_ref, q_ref, kv_ref, kvmem_ref, *seg_refs):
     rows = tokens_ref.shape[0]
-    columns = weight("small")[:, :128]
+    columns = weight("small")
+    if seg_refs:
+        seg_ref, number_ref = seg_refs
+        number_ref[...] = columns[:, 128:256].astype(F32)
+        high, size = rows_of["sizes"][0], lax.axis_size("blk")
+        for other in range(size):
+            shard = lax.axis_index("dp") * size + (lax.axis_index("blk") ^ other)
+            numbers = number_ref[pl.ds(pl.multiple_of(shard * high, high), high), :]
+            for line in range(rows // 128):
+                seg_ref[other : other + 1, line * 128 : (line + 1) * 128] = numbers[line : line + 1]
+    columns = columns[:, :128]
     small = columns.astype(F32).T
     width = small.shape[1]
     small_ref[...] = small
@@ -184,14 +192,14 @@
 
 
 def attend_kernel(
-    weight, put, rows_of, z_ref, q_ref, own_ref, core_ref, chip_ref, both_ref, kvmem_ref, sega_ref, segb_ref, segc_ref, segd_ref, segq_ref, small_ref,
+    weight, put, rows_of, z_ref, q_ref, own_ref, core_ref, chip_ref, both_ref, kvmem_ref, segs_ref, segq_ref, small_ref,
     att_ref, lse_ref, pre_ref, one_ref, rq_ref, rkv_ref, wq_ref, part_ref,
     keys_ref, bound_ref,
 ):
     rows = core_ref.shape[0]
     width = z_ref.shape[1]
     place_keys(keys_ref, own_ref, core_ref, chip_ref, both_ref, kvmem_ref)
-    place_bounds(bound_ref, (sega_ref, segb_ref, segc_ref, segd_ref), segq_ref[...])
+    place_bounds(bound_ref, segs_ref, segq_ref[...])
 
     def pair(step, carry):
         lanes = pl.ds(pl.multiple_of(step * 128, 128), 128)
@@ -399,14 +407,14 @@
 
 def attend_back_kernel(
     share, weight, put, rows_of, z_ref, part_ref, corepart_ref, chippart_ref, bothpart_ref, memgrad_ref, seqjoint_ref, one_ref, pre_ref, att_ref, lse_ref,
-    q_ref, own_ref, core_ref, chip_ref, both_ref, kvmem_ref, sega_ref, segb_ref, segc_ref, segd_ref, segq_ref, small_ref,
+    q_ref, own_ref, core_ref, chip_ref, both_ref, kvmem_ref, segs_ref, segq_ref, small_ref,
     gsmall_ref, joint_ref, qgrad_ref, keep_ref, pass_ref, send_ref,
     keys_ref, bound_ref, out_ref, kvgrad_ref,
 ):
     rows, width = seqjoint_ref.shape
     full = att_ref.shape[0]
     place_keys(keys_ref, own_ref, core_ref, chip_ref, both_ref, kvmem_ref)
-    place_bounds(bound_ref, (sega_ref, segb_ref, segc_ref, segd_ref), segq_ref[...])
+    place_bounds(bound_ref, segs_ref, segq_ref[...])
     parts = (part_ref, corepart_ref, chippart_ref, bothpart_ref)
     q_low = in_pairs([part[...].astype(F32) for part in parts]).astype(LOW)
     put(4, dot_tn(one_ref[rows:, :].astype(LOW), q_low) * share)
@@ -627,9 +635,16 @@
     return lax.ppermute(value, "blk", [(source, source ^ bit) for source in range(size)])
 
 
+def fence(*arrays):
+    return list(lax.optimization_barrier(tuple(arrays)))
+
+
 def quartet(value):
-    chip = flipped(value, 2)
-    return [value, flipped(value, 1), chip, flipped(chip, 1)]
+    return both_chips(value, flipped(value, 2))
+
+
+def both_chips(own, chip):
+    return [own, flipped(own, 1), chip, flipped(chip, 1)]
 
 
 def bits_of(axis):
@@ -641,13 +656,77 @@
     return bit if axis == "blk" else bits_of("blk") + bit
 
 
+def pack_kernel(attn_ref, *refs):
+    inputs, out_ref, (lines_ref, wide_ref, *held, sems) = refs[:5], refs[5], refs[6:]
+    count, high, width = out_ref.shape
+    origins = (attn_ref.at[0, pl.ds(0, count - 1)],) + inputs
+    copies = [
+        pltpu.make_async_copy(origin, goal, sems.at[place])
+        for place, (origin, goal) in enumerate(zip(origins, [wide_ref] + held))
+    ]
+    for copy in copies:
+        copy.start()
+    lines_ref[...] = jnp.zeros(lines_ref.shape, F32)
+    for copy in copies:
+        copy.wait()
+    gain_ref, shift_ref, bias_ref, memory_ref, seg_ref = held
+    layers, rows, _ = gain_ref.shape
+    place = layers * rows
+    for layer in range(layers):
+        lines_ref[layer * rows : (layer + 1) * rows, 0:high] = gain_ref[layer]
+    rows = shift_ref.shape[0]
+    for line in range(rows):
+        for layer in range(layers):
+            goal = place + layer * rows + line
+            lines_ref[goal : goal + 1, 0:high] = shift_ref[line, layer : layer + 1]
+    place += layers * rows
+    layers, hidden = bias_ref.shape
+    for layer in range(layers):
+        for part in range(hidden // high):
+            lines_ref[place : place + 1, 0:high] = bias_ref[layer : layer + 1, part * high : (part + 1) * high]
+            place += 1
+    columns = lines_ref[...].T
+    lines_ref[...] = columns
+    lines_ref[0:high, place : place + MEM] = memory_ref[...]
+    out_ref[count - 1] = jnp.zeros((high, width), LOW)
+    out_ref[count - 1, :, 0:128] = lines_ref[0:high, :].astype(LOW)
+    lines_ref[...] = jnp.zeros(lines_ref.shape, F32)
+    for line in range(seg_ref.shape[1] // 128):
+        lines_ref[line : line + 1, :] = seg_ref[:, line * 128 : (line + 1) * 128].astype(F32)
+    out_ref[count - 1, :, 128:256] = lines_ref[0:high, :].astype(LOW)
+    out_ref[0 : count - 1] = wide_ref[...].astype(LOW)
+
+
+def unpack_kernel(slot, sums_ref, gain_ref, shift_ref, bias_ref, memory_ref, lines_ref):
+    high = sums_ref.shape[1]
+    lines_ref[...] = jnp.zeros(lines_ref.shape, F32)
+    lines_ref[0:high, :] = sums_ref[slot, :, 0:128]
+    lines = lines_ref[...].T
+    place = 0
+    for ref in (gain_ref, shift_ref):
+        layers, rows, _ = ref.shape
+        for layer in range(layers):
+            ref[layer] = lines[place : place + rows, 0:high]
+            place += rows
+    layers, hidden = bias_ref.shape
+    for layer in range(layers):
+        for part in range(hidden // high):
+            bias_ref[layer : layer + 1, part * high : (part + 1) * high] = lines[place : place + 1, 0:high]
+            place += 1
+    memory_ref[...] = lines[place : place + MEM, 0:high]
+
+
+def flat(stages):
+    return [bit for stage in stages for bit in (stage if isinstance(stage[0], tuple) else (stage,))]
+
+
 def swapped(value, stage):
+    if isinstance(stage[0], tuple):
+        mask = sum(1 << bit_place(bit) for bit in stage)
+        everyone = lax.axis_size("dp") * lax.axis_size("blk")
+        return lax.ppermute(value, ALL, [(source, source ^ mask) for source in range(everyone)])
     axis, bit = stage
     return lax.ppermute(value, axis, [(source, source ^ (1 << bit)) for source in range(lax.axis_size(axis))])
-
-
-def fence(*arrays):
-    return list(lax.optimization_barrier(tuple(arrays)))
 
 
 class Gathering:
@@ -689,23 +768,32 @@
 class Scattering:
     def __init__(self, arrays, stages):
         self.keeps = [keep for keep, _ in arrays]
-        self.sends = [send for _, send in arrays]
+        self.sends = [[send for _, send in arrays]]
         self.stages = list(stages)
         self.gots, self.result = None, None
 
     def begin(self):
-        stage = self.stages.pop(0)
-        self.gots = [swapped(send, stage) for send in self.sends]
+        bits = flat([self.stages.pop(0)])
+        self.gots = []
+        for piece, sends in enumerate(self.sends):
+            some = tuple(bit for place, bit in enumerate(bits) if (piece + 1) >> (len(bits) - 1 - place) & 1)
+            self.gots.extend(swapped(send, some if len(some) > 1 else some[0]) for send in sends)
 
     def end(self):
-        sums = [keep.astype(F32) + got.astype(F32) for keep, got in zip(self.keeps, self.gots)]
+        sums = []
+        for place, keep in enumerate(self.keeps):
+            value = keep.astype(F32)
+            for got in self.gots[place :: len(self.keeps)]:
+                value = value + got.astype(F32)
+            sums.append(value)
         self.gots = None
         if not self.stages:
             self.result = joined(sums)[0]
             return
-        half = sums[0].shape[0] // 2
-        self.keeps = [joined([value[:half] for value in sums]).astype(LOW)]
-        self.sends = [joined([value[half:] for value in sums]).astype(LOW)]
+        pieces = 2 ** len(flat(self.stages[:1]))
+        size = sums[0].shape[0] // pieces
+        parts = [joined([value[k * size : (k + 1) * size] for value in sums]).astype(LOW) for k in range(pieces)]
+        self.keeps, self.sends = parts[:1], [[part] for part in parts[1:]]
 
 
 class Background:
@@ -724,6 +812,13 @@
                 self.running.append(short)
                 if short != name:
                     self.staying.add(short)
+
+    def merge(self, name, other):
+        one, two = self.sums[name], self.sums[other]
+        if one.stages and one.stages == two.stages:
+            one.keeps = [joined(one.keeps + two.keeps)]
+            one.sends = [[joined(first + second)] for first, second in zip(one.sends, two.sends)]
+            two.stages = []
 
     def end(self, *others):
         ending = [self.sums[name] for name in self.running if name not in self.staying]
@@ -753,6 +848,8 @@
     starts = [sum(part.shape[0] for part in small[:k]) for k in range(5)]
     gain_rows, shift_rows = norm_gain.shape[1], norm_shift.shape[1]
     small = jnp.concatenate(small, 0).T.astype(LOW)
+    numbers = jnp.pad(segments.reshape(-1, 128).astype(LOW), ((0, rows - segments.size // 128), (0, 0)))
+    small = jnp.concatenate([jnp.pad(small, ((0, 0), (0, 128 - small.shape[1]))), numbers], 1)
     small = jnp.pad(small, ((0, 0), (0, width - small.shape[1])))[None]
 
     def rows_of(index):
@@ -764,8 +861,6 @@
             sizes=(rows, per, starts[2]),
         )
 
-    seg_low = segments.astype(LOW)
-
     def lowered(attn, up, down):
         up = up.astype(LOW).reshape(layers, rows, per, width).transpose(0, 2, 1, 3)
         return attn, up, down.astype(LOW).reshape(layers, per, rows, width)
@@ -790,14 +885,30 @@
         far, line = line_bits[:1], line_bits[1:]
         last = [core_bit]
         pause = [None]
+        inside, anywhere = pl.BlockSpec(memory_space=pltpu.VMEM), pl.BlockSpec(memory_space=pl.ANY)
+        packed_small = (norm_gain, norm_shift.transpose(1, 0, 2), ffn_bias, memory_init.T, segments)
+        first_shard = pl.pallas_call(
+            pack_kernel,
+            out_shape=jax.ShapeDtypeStruct((len(early) + 1, rows, width), LOW),
+            in_specs=[pl.BlockSpec(memory_space=pltpu.HBM)] * 6,
+            out_specs=inside,
+            scratch_shapes=[pltpu.VMEM((128, 128), F32), pltpu.VMEM((len(early), rows, width), F32)]
+            + [
+                pltpu.VMEM(part.shape, part.dtype)
+                for part in packed_small
+            ]
+            + [pltpu.SemaphoreType.DMA((6,))],
+            compiler_params=pltpu.CompilerParams(vmem_limit_bytes=3 * VMEM_LIMIT),
+            name="pack",
+        )(attn_weights, *packed_small)
         gathering = Gathering(
             [
-                (jnp.concatenate(picked(0, early) + [small]), far + line + chip_bits + near_bit + last, 0),
+                (first_shard, far + line + chip_bits + near_bit + last, 0),
                 (jnp.concatenate(picked(0, middle)), far + line + near_bit + chip_bits + last, 0),
             ]
         )
         gathering.begin()
-        attn_weights, ffn_in, ffn_out, seg_low = gathering.end(attn_weights, ffn_in, ffn_out, seg_low)
+        attn_weights, ffn_in, ffn_out = gathering.end(attn_weights, ffn_in, ffn_out)
         attn_low, up_low, down_low = lowered(attn_weights, ffn_in, ffn_out)
         gathering.groups += [
             (
@@ -812,19 +923,23 @@
             ),
             (
                 jnp.concatenate([up_low[0, 2:]] + picked(1, early)),
-                near_bit + chip_bits + pause + far + line + last,
+                far + chip_bits + pause + near_bit + line + last,
                 1,
             ),
             (jnp.concatenate(picked(1, middle)), far + line + chip_bits + near_bit + last, 4),
-            (jnp.concatenate(picked(1, late) + [up_low[1], down_low[1]]), far + line, 6),
+            (jnp.concatenate(picked(1, late) + [up_low[1]]), far + line, 6),
+            (down_low[1], near_bit + far + chip_bits + line + last, 6),
         ]
         gathering.held += [shard[None] for shard, _, _ in gathering.groups[2:]]
         gathering.begin()
-        seg_all = gathering.end(*quartet(seg_low))
+        gathering.end()
         for turn in range(2, 4):
             gathering.begin()
             gathering.end()
         found = gathering.begin()
+        arrived = fence(*[source[0][1] for source in (found[0], found[1])])
+        for number, got in enumerate(arrived):
+            found[number] = ((found[number][0][0], got), found[number][1])
         listed(found[0], 0, early + ("small",))
         listed(found[1], 0, middle)
     else:
@@ -857,7 +972,6 @@
     share = 1.0 / size
     me = lax.axis_index("blk")
     seg = segments[0].astype(F32)
-    seg_all = seg_all if direct else quartet(seg_low)
     seg_row = jnp.concatenate([seg, jnp.full((PAD,), -1.0, F32)])
     seg_queries = jnp.concatenate([seg_row, seg_row]).reshape(1, -1)
     every = size * length + PAD
@@ -865,32 +979,33 @@
     bound_scratch = pltpu.VMEM((every, 2 * full), F32)
     projected = [((full, width), LOW), ((length, 2 * width), LOW), ((PAD, 2 * width), LOW)]
 
-    smalls, z, q, own, kvmem = call(
+    smalls, z, q, own, kvmem, *numbers = call(
         first_kernel,
         "first",
         4,
         [tokens[0]],
-        [((128, width), F32), ((full, width), F32)] + projected,
+        [((128, width), F32), ((full, width), F32)] + projected + ([((size, length), F32)] if direct else []),
         attn(0, *early, "small"),
+        [pltpu.VMEM((width, 128), F32)] if direct else [],
         rows_of=rows_of(0),
     )
+    seg_all = numbers[0] if direct else jnp.concatenate(quartet(segments.astype(LOW))).astype(F32)
     kept = []
     for index in range(layers):
-        core = flipped(own, 1)
         chip = flipped(own, 2)
-        both = flipped(chip, 1)
         if direct:
-            core, chip, both = gathering.end(core, chip, both)
+            own, chip = gathering.end(own, chip)
             if index > 0:
-                gathering.split(6, len(late) + 2, [chip_bits + near_bit + [core_bit], near_bit + chip_bits + [core_bit]])
+                gathering.split(6, len(late), [chip_bits + near_bit + [core_bit], near_bit + chip_bits + [core_bit]])
             found = gathering.begin()
             if index > 0:
                 listed(found[5], index, middle)
+        _, core, _, both = both_chips(own, chip)
         att, lse, pre, first, rq, rkv, wq, part = call(
             attend_kernel,
             f"attend_{index}",
             13,
-            [z, q, own, core, chip, both, kvmem, *seg_all, seg_queries, smalls],
+            [z, q, own, core, chip, both, kvmem, seg_all, seg_queries, smalls],
             [
                 ((full, width), LOW), ((width // 128, 2 * full), F32), ((full, width), F32), ((full, width), F32),
                 ((PAD, width), LOW),
@@ -903,20 +1018,21 @@
         if direct and index > 0:
             (part,) = gathering.end(part)
             gathering.begin()
-        parts = quartet(part)
-        if direct and index > 0:
-            parts = gathering.end(*parts)
+        part_chip = flipped(part, 2)
+        if direct:
+            part, part_chip = gathering.end(part, part_chip)
             found = gathering.begin()
-            listed(found[6], 1, late + ups[:2])
-            listed(found[7], 1, ups[2:] + ("down",))
-        if direct and index == 0:
-            parts = gathering.end(*parts)
-            found = gathering.begin()
-            listed(found[2], 0, late + ups[:1])
-            listed(found[3], 0, ("down",) + ups[1:2])
-            listed(found[4], 0, ups[2:])
-            for key in early:
-                table[1, key] = (found[4], per - 2 + key, 1)
+            if index == 0:
+                listed(found[2], 0, late + ups[:1])
+                listed(found[3], 0, ("down",) + ups[1:2])
+                listed(found[4], 0, ups[2:])
+                for key in early:
+                    table[1, key] = (found[4], per - 2 + key, 1)
+            else:
+                listed(found[6], 1, late)
+                listed(found[7], 1, ("down",))
+                listed(found[8], 1, ups)
+        parts = both_chips(part, part_chip)
         last = index + 1 == layers
         results = call(
             functools.partial(finish_kernel, last),
@@ -960,7 +1076,8 @@
         "down_0": upward[:1] + y + upward[1:] + x,
         "first_1": y + upward + x,
         "second_1": x + upward[:1] + y + upward[1:],
-        "second_0": upward[:1] + y + x + upward[1:],
+        "second_0": y + x + [tuple(upward)],
+        "last": [tuple(y + x), tuple(upward)],
     }
 
     def order_of(name):
@@ -969,9 +1086,9 @@
     def group(name, keys, slots=None, into=None):
         if not direct:
             return (keys, None, per, None, None)
-        return (keys, Order(order_of(name)), per, slots, into)
-
-    group_keys = [ups, ("down",), (11, 8), (9, 10, 7, 5, 6), (4, 3, 0), (1, 2)]
+        return (keys, Order(flat(order_of(name))), per, slots, into)
+
+    group_keys = [ups + (11,), ("down", 8), (9, 10, 7, 5, 6), (4, 3, 0), (1, 2)]
     made = [None] * layers
     for index in reversed(range(layers)):
         k = kept[index]
@@ -983,7 +1100,7 @@
             if direct:
                 background.add(name, [arrays], [core_bit] + order_of(name))
 
-        grads_up, grads_down, grads_first, gbias, small_one, mem, seq, part = call(
+        grads_up, grads_down, gbias, small_one, mem, seq, part = call(
             functools.partial(feed_back_kernel, share),
             f"feed_back_{index}",
             11,
@@ -996,7 +1113,6 @@
             grads=[
                 group(names["up"], group_keys[0]),
                 group(names["down"], group_keys[1]),
-                group(names["first"], group_keys[2], 7),
             ],
             rows_of=rows_of(index),
         )
@@ -1008,8 +1124,9 @@
         if index + 1 < layers:
             start(*waiting)
         background.begin(*next(plan))
-        parts = background.end(*quartet(part))
+        part, chip = background.end(part, flipped(part, 2))
         background.begin(*next(plan))
+        parts = both_chips(part, chip)
         grads_read, small_two, mem, seq, part = call(
             functools.partial(read_back_kernel, share),
             f"read_back_{index}",
@@ -1018,28 +1135,29 @@
              k["first"], k["pre"], smalls],
             [((4, width), F32), ((PAD, width), F32), ((length, width), F32), ((PAD, width), LOW)],
             attn(index, 9, 10, 7, 5, 6),
-            grads=[group(names["first"], group_keys[3], 7, (grads_first, 2))],
+            grads=[group(names["first"], group_keys[2])],
             rows_of=rows_of(index),
         )
-        count_read = len(grads_read)
-        mem, seq, *rest = background.end(mem, seq, *grads_read, *quartet(part))
-        grads_read, parts = rest[:count_read], rest[count_read:]
+        mem, seq, part, chip, *grads_read = background.end(mem, seq, part, flipped(part, 2), *grads_read)
         start(names["first"], grads_read)
         background.begin(*next(plan))
+        parts = both_chips(part, chip)
         grads_attend, small_three, joint, qgrad, keep, pass_on, send = call(
             functools.partial(attend_back_kernel, share),
             f"attend_back_{index}",
             14,
             [k["z"], *parts, mem, seq, k["first"], k["pre"], k["att"], k["lse"], k["q"], k["own"], k["core"], k["chip"],
-             k["both"], k["kvmem"], *seg_all, seg_queries, smalls],
+             k["both"], k["kvmem"], seg_all, seg_queries, smalls],
             [((2, width), F32), ((full, width), F32), ((full, width), LOW),
              ((length, 2 * width), LOW), ((length + PAD, 2 * width), LOW), ((2 * length + PAD, 2 * width), LOW)],
             attn(index, 4, 3),
             [keys_scratch, bound_scratch, pltpu.VMEM((full, width), LOW), keys_scratch],
-            grads=[group(names["second"], group_keys[4], 5 if index > 0 else 3)],
+            grads=[group(names["second"], group_keys[3], 5 if index > 0 else 3)],
             rows_of=rows_of(index),
         )
         pass_on, send, *grads_attend = background.end(pass_on, send, *grads_attend)
+        if index == 0:
+            start(names["second"], grads_attend)
         background.begin(*next(plan))
         near = flipped(send, 1)
         theirs = (pass_on.astype(F32) + near[length:].astype(F32)).astype(LOW)
@@ -1059,32 +1177,35 @@
             grads=[
                 group(
                     end_name,
-                    group_keys[5] + (("small",) if tiny else ()),
+                    group_keys[4] + (("small",) if tiny else ()),
                     *((5, (grads_attend, 3)) if index > 0 else ()),
                 )
             ],
             rows_of=rows_of(index),
         )
         waiting = (end_name, grads_last)
-        made[index]["grads"] = (grads_up, grads_down, grads_first, grads_read, grads_attend, grads_last)
+        made[index]["grads"] = (grads_up, grads_down, grads_read, grads_attend, grads_last)
 
     mine = [{} for _ in range(layers)]
     if direct:
         start("last", grads_last)
-        start("second_0", grads_attend)
         background.begin(*next(plan))
         background.end()
         for moves in plan:
             background.begin(*moves)
             background.end()
+            background.merge("last", "second_0")
         for index in range(layers):
             wanted = [f"{name}_{index}" for name in ("up", "down", "first", "second")] + (["last"] if index == 0 else [])
+            if index == 0:
+                both = last_sums = background.sums["last"].result
+                background.sums["last"].result, background.sums["second_0"].result = both[:3], both[3:]
             results = [background.sums[name].result for name in wanted]
-            keys = [group_keys[0], group_keys[1], group_keys[2] + group_keys[3], group_keys[4]]
+            keys = list(group_keys[:4])
             if index > 0:
-                keys[3] = keys[3] + group_keys[5]
+                keys[3] = keys[3] + group_keys[4]
             else:
-                keys.append(group_keys[5] + ("small",))
+                keys.append(group_keys[4] + ("small",))
             for result, held in zip(results, keys):
                 place = 0
                 for key in held:
@@ -1112,18 +1233,34 @@
             mine[index][key] = result[place]
         for m in mine:
             m["down"] = jnp.concatenate([m["down", part] for part in range(per)])
-    back = mine[0]["small"].T
+    if direct:
+        small_grads = pl.pallas_call(
+            functools.partial(unpack_kernel, 2),
+            out_shape=[
+                jax.ShapeDtypeStruct(part.shape, F32) for part in (norm_gain, norm_shift, ffn_bias, memory_init)
+            ],
+            in_specs=[inside],
+            out_specs=[inside] * 4,
+            scratch_shapes=[pltpu.VMEM((128, 128), F32)],
+            compiler_params=pltpu.CompilerParams(vmem_limit_bytes=VMEM_LIMIT),
+            name="unpack",
+        )(last_sums)
+    else:
+        back = mine[0]["small"].T
+        small_grads = [back[starts[k] : starts[k + 1]].reshape(part.shape) for k, part in enumerate(
+            (norm_gain, norm_shift, ffn_bias, memory_init)
+        )]
     return (
         final[:length].astype(LOW)[None],
         final[length : length + MEM][None],
         grad[:length][None],
-        back[starts[3] : starts[4]],
+        small_grads[3],
         jnp.stack([jnp.stack([m[key] for key in range(count)]) for m in mine]),
         jnp.stack([jnp.concatenate([m["up", part] for part in range(per)], -1) for m in mine]),
         jnp.stack([m["down"] for m in mine]),
-        back[starts[2] : starts[3]].reshape(ffn_bias.shape),
-        back[starts[0] : starts[1]].reshape(norm_gain.shape),
-        back[starts[1] : starts[2]].reshape(norm_shift.shape),
+        small_grads[2],
+        small_grads[0],
+        small_grads[1],
     )
 
 

time: 424 us -> 391 us (0.922)
  waiting for transfers between devices: 205 us -> 159 us
  starting transfers between devices: 90.8 us -> 109 us
  other arithmetic: 16.2 us -> 11.9 us
    ppermute x31 -> x28, waiting for transfers between devices: 68.3 us -> 41.2 us  [flipped(): lax.ppermute(value, 'blk', [(source, source ^ bit) for source in range(si...]
    ppermute x83 -> x86, waiting for transfers between devices: 136 us -> 118 us  [swapped(): lax.ppermute(value, axis, [(source, source ^ 1 << bit) for source in rang...]
    ppermute x83 -> x86, starting transfers between devices: 76.4 us -> 91 us  [swapped(): lax.ppermute(value, axis, [(source, source ^ 1 << bit) for source in rang...]
    another operation x42 -> x35, other arithmetic: 11.6 us -> 7.43 us
    ppermute x31 -> x28, starting transfers between devices: 14.5 us -> 15.7 us  [flipped(): lax.ppermute(value, 'blk', [(source, source ^ bit) for source in range(si...]
  transfers between devices with their start and end apart: 114 -> 116, of which waited for: 59 -> 48; matrix products, arithmetic and copies ran while one was open for 3% -> 3% of each run, Pallas kernels for 18% -> 20%
where the time goes in v5:
time: 391 us; the launch traced here: 383 us
  waiting for transfers between devices  159 us (41%)
  starting transfers between devices  109 us (28%)
  Pallas kernels  95.1 us (24%)
  other arithmetic  11.9 us (3%)
  local copies, waits for them, and re-layouts  5.24 us (1%)
    ppermute x86, waiting for transfers between devices, swapped(): lax.ppermute(value, axis, [(source, source ^ 1 << bit) for source in rang...  118 us
    pallas_call x13, Pallas kernels, call(): pl.pallas_call(body, out_shape=shapes + [jax.ShapeDtypeStruct(shape, kind...  92.6 us
    ppermute x86, starting transfers between devices, swapped(): lax.ppermute(value, axis, [(source, source ^ 1 << bit) for source in rang...  91 us
    ppermute x28, waiting for transfers between devices, flipped(): lax.ppermute(value, 'blk', [(source, source ^ bit) for source in range(si...  41.2 us
    ppermute x28, starting transfers between devices, flipped(): lax.ppermute(value, 'blk', [(source, source ^ bit) for source in range(si...  15.7 us
  transfers between devices with their start and end apart: 116, of which 48 were waited for; matrix products, arithmetic and copies ran while one was open for 3% of the time, Pallas kernels for 20%

profile of v5, /device:TPU:0, one launch (start us, length us, event | category | flops | bytes accessed | tf_op | source)
XLA Modules:
  0.0 383.3 jit_solution(10233282423633945515)
XLA Ops:
  0.7 1.8 pack.1
  2.5 4.1 %collective-permute-start = (bf16[1,4,16,512]{3,2,1,0:T(8,128)(2,1)}, bf16[1,4,16,512]{3,2,1,0:T(8,128)(2,1)S(1)}, u32[]{:S(2)}, u32[]{:S(2)}) collective-permute-start(bf16[1,4,16,512]{3,2,1,0:T(8,128)(2,1)} %bitcast.256), channel_id=1, source_target_pairs={{0,16},{4,20},{8,24},{12,28},{16,0},{20,4},{24,8},{28,12},{1,17},{... | collective-permute-start | bytes 196616 | tf_op jit(solution)/shard_map/ppermute | solution.py:729
  6.9 3.6 collective-permute-done
  10.5 3.5 collective-permute-done.1
  18.2 1.8 collective-permute-start.5
  20.9 2.8 collective-permute-done.5
  24.5 2.0 collective-permute-start.6
  31.8 8.9 %collective-permute-done.8 = bf16[1,5,16,512]{3,2,1,0:T(8,128)(2,1)S(1)} collective-permute-done((bf16[1,5,16,512]{3,2,1,0:T(8,128)(2,1)S(1)}, bf16[1,5,16,512]{3,2,1,0:T(8,128)(2,1)S(1)}, u32[]{:S(2)}, u32[]{:S(2)}) %collective-permute-start.8) | collective-permute-done | bytes 81952 | tf_op jit(solution)/shard_map/ppermute | solution.py:729
  42.5 2.1 collective-permute-start.13
  44.6 8.9 %collective-permute-done.13 = bf16[2,5,16,512]{3,2,1,0:T(8,128)(2,1)S(1)} collective-permute-done((bf16[2,5,16,512]{3,2,1,0:T(8,128)(2,1)S(1)}, bf16[2,5,16,512]{3,2,1,0:T(8,128)(2,1)S(1)}, u32[]{:S(2)}, u32[]{:S(2)}) %collective-permute-start.13) | collective-permute-done | bytes 163872 | tf_op jit(solution)/shard_map/ppermute | solution.py:729
  59.9 2.5 first.1
  66.4 8.4 %collective-permute-done.17 = bf16[4,5,16,512]{3,2,1,0:T(8,128)(2,1)S(1)} collective-permute-done((bf16[4,5,16,512]{3,2,1,0:T(8,128)(2,1)S(1)}, bf16[4,5,16,512]{3,2,1,0:T(8,128)(2,1)S(1)}, u32[]{:S(2)}, u32[]{:S(2)}) %collective-permute-start.17) | collective-permute-done | bytes 327712 | tf_op jit(solution)/shard_map/ppermute | solution.py:729
  74.8 1.7 collective-permute-done.20.refs_4_.refs_14_
  81.1 9.1 %attend_0.1 = (bf16[288,512]{1,0:T(8,128)(2,1)S(1)}, f32[4,576]{1,0:T(4,128)S(1)}, f32[288,512]{1,0:T(8,128)S(1)}, f32[288,512]{1,0:T(8,128)S(1)}, bf16[32,512]{...) custom-call(f32[288,512]{1,0:T(8,128)S(1)} %get-tuple-element.265.refs_0_,, ...), custom_call_target="tpu_custom_call" | custom-call | flops 4289999872 | tf_op jit(solution)/shard_map/attend_0/pallas_call | solution.py:616
  91.3 7.3 %collective-permute-done.26 = bf16[2,5,16,512]{3,2,1,0:T(8,128)(2,1)S(1)} collective-permute-done((bf16[2,5,16,512]{3,2,1,0:T(8,128)(2,1)S(1)}, bf16[2,5,16,512]{3,2,1,0:T(8,128)(2,1)S(1)}, u32[]{:S(2)}, u32[]{:S(2)}) %collective-permute-start.26) | collective-permute-done | bytes 163872 | tf_op jit(solution)/shard_map/ppermute | solution.py:729
  100.2 5.5 %collective-permute-done.28.refs_2_ = f32[32,640]{1,0:T(8,128)S(1)} collective-permute-done((f32[32,640]{1,0:T(8,128)S(1)}, f32[32,640]{1,0:T(8,128)S(1)}, u32[]{:S(2)}, u32[]{:S(2)}) %collective-permute-start.28) | collective-permute-done | bytes 81952 | tf_op jit(solution)/shard_map/ppermute | solution.py:635
  107.2 2.5 collective-permute-start.34
  110.3 7.1 %finish_0.1 = (f32[288,512]{1,0:T(8,128)S(1)}, bf16[288,512]{1,0:T(8,128)(2,1)S(1)}, bf16[256,1024]{1,0:T(8,128)(2,1)S(1)}, bf16[32,1024]{1,0:T(8,128)(2,1)S(1)}...) custom-call(f32[288,512]{1,0:T(8,128)S(1)} %get-tuple-element.276.re, ...), custom_call_target="tpu_custom_call" | custom-call | flops 3300000000 | tf_op jit(solution)/shard_map/finish_0/pallas_call | solution.py:616
  119.4 1.8 collective-permute-start.37
  122.0 6.5 %collective-permute-done.38 = bf16[2,4,16,512]{3,2,1,0:T(8,128)(2,1)S(1)} collective-permute-done((bf16[2,4,16,512]{3,2,1,0:T(8,128)(2,1)S(1)}, bf16[2,4,16,512]{3,2,1,0:T(8,128)(2,1)S(1)}, u32[]{:S(2)}, u32[]{:S(2)}) %collective-permute-start.38) | collective-permute-done | bytes 131104 | tf_op jit(solution)/shard_map/ppermute | solution.py:729
  129.3 2.7 collective-permute-done.39.refs_4_.refs_14_
  134.7 1.8 collective-permute-start.44
  138.9 9.1 %attend_1.1 = (bf16[288,512]{1,0:T(8,128)(2,1)S(1)}, f32[4,576]{1,0:T(4,128)S(1)}, f32[288,512]{1,0:T(8,128)S(1)}, f32[288,512]{1,0:T(8,128)S(1)}, bf16[32,512]{...) custom-call(f32[288,512]{1,0:T(8,128)S(1)} %get-tuple-element.288.refs_0_,, ...), custom_call_target="tpu_custom_call" | custom-call | flops 4289999872 | tf_op jit(solution)/shard_map/attend_1/pallas_call | solution.py:616
  150.3 1.8 collective-permute-start.47
  152.6 1.8 collective-permute-start.49
  154.4 12.5 %collective-permute-done.49.refs_3_ = f32[32,640]{1,0:T(8,128)S(1)} collective-permute-done((f32[32,640]{1,0:T(8,128)S(1)}, f32[32,640]{1,0:T(8,128)S(1)}, u32[]{:S(2)}, u32[]{:S(2)}) %collective-permute-start.49) | collective-permute-done | bytes 81952 | tf_op jit(solution)/shard_map/ppermute | solution.py:635
  168.6 4.3 %collective-permute-done.50.refs_2_ = f32[32,640]{1,0:T(8,128)S(1)} collective-permute-done((f32[32,640]{1,0:T(8,128)S(1)}, f32[32,640]{1,0:T(8,128)S(1)}, u32[]{:S(2)}, u32[]{:S(2)}) %collective-permute-start.50) | collective-permute-done | bytes 81952 | tf_op jit(solution)/shard_map/ppermute | solution.py:635
  173.1 6.0 %finish_1.1 = (f32[288,512]{1,0:T(8,128)S(1)}, f32[32,512]{1,0:T(8,128)S(1)}, f32[32,512]{1,0:T(8,128)S(1)}, f32[32,512]{1,0:T(8,128)S(1)}, f32[288,512]{1,0:T(8...) custom-call(f32[288,512]{1,0:T(8,128)S(1)} %get-tuple-element.302.re, ...), custom_call_target="tpu_custom_call" | custom-call | flops 3300000000 | tf_op jit(solution)/shard_map/finish_1/pallas_call | solution.py:616
  179.1 11.8 %feed_back_1.1 = (bf16[16,5,16,512]{3,2,1,0:T(8,128)(2,1)S(1)}, bf16[16,5,16,512]{3,2,1,0:T(8,128)(2,1)S(1)}, bf16[16,5,16,512]{3,2,1,0:T(8,128)(2,1)S(1)}, bf16...) custom-call(f32[288,512]{1,0:T(8,128)S(1)} %fusion.2.refs_0_, ...), custom_call_target="tpu_custom_call" | custom-call | flops 3630000128 | tf_op jit(solution)/shard_map/feed_back_1/pallas_call | solution.py:616
  191.8 3.9 %collective-permute-done.57.refs_2_ = bf16[64,512]{1,0:T(8,128)(2,1)S(1)} collective-permute-done((bf16[64,512]{1,0:T(8,128)(2,1)S(1)}, bf16[64,512]{1,0:T(8,128)(2,1)S(1)}, u32[]{:S(2)}, u32[]{:S(2)}) %collective-permute-start.57) | collective-permute-done | bytes 65568 | tf_op jit(solution)/shard_map/ppermute | solution.py:635
  199.4 4.1 %read_back_1.1 = (bf16[16,5,16,512]{3,2,1,0:T(8,128)(2,1)S(1)}, bf16[16,5,16,512]{3,2,1,0:T(8,128)(2,1)S(1)}, f32[4,512]{1,0:T(4,128)S(1)}, f32[32,512]{1,0:T(8,...) custom-call(bf16[64,512]{1,0:T(8,128)(2,1)S(1)} %get-tuple-element.336.refs_0_, ...), custom_call_target="tpu_custom_call" | custom-call | flops 1320000000 | tf_op jit(solution)/shard_map/read_back_1/pallas_call | solution.py:616
  203.9 3.6 collective-permute-done.62.refs_3_
  207.4 5.8 %collective-permute-done.58 = bf16[8,5,16,512]{3,2,1,0:T(8,128)(2,1)S(1)} collective-permute-done((bf16[8,5,16,512]{3,2,1,0:T(8,128)(2,1)S(1)}, bf16[8,5,16,512]{3,2,1,0:T(8,128)(2,1)S(1)}, u32[]{:S(2)}, u32[]{:S(2)}) %collective-permute-start.58) | collective-permute-done | bytes 655392 | tf_op jit(solution)/shard_map/ppermute | solution.py:729
  217.3 11.1 %attend_back_1.1 = (bf16[16,5,16,512]{3,2,1,0:T(8,128)(2,1)S(1)}, bf16[16,5,16,512]{3,2,1,0:T(8,128)(2,1)S(1)}, f32[2,512]{1,0:T(2,128)S(1)}, f32[288,512]{1,0:T...) custom-call(f32[288,512]{1,0:T(8,128)S(1)} %get-tuple-element.288.re, ...), custom_call_target="tpu_custom_call" | custom-call | flops 4620000256 | tf_op jit(solution)/shard_map/attend_back_1/pallas_call | solution.py:616
  232.1 1.8 collective-permute-start.68
  235.3 11.9 %collective-permute-done.68 = bf16[2,5,16,512]{3,2,1,0:T(8,128)(2,1)S(1)} collective-permute-done((bf16[2,5,16,512]{3,2,1,0:T(8,128)(2,1)S(1)}, bf16[2,5,16,512]{3,2,1,0:T(8,128)(2,1)S(1)}, u32[]{:S(2)}, u32[]{:S(2)}) %collective-permute-start.68) | collective-permute-done | bytes 163872 | tf_op jit(solution)/shard_map/ppermute | solution.py:729
  247.1 2.4 collective-permute-done.69
  249.6 1.8 collective-permute-start.73
  252.2 2.4 input_back_1.1
  254.6 11.6 %feed_back_0.1 = (bf16[16,5,16,512]{3,2,1,0:T(8,128)(2,1)S(1)}, bf16[16,5,16,512]{3,2,1,0:T(8,128)(2,1)S(1)}, bf16[16,5,16,512]{3,2,1,0:T(8,128)(2,1)S(1)}, bf16...) custom-call(f32[288,512]{1,0:T(8,128)S(1)} %get-tuple-element.381.re, ...), custom_call_target="tpu_custom_call" | custom-call | flops 3630000128 | tf_op jit(solution)/shard_map/feed_back_0/pallas_call | solution.py:616
  268.5 2.8 collective-permute-done.79.refs_2_
  274.1 2.1 collective-permute-start.81
  277.5 4.1 %read_back_0.1 = (bf16[16,5,16,512]{3,2,1,0:T(8,128)(2,1)S(1)}, bf16[16,5,16,512]{3,2,1,0:T(8,128)(2,1)S(1)}, f32[4,512]{1,0:T(4,128)S(1)}, f32[32,512]{1,0:T(8,...) custom-call(bf16[64,512]{1,0:T(8,128)(2,1)S(1)} %get-tuple-element.402.refs_0_, ...), custom_call_target="tpu_custom_call" | custom-call | flops 1320000000 | tf_op jit(solution)/shard_map/read_back_0/pallas_call | solution.py:616
  281.6 1.8 collective-permute-start.84
  285.6 3.3 collective-permute-done.80
  289.0 2.1 collective-permute-done.81
  291.8 1.8 collective-permute-start.90
  294.4 1.8 collective-permute-start.87
  297.1 11.2 %attend_back_0.1 = (bf16[16,3,16,512]{3,2,1,0:T(8,128)(2,1)S(1)}, bf16[16,3,16,512]{3,2,1,0:T(8,128)(2,1)S(1)}, f32[2,512]{1,0:T(2,128)S(1)}, f32[288,512]{1,0:T...) custom-call(f32[288,512]{1,0:T(8,128)S(1)} %get-tuple-element.265.re, ...), custom_call_target="tpu_custom_call" | custom-call | flops 4620000256 | tf_op jit(solution)/shard_map/attend_back_0/pallas_call | solution.py:616
  309.4 2.0 collective-permute-start.92
  316.1 4.5 %collective-permute-done.92 = bf16[2,5,16,512]{3,2,1,0:T(8,128)(2,1)S(1)} collective-permute-done((bf16[2,5,16,512]{3,2,1,0:T(8,128)(2,1)S(1)}, bf16[2,5,16,512]{3,2,1,0:T(8,128)(2,1)S(1)}, u32[]{:S(2)}, u32[]{:S(2)}) %collective-permute-start.92) | collective-permute-done | bytes 163872 | tf_op jit(solution)/shard_map/ppermute | solution.py:729
  320.6 10.3 %collective-permute-done.93 = bf16[2,5,16,512]{3,2,1,0:T(8,128)(2,1)S(1)} collective-permute-done((bf16[2,5,16,512]{3,2,1,0:T(8,128)(2,1)S(1)}, bf16[2,5,16,512]{3,2,1,0:T(8,128)(2,1)S(1)}, u32[]{:S(2)}, u32[]{:S(2)}) %collective-permute-start.93) | collective-permute-done | bytes 163872 | tf_op jit(solution)/shard_map/ppermute | solution.py:729
  334.2 2.5 input_back_0.1
  336.9 2.1 collective-permute-start.100
  339.3 2.8 collective-permute-done.100
  342.1 1.7 collective-permute-start.104
  344.7 1.9 collective-permute-done.104
  347.4 1.8 collective-permute-start.105
  349.2 1.7 collective-permute-start.106
  354.8 3.4 collective-permute-done.110
  364.0 2.8 collective-permute-done.109
  367.1 3.6 collective-permute-start.112
  372.4 2.1 collective-permute-start.115
  374.7 5.1 %collective-permute-done.115 = bf16[1,5,16,512]{3,2,1,0:T(8,128)(2,1)S(1)} collective-permute-done((bf16[1,5,16,512]{3,2,1,0:T(8,128)(2,1)S(1)}, bf16[1,5,16,512]{3,2,1,0:T(8,128)(2,1)S(1)}, u32[]{:S(2)}, u32[]{:S(2)}) %collective-permute-start.115) | collective-permute-done | bytes 81952 | tf_op jit(solution)/shard_map/ppermute | solution.py:729
  (436 shorter events, 97.1 us)
Async XLA Ops:
  24.5 16.2 %collective-permute-start.6 = (bf16[4,4,16,512]{3,2,1,0:T(8,128)(2,1)S(1)}, bf16[4,4,16,512]{3,2,1,0:T(8,128)(2,1)S(1)}, u32[]{:S(2)}, u32[]{:S(2)}) collective-permute-start(bf16[4,4,16,512]{3,2,1,0:T(8,128)(2,1)S(1)} %pad_maximum_fusion.18), channel_id=1, source_target_pairs={{0,2},{1,3},{2,0},{3,1},{4,6},{5,7},{6,4},{7,5},{8,10},{9,11},{10,... | collective-permute-start | bytes 786440 | tf_op jit(solution)/shard_map/ppermute | solution.py:729
  26.6 14.1 %collective-permute-start.7 = (bf16[4,5,16,512]{3,2,1,0:T(8,128)(2,1)S(1)}, bf16[4,5,16,512]{3,2,1,0:T(8,128)(2,1)S(1)}, u32[]{:S(2)}, u32[]{:S(2)}) collective-permute-start(bf16[4,5,16,512]{3,2,1,0:T(8,128)(2,1)S(1)} %pad_maximum_fusion.13), channel_id=1, source_target_pairs={{0,4},{4,0},{8,12},{12,8},{16,20},{20,16},{24,28},{28,24},{1,5},{5... | collective-permute-start | bytes 983048 | tf_op jit(solution)/shard_map/ppermute | solution.py:729
  28.2 12.5 %collective-permute-start.9 = (bf16[2,5,16,512]{3,2,1,0:T(8,128)(2,1)S(1)}, bf16[2,5,16,512]{3,2,1,0:T(8,128)(2,1)S(1)}, u32[]{:S(2)}, u32[]{:S(2)}) collective-permute-start(bf16[2,5,16,512]{3,2,1,0:T(8,128)(2,1)S(1)} %pad_maximum_fusion.24), channel_id=1, source_target_pairs={{0,16},{4,20},{8,24},{12,28},{16,0},{20,4},{24,8},{28,12},{1,17},{... | collective-permute-start | bytes 491528 | tf_op jit(solution)/shard_map/ppermute | solution.py:729
  29.8 10.9 %collective-permute-start.10 = (bf16[2,5,16,512]{3,2,1,0:T(8,128)(2,1)S(1)}, bf16[2,5,16,512]{3,2,1,0:T(8,128)(2,1)S(1)}, u32[]{:S(2)}, u32[]{:S(2)}) collective-permute-start(bf16[2,5,16,512]{3,2,1,0:T(8,128)(2,1)S(1)} %pad_maximum_fusion.25), channel_id=1, source_target_pairs={{0,2},{1,3},{2,0},{3,1},{4,6},{5,7},{6,4},{7,5},{8,10},{9,11},{10,... | collective-permute-start | bytes 491528 | tf_op jit(solution)/shard_map/ppermute | solution.py:729
  30.4 10.3 %collective-permute-start.8 = (bf16[1,5,16,512]{3,2,1,0:T(8,128)(2,1)S(1)}, bf16[1,5,16,512]{3,2,1,0:T(8,128)(2,1)S(1)}, u32[]{:S(2)}, u32[]{:S(2)}) collective-permute-start(bf16[1,5,16,512]{3,2,1,0:T(8,128)(2,1)S(1)} %bitcast.268), channel_id=1, source_target_pairs={{0,16},{4,20},{8,24},{12,28},{16,0},{20,4},{24,8},{28,12},{1,17},{... | collective-permute-start | bytes 245768 | tf_op jit(solution)/shard_map/ppermute | solution.py:729
  40.8 14.5 %collective-permute-start.12 = (bf16[8,5,16,512]{3,2,1,0:T(8,128)(2,1)S(1)}, bf16[8,5,16,512]{3,2,1,0:T(8,128)(2,1)S(1)}, u32[]{:S(2)}, u32[]{:S(2)}) collective-permute-start(bf16[8,5,16,512]{3,2,1,0:T(8,128)(2,1)S(1)} %pad_maximum_fusion.3), channel_id=1, source_target_pairs={{0,2},{1,3},{2,0},{3,1},{4,6},{5,7},{6,4},{7,5},{8,10},{9,11},{10,... | collective-permute-start | bytes 1966088 | tf_op jit(solution)/shard_map/ppermute | solution.py:729
  41.8 12.0 %collective-permute-start.11 = (bf16[8,4,16,512]{3,2,1,0:T(8,128)(2,1)S(1)}, bf16[8,4,16,512]{3,2,1,0:T(8,128)(2,1)S(1)}, u32[]{:S(2)}, u32[]{:S(2)}) collective-permute-start(bf16[8,4,16,512]{3,2,1,0:T(8,128)(2,1)S(1)} %pad_maximum_fusion.8), channel_id=1, source_target_pairs={{0,4},{4,0},{8,12},{12,8},{16,20},{20,16},{24,28},{28,24},{1,5},{5... | collective-permute-start | bytes 1572872 | tf_op jit(solution)/shard_map/ppermute | solution.py:729
  42.4 11.1 %collective-permute-start.14 = (bf16[4,5,16,512]{3,2,1,0:T(8,128)(2,1)S(1)}, bf16[4,5,16,512]{3,2,1,0:T(8,128)(2,1)S(1)}, u32[]{:S(2)}, u32[]{:S(2)}) collective-permute-start(bf16[4,5,16,512]{3,2,1,0:T(8,128)(2,1)S(1)} %pad_maximum_fusion.14), channel_id=1, source_target_pairs={{0,8},{4,12},{8,0},{12,4},{16,24},{20,28},{24,16},{28,20},{1,9},{5... | collective-permute-start | bytes 983048 | tf_op jit(solution)/shard_map/ppermute | solution.py:729
  42.5 11.0 %collective-permute-start.13 = (bf16[2,5,16,512]{3,2,1,0:T(8,128)(2,1)S(1)}, bf16[2,5,16,512]{3,2,1,0:T(8,128)(2,1)S(1)}, u32[]{:S(2)}, u32[]{:S(2)}) collective-permute-start(bf16[2,5,16,512]{3,2,1,0:T(8,128)(2,1)S(1)} %pad_maximum_fusion.26), channel_id=1, source_target_pairs={{0,8},{4,12},{8,0},{12,4},{16,24},{20,28},{24,16},{28,20},{1,9},{5... | collective-permute-start | bytes 491528 | tf_op jit(solution)/shard_map/ppermute | solution.py:729
  56.1 10.2 %collective-permute-start.19 = (bf16[1,5,16,512]{3,2,1,0:T(8,128)(2,1)S(1)}, bf16[1,5,16,512]{3,2,1,0:T(8,128)(2,1)S(1)}, u32[]{:S(2)}, u32[]{:S(2)}) collective-permute-start(bf16[1,5,16,512]{3,2,1,0:T(8,128)(2,1)S(1)} %bitcast.260), channel_id=1, source_target_pairs={{0,16},{4,20},{8,24},{12,28},{16,0},{20,4},{24,8},{28,12},{1,17},{... | collective-permute-start | bytes 245768 | tf_op jit(solution)/shard_map/ppermute | solution.py:729
  56.7 9.7 %collective-permute-start.18 = (bf16[4,5,16,512]{3,2,1,0:T(8,128)(2,1)S(1)}, bf16[4,5,16,512]{3,2,1,0:T(8,128)(2,1)S(1)}, u32[]{:S(2)}, u32[]{:S(2)}) collective-permute-start(bf16[4,5,16,512]{3,2,1,0:T(8,128)(2,1)S(1)} %pad_maximum_fusion.16), channel_id=1, source_target_pairs={{0,4},{4,0},{8,12},{12,8},{16,20},{20,16},{24,28},{28,24},{1,5},{5... | collective-permute-start | bytes 983048 | tf_op jit(solution)/shard_map/ppermute | solution.py:729
  62.5 14.0 %collective-permute-start.20 = (bf16[256,1024]{1,0:T(8,128)(2,1)S(1)}, bf16[256,1024]{1,0:T(8,128)(2,1)S(1)}, u32[]{:S(2)}, u32[]{:S(2)}) collective-permute-start(bf16[256,1024]{1,0:T(8,128)(2,1)S(1)} %get-tuple-element.270.refs_2_.refs_12_), channel_id=1, source_target_pairs={{0,2},{1,3},{2,0},{3,1},{4,6},{5,7},{6,4},{7,5},{8,10},{9,11},{10,... | collective-permute-start | bytes 1572872 | tf_op jit(solution)/shard_map/ppermute | solution.py:635
  64.1 10.7 %collective-permute-start.17 = (bf16[4,5,16,512]{3,2,1,0:T(8,128)(2,1)S(1)}, bf16[4,5,16,512]{3,2,1,0:T(8,128)(2,1)S(1)}, u32[]{:S(2)}, u32[]{:S(2)}) collective-permute-start(bf16[4,5,16,512]{3,2,1,0:T(8,128)(2,1)S(1)} %pad_maximum_fusion.15), channel_id=1, source_target_pairs={{0,4},{4,0},{8,12},{12,8},{16,20},{20,16},{24,28},{28,24},{1,5},{5... | collective-permute-start | bytes 983048 | tf_op jit(solution)/shard_map/ppermute | solution.py:729
  64.8 26.5 %collective-permute-start.24 = (bf16[8,5,16,512]{3,2,1,0:T(8,128)(2,1)S(1)}, bf16[8,5,16,512]{3,2,1,0:T(8,128)(2,1)S(1)}, u32[]{:S(2)}, u32[]{:S(2)}) collective-permute-start(bf16[8,5,16,512]{3,2,1,0:T(8,128)(2,1)S(1)} %pad_maximum_fusion.5), channel_id=1, source_target_pairs={{0,4},{4,0},{8,12},{12,8},{16,20},{20,16},{24,28},{28,24},{1,5},{5... | collective-permute-start | bytes 1966088 | tf_op jit(solution)/shard_map/ppermute | solution.py:729
  77.1 21.6 %collective-permute-start.23 = (bf16[8,5,16,512]{3,2,1,0:T(8,128)(2,1)S(1)}, bf16[8,5,16,512]{3,2,1,0:T(8,128)(2,1)S(1)}, u32[]{:S(2)}, u32[]{:S(2)}) collective-permute-start(bf16[8,5,16,512]{3,2,1,0:T(8,128)(2,1)S(1)} %pad_maximum_fusion.4), channel_id=1, source_target_pairs={{0,2},{1,3},{2,0},{3,1},{4,6},{5,7},{6,4},{7,5},{8,10},{9,11},{10,... | collective-permute-start | bytes 1966088 | tf_op jit(solution)/shard_map/ppermute | solution.py:729
  78.7 19.9 %collective-permute-start.25 = (bf16[8,5,16,512]{3,2,1,0:T(8,128)(2,1)S(1)}, bf16[8,5,16,512]{3,2,1,0:T(8,128)(2,1)S(1)}, u32[]{:S(2)}, u32[]{:S(2)}) collective-permute-start(bf16[8,5,16,512]{3,2,1,0:T(8,128)(2,1)S(1)} %pad_maximum_fusion.6), channel_id=1, source_target_pairs={{0,8},{4,12},{8,0},{12,4},{16,24},{20,28},{24,16},{28,20},{1,9},{5... | collective-permute-start | bytes 1966088 | tf_op jit(solution)/shard_map/ppermute | solution.py:729
  80.3 18.4 %collective-permute-start.26 = (bf16[2,5,16,512]{3,2,1,0:T(8,128)(2,1)S(1)}, bf16[2,5,16,512]{3,2,1,0:T(8,128)(2,1)S(1)}, u32[]{:S(2)}, u32[]{:S(2)}) collective-permute-start(bf16[2,5,16,512]{3,2,1,0:T(8,128)(2,1)S(1)} %pad_maximum_fusion.27), channel_id=1, source_target_pairs={{0,8},{4,12},{8,0},{12,4},{16,24},{20,28},{24,16},{28,20},{1,9},{5... | collective-permute-start | bytes 491528 | tf_op jit(solution)/shard_map/ppermute | solution.py:729
  98.7 11.0 %collective-permute-start.30 = (bf16[16,5,16,512]{3,2,1,0:T(8,128)(2,1)S(1)}, bf16[16,5,16,512]{3,2,1,0:T(8,128)(2,1)S(1)}, u32[]{:S(2)}, u32[]{:S(2)}) collective-permute-start(bf16[16,5,16,512]{3,2,1,0:T(8,128)(2,1)S(1)} %constant_dynamic-update-slice_fusion.25.refs_7_.refs_9_.refs_15_), channel_id=1, source_target_pairs={{0,1},{1,0},{2,3},{3,2},{4,5},{5,4},{6,7},{7,6},{8,9},{9,8},{10,11... | collective-permute-start | bytes 3932168 | tf_op jit(solution)/shard_map/ppermute | solution.py:729
  98.9 11.4 %collective-permute-start.31 = (bf16[16,5,16,512]{3,2,1,0:T(8,128)(2,1)S(1)}, bf16[16,5,16,512]{3,2,1,0:T(8,128)(2,1)S(1)}, u32[]{:S(2)}, u32[]{:S(2)}) collective-permute-start(bf16[16,5,16,512]{3,2,1,0:T(8,128)(2,1)S(1)} %constant_dynamic-update-slice_fusion.30.refs_9_.refs_11_), channel_id=1, source_target_pairs={{0,1},{1,0},{2,3},{3,2},{4,5},{5,4},{6,7},{7,6},{8,9},{9,8},{10,11... | collective-permute-start | bytes 3932168 | tf_op jit(solution)/shard_map/ppermute | solution.py:729
  99.5 10.8 %collective-permute-start.32 = (bf16[16,5,16,512]{3,2,1,0:T(8,128)(2,1)S(1)}, bf16[16,5,16,512]{3,2,1,0:T(8,128)(2,1)S(1)}, u32[]{:S(2)}, u32[]{:S(2)}) collective-permute-start(bf16[16,5,16,512]{3,2,1,0:T(8,128)(2,1)S(1)} %constant_dynamic-update-slice_fusion.35.refs_11_.refs_7_.refs_13_), channel_id=1, source_target_pairs={{0,1},{1,0},{2,3},{3,2},{4,5},{5,4},{6,7},{7,6},{8,9},{9,8},{10,11... | collective-permute-start | bytes 3932168 | tf_op jit(solution)/shard_map/ppermute | solution.py:729
  105.7 11.7 %collective-permute-start.33 = (bf16[4,5,16,512]{3,2,1,0:T(8,128)(2,1)S(1)}, bf16[4,5,16,512]{3,2,1,0:T(8,128)(2,1)S(1)}, u32[]{:S(2)}, u32[]{:S(2)}) collective-permute-start(bf16[4,5,16,512]{3,2,1,0:T(8,128)(2,1)S(1)} %pad_maximum_fusion.17), channel_id=1, source_target_pairs={{0,2},{1,3},{2,0},{3,1},{4,6},{5,7},{6,4},{7,5},{8,10},{9,11},{10,... | collective-permute-start | bytes 983048 | tf_op jit(solution)/shard_map/ppermute | solution.py:729
  107.2 10.2 %collective-permute-start.34 = (bf16[1,8,16,512]{3,2,1,0:T(8,128)(2,1)S(1)}, bf16[1,8,16,512]{3,2,1,0:T(8,128)(2,1)S(1)}, u32[]{:S(2)}, u32[]{:S(2)}) collective-permute-start(bf16[1,8,16,512]{3,2,1,0:T(8,128)(2,1)S(1)} %bitcast.273), channel_id=1, source_target_pairs={{0,16},{4,20},{8,24},{12,28},{16,0},{20,4},{24,8},{28,12},{1,17},{... | collective-permute-start | bytes 393224 | tf_op jit(solution)/shard_map/ppermute | solution.py:729
  117.5 16.0 %collective-permute-start.36 = (bf16[8,5,16,512]{3,2,1,0:T(8,128)(2,1)S(1)}, bf16[8,5,16,512]{3,2,1,0:T(8,128)(2,1)S(1)}, u32[]{:S(2)}, u32[]{:S(2)}) collective-permute-start(bf16[8,5,16,512]{3,2,1,0:T(8,128)(2,1)S(1)} %pad_maximum_fusion.7), channel_id=1, source_target_pairs={{0,4},{4,0},{8,12},{12,8},{16,20},{20,16},{24,28},{28,24},{1,5},{5... | collective-permute-start | bytes 1966088 | tf_op jit(solution)/shard_map/ppermute | solution.py:729
  119.1 12.8 %collective-permute-start.39 = (bf16[256,1024]{1,0:T(8,128)(2,1)S(1)}, bf16[256,1024]{1,0:T(8,128)(2,1)S(1)}, u32[]{:S(2)}, u32[]{:S(2)}) collective-permute-start(bf16[256,1024]{1,0:T(8,128)(2,1)S(1)} %get-tuple-element.298.refs_2_.refs_12_), channel_id=1, source_target_pairs={{0,2},{1,3},{2,0},{3,1},{4,6},{5,7},{6,4},{7,5},{8,10},{9,11},{10,... | collective-permute-start | bytes 1572872 | tf_op jit(solution)/shard_map/ppermute | solution.py:635
  119.4 9.8 %collective-permute-start.37 = (bf16[2,8,16,512]{3,2,1,0:T(8,128)(2,1)S(1)}, bf16[2,8,16,512]{3,2,1,0:T(8,128)(2,1)S(1)}, u32[]{:S(2)}, u32[]{:S(2)}) collective-permute-start(bf16[2,8,16,512]{3,2,1,0:T(8,128)(2,1)S(1)} %pad_maximum_fusion.19), channel_id=1, source_target_pairs={{0,8},{4,12},{8,0},{12,4},{16,24},{20,28},{24,16},{28,20},{1,9},{5... | collective-permute-start | bytes 786440 | tf_op jit(solution)/shard_map/ppermute | solution.py:729
  134.3 13.7 %collective-permute-start.43 = (bf16[4,4,16,512]{3,2,1,0:T(8,128)(2,1)S(1)}, bf16[4,4,16,512]{3,2,1,0:T(8,128)(2,1)S(1)}, u32[]{:S(2)}, u32[]{:S(2)}) collective-permute-start(bf16[4,4,16,512]{3,2,1,0:T(8,128)(2,1)S(1)} %get-tuple-element.512), channel_id=1, source_target_pairs={{0,2},{1,3},{2,0},{3,1},{4,6},{5,7},{6,4},{7,5},{8,10},{9,11},{10,... | collective-permute-start | bytes 786440 | tf_op jit(solution)/shard_map/ppermute | solution.py:729
  134.7 13.9 %collective-permute-start.44 = (bf16[4,4,16,512]{3,2,1,0:T(8,128)(2,1)S(1)}, bf16[4,4,16,512]{3,2,1,0:T(8,128)(2,1)S(1)}, u32[]{:S(2)}, u32[]{:S(2)}) collective-permute-start(bf16[4,4,16,512]{3,2,1,0:T(8,128)(2,1)S(1)} %pad_maximum_fusion.20), channel_id=1, source_target_pairs={{0,2},{1,3},{2,0},{3,1},{4,6},{5,7},{6,4},{7,5},{8,10},{9,11},{10,... | collective-permute-start | bytes 786440 | tf_op jit(solution)/shard_map/ppermute | solution.py:729
  137.4 11.2 %collective-permute-start.45 = (bf16[4,4,16,512]{3,2,1,0:T(8,128)(2,1)S(1)}, bf16[4,4,16,512]{3,2,1,0:T(8,128)(2,1)S(1)}, u32[]{:S(2)}, u32[]{:S(2)}) collective-permute-start(bf16[4,4,16,512]{3,2,1,0:T(8,128)(2,1)S(1)} %get-tuple-element.511), channel_id=1, source_target_pairs={{0,4},{4,0},{8,12},{12,8},{16,20},{20,16},{24,28},{28,24},{1,5},{5... | collective-permute-start | bytes 786440 | tf_op jit(solution)/shard_map/ppermute | solution.py:729
  148.7 18.2 %collective-permute-start.46 = (bf16[8,4,16,512]{3,2,1,0:T(8,128)(2,1)S(1)}, bf16[8,4,16,512]{3,2,1,0:T(8,128)(2,1)S(1)}, u32[]{:S(2)}, u32[]{:S(2)}) collective-permute-start(bf16[8,4,16,512]{3,2,1,0:T(8,128)(2,1)S(1)} %pad_maximum_fusion.10), channel_id=1, source_target_pairs={{0,4},{4,0},{8,12},{12,8},{16,20},{20,16},{24,28},{28,24},{1,5},{5... | collective-permute-start | bytes 1572872 | tf_op jit(solution)/shard_map/ppermute | solution.py:729
  150.3 16.6 %collective-permute-start.47 = (bf16[8,4,16,512]{3,2,1,0:T(8,128)(2,1)S(1)}, bf16[8,4,16,512]{3,2,1,0:T(8,128)(2,1)S(1)}, u32[]{:S(2)}, u32[]{:S(2)}) collective-permute-start(bf16[8,4,16,512]{3,2,1,0:T(8,128)(2,1)S(1)} %pad_maximum_fusion.11), channel_id=1, source_target_pairs={{0,8},{4,12},{8,0},{12,4},{16,24},{20,28},{24,16},{28,20},{1,9},{5... | collective-permute-start | bytes 1572872 | tf_op jit(solution)/shard_map/ppermute | solution.py:729
  152.2 14.8 %collective-permute-start.48 = (bf16[8,4,16,512]{3,2,1,0:T(8,128)(2,1)S(1)}, bf16[8,4,16,512]{3,2,1,0:T(8,128)(2,1)S(1)}, u32[]{:S(2)}, u32[]{:S(2)}) collective-permute-start(bf16[8,4,16,512]{3,2,1,0:T(8,128)(2,1)S(1)} %pad_maximum_fusion.12), channel_id=1, source_target_pairs={{0,2},{1,3},{2,0},{3,1},{4,6},{5,7},{6,4},{7,5},{8,10},{9,11},{10,... | collective-permute-start | bytes 1572872 | tf_op jit(solution)/shard_map/ppermute | solution.py:729
  152.6 14.3 %collective-permute-start.49 = (f32[32,640]{1,0:T(8,128)S(1)}, f32[32,640]{1,0:T(8,128)S(1)}, u32[]{:S(2)}, u32[]{:S(2)}) collective-permute-start(f32[32,640]{1,0:T(8,128)S(1)} %get-tuple-element.310.refs_1_), channel_id=1, source_target_pairs={{0,2},{1,3},{2,0},{3,1},{4,6},{5,7},{6,4},{7,5},{8,10},{9,11},{10,... | collective-permute-start | bytes 245768 | tf_op jit(solution)/shard_map/ppermute | solution.py:635
  196.4 16.9 %collective-permute-start.58 = (bf16[8,5,16,512]{3,2,1,0:T(8,128)(2,1)S(1)}, bf16[8,5,16,512]{3,2,1,0:T(8,128)(2,1)S(1)}, u32[]{:S(2)}, u32[]{:S(2)}) collective-permute-start(bf16[8,5,16,512]{3,2,1,0:T(8,128)(2,1)S(1)} %slice.805), channel_id=1, source_target_pairs={{0,4},{4,0},{8,12},{12,8},{16,20},{20,16},{24,28},{28,24},{1,5},{5... | collective-permute-start | bytes 1966088 | tf_op jit(solution)/shard_map/ppermute | solution.py:729
  197.6 16.6 %collective-permute-start.59 = (bf16[8,5,16,512]{3,2,1,0:T(8,128)(2,1)S(1)}, bf16[8,5,16,512]{3,2,1,0:T(8,128)(2,1)S(1)}, u32[]{:S(2)}, u32[]{:S(2)}) collective-permute-start(bf16[8,5,16,512]{3,2,1,0:T(8,128)(2,1)S(1)} %slice.806), channel_id=1, source_target_pairs={{0,8},{4,12},{8,0},{12,4},{16,24},{20,28},{24,16},{28,20},{1,9},{5... | collective-permute-start | bytes 1966088 | tf_op jit(solution)/shard_map/ppermute | solution.py:729
  214.2 14.3 %collective-permute-start.65 = (bf16[16,5,16,512]{3,2,1,0:T(8,128)(2,1)S(1)}, bf16[16,5,16,512]{3,2,1,0:T(8,128)(2,1)S(1)}, u32[]{:S(2)}, u32[]{:S(2)}) collective-permute-start(bf16[16,5,16,512]{3,2,1,0:T(8,128)(2,1)S(1)} %get-tuple-element.354), channel_id=1, source_target_pairs={{0,1},{1,0},{2,3},{3,2},{4,5},{5,4},{6,7},{7,6},{8,9},{9,8},{10,11... | collective-permute-start | bytes 3932168 | tf_op jit(solution)/shard_map/ppermute | solution.py:729
  214.5 14.0 %collective-permute-start.63 = (bf16[4,5,16,512]{3,2,1,0:T(8,128)(2,1)S(1)}, bf16[4,5,16,512]{3,2,1,0:T(8,128)(2,1)S(1)}, u32[]{:S(2)}, u32[]{:S(2)}) collective-permute-start(bf16[4,5,16,512]{3,2,1,0:T(8,128)(2,1)S(1)} %slice.808), channel_id=1, source_target_pairs={{0,8},{4,12},{8,0},{12,4},{16,24},{20,28},{24,16},{28,20},{1,9},{5... | collective-permute-start | bytes 983048 | tf_op jit(solution)/shard_map/ppermute | solution.py:729
  215.6 12.8 %collective-permute-start.64 = (bf16[4,5,16,512]{3,2,1,0:T(8,128)(2,1)S(1)}, bf16[4,5,16,512]{3,2,1,0:T(8,128)(2,1)S(1)}, u32[]{:S(2)}, u32[]{:S(2)}) collective-permute-start(bf16[4,5,16,512]{3,2,1,0:T(8,128)(2,1)S(1)} %slice.810), channel_id=1, source_target_pairs={{0,4},{4,0},{8,12},{12,8},{16,20},{20,16},{24,28},{28,24},{1,5},{5... | collective-permute-start | bytes 983048 | tf_op jit(solution)/shard_map/ppermute | solution.py:729
  229.3 20.3 %collective-permute-start.70 = (bf16[8,5,16,512]{3,2,1,0:T(8,128)(2,1)S(1)}, bf16[8,5,16,512]{3,2,1,0:T(8,128)(2,1)S(1)}, u32[]{:S(2)}, u32[]{:S(2)}) collective-permute-start(bf16[8,5,16,512]{3,2,1,0:T(8,128)(2,1)S(1)} %slice.815), channel_id=1, source_target_pairs={{0,4},{4,0},{8,12},{12,8},{16,20},{20,16},{24,28},{28,24},{1,5},{5... | collective-permute-start | bytes 1966088 | tf_op jit(solution)/shard_map/ppermute | solution.py:729
  231.5 18.0 %collective-permute-start.72 = (bf16[288,1024]{1,0:T(8,128)(2,1)S(1)}, bf16[288,1024]{1,0:T(8,128)(2,1)S(1)}, u32[]{:S(2)}, u32[]{:S(2)}) collective-permute-start(bf16[288,1024]{1,0:T(8,128)(2,1)S(1)} %add_convert_fusion.17.refs_5_), channel_id=1, source_target_pairs={{0,2},{1,3},{2,0},{3,1},{4,6},{5,7},{6,4},{7,5},{8,10},{9,11},{10,... | collective-permute-start | bytes 1769480 | tf_op jit(solution)/shard_map/ppermute | solution.py:635
  232.1 15.1 %collective-permute-start.68 = (bf16[2,5,16,512]{3,2,1,0:T(8,128)(2,1)S(1)}, bf16[2,5,16,512]{3,2,1,0:T(8,128)(2,1)S(1)}, u32[]{:S(2)}, u32[]{:S(2)}) collective-permute-start(bf16[2,5,16,512]{3,2,1,0:T(8,128)(2,1)S(1)} %slice.812), channel_id=1, source_target_pairs={{0,16},{4,20},{8,24},{12,28},{16,0},{20,4},{24,8},{28,12},{1,17},{... | collective-permute-start | bytes 491528 | tf_op jit(solution)/shard_map/ppermute | solution.py:729
  234.0 15.5 %collective-permute-start.69 = (bf16[2,5,16,512]{3,2,1,0:T(8,128)(2,1)S(1)}, bf16[2,5,16,512]{3,2,1,0:T(8,128)(2,1)S(1)}, u32[]{:S(2)}, u32[]{:S(2)}) collective-permute-start(bf16[2,5,16,512]{3,2,1,0:T(8,128)(2,1)S(1)} %slice.814), channel_id=1, source_target_pairs={{0,16},{4,20},{8,24},{12,28},{16,0},{20,4},{24,8},{28,12},{1,17},{... | collective-permute-start | bytes 491528 | tf_op jit(solution)/shard_map/ppermute | solution.py:729
  249.6 16.6 %collective-permute-start.73 = (bf16[1,5,16,512]{3,2,1,0:T(8,128)(2,1)S(1)}, bf16[1,5,16,512]{3,2,1,0:T(8,128)(2,1)S(1)}, u32[]{:S(2)}, u32[]{:S(2)}) collective-permute-start(bf16[1,5,16,512]{3,2,1,0:T(8,128)(2,1)S(1)} %slice.817), channel_id=1, source_target_pairs={{0,2},{1,3},{2,0},{3,1},{4,6},{5,7},{6,4},{7,5},{8,10},{9,11},{10,... | collective-permute-start | bytes 245768 | tf_op jit(solution)/shard_map/ppermute | solution.py:729
  251.4 14.8 %collective-permute-start.74 = (bf16[1,5,16,512]{3,2,1,0:T(8,128)(2,1)S(1)}, bf16[1,5,16,512]{3,2,1,0:T(8,128)(2,1)S(1)}, u32[]{:S(2)}, u32[]{:S(2)}) collective-permute-start(bf16[1,5,16,512]{3,2,1,0:T(8,128)(2,1)S(1)} %slice.819), channel_id=1, source_target_pairs={{0,2},{1,3},{2,0},{3,1},{4,6},{5,7},{6,4},{7,5},{8,10},{9,11},{10,... | collective-permute-start | bytes 245768 | tf_op jit(solution)/shard_map/ppermute | solution.py:729
  252.1 14.2 %collective-permute-start.75 = (bf16[4,5,16,512]{3,2,1,0:T(8,128)(2,1)S(1)}, bf16[4,5,16,512]{3,2,1,0:T(8,128)(2,1)S(1)}, u32[]{:S(2)}, u32[]{:S(2)}) collective-permute-start(bf16[4,5,16,512]{3,2,1,0:T(8,128)(2,1)S(1)} %slice.821), channel_id=1, source_target_pairs={{0,8},{4,12},{8,0},{12,4},{16,24},{20,28},{24,16},{28,20},{1,9},{5... | collective-permute-start | bytes 983048 | tf_op jit(solution)/shard_map/ppermute | solution.py:729
  254.5 16.8 %collective-permute-start.78 = (bf16[16,5,16,512]{3,2,1,0:T(8,128)(2,1)S(1)}, bf16[16,5,16,512]{3,2,1,0:T(8,128)(2,1)S(1)}, u32[]{:S(2)}, u32[]{:S(2)}) collective-permute-start(bf16[16,5,16,512]{3,2,1,0:T(8,128)(2,1)S(1)} %get-tuple-element.397), channel_id=1, source_target_pairs={{0,1},{1,0},{2,3},{3,2},{4,5},{5,4},{6,7},{7,6},{8,9},{9,8},{10,11... | collective-permute-start | bytes 3932168 | tf_op jit(solution)/shard_map/ppermute | solution.py:729
  271.9 17.1 %collective-permute-start.80 = (bf16[8,5,16,512]{3,2,1,0:T(8,128)(2,1)S(1)}, bf16[8,5,16,512]{3,2,1,0:T(8,128)(2,1)S(1)}, u32[]{:S(2)}, u32[]{:S(2)}) collective-permute-start(bf16[8,5,16,512]{3,2,1,0:T(8,128)(2,1)S(1)} %slice.822), channel_id=1, source_target_pairs={{0,4},{4,0},{8,12},{12,8},{16,20},{20,16},{24,28},{28,24},{1,5},{5... | collective-permute-start | bytes 1966088 | tf_op jit(solution)/shard_map/ppermute | solution.py:729
  274.1 17.0 %collective-permute-start.81 = (bf16[8,5,16,512]{3,2,1,0:T(8,128)(2,1)S(1)}, bf16[8,5,16,512]{3,2,1,0:T(8,128)(2,1)S(1)}, u32[]{:S(2)}, u32[]{:S(2)}) collective-permute-start(bf16[8,5,16,512]{3,2,1,0:T(8,128)(2,1)S(1)} %slice.823), channel_id=1, source_target_pairs={{0,8},{4,12},{8,0},{12,4},{16,24},{20,28},{24,16},{28,20},{1,9},{5... | collective-permute-start | bytes 1966088 | tf_op jit(solution)/shard_map/ppermute | solution.py:729
  291.1 17.9 %collective-permute-start.89 = (bf16[16,5,16,512]{3,2,1,0:T(8,128)(2,1)S(1)}, bf16[16,5,16,512]{3,2,1,0:T(8,128)(2,1)S(1)}, u32[]{:S(2)}, u32[]{:S(2)}) collective-permute-start(bf16[16,5,16,512]{3,2,1,0:T(8,128)(2,1)S(1)} %get-tuple-element.429), channel_id=1, source_target_pairs={{0,1},{1,0},{2,3},{3,2},{4,5},{5,4},{6,7},{7,6},{8,9},{9,8},{10,11... | collective-permute-start | bytes 3932168 | tf_op jit(solution)/shard_map/ppermute | solution.py:729
  291.8 17.2 %collective-permute-start.90 = (bf16[8,5,16,512]{3,2,1,0:T(8,128)(2,1)S(1)}, bf16[8,5,16,512]{3,2,1,0:T(8,128)(2,1)S(1)}, u32[]{:S(2)}, u32[]{:S(2)}) collective-permute-start(bf16[8,5,16,512]{3,2,1,0:T(8,128)(2,1)S(1)} %slice.828), channel_id=1, source_target_pairs={{0,2},{1,3},{2,0},{3,1},{4,6},{5,7},{6,4},{7,5},{8,10},{9,11},{10,... | collective-permute-start | bytes 1966088 | tf_op jit(solution)/shard_map/ppermute | solution.py:729
  294.4 14.6 %collective-permute-start.87 = (bf16[4,5,16,512]{3,2,1,0:T(8,128)(2,1)S(1)}, bf16[4,5,16,512]{3,2,1,0:T(8,128)(2,1)S(1)}, u32[]{:S(2)}, u32[]{:S(2)}) collective-permute-start(bf16[4,5,16,512]{3,2,1,0:T(8,128)(2,1)S(1)} %slice.825), channel_id=1, source_target_pairs={{0,8},{4,12},{8,0},{12,4},{16,24},{20,28},{24,16},{28,20},{1,9},{5... | collective-permute-start | bytes 983048 | tf_op jit(solution)/shard_map/ppermute | solution.py:729
  296.5 12.5 %collective-permute-start.88 = (bf16[4,5,16,512]{3,2,1,0:T(8,128)(2,1)S(1)}, bf16[4,5,16,512]{3,2,1,0:T(8,128)(2,1)S(1)}, u32[]{:S(2)}, u32[]{:S(2)}) collective-permute-start(bf16[4,5,16,512]{3,2,1,0:T(8,128)(2,1)S(1)} %slice.827), channel_id=1, source_target_pairs={{0,4},{4,0},{8,12},{12,8},{16,20},{20,16},{24,28},{28,24},{1,5},{5... | collective-permute-start | bytes 983048 | tf_op jit(solution)/shard_map/ppermute | solution.py:729
  309.4 11.2 %collective-permute-start.92 = (bf16[2,5,16,512]{3,2,1,0:T(8,128)(2,1)S(1)}, bf16[2,5,16,512]{3,2,1,0:T(8,128)(2,1)S(1)}, u32[]{:S(2)}, u32[]{:S(2)}) collective-permute-start(bf16[2,5,16,512]{3,2,1,0:T(8,128)(2,1)S(1)} %slice.830), channel_id=1, source_target_pairs={{0,16},{4,20},{8,24},{12,28},{16,0},{20,4},{24,8},{28,12},{1,17},{... | collective-permute-start | bytes 491528 | tf_op jit(solution)/shard_map/ppermute | solution.py:729
  311.9 18.9 %collective-permute-start.94 = (bf16[8,5,16,512]{3,2,1,0:T(8,128)(2,1)S(1)}, bf16[8,5,16,512]{3,2,1,0:T(8,128)(2,1)S(1)}, u32[]{:S(2)}, u32[]{:S(2)}) collective-permute-start(bf16[8,5,16,512]{3,2,1,0:T(8,128)(2,1)S(1)} %slice.833), channel_id=1, source_target_pairs={{0,4},{4,0},{8,12},{12,8},{16,20},{20,16},{24,28},{28,24},{1,5},{5... | collective-permute-start | bytes 1966088 | tf_op jit(solution)/shard_map/ppermute | solution.py:729
  312.9 17.9 %collective-permute-start.96 = (bf16[16,3,16,512]{3,2,1,0:T(8,128)(2,1)S(1)}, bf16[16,3,16,512]{3,2,1,0:T(8,128)(2,1)S(1)}, u32[]{:S(2)}, u32[]{:S(2)}) collective-permute-start(bf16[16,3,16,512]{3,2,1,0:T(8,128)(2,1)S(1)} %get-tuple-element.442), channel_id=1, source_target_pairs={{0,1},{1,0},{2,3},{3,2},{4,5},{5,4},{6,7},{7,6},{8,9},{9,8},{10,11... | collective-permute-start | bytes 2359304 | tf_op jit(solution)/shard_map/ppermute | solution.py:729
  313.2 17.7 %collective-permute-start.97 = (bf16[288,1024]{1,0:T(8,128)(2,1)S(1)}, bf16[288,1024]{1,0:T(8,128)(2,1)S(1)}, u32[]{:S(2)}, u32[]{:S(2)}) collective-permute-start(bf16[288,1024]{1,0:T(8,128)(2,1)S(1)} %add_convert_fusion.16.refs_5_), channel_id=1, source_target_pairs={{0,2},{1,3},{2,0},{3,1},{4,6},{5,7},{6,4},{7,5},{8,10},{9,11},{10,... | collective-permute-start | bytes 1769480 | tf_op jit(solution)/shard_map/ppermute | solution.py:635
  315.2 15.7 %collective-permute-start.95 = (bf16[4,5,16,512]{3,2,1,0:T(8,128)(2,1)S(1)}, bf16[4,5,16,512]{3,2,1,0:T(8,128)(2,1)S(1)}, u32[]{:S(2)}, u32[]{:S(2)}) collective-permute-start(bf16[4,5,16,512]{3,2,1,0:T(8,128)(2,1)S(1)} %slice.835), channel_id=1, source_target_pairs={{0,8},{4,12},{8,0},{12,4},{16,24},{20,28},{24,16},{28,20},{1,9},{5... | collective-permute-start | bytes 983048 | tf_op jit(solution)/shard_map/ppermute | solution.py:729
  320.5 10.3 %collective-permute-start.93 = (bf16[2,5,16,512]{3,2,1,0:T(8,128)(2,1)S(1)}, bf16[2,5,16,512]{3,2,1,0:T(8,128)(2,1)S(1)}, u32[]{:S(2)}, u32[]{:S(2)}) collective-permute-start(bf16[2,5,16,512]{3,2,1,0:T(8,128)(2,1)S(1)} %slice.832), channel_id=1, source_target_pairs={{0,16},{4,20},{8,24},{12,28},{16,0},{20,4},{24,8},{28,12},{1,17},{... | collective-permute-start | bytes 491528 | tf_op jit(solution)/shard_map/ppermute | solution.py:729
  331.1 15.9 %collective-permute-start.98 = (bf16[4,5,16,512]{3,2,1,0:T(8,128)(2,1)S(1)}, bf16[4,5,16,512]{3,2,1,0:T(8,128)(2,1)S(1)}, u32[]{:S(2)}, u32[]{:S(2)}) collective-permute-start(bf16[4,5,16,512]{3,2,1,0:T(8,128)(2,1)S(1)} %slice.838), channel_id=1, source_target_pairs={{0,2},{1,3},{2,0},{3,1},{4,6},{5,7},{6,4},{7,5},{8,10},{9,11},{10,... | collective-permute-start | bytes 983048 | tf_op jit(solution)/shard_map/ppermute | solution.py:729
  333.2 13.9 %collective-permute-start.99 = (bf16[8,3,16,512]{3,2,1,0:T(8,128)(2,1)S(1)}, bf16[8,3,16,512]{3,2,1,0:T(8,128)(2,1)S(1)}, u32[]{:S(2)}, u32[]{:S(2)}) collective-permute-start(bf16[8,3,16,512]{3,2,1,0:T(8,128)(2,1)S(1)} %slice.839), channel_id=1, source_target_pairs={{0,4},{4,0},{8,12},{12,8},{16,20},{20,16},{24,28},{28,24},{1,5},{5... | collective-permute-start | bytes 1179656 | tf_op jit(solution)/shard_map/ppermute | solution.py:729
  336.8 10.3 %collective-permute-start.103 = (bf16[16,3,16,512]{3,2,1,0:T(8,128)(2,1)S(1)}, bf16[16,3,16,512]{3,2,1,0:T(8,128)(2,1)S(1)}, u32[]{:S(2)}, u32[]{:S(2)}) collective-permute-start(bf16[16,3,16,512]{3,2,1,0:T(8,128)(2,1)S(1)} %get-tuple-element.462), channel_id=1, source_target_pairs={{0,1},{1,0},{2,3},{3,2},{4,5},{5,4},{6,7},{7,6},{8,9},{9,8},{10,11... | collective-permute-start | bytes 2359304 | tf_op jit(solution)/shard_map/ppermute | solution.py:729
  347.4 19.3 %collective-permute-start.105 = (bf16[4,3,16,512]{3,2,1,0:T(8,128)(2,1)S(1)}, bf16[4,3,16,512]{3,2,1,0:T(8,128)(2,1)S(1)}, u32[]{:S(2)}, u32[]{:S(2)}) collective-permute-start(bf16[4,3,16,512]{3,2,1,0:T(8,128)(2,1)S(1)} %get-tuple-element.510), channel_id=1, source_target_pairs={{0,2},{1,3},{2,0},{3,1},{4,6},{5,7},{6,4},{7,5},{8,10},{9,11},{10,... | collective-permute-start | bytes 589832 | tf_op jit(solution)/shard_map/ppermute | solution.py:729
  349.2 17.5 %collective-permute-start.106 = (bf16[4,3,16,512]{3,2,1,0:T(8,128)(2,1)S(1)}, bf16[4,3,16,512]{3,2,1,0:T(8,128)(2,1)S(1)}, u32[]{:S(2)}, u32[]{:S(2)}) collective-permute-start(bf16[4,3,16,512]{3,2,1,0:T(8,128)(2,1)S(1)} %get-tuple-element.509), channel_id=1, source_target_pairs={{0,4},{4,0},{8,12},{12,8},{16,20},{20,16},{24,28},{28,24},{1,5},{5... | collective-permute-start | bytes 589832 | tf_op jit(solution)/shard_map/ppermute | solution.py:729
  351.0 15.8 %collective-permute-start.107 = (bf16[4,3,16,512]{3,2,1,0:T(8,128)(2,1)S(1)}, bf16[4,3,16,512]{3,2,1,0:T(8,128)(2,1)S(1)}, u32[]{:S(2)}, u32[]{:S(2)}) collective-permute-start(bf16[4,3,16,512]{3,2,1,0:T(8,128)(2,1)S(1)} %get-tuple-element.508), channel_id=1, source_target_pairs={{0,6},{1,7},{2,4},{3,5},{4,2},{5,3},{6,0},{7,1},{8,14},{9,15},{10,... | collective-permute-start | bytes 589832 | tf_op jit(solution)/shard_map/ppermute | solution.py:727
  367.1 12.7 %collective-permute-start.112 = (bf16[1,6,16,512]{3,2,1,0:T(8,128)(2,1)S(1)}, bf16[1,6,16,512]{3,2,1,0:T(8,128)(2,1)S(1)}, u32[]{:S(2)}, u32[]{:S(2)}) collective-permute-start(bf16[1,6,16,512]{3,2,1,0:T(8,128)(2,1)S(1)} %pad_maximum_fusion.30), channel_id=1, source_target_pairs={{0,16},{4,20},{8,24},{12,28},{16,0},{20,4},{24,8},{28,12},{1,17},{... | collective-permute-start | bytes 294920 | tf_op jit(solution)/shard_map/ppermute | solution.py:729
  (75 other events, 415.8 us)

commit v6 on v5

--- a/solution.py
+++ b/solution.py
@@ -30,11 +30,11 @@
     0: [
         ("up_0", "down_0", "second_1"),
         ("up_0", "down_0"),
-        ("up_0", "down_0", "first_0", "second_1"),
+        ("up_0", "down_0", "first_0", "second_1", "first_1"),
         ("up_0", "down_0", "first_0", "second_1", "second_0"),
         ("first_0", "second_0", "up_0", "first_1", "second_1"),
         ("last", "down_0"),
-        ("last", "second_0", "first_0", "second_1", "first_1"),
+        ("last", "second_0", "first_0", "second_1"),
         ("last", "first_0"),
     ],
 }
@@ -700,20 +700,25 @@
 def unpack_kernel(slot, sums_ref, gain_ref, shift_ref, bias_ref, memory_ref, lines_ref):
     high = sums_ref.shape[1]
     lines_ref[...] = jnp.zeros(lines_ref.shape, F32)
-    lines_ref[0:high, :] = sums_ref[slot, :, 0:128]
+    columns = sums_ref[slot, :, 0:128]
+    lines_ref[0:high, :] = columns
     lines = lines_ref[...].T
-    place = 0
-    for ref in (gain_ref, shift_ref):
-        layers, rows, _ = ref.shape
+    layers, rows, _ = gain_ref.shape
+    place = layers * rows
+    for layer in range(layers):
+        gain_ref[layer] = lines[layer * rows : (layer + 1) * rows, 0:high]
+    rows = shift_ref.shape[0]
+    for line in range(rows):
         for layer in range(layers):
-            ref[layer] = lines[place : place + rows, 0:high]
-            place += rows
+            goal = place + layer * rows + line
+            shift_ref[line, layer : layer + 1] = lines[goal : goal + 1, 0:high]
+    place += layers * rows
     layers, hidden = bias_ref.shape
     for layer in range(layers):
         for part in range(hidden // high):
             bias_ref[layer : layer + 1, part * high : (part + 1) * high] = lines[place : place + 1, 0:high]
             place += 1
-    memory_ref[...] = lines[place : place + MEM, 0:high]
+    memory_ref[...] = columns[:, place : place + MEM]
 
 
 def flat(stages):
@@ -926,7 +931,7 @@
                 far + chip_bits + pause + near_bit + line + last,
                 1,
             ),
-            (jnp.concatenate(picked(1, middle)), far + line + chip_bits + near_bit + last, 4),
+            (jnp.concatenate(picked(1, middle)), far + line + pause + chip_bits + near_bit + last, 3),
             (jnp.concatenate(picked(1, late) + [up_low[1]]), far + line, 6),
             (down_low[1], near_bit + far + chip_bits + line + last, 6),
         ]
@@ -1191,10 +1196,18 @@
         start("last", grads_last)
         background.begin(*next(plan))
         background.end()
+        ffn_grads = ()
         for moves in plan:
             background.begin(*moves)
-            background.end()
+            ffn_grads = background.end(*ffn_grads)
             background.merge("last", "second_0")
+            if not ffn_grads:
+                ups_grads, down_grads = [], []
+                for index in range(layers):
+                    value = background.sums[f"up_{index}"].result
+                    ups_grads.append(jnp.concatenate([value[part] for part in range(per)], -1))
+                    down_grads.append(background.sums[f"down_{index}"].result[:per].reshape(per * rows, width))
+                ffn_grads = [jnp.stack(ups_grads), jnp.stack(down_grads)]
         for index in range(layers):
             wanted = [f"{name}_{index}" for name in ("up", "down", "first", "second")] + (["last"] if index == 0 else [])
             if index == 0:
@@ -1233,11 +1246,16 @@
             mine[index][key] = result[place]
         for m in mine:
             m["down"] = jnp.concatenate([m["down", part] for part in range(per)])
+    if not direct:
+        ffn_grads = [
+            jnp.stack([jnp.concatenate([m["up", part] for part in range(per)], -1) for m in mine]),
+            jnp.stack([m["down"] for m in mine]),
+        ]
     if direct:
         small_grads = pl.pallas_call(
             functools.partial(unpack_kernel, 2),
             out_shape=[
-                jax.ShapeDtypeStruct(part.shape, F32) for part in (norm_gain, norm_shift, ffn_bias, memory_init)
+                jax.ShapeDtypeStruct(part.shape, F32) for part in packed_small[:4]
             ],
             in_specs=[inside],
             out_specs=[inside] * 4,
@@ -1245,6 +1263,7 @@
             compiler_params=pltpu.CompilerParams(vmem_limit_bytes=VMEM_LIMIT),
             name="unpack",
         )(last_sums)
+        small_grads = [small_grads[0], small_grads[1].transpose(1, 0, 2), small_grads[2], small_grads[3].T]
     else:
         back = mine[0]["small"].T
         small_grads = [back[starts[k] : starts[k + 1]].reshape(part.shape) for k, part in enumerate(
@@ -1256,8 +1275,7 @@
         grad[:length][None],
         small_grads[3],
         jnp.stack([jnp.stack([m[key] for key in range(count)]) for m in mine]),
-        jnp.stack([jnp.concatenate([m["up", part] for part in range(per)], -1) for m in mine]),
-        jnp.stack([m["down"] for m in mine]),
+        *ffn_grads,
         small_grads[2],
         small_grads[0],
         small_grads[1],

time: 391 us -> 389 us (level)
  transfers between devices with their start and end apart: 116 -> 116, of which waited for: 48 -> 51; matrix products, arithmetic and copies ran while one was open for 3% -> 3% of each run, Pallas kernels for 20% -> 20%
where the time goes in v6:
time: 389 us; the launch traced here: 381 us
  waiting for transfers between devices  158 us (41%)
  starting transfers between devices  109 us (28%)
  Pallas kernels  95.1 us (24%)
  other arithmetic  11.9 us (3%)
  local copies, waits for them, and re-layouts  3.97 us (1%)
    ppermute x86, waiting for transfers between devices, swapped(): lax.ppermute(value, axis, [(source, source ^ 1 << bit) for source in rang...  117 us
    pallas_call x13, Pallas kernels, call(): pl.pallas_call(body, out_shape=shapes + [jax.ShapeDtypeStruct(shape, kind...  92.6 us
    ppermute x86, starting transfers between devices, swapped(): lax.ppermute(value, axis, [(source, source ^ 1 << bit) for source in rang...  87.5 us
    ppermute x28, waiting for transfers between devices, flipped(): lax.ppermute(value, 'blk', [(source, source ^ bit) for source in range(si...  41.4 us
    ppermute x28, starting transfers between devices, flipped(): lax.ppermute(value, 'blk', [(source, source ^ bit) for source in range(si...  18 us
  transfers between devices with their start and end apart: 116, of which 51 were waited for; matrix products, arithmetic and copies ran while one was open for 3% of the time, Pallas kernels for 20%

profile of v6, /device:TPU:0, one launch (start us, length us, event | category | flops | bytes accessed | tf_op | source)
XLA Modules:
  0.0 381.4 jit_solution(16893069559797841455)
XLA Ops:
  0.7 1.8 pack.1
  2.5 4.1 %collective-permute-start = (bf16[1,4,16,512]{3,2,1,0:T(8,128)(2,1)}, bf16[1,4,16,512]{3,2,1,0:T(8,128)(2,1)S(1)}, u32[]{:S(2)}, u32[]{:S(2)}) collective-permute-start(bf16[1,4,16,512]{3,2,1,0:T(8,128)(2,1)} %bitcast.258), channel_id=1, source_target_pairs={{0,16},{4,20},{8,24},{12,28},{16,0},{20,4},{24,8},{28,12},{1,17},{... | collective-permute-start | bytes 196616 | tf_op jit(solution)/shard_map/ppermute | solution.py:734
  6.9 3.6 collective-permute-done
  10.5 3.5 collective-permute-done.1
  18.2 1.8 collective-permute-start.5
  20.9 2.8 collective-permute-done.5
  24.5 2.0 collective-permute-start.6
  31.8 8.9 %collective-permute-done.8 = bf16[1,5,16,512]{3,2,1,0:T(8,128)(2,1)S(1)} collective-permute-done((bf16[1,5,16,512]{3,2,1,0:T(8,128)(2,1)S(1)}, bf16[1,5,16,512]{3,2,1,0:T(8,128)(2,1)S(1)}, u32[]{:S(2)}, u32[]{:S(2)}) %collective-permute-start.8) | collective-permute-done | bytes 81952 | tf_op jit(solution)/shard_map/ppermute | solution.py:734
  42.4 2.5 collective-permute-start.14
  46.7 9.6 %collective-permute-done.13 = bf16[2,5,16,512]{3,2,1,0:T(8,128)(2,1)S(1)} collective-permute-done((bf16[2,5,16,512]{3,2,1,0:T(8,128)(2,1)S(1)}, bf16[2,5,16,512]{3,2,1,0:T(8,128)(2,1)S(1)}, u32[]{:S(2)}, u32[]{:S(2)}) %collective-permute-start.13) | collective-permute-done | bytes 163872 | tf_op jit(solution)/shard_map/ppermute | solution.py:734
  58.7 2.2 collective-permute-done.16.refs_2_.refs_16_
  60.9 2.5 first.1
  66.1 2.4 collective-permute-start.20
  70.1 2.3 collective-permute-done.20
  72.4 3.1 collective-permute-done.18
  75.5 2.0 collective-permute-done.21.refs_4_.refs_14_
  79.5 3.0 collective-permute-start.26
  82.6 9.1 %attend_0.1 = (bf16[288,512]{1,0:T(8,128)(2,1)S(1)}, f32[4,576]{1,0:T(4,128)S(1)}, f32[288,512]{1,0:T(8,128)S(1)}, f32[288,512]{1,0:T(8,128)S(1)}, bf16[32,512]{...) custom-call(f32[288,512]{1,0:T(8,128)S(1)} %get-tuple-element.267.refs_0_,, ...), custom_call_target="tpu_custom_call" | custom-call | flops 4289999872 | tf_op jit(solution)/shard_map/attend_0/pallas_call | solution.py:616
  91.7 1.8 collective-permute-start.27
  93.5 3.1 collective-permute-done.27.refs_3_
  98.5 1.8 collective-permute-start.33
  100.3 3.8 %collective-permute-done.28.refs_2_ = f32[32,640]{1,0:T(8,128)S(1)} collective-permute-done((f32[32,640]{1,0:T(8,128)S(1)}, f32[32,640]{1,0:T(8,128)S(1)}, u32[]{:S(2)}, u32[]{:S(2)}) %collective-permute-start.28) | collective-permute-done | bytes 81952 | tf_op jit(solution)/shard_map/ppermute | solution.py:635
  107.0 7.1 %finish_0.1 = (f32[288,512]{1,0:T(8,128)S(1)}, bf16[288,512]{1,0:T(8,128)(2,1)S(1)}, bf16[256,1024]{1,0:T(8,128)(2,1)S(1)}, bf16[32,1024]{1,0:T(8,128)(2,1)S(1)}...) custom-call(f32[288,512]{1,0:T(8,128)S(1)} %get-tuple-element.279.re, ...), custom_call_target="tpu_custom_call" | custom-call | flops 3300000000 | tf_op jit(solution)/shard_map/finish_0/pallas_call | solution.py:616
  118.8 2.7 collective-permute-start.38
  121.6 4.8 %collective-permute-done.38 = bf16[2,4,16,512]{3,2,1,0:T(8,128)(2,1)S(1)} collective-permute-done((bf16[2,4,16,512]{3,2,1,0:T(8,128)(2,1)S(1)}, bf16[2,4,16,512]{3,2,1,0:T(8,128)(2,1)S(1)}, u32[]{:S(2)}, u32[]{:S(2)}) %collective-permute-start.38) | collective-permute-done | bytes 131104 | tf_op jit(solution)/shard_map/ppermute | solution.py:734
  131.4 2.0 collective-permute-start.43
  136.0 9.1 %attend_1.1 = (bf16[288,512]{1,0:T(8,128)(2,1)S(1)}, f32[4,576]{1,0:T(4,128)S(1)}, f32[288,512]{1,0:T(8,128)S(1)}, f32[288,512]{1,0:T(8,128)S(1)}, bf16[32,512]{...) custom-call(f32[288,512]{1,0:T(8,128)S(1)} %get-tuple-element.290.refs_0_,, ...), custom_call_target="tpu_custom_call" | custom-call | flops 4289999872 | tf_op jit(solution)/shard_map/attend_1/pallas_call | solution.py:616
  147.4 2.6 collective-permute-start.47
  150.5 1.8 collective-permute-start.49
  152.3 12.5 %collective-permute-done.49.refs_3_ = f32[32,640]{1,0:T(8,128)S(1)} collective-permute-done((f32[32,640]{1,0:T(8,128)S(1)}, f32[32,640]{1,0:T(8,128)S(1)}, u32[]{:S(2)}, u32[]{:S(2)}) %collective-permute-start.49) | collective-permute-done | bytes 81952 | tf_op jit(solution)/shard_map/ppermute | solution.py:635
  166.5 4.3 %collective-permute-done.50.refs_2_ = f32[32,640]{1,0:T(8,128)S(1)} collective-permute-done((f32[32,640]{1,0:T(8,128)S(1)}, f32[32,640]{1,0:T(8,128)S(1)}, u32[]{:S(2)}, u32[]{:S(2)}) %collective-permute-start.50) | collective-permute-done | bytes 81952 | tf_op jit(solution)/shard_map/ppermute | solution.py:635
  170.9 6.0 %finish_1.1 = (f32[288,512]{1,0:T(8,128)S(1)}, f32[32,512]{1,0:T(8,128)S(1)}, f32[32,512]{1,0:T(8,128)S(1)}, f32[32,512]{1,0:T(8,128)S(1)}, f32[288,512]{1,0:T(8...) custom-call(f32[288,512]{1,0:T(8,128)S(1)} %get-tuple-element.304.re, ...), custom_call_target="tpu_custom_call" | custom-call | flops 3300000000 | tf_op jit(solution)/shard_map/finish_1/pallas_call | solution.py:616
  177.0 11.8 %feed_back_1.1 = (bf16[16,5,16,512]{3,2,1,0:T(8,128)(2,1)S(1)}, bf16[16,5,16,512]{3,2,1,0:T(8,128)(2,1)S(1)}, bf16[16,5,16,512]{3,2,1,0:T(8,128)(2,1)S(1)}, bf16...) custom-call(f32[288,512]{1,0:T(8,128)S(1)} %fusion.2.refs_0_, ...), custom_call_target="tpu_custom_call" | custom-call | flops 3630000128 | tf_op jit(solution)/shard_map/feed_back_1/pallas_call | solution.py:616
  189.6 4.0 %collective-permute-done.57.refs_2_ = bf16[64,512]{1,0:T(8,128)(2,1)S(1)} collective-permute-done((bf16[64,512]{1,0:T(8,128)(2,1)S(1)}, bf16[64,512]{1,0:T(8,128)(2,1)S(1)}, u32[]{:S(2)}, u32[]{:S(2)}) %collective-permute-start.57) | collective-permute-done | bytes 65568 | tf_op jit(solution)/shard_map/ppermute | solution.py:635
  197.2 4.1 %read_back_1.1 = (bf16[16,5,16,512]{3,2,1,0:T(8,128)(2,1)S(1)}, bf16[16,5,16,512]{3,2,1,0:T(8,128)(2,1)S(1)}, f32[4,512]{1,0:T(4,128)S(1)}, f32[32,512]{1,0:T(8,...) custom-call(bf16[64,512]{1,0:T(8,128)(2,1)S(1)} %get-tuple-element.338.refs_0_, ...), custom_call_target="tpu_custom_call" | custom-call | flops 1320000000 | tf_op jit(solution)/shard_map/read_back_1/pallas_call | solution.py:616
  202.5 2.8 collective-permute-done.62.refs_3_
  205.3 5.8 %collective-permute-done.58 = bf16[8,5,16,512]{3,2,1,0:T(8,128)(2,1)S(1)} collective-permute-done((bf16[8,5,16,512]{3,2,1,0:T(8,128)(2,1)S(1)}, bf16[8,5,16,512]{3,2,1,0:T(8,128)(2,1)S(1)}, u32[]{:S(2)}, u32[]{:S(2)}) %collective-permute-start.58) | collective-permute-done | bytes 655392 | tf_op jit(solution)/shard_map/ppermute | solution.py:734
  215.2 11.1 %attend_back_1.1 = (bf16[16,5,16,512]{3,2,1,0:T(8,128)(2,1)S(1)}, bf16[16,5,16,512]{3,2,1,0:T(8,128)(2,1)S(1)}, f32[2,512]{1,0:T(2,128)S(1)}, f32[288,512]{1,0:T...) custom-call(f32[288,512]{1,0:T(8,128)S(1)} %get-tuple-element.290.re, ...), custom_call_target="tpu_custom_call" | custom-call | flops 4620000256 | tf_op jit(solution)/shard_map/attend_back_1/pallas_call | solution.py:616
  230.2 2.4 collective-permute-start.68
  233.4 11.6 %collective-permute-done.68 = bf16[2,5,16,512]{3,2,1,0:T(8,128)(2,1)S(1)} collective-permute-done((bf16[2,5,16,512]{3,2,1,0:T(8,128)(2,1)S(1)}, bf16[2,5,16,512]{3,2,1,0:T(8,128)(2,1)S(1)}, u32[]{:S(2)}, u32[]{:S(2)}) %collective-permute-start.68) | collective-permute-done | bytes 163872 | tf_op jit(solution)/shard_map/ppermute | solution.py:734
  245.1 2.6 collective-permute-done.69
  250.7 2.3 input_back_1.1
  253.1 11.6 %feed_back_0.1 = (bf16[16,5,16,512]{3,2,1,0:T(8,128)(2,1)S(1)}, bf16[16,5,16,512]{3,2,1,0:T(8,128)(2,1)S(1)}, bf16[16,5,16,512]{3,2,1,0:T(8,128)(2,1)S(1)}, bf16...) custom-call(f32[288,512]{1,0:T(8,128)S(1)} %get-tuple-element.383.re, ...), custom_call_target="tpu_custom_call" | custom-call | flops 3630000128 | tf_op jit(solution)/shard_map/feed_back_0/pallas_call | solution.py:616
  267.1 2.7 collective-permute-done.79.refs_2_
  272.0 2.0 collective-permute-start.81
  276.1 4.1 %read_back_0.1 = (bf16[16,5,16,512]{3,2,1,0:T(8,128)(2,1)S(1)}, bf16[16,5,16,512]{3,2,1,0:T(8,128)(2,1)S(1)}, f32[4,512]{1,0:T(4,128)S(1)}, f32[32,512]{1,0:T(8,...) custom-call(bf16[64,512]{1,0:T(8,128)(2,1)S(1)} %get-tuple-element.404.refs_0_, ...), custom_call_target="tpu_custom_call" | custom-call | flops 1320000000 | tf_op jit(solution)/shard_map/read_back_0/pallas_call | solution.py:616
  280.2 1.8 collective-permute-start.84
  284.2 3.3 collective-permute-done.80
  287.5 5.0 %collective-permute-done.81 = bf16[8,5,16,512]{3,2,1,0:T(8,128)(2,1)S(1)} collective-permute-done((bf16[8,5,16,512]{3,2,1,0:T(8,128)(2,1)S(1)}, bf16[8,5,16,512]{3,2,1,0:T(8,128)(2,1)S(1)}, u32[]{:S(2)}, u32[]{:S(2)}) %collective-permute-start.81) | collective-permute-done | bytes 655392 | tf_op jit(solution)/shard_map/ppermute | solution.py:734
  293.1 1.8 collective-permute-start.90
  297.3 11.2 %attend_back_0.1 = (bf16[16,3,16,512]{3,2,1,0:T(8,128)(2,1)S(1)}, bf16[16,3,16,512]{3,2,1,0:T(8,128)(2,1)S(1)}, f32[2,512]{1,0:T(2,128)S(1)}, f32[288,512]{1,0:T...) custom-call(f32[288,512]{1,0:T(8,128)S(1)} %get-tuple-element.267.re, ...), custom_call_target="tpu_custom_call" | custom-call | flops 4620000256 | tf_op jit(solution)/shard_map/attend_back_0/pallas_call | solution.py:616
  308.5 1.8 collective-permute-done.90
  315.8 2.5 collective-permute-start.96
  318.5 3.3 collective-permute-done.93
  321.9 10.4 %collective-permute-done.94 = bf16[2,5,16,512]{3,2,1,0:T(8,128)(2,1)S(1)} collective-permute-done((bf16[2,5,16,512]{3,2,1,0:T(8,128)(2,1)S(1)}, bf16[2,5,16,512]{3,2,1,0:T(8,128)(2,1)S(1)}, u32[]{:S(2)}, u32[]{:S(2)}) %collective-permute-start.94) | collective-permute-done | bytes 163872 | tf_op jit(solution)/shard_map/ppermute | solution.py:734
  335.8 2.5 input_back_0.1
  341.6 3.9 %collective-permute-done.101 = bf16[1,5,16,512]{3,2,1,0:T(8,128)(2,1)S(1)} collective-permute-done((bf16[1,5,16,512]{3,2,1,0:T(8,128)(2,1)S(1)}, bf16[1,5,16,512]{3,2,1,0:T(8,128)(2,1)S(1)}, u32[]{:S(2)}, u32[]{:S(2)}) %collective-permute-start.101) | collective-permute-done | bytes 81952 | tf_op jit(solution)/shard_map/ppermute | solution.py:734
  347.1 2.7 collective-permute-done.105
  352.0 1.8 collective-permute-start.108
  355.4 5.6 %collective-permute-done.111 = bf16[1,5,16,512]{3,2,1,0:T(8,128)(2,1)S(1)} collective-permute-done((bf16[1,5,16,512]{3,2,1,0:T(8,128)(2,1)S(1)}, bf16[1,5,16,512]{3,2,1,0:T(8,128)(2,1)S(1)}, u32[]{:S(2)}, u32[]{:S(2)}) %collective-permute-start.111) | collective-permute-done | bytes 81952 | tf_op jit(solution)/shard_map/ppermute | solution.py:734
  362.4 5.5 %collective-permute-done.110 = bf16[2,5,16,512]{3,2,1,0:T(8,128)(2,1)S(1)} collective-permute-done((bf16[2,5,16,512]{3,2,1,0:T(8,128)(2,1)S(1)}, bf16[2,5,16,512]{3,2,1,0:T(8,128)(2,1)S(1)}, u32[]{:S(2)}, u32[]{:S(2)}) %collective-permute-start.110) | collective-permute-done | bytes 163872 | tf_op jit(solution)/shard_map/ppermute | solution.py:734
  368.3 2.5 collective-permute-start.113
  370.8 2.0 collective-permute-start.114
  373.2 5.9 %collective-permute-done.115 = bf16[1,5,16,512]{3,2,1,0:T(8,128)(2,1)S(1)} collective-permute-done((bf16[1,5,16,512]{3,2,1,0:T(8,128)(2,1)S(1)}, bf16[1,5,16,512]{3,2,1,0:T(8,128)(2,1)S(1)}, u32[]{:S(2)}, u32[]{:S(2)}) %collective-permute-start.115) | collective-permute-done | bytes 81952 | tf_op jit(solution)/shard_map/ppermute | solution.py:734
  (434 shorter events, 95.2 us)
Async XLA Ops:
  14.2 9.5 %collective-permute-start.2 = (bf16[2,4,16,512]{3,2,1,0:T(8,128)(2,1)S(1)}, bf16[2,4,16,512]{3,2,1,0:T(8,128)(2,1)S(1)}, u32[]{:S(2)}, u32[]{:S(2)}) collective-permute-start(bf16[2,4,16,512]{3,2,1,0:T(8,128)(2,1)S(1)} %pad_maximum_fusion.28), channel_id=1, source_target_pairs={{0,8},{4,12},{8,0},{12,4},{16,24},{20,28},{24,16},{28,20},{1,9},{5... | collective-permute-start | bytes 393224 | tf_op jit(solution)/shard_map/ppermute | solution.py:734
  14.8 9.7 %collective-permute-start.3 = (bf16[2,5,16,512]{3,2,1,0:T(8,128)(2,1)S(1)}, bf16[2,5,16,512]{3,2,1,0:T(8,128)(2,1)S(1)}, u32[]{:S(2)}, u32[]{:S(2)}) collective-permute-start(bf16[2,5,16,512]{3,2,1,0:T(8,128)(2,1)S(1)} %pad_maximum_fusion.23), channel_id=1, source_target_pairs={{0,8},{4,12},{8,0},{12,4},{16,24},{20,28},{24,16},{28,20},{1,9},{5... | collective-permute-start | bytes 491528 | tf_op jit(solution)/shard_map/ppermute | solution.py:734
  24.5 16.2 %collective-permute-start.6 = (bf16[4,4,16,512]{3,2,1,0:T(8,128)(2,1)S(1)}, bf16[4,4,16,512]{3,2,1,0:T(8,128)(2,1)S(1)}, u32[]{:S(2)}, u32[]{:S(2)}) collective-permute-start(bf16[4,4,16,512]{3,2,1,0:T(8,128)(2,1)S(1)} %pad_maximum_fusion.18), channel_id=1, source_target_pairs={{0,2},{1,3},{2,0},{3,1},{4,6},{5,7},{6,4},{7,5},{8,10},{9,11},{10,... | collective-permute-start | bytes 786440 | tf_op jit(solution)/shard_map/ppermute | solution.py:734
  26.6 14.1 %collective-permute-start.7 = (bf16[4,5,16,512]{3,2,1,0:T(8,128)(2,1)S(1)}, bf16[4,5,16,512]{3,2,1,0:T(8,128)(2,1)S(1)}, u32[]{:S(2)}, u32[]{:S(2)}) collective-permute-start(bf16[4,5,16,512]{3,2,1,0:T(8,128)(2,1)S(1)} %pad_maximum_fusion.13), channel_id=1, source_target_pairs={{0,4},{4,0},{8,12},{12,8},{16,20},{20,16},{24,28},{28,24},{1,5},{5... | collective-permute-start | bytes 983048 | tf_op jit(solution)/shard_map/ppermute | solution.py:734
  28.2 12.5 %collective-permute-start.9 = (bf16[2,5,16,512]{3,2,1,0:T(8,128)(2,1)S(1)}, bf16[2,5,16,512]{3,2,1,0:T(8,128)(2,1)S(1)}, u32[]{:S(2)}, u32[]{:S(2)}) collective-permute-start(bf16[2,5,16,512]{3,2,1,0:T(8,128)(2,1)S(1)} %pad_maximum_fusion.24), channel_id=1, source_target_pairs={{0,16},{4,20},{8,24},{12,28},{16,0},{20,4},{24,8},{28,12},{1,17},{... | collective-permute-start | bytes 491528 | tf_op jit(solution)/shard_map/ppermute | solution.py:734
  29.8 10.9 %collective-permute-start.10 = (bf16[2,5,16,512]{3,2,1,0:T(8,128)(2,1)S(1)}, bf16[2,5,16,512]{3,2,1,0:T(8,128)(2,1)S(1)}, u32[]{:S(2)}, u32[]{:S(2)}) collective-permute-start(bf16[2,5,16,512]{3,2,1,0:T(8,128)(2,1)S(1)} %pad_maximum_fusion.25), channel_id=1, source_target_pairs={{0,2},{1,3},{2,0},{3,1},{4,6},{5,7},{6,4},{7,5},{8,10},{9,11},{10,... | collective-permute-start | bytes 491528 | tf_op jit(solution)/shard_map/ppermute | solution.py:734
  30.4 10.3 %collective-permute-start.8 = (bf16[1,5,16,512]{3,2,1,0:T(8,128)(2,1)S(1)}, bf16[1,5,16,512]{3,2,1,0:T(8,128)(2,1)S(1)}, u32[]{:S(2)}, u32[]{:S(2)}) collective-permute-start(bf16[1,5,16,512]{3,2,1,0:T(8,128)(2,1)S(1)} %bitcast.270), channel_id=1, source_target_pairs={{0,16},{4,20},{8,24},{12,28},{16,0},{20,4},{24,8},{28,12},{1,17},{... | collective-permute-start | bytes 245768 | tf_op jit(solution)/shard_map/ppermute | solution.py:734
  40.8 15.5 %collective-permute-start.12 = (bf16[8,5,16,512]{3,2,1,0:T(8,128)(2,1)S(1)}, bf16[8,5,16,512]{3,2,1,0:T(8,128)(2,1)S(1)}, u32[]{:S(2)}, u32[]{:S(2)}) collective-permute-start(bf16[8,5,16,512]{3,2,1,0:T(8,128)(2,1)S(1)} %pad_maximum_fusion.3), channel_id=1, source_target_pairs={{0,2},{1,3},{2,0},{3,1},{4,6},{5,7},{6,4},{7,5},{8,10},{9,11},{10,... | collective-permute-start | bytes 1966088 | tf_op jit(solution)/shard_map/ppermute | solution.py:734
  41.8 14.4 %collective-permute-start.11 = (bf16[8,4,16,512]{3,2,1,0:T(8,128)(2,1)S(1)}, bf16[8,4,16,512]{3,2,1,0:T(8,128)(2,1)S(1)}, u32[]{:S(2)}, u32[]{:S(2)}) collective-permute-start(bf16[8,4,16,512]{3,2,1,0:T(8,128)(2,1)S(1)} %pad_maximum_fusion.8), channel_id=1, source_target_pairs={{0,4},{4,0},{8,12},{12,8},{16,20},{20,16},{24,28},{28,24},{1,5},{5... | collective-permute-start | bytes 1572872 | tf_op jit(solution)/shard_map/ppermute | solution.py:734
  42.4 13.9 %collective-permute-start.14 = (bf16[4,5,16,512]{3,2,1,0:T(8,128)(2,1)S(1)}, bf16[4,5,16,512]{3,2,1,0:T(8,128)(2,1)S(1)}, u32[]{:S(2)}, u32[]{:S(2)}) collective-permute-start(bf16[4,5,16,512]{3,2,1,0:T(8,128)(2,1)S(1)} %pad_maximum_fusion.14), channel_id=1, source_target_pairs={{0,8},{4,12},{8,0},{12,4},{16,24},{20,28},{24,16},{28,20},{1,9},{5... | collective-permute-start | bytes 983048 | tf_op jit(solution)/shard_map/ppermute | solution.py:734
  44.9 11.3 %collective-permute-start.13 = (bf16[2,5,16,512]{3,2,1,0:T(8,128)(2,1)S(1)}, bf16[2,5,16,512]{3,2,1,0:T(8,128)(2,1)S(1)}, u32[]{:S(2)}, u32[]{:S(2)}) collective-permute-start(bf16[2,5,16,512]{3,2,1,0:T(8,128)(2,1)S(1)} %pad_maximum_fusion.26), channel_id=1, source_target_pairs={{0,8},{4,12},{8,0},{12,4},{16,24},{20,28},{24,16},{28,20},{1,9},{5... | collective-permute-start | bytes 491528 | tf_op jit(solution)/shard_map/ppermute | solution.py:734
  57.3 12.8 %collective-permute-start.19 = (bf16[4,5,16,512]{3,2,1,0:T(8,128)(2,1)S(1)}, bf16[4,5,16,512]{3,2,1,0:T(8,128)(2,1)S(1)}, u32[]{:S(2)}, u32[]{:S(2)}) collective-permute-start(bf16[4,5,16,512]{3,2,1,0:T(8,128)(2,1)S(1)} %pad_maximum_fusion.16), channel_id=1, source_target_pairs={{0,4},{4,0},{8,12},{12,8},{16,20},{20,16},{24,28},{28,24},{1,5},{5... | collective-permute-start | bytes 983048 | tf_op jit(solution)/shard_map/ppermute | solution.py:734
  63.5 14.0 %collective-permute-start.21 = (bf16[256,1024]{1,0:T(8,128)(2,1)S(1)}, bf16[256,1024]{1,0:T(8,128)(2,1)S(1)}, u32[]{:S(2)}, u32[]{:S(2)}) collective-permute-start(bf16[256,1024]{1,0:T(8,128)(2,1)S(1)} %get-tuple-element.273.refs_2_.refs_12_), channel_id=1, source_target_pairs={{0,2},{1,3},{2,0},{3,1},{4,6},{5,7},{6,4},{7,5},{8,10},{9,11},{10,... | collective-permute-start | bytes 1572872 | tf_op jit(solution)/shard_map/ppermute | solution.py:635
  64.8 10.7 %collective-permute-start.18 = (bf16[4,5,16,512]{3,2,1,0:T(8,128)(2,1)S(1)}, bf16[4,5,16,512]{3,2,1,0:T(8,128)(2,1)S(1)}, u32[]{:S(2)}, u32[]{:S(2)}) collective-permute-start(bf16[4,5,16,512]{3,2,1,0:T(8,128)(2,1)S(1)} %pad_maximum_fusion.15), channel_id=1, source_target_pairs={{0,4},{4,0},{8,12},{12,8},{16,20},{20,16},{24,28},{28,24},{1,5},{5... | collective-permute-start | bytes 983048 | tf_op jit(solution)/shard_map/ppermute | solution.py:734
  68.5 25.0 %collective-permute-start.25 = (bf16[8,5,16,512]{3,2,1,0:T(8,128)(2,1)S(1)}, bf16[8,5,16,512]{3,2,1,0:T(8,128)(2,1)S(1)}, u32[]{:S(2)}, u32[]{:S(2)}) collective-permute-start(bf16[8,5,16,512]{3,2,1,0:T(8,128)(2,1)S(1)} %pad_maximum_fusion.5), channel_id=1, source_target_pairs={{0,4},{4,0},{8,12},{12,8},{16,20},{20,16},{24,28},{28,24},{1,5},{5... | collective-permute-start | bytes 1966088 | tf_op jit(solution)/shard_map/ppermute | solution.py:734
  78.1 18.5 %collective-permute-start.24 = (bf16[8,5,16,512]{3,2,1,0:T(8,128)(2,1)S(1)}, bf16[8,5,16,512]{3,2,1,0:T(8,128)(2,1)S(1)}, u32[]{:S(2)}, u32[]{:S(2)}) collective-permute-start(bf16[8,5,16,512]{3,2,1,0:T(8,128)(2,1)S(1)} %pad_maximum_fusion.4), channel_id=1, source_target_pairs={{0,2},{1,3},{2,0},{3,1},{4,6},{5,7},{6,4},{7,5},{8,10},{9,11},{10,... | collective-permute-start | bytes 1966088 | tf_op jit(solution)/shard_map/ppermute | solution.py:734
  79.5 17.7 %collective-permute-start.26 = (bf16[8,5,16,512]{3,2,1,0:T(8,128)(2,1)S(1)}, bf16[8,5,16,512]{3,2,1,0:T(8,128)(2,1)S(1)}, u32[]{:S(2)}, u32[]{:S(2)}) collective-permute-start(bf16[8,5,16,512]{3,2,1,0:T(8,128)(2,1)S(1)} %pad_maximum_fusion.6), channel_id=1, source_target_pairs={{0,8},{4,12},{8,0},{12,4},{16,24},{20,28},{24,16},{28,20},{1,9},{5... | collective-permute-start | bytes 1966088 | tf_op jit(solution)/shard_map/ppermute | solution.py:734
  97.3 9.7 %collective-permute-start.31 = (bf16[16,5,16,512]{3,2,1,0:T(8,128)(2,1)S(1)}, bf16[16,5,16,512]{3,2,1,0:T(8,128)(2,1)S(1)}, u32[]{:S(2)}, u32[]{:S(2)}) collective-permute-start(bf16[16,5,16,512]{3,2,1,0:T(8,128)(2,1)S(1)} %constant_dynamic-update-slice_fusion.30.refs_9_.refs_11_), channel_id=1, source_target_pairs={{0,1},{1,0},{2,3},{3,2},{4,5},{5,4},{6,7},{7,6},{8,9},{9,8},{10,11... | collective-permute-start | bytes 3932168 | tf_op jit(solution)/shard_map/ppermute | solution.py:734
  98.5 15.7 %collective-permute-start.33 = (bf16[4,5,16,512]{3,2,1,0:T(8,128)(2,1)S(1)}, bf16[4,5,16,512]{3,2,1,0:T(8,128)(2,1)S(1)}, u32[]{:S(2)}, u32[]{:S(2)}) collective-permute-start(bf16[4,5,16,512]{3,2,1,0:T(8,128)(2,1)S(1)} %pad_maximum_fusion.17), channel_id=1, source_target_pairs={{0,2},{1,3},{2,0},{3,1},{4,6},{5,7},{6,4},{7,5},{8,10},{9,11},{10,... | collective-permute-start | bytes 983048 | tf_op jit(solution)/shard_map/ppermute | solution.py:734
  114.3 16.3 %collective-permute-start.36 = (bf16[8,5,16,512]{3,2,1,0:T(8,128)(2,1)S(1)}, bf16[8,5,16,512]{3,2,1,0:T(8,128)(2,1)S(1)}, u32[]{:S(2)}, u32[]{:S(2)}) collective-permute-start(bf16[8,5,16,512]{3,2,1,0:T(8,128)(2,1)S(1)} %pad_maximum_fusion.7), channel_id=1, source_target_pairs={{0,4},{4,0},{8,12},{12,8},{16,20},{20,16},{24,28},{28,24},{1,5},{5... | collective-permute-start | bytes 1966088 | tf_op jit(solution)/shard_map/ppermute | solution.py:734
  115.9 13.2 %collective-permute-start.39 = (bf16[256,1024]{1,0:T(8,128)(2,1)S(1)}, bf16[256,1024]{1,0:T(8,128)(2,1)S(1)}, u32[]{:S(2)}, u32[]{:S(2)}) collective-permute-start(bf16[256,1024]{1,0:T(8,128)(2,1)S(1)} %get-tuple-element.300.refs_2_.refs_12_), channel_id=1, source_target_pairs={{0,2},{1,3},{2,0},{3,1},{4,6},{5,7},{6,4},{7,5},{8,10},{9,11},{10,... | collective-permute-start | bytes 1572872 | tf_op jit(solution)/shard_map/ppermute | solution.py:635
  117.4 10.1 %collective-permute-start.37 = (bf16[2,8,16,512]{3,2,1,0:T(8,128)(2,1)S(1)}, bf16[2,8,16,512]{3,2,1,0:T(8,128)(2,1)S(1)}, u32[]{:S(2)}, u32[]{:S(2)}) collective-permute-start(bf16[2,8,16,512]{3,2,1,0:T(8,128)(2,1)S(1)} %pad_maximum_fusion.19), channel_id=1, source_target_pairs={{0,8},{4,12},{8,0},{12,4},{16,24},{20,28},{24,16},{28,20},{1,9},{5... | collective-permute-start | bytes 786440 | tf_op jit(solution)/shard_map/ppermute | solution.py:734
  131.4 13.7 %collective-permute-start.43 = (bf16[4,4,16,512]{3,2,1,0:T(8,128)(2,1)S(1)}, bf16[4,4,16,512]{3,2,1,0:T(8,128)(2,1)S(1)}, u32[]{:S(2)}, u32[]{:S(2)}) collective-permute-start(bf16[4,4,16,512]{3,2,1,0:T(8,128)(2,1)S(1)} %get-tuple-element.516), channel_id=1, source_target_pairs={{0,2},{1,3},{2,0},{3,1},{4,6},{5,7},{6,4},{7,5},{8,10},{9,11},{10,... | collective-permute-start | bytes 786440 | tf_op jit(solution)/shard_map/ppermute | solution.py:734
  133.4 12.5 %collective-permute-start.44 = (bf16[4,4,16,512]{3,2,1,0:T(8,128)(2,1)S(1)}, bf16[4,4,16,512]{3,2,1,0:T(8,128)(2,1)S(1)}, u32[]{:S(2)}, u32[]{:S(2)}) collective-permute-start(bf16[4,4,16,512]{3,2,1,0:T(8,128)(2,1)S(1)} %pad_maximum_fusion.20), channel_id=1, source_target_pairs={{0,2},{1,3},{2,0},{3,1},{4,6},{5,7},{6,4},{7,5},{8,10},{9,11},{10,... | collective-permute-start | bytes 786440 | tf_op jit(solution)/shard_map/ppermute | solution.py:734
  134.5 11.4 %collective-permute-start.45 = (bf16[4,4,16,512]{3,2,1,0:T(8,128)(2,1)S(1)}, bf16[4,4,16,512]{3,2,1,0:T(8,128)(2,1)S(1)}, u32[]{:S(2)}, u32[]{:S(2)}) collective-permute-start(bf16[4,4,16,512]{3,2,1,0:T(8,128)(2,1)S(1)} %get-tuple-element.515), channel_id=1, source_target_pairs={{0,4},{4,0},{8,12},{12,8},{16,20},{20,16},{24,28},{28,24},{1,5},{5... | collective-permute-start | bytes 786440 | tf_op jit(solution)/shard_map/ppermute | solution.py:734
  146.0 18.9 %collective-permute-start.46 = (bf16[8,4,16,512]{3,2,1,0:T(8,128)(2,1)S(1)}, bf16[8,4,16,512]{3,2,1,0:T(8,128)(2,1)S(1)}, u32[]{:S(2)}, u32[]{:S(2)}) collective-permute-start(bf16[8,4,16,512]{3,2,1,0:T(8,128)(2,1)S(1)} %pad_maximum_fusion.10), channel_id=1, source_target_pairs={{0,4},{4,0},{8,12},{12,8},{16,20},{20,16},{24,28},{28,24},{1,5},{5... | collective-permute-start | bytes 1572872 | tf_op jit(solution)/shard_map/ppermute | solution.py:734
  147.4 17.4 %collective-permute-start.47 = (bf16[8,4,16,512]{3,2,1,0:T(8,128)(2,1)S(1)}, bf16[8,4,16,512]{3,2,1,0:T(8,128)(2,1)S(1)}, u32[]{:S(2)}, u32[]{:S(2)}) collective-permute-start(bf16[8,4,16,512]{3,2,1,0:T(8,128)(2,1)S(1)} %pad_maximum_fusion.11), channel_id=1, source_target_pairs={{0,8},{4,12},{8,0},{12,4},{16,24},{20,28},{24,16},{28,20},{1,9},{5... | collective-permute-start | bytes 1572872 | tf_op jit(solution)/shard_map/ppermute | solution.py:734
  150.1 14.8 %collective-permute-start.48 = (bf16[8,4,16,512]{3,2,1,0:T(8,128)(2,1)S(1)}, bf16[8,4,16,512]{3,2,1,0:T(8,128)(2,1)S(1)}, u32[]{:S(2)}, u32[]{:S(2)}) collective-permute-start(bf16[8,4,16,512]{3,2,1,0:T(8,128)(2,1)S(1)} %pad_maximum_fusion.12), channel_id=1, source_target_pairs={{0,2},{1,3},{2,0},{3,1},{4,6},{5,7},{6,4},{7,5},{8,10},{9,11},{10,... | collective-permute-start | bytes 1572872 | tf_op jit(solution)/shard_map/ppermute | solution.py:734
  150.5 14.4 %collective-permute-start.49 = (f32[32,640]{1,0:T(8,128)S(1)}, f32[32,640]{1,0:T(8,128)S(1)}, u32[]{:S(2)}, u32[]{:S(2)}) collective-permute-start(f32[32,640]{1,0:T(8,128)S(1)} %get-tuple-element.312.refs_1_), channel_id=1, source_target_pairs={{0,2},{1,3},{2,0},{3,1},{4,6},{5,7},{6,4},{7,5},{8,10},{9,11},{10,... | collective-permute-start | bytes 245768 | tf_op jit(solution)/shard_map/ppermute | solution.py:635
  194.3 16.8 %collective-permute-start.58 = (bf16[8,5,16,512]{3,2,1,0:T(8,128)(2,1)S(1)}, bf16[8,5,16,512]{3,2,1,0:T(8,128)(2,1)S(1)}, u32[]{:S(2)}, u32[]{:S(2)}) collective-permute-start(bf16[8,5,16,512]{3,2,1,0:T(8,128)(2,1)S(1)} %slice.805), channel_id=1, source_target_pairs={{0,4},{4,0},{8,12},{12,8},{16,20},{20,16},{24,28},{28,24},{1,5},{5... | collective-permute-start | bytes 1966088 | tf_op jit(solution)/shard_map/ppermute | solution.py:734
  195.5 16.6 %collective-permute-start.59 = (bf16[8,5,16,512]{3,2,1,0:T(8,128)(2,1)S(1)}, bf16[8,5,16,512]{3,2,1,0:T(8,128)(2,1)S(1)}, u32[]{:S(2)}, u32[]{:S(2)}) collective-permute-start(bf16[8,5,16,512]{3,2,1,0:T(8,128)(2,1)S(1)} %slice.806), channel_id=1, source_target_pairs={{0,8},{4,12},{8,0},{12,4},{16,24},{20,28},{24,16},{28,20},{1,9},{5... | collective-permute-start | bytes 1966088 | tf_op jit(solution)/shard_map/ppermute | solution.py:734
  212.0 14.3 %collective-permute-start.65 = (bf16[16,5,16,512]{3,2,1,0:T(8,128)(2,1)S(1)}, bf16[16,5,16,512]{3,2,1,0:T(8,128)(2,1)S(1)}, u32[]{:S(2)}, u32[]{:S(2)}) collective-permute-start(bf16[16,5,16,512]{3,2,1,0:T(8,128)(2,1)S(1)} %get-tuple-element.356), channel_id=1, source_target_pairs={{0,1},{1,0},{2,3},{3,2},{4,5},{5,4},{6,7},{7,6},{8,9},{9,8},{10,11... | collective-permute-start | bytes 3932168 | tf_op jit(solution)/shard_map/ppermute | solution.py:734
  212.4 14.0 %collective-permute-start.63 = (bf16[4,5,16,512]{3,2,1,0:T(8,128)(2,1)S(1)}, bf16[4,5,16,512]{3,2,1,0:T(8,128)(2,1)S(1)}, u32[]{:S(2)}, u32[]{:S(2)}) collective-permute-start(bf16[4,5,16,512]{3,2,1,0:T(8,128)(2,1)S(1)} %slice.808), channel_id=1, source_target_pairs={{0,8},{4,12},{8,0},{12,4},{16,24},{20,28},{24,16},{28,20},{1,9},{5... | collective-permute-start | bytes 983048 | tf_op jit(solution)/shard_map/ppermute | solution.py:734
  213.5 12.8 %collective-permute-start.64 = (bf16[4,5,16,512]{3,2,1,0:T(8,128)(2,1)S(1)}, bf16[4,5,16,512]{3,2,1,0:T(8,128)(2,1)S(1)}, u32[]{:S(2)}, u32[]{:S(2)}) collective-permute-start(bf16[4,5,16,512]{3,2,1,0:T(8,128)(2,1)S(1)} %slice.810), channel_id=1, source_target_pairs={{0,4},{4,0},{8,12},{12,8},{16,20},{20,16},{24,28},{28,24},{1,5},{5... | collective-permute-start | bytes 983048 | tf_op jit(solution)/shard_map/ppermute | solution.py:734
  227.1 20.6 %collective-permute-start.70 = (bf16[8,5,16,512]{3,2,1,0:T(8,128)(2,1)S(1)}, bf16[8,5,16,512]{3,2,1,0:T(8,128)(2,1)S(1)}, u32[]{:S(2)}, u32[]{:S(2)}) collective-permute-start(bf16[8,5,16,512]{3,2,1,0:T(8,128)(2,1)S(1)} %slice.815), channel_id=1, source_target_pairs={{0,4},{4,0},{8,12},{12,8},{16,20},{20,16},{24,28},{28,24},{1,5},{5... | collective-permute-start | bytes 1966088 | tf_op jit(solution)/shard_map/ppermute | solution.py:734
  229.4 18.3 %collective-permute-start.72 = (bf16[288,1024]{1,0:T(8,128)(2,1)S(1)}, bf16[288,1024]{1,0:T(8,128)(2,1)S(1)}, u32[]{:S(2)}, u32[]{:S(2)}) collective-permute-start(bf16[288,1024]{1,0:T(8,128)(2,1)S(1)} %add_convert_fusion.17.refs_5_), channel_id=1, source_target_pairs={{0,2},{1,3},{2,0},{3,1},{4,6},{5,7},{6,4},{7,5},{8,10},{9,11},{10,... | collective-permute-start | bytes 1769480 | tf_op jit(solution)/shard_map/ppermute | solution.py:635
  230.2 14.8 %collective-permute-start.68 = (bf16[2,5,16,512]{3,2,1,0:T(8,128)(2,1)S(1)}, bf16[2,5,16,512]{3,2,1,0:T(8,128)(2,1)S(1)}, u32[]{:S(2)}, u32[]{:S(2)}) collective-permute-start(bf16[2,5,16,512]{3,2,1,0:T(8,128)(2,1)S(1)} %slice.812), channel_id=1, source_target_pairs={{0,16},{4,20},{8,24},{12,28},{16,0},{20,4},{24,8},{28,12},{1,17},{... | collective-permute-start | bytes 491528 | tf_op jit(solution)/shard_map/ppermute | solution.py:734
  232.8 14.9 %collective-permute-start.69 = (bf16[2,5,16,512]{3,2,1,0:T(8,128)(2,1)S(1)}, bf16[2,5,16,512]{3,2,1,0:T(8,128)(2,1)S(1)}, u32[]{:S(2)}, u32[]{:S(2)}) collective-permute-start(bf16[2,5,16,512]{3,2,1,0:T(8,128)(2,1)S(1)} %slice.814), channel_id=1, source_target_pairs={{0,16},{4,20},{8,24},{12,28},{16,0},{20,4},{24,8},{28,12},{1,17},{... | collective-permute-start | bytes 491528 | tf_op jit(solution)/shard_map/ppermute | solution.py:734
  247.8 17.0 %collective-permute-start.73 = (bf16[1,5,16,512]{3,2,1,0:T(8,128)(2,1)S(1)}, bf16[1,5,16,512]{3,2,1,0:T(8,128)(2,1)S(1)}, u32[]{:S(2)}, u32[]{:S(2)}) collective-permute-start(bf16[1,5,16,512]{3,2,1,0:T(8,128)(2,1)S(1)} %slice.817), channel_id=1, source_target_pairs={{0,2},{1,3},{2,0},{3,1},{4,6},{5,7},{6,4},{7,5},{8,10},{9,11},{10,... | collective-permute-start | bytes 245768 | tf_op jit(solution)/shard_map/ppermute | solution.py:734
  249.3 15.5 %collective-permute-start.74 = (bf16[1,5,16,512]{3,2,1,0:T(8,128)(2,1)S(1)}, bf16[1,5,16,512]{3,2,1,0:T(8,128)(2,1)S(1)}, u32[]{:S(2)}, u32[]{:S(2)}) collective-permute-start(bf16[1,5,16,512]{3,2,1,0:T(8,128)(2,1)S(1)} %slice.819), channel_id=1, source_target_pairs={{0,2},{1,3},{2,0},{3,1},{4,6},{5,7},{6,4},{7,5},{8,10},{9,11},{10,... | collective-permute-start | bytes 245768 | tf_op jit(solution)/shard_map/ppermute | solution.py:734
  250.2 14.5 %collective-permute-start.75 = (bf16[4,5,16,512]{3,2,1,0:T(8,128)(2,1)S(1)}, bf16[4,5,16,512]{3,2,1,0:T(8,128)(2,1)S(1)}, u32[]{:S(2)}, u32[]{:S(2)}) collective-permute-start(bf16[4,5,16,512]{3,2,1,0:T(8,128)(2,1)S(1)} %slice.821), channel_id=1, source_target_pairs={{0,8},{4,12},{8,0},{12,4},{16,24},{20,28},{24,16},{28,20},{1,9},{5... | collective-permute-start | bytes 983048 | tf_op jit(solution)/shard_map/ppermute | solution.py:734
  253.1 16.8 %collective-permute-start.78 = (bf16[16,5,16,512]{3,2,1,0:T(8,128)(2,1)S(1)}, bf16[16,5,16,512]{3,2,1,0:T(8,128)(2,1)S(1)}, u32[]{:S(2)}, u32[]{:S(2)}) collective-permute-start(bf16[16,5,16,512]{3,2,1,0:T(8,128)(2,1)S(1)} %get-tuple-element.399), channel_id=1, source_target_pairs={{0,1},{1,0},{2,3},{3,2},{4,5},{5,4},{6,7},{7,6},{8,9},{9,8},{10,11... | collective-permute-start | bytes 3932168 | tf_op jit(solution)/shard_map/ppermute | solution.py:734
  270.4 17.1 %collective-permute-start.80 = (bf16[8,5,16,512]{3,2,1,0:T(8,128)(2,1)S(1)}, bf16[8,5,16,512]{3,2,1,0:T(8,128)(2,1)S(1)}, u32[]{:S(2)}, u32[]{:S(2)}) collective-permute-start(bf16[8,5,16,512]{3,2,1,0:T(8,128)(2,1)S(1)} %slice.822), channel_id=1, source_target_pairs={{0,4},{4,0},{8,12},{12,8},{16,20},{20,16},{24,28},{28,24},{1,5},{5... | collective-permute-start | bytes 1966088 | tf_op jit(solution)/shard_map/ppermute | solution.py:734
  272.0 20.5 %collective-permute-start.81 = (bf16[8,5,16,512]{3,2,1,0:T(8,128)(2,1)S(1)}, bf16[8,5,16,512]{3,2,1,0:T(8,128)(2,1)S(1)}, u32[]{:S(2)}, u32[]{:S(2)}) collective-permute-start(bf16[8,5,16,512]{3,2,1,0:T(8,128)(2,1)S(1)} %slice.823), channel_id=1, source_target_pairs={{0,8},{4,12},{8,0},{12,4},{16,24},{20,28},{24,16},{28,20},{1,9},{5... | collective-permute-start | bytes 1966088 | tf_op jit(solution)/shard_map/ppermute | solution.py:734
  282.2 26.3 %collective-permute-start.91 = (bf16[2,5,16,512]{3,2,1,0:T(8,128)(2,1)S(1)}, bf16[2,5,16,512]{3,2,1,0:T(8,128)(2,1)S(1)}, u32[]{:S(2)}, u32[]{:S(2)}) collective-permute-start(bf16[2,5,16,512]{3,2,1,0:T(8,128)(2,1)S(1)} %slice.830), channel_id=1, source_target_pairs={{0,16},{4,20},{8,24},{12,28},{16,0},{20,4},{24,8},{28,12},{1,17},{... | collective-permute-start | bytes 491528 | tf_op jit(solution)/shard_map/ppermute | solution.py:734
  292.5 17.9 %collective-permute-start.89 = (bf16[16,5,16,512]{3,2,1,0:T(8,128)(2,1)S(1)}, bf16[16,5,16,512]{3,2,1,0:T(8,128)(2,1)S(1)}, u32[]{:S(2)}, u32[]{:S(2)}) collective-permute-start(bf16[16,5,16,512]{3,2,1,0:T(8,128)(2,1)S(1)} %get-tuple-element.431), channel_id=1, source_target_pairs={{0,1},{1,0},{2,3},{3,2},{4,5},{5,4},{6,7},{7,6},{8,9},{9,8},{10,11... | collective-permute-start | bytes 3932168 | tf_op jit(solution)/shard_map/ppermute | solution.py:734
  293.1 17.2 %collective-permute-start.90 = (bf16[8,5,16,512]{3,2,1,0:T(8,128)(2,1)S(1)}, bf16[8,5,16,512]{3,2,1,0:T(8,128)(2,1)S(1)}, u32[]{:S(2)}, u32[]{:S(2)}) collective-permute-start(bf16[8,5,16,512]{3,2,1,0:T(8,128)(2,1)S(1)} %slice.828), channel_id=1, source_target_pairs={{0,2},{1,3},{2,0},{3,1},{4,6},{5,7},{6,4},{7,5},{8,10},{9,11},{10,... | collective-permute-start | bytes 1966088 | tf_op jit(solution)/shard_map/ppermute | solution.py:734
  296.1 14.2 %collective-permute-start.87 = (bf16[4,5,16,512]{3,2,1,0:T(8,128)(2,1)S(1)}, bf16[4,5,16,512]{3,2,1,0:T(8,128)(2,1)S(1)}, u32[]{:S(2)}, u32[]{:S(2)}) collective-permute-start(bf16[4,5,16,512]{3,2,1,0:T(8,128)(2,1)S(1)} %slice.825), channel_id=1, source_target_pairs={{0,8},{4,12},{8,0},{12,4},{16,24},{20,28},{24,16},{28,20},{1,9},{5... | collective-permute-start | bytes 983048 | tf_op jit(solution)/shard_map/ppermute | solution.py:734
  296.3 14.0 %collective-permute-start.88 = (bf16[4,5,16,512]{3,2,1,0:T(8,128)(2,1)S(1)}, bf16[4,5,16,512]{3,2,1,0:T(8,128)(2,1)S(1)}, u32[]{:S(2)}, u32[]{:S(2)}) collective-permute-start(bf16[4,5,16,512]{3,2,1,0:T(8,128)(2,1)S(1)} %slice.827), channel_id=1, source_target_pairs={{0,4},{4,0},{8,12},{12,8},{16,20},{20,16},{24,28},{28,24},{1,5},{5... | collective-permute-start | bytes 983048 | tf_op jit(solution)/shard_map/ppermute | solution.py:734
  310.6 11.2 %collective-permute-start.93 = (bf16[2,5,16,512]{3,2,1,0:T(8,128)(2,1)S(1)}, bf16[2,5,16,512]{3,2,1,0:T(8,128)(2,1)S(1)}, u32[]{:S(2)}, u32[]{:S(2)}) collective-permute-start(bf16[2,5,16,512]{3,2,1,0:T(8,128)(2,1)S(1)} %slice.832), channel_id=1, source_target_pairs={{0,16},{4,20},{8,24},{12,28},{16,0},{20,4},{24,8},{28,12},{1,17},{... | collective-permute-start | bytes 491528 | tf_op jit(solution)/shard_map/ppermute | solution.py:734
  313.0 20.8 %collective-permute-start.95 = (bf16[8,5,16,512]{3,2,1,0:T(8,128)(2,1)S(1)}, bf16[8,5,16,512]{3,2,1,0:T(8,128)(2,1)S(1)}, u32[]{:S(2)}, u32[]{:S(2)}) collective-permute-start(bf16[8,5,16,512]{3,2,1,0:T(8,128)(2,1)S(1)} %slice.835), channel_id=1, source_target_pairs={{0,4},{4,0},{8,12},{12,8},{16,20},{20,16},{24,28},{28,24},{1,5},{5... | collective-permute-start | bytes 1966088 | tf_op jit(solution)/shard_map/ppermute | solution.py:734
  313.9 19.8 %collective-permute-start.97 = (bf16[16,3,16,512]{3,2,1,0:T(8,128)(2,1)S(1)}, bf16[16,3,16,512]{3,2,1,0:T(8,128)(2,1)S(1)}, u32[]{:S(2)}, u32[]{:S(2)}) collective-permute-start(bf16[16,3,16,512]{3,2,1,0:T(8,128)(2,1)S(1)} %get-tuple-element.445), channel_id=1, source_target_pairs={{0,1},{1,0},{2,3},{3,2},{4,5},{5,4},{6,7},{7,6},{8,9},{9,8},{10,11... | collective-permute-start | bytes 2359304 | tf_op jit(solution)/shard_map/ppermute | solution.py:734
  314.2 19.6 %collective-permute-start.98 = (bf16[288,1024]{1,0:T(8,128)(2,1)S(1)}, bf16[288,1024]{1,0:T(8,128)(2,1)S(1)}, u32[]{:S(2)}, u32[]{:S(2)}) collective-permute-start(bf16[288,1024]{1,0:T(8,128)(2,1)S(1)} %add_convert_fusion.16.refs_5_), channel_id=1, source_target_pairs={{0,2},{1,3},{2,0},{3,1},{4,6},{5,7},{6,4},{7,5},{8,10},{9,11},{10,... | collective-permute-start | bytes 1769480 | tf_op jit(solution)/shard_map/ppermute | solution.py:635
  315.8 18.0 %collective-permute-start.96 = (bf16[4,5,16,512]{3,2,1,0:T(8,128)(2,1)S(1)}, bf16[4,5,16,512]{3,2,1,0:T(8,128)(2,1)S(1)}, u32[]{:S(2)}, u32[]{:S(2)}) collective-permute-start(bf16[4,5,16,512]{3,2,1,0:T(8,128)(2,1)S(1)} %slice.837), channel_id=1, source_target_pairs={{0,8},{4,12},{8,0},{12,4},{16,24},{20,28},{24,16},{28,20},{1,9},{5... | collective-permute-start | bytes 983048 | tf_op jit(solution)/shard_map/ppermute | solution.py:734
  321.8 10.4 %collective-permute-start.94 = (bf16[2,5,16,512]{3,2,1,0:T(8,128)(2,1)S(1)}, bf16[2,5,16,512]{3,2,1,0:T(8,128)(2,1)S(1)}, u32[]{:S(2)}, u32[]{:S(2)}) collective-permute-start(bf16[2,5,16,512]{3,2,1,0:T(8,128)(2,1)S(1)} %slice.834), channel_id=1, source_target_pairs={{0,16},{4,20},{8,24},{12,28},{16,0},{20,4},{24,8},{28,12},{1,17},{... | collective-permute-start | bytes 491528 | tf_op jit(solution)/shard_map/ppermute | solution.py:734
  334.0 15.8 %collective-permute-start.99 = (bf16[4,5,16,512]{3,2,1,0:T(8,128)(2,1)S(1)}, bf16[4,5,16,512]{3,2,1,0:T(8,128)(2,1)S(1)}, u32[]{:S(2)}, u32[]{:S(2)}) collective-permute-start(bf16[4,5,16,512]{3,2,1,0:T(8,128)(2,1)S(1)} %slice.840), channel_id=1, source_target_pairs={{0,2},{1,3},{2,0},{3,1},{4,6},{5,7},{6,4},{7,5},{8,10},{9,11},{10,... | collective-permute-start | bytes 983048 | tf_op jit(solution)/shard_map/ppermute | solution.py:734
  334.9 14.9 %collective-permute-start.100 = (bf16[8,3,16,512]{3,2,1,0:T(8,128)(2,1)S(1)}, bf16[8,3,16,512]{3,2,1,0:T(8,128)(2,1)S(1)}, u32[]{:S(2)}, u32[]{:S(2)}) collective-permute-start(bf16[8,3,16,512]{3,2,1,0:T(8,128)(2,1)S(1)} %slice.841), channel_id=1, source_target_pairs={{0,4},{4,0},{8,12},{12,8},{16,20},{20,16},{24,28},{28,24},{1,5},{5... | collective-permute-start | bytes 1179656 | tf_op jit(solution)/shard_map/ppermute | solution.py:734
  338.4 11.5 %collective-permute-start.104 = (bf16[16,3,16,512]{3,2,1,0:T(8,128)(2,1)S(1)}, bf16[16,3,16,512]{3,2,1,0:T(8,128)(2,1)S(1)}, u32[]{:S(2)}, u32[]{:S(2)}) collective-permute-start(bf16[16,3,16,512]{3,2,1,0:T(8,128)(2,1)S(1)} %get-tuple-element.465), channel_id=1, source_target_pairs={{0,1},{1,0},{2,3},{3,2},{4,5},{5,4},{6,7},{7,6},{8,9},{9,8},{10,11... | collective-permute-start | bytes 2359304 | tf_op jit(solution)/shard_map/ppermute | solution.py:734
  350.2 17.7 %collective-permute-start.106 = (bf16[4,3,16,512]{3,2,1,0:T(8,128)(2,1)S(1)}, bf16[4,3,16,512]{3,2,1,0:T(8,128)(2,1)S(1)}, u32[]{:S(2)}, u32[]{:S(2)}) collective-permute-start(bf16[4,3,16,512]{3,2,1,0:T(8,128)(2,1)S(1)} %get-tuple-element.514), channel_id=1, source_target_pairs={{0,2},{1,3},{2,0},{3,1},{4,6},{5,7},{6,4},{7,5},{8,10},{9,11},{10,... | collective-permute-start | bytes 589832 | tf_op jit(solution)/shard_map/ppermute | solution.py:734
  351.2 16.8 %collective-permute-start.107 = (bf16[4,3,16,512]{3,2,1,0:T(8,128)(2,1)S(1)}, bf16[4,3,16,512]{3,2,1,0:T(8,128)(2,1)S(1)}, u32[]{:S(2)}, u32[]{:S(2)}) collective-permute-start(bf16[4,3,16,512]{3,2,1,0:T(8,128)(2,1)S(1)} %get-tuple-element.513), channel_id=1, source_target_pairs={{0,4},{4,0},{8,12},{12,8},{16,20},{20,16},{24,28},{28,24},{1,5},{5... | collective-permute-start | bytes 589832 | tf_op jit(solution)/shard_map/ppermute | solution.py:734
  352.0 16.0 %collective-permute-start.108 = (bf16[4,3,16,512]{3,2,1,0:T(8,128)(2,1)S(1)}, bf16[4,3,16,512]{3,2,1,0:T(8,128)(2,1)S(1)}, u32[]{:S(2)}, u32[]{:S(2)}) collective-permute-start(bf16[4,3,16,512]{3,2,1,0:T(8,128)(2,1)S(1)} %get-tuple-element.512), channel_id=1, source_target_pairs={{0,6},{1,7},{2,4},{3,5},{4,2},{5,3},{6,0},{7,1},{8,14},{9,15},{10,... | collective-permute-start | bytes 589832 | tf_op jit(solution)/shard_map/ppermute | solution.py:732
  354.0 14.0 %collective-permute-start.109 = (bf16[4,3,16,512]{3,2,1,0:T(8,128)(2,1)S(1)}, bf16[4,3,16,512]{3,2,1,0:T(8,128)(2,1)S(1)}, u32[]{:S(2)}, u32[]{:S(2)}) collective-permute-start(bf16[4,3,16,512]{3,2,1,0:T(8,128)(2,1)S(1)} %slice.855), channel_id=1, source_target_pairs={{0,2},{1,3},{2,0},{3,1},{4,6},{5,7},{6,4},{7,5},{8,10},{9,11},{10,... | collective-permute-start | bytes 589832 | tf_op jit(solution)/shard_map/ppermute | solution.py:734
  368.2 10.8 %collective-permute-start.112 = (bf16[1,6,16,512]{3,2,1,0:T(8,128)(2,1)S(1)}, bf16[1,6,16,512]{3,2,1,0:T(8,128)(2,1)S(1)}, u32[]{:S(2)}, u32[]{:S(2)}) collective-permute-start(bf16[1,6,16,512]{3,2,1,0:T(8,128)(2,1)S(1)} %pad_maximum_fusion.30), channel_id=1, source_target_pairs={{0,16},{4,20},{8,24},{12,28},{16,0},{20,4},{24,8},{28,12},{1,17},{... | collective-permute-start | bytes 294920 | tf_op jit(solution)/shard_map/ppermute | solution.py:734
  368.3 10.7 %collective-permute-start.113 = (bf16[1,6,16,512]{3,2,1,0:T(8,128)(2,1)S(1)}, bf16[1,6,16,512]{3,2,1,0:T(8,128)(2,1)S(1)}, u32[]{:S(2)}, u32[]{:S(2)}) collective-permute-start(bf16[1,6,16,512]{3,2,1,0:T(8,128)(2,1)S(1)} %pad_maximum_fusion.31), channel_id=1, source_target_pairs={{0,8},{4,12},{8,0},{12,4},{16,24},{20,28},{24,16},{28,20},{1,9},{5... | collective-permute-start | bytes 294920 | tf_op jit(solution)/shard_map/ppermute | solution.py:734
  (75 other events, 392.6 us)

commit v7 on v6

--- a/solution.py
+++ b/solution.py
@@ -623,7 +623,7 @@
         + made_shapes,
         input_output_aliases=aliases,
         compiler_params=pltpu.CompilerParams(vmem_limit_bytes=VMEM_LIMIT),
-        cost_estimate=pl.CostEstimate(flops=int(cost * 3.3e8), bytes_accessed=0, transcendentals=0),
+        cost_estimate=pl.CostEstimate(flops=int(cost * 1.1e9), bytes_accessed=0, transcendentals=0),
         name=name,
     )(*ins, *operands, *goals)
     made = [results[begin : begin + halves] for _, halves, begin, _ in groups]

time: 389 us -> 385 us (0.990)
  starting transfers between devices: 109 us -> 105 us
  transfers between devices with their start and end apart: 116 -> 116, of which waited for: 51 -> 46; matrix products, arithmetic and copies ran while one was open for 3% -> 3% of each run, Pallas kernels for 20% -> 20%
where the time goes in v7:
time: 385 us; the launch traced here: 378 us
  waiting for transfers between devices  159 us (41%)
  starting transfers between devices  105 us (27%)
  Pallas kernels  95.1 us (25%)
  other arithmetic  11.9 us (3%)
  local copies, waits for them, and re-layouts  3.92 us (1%)
    ppermute x86, waiting for transfers between devices, swapped(): lax.ppermute(value, axis, [(source, source ^ 1 << bit) for source in rang...  118 us
    pallas_call x13, Pallas kernels, call(): pl.pallas_call(body, out_shape=shapes + [jax.ShapeDtypeStruct(shape, kind...  92.5 us
    ppermute x86, starting transfers between devices, swapped(): lax.ppermute(value, axis, [(source, source ^ 1 << bit) for source in rang...  84.2 us
    ppermute x28, waiting for transfers between devices, flipped(): lax.ppermute(value, 'blk', [(source, source ^ bit) for source in range(si...  40.7 us
    ppermute x28, starting transfers between devices, flipped(): lax.ppermute(value, 'blk', [(source, source ^ bit) for source in range(si...  17.5 us
  transfers between devices with their start and end apart: 116, of which 46 were waited for; matrix products, arithmetic and copies ran while one was open for 3% of the time, Pallas kernels for 20%

profile of v7, /device:TPU:0, one launch (start us, length us, event | category | flops | bytes accessed | tf_op | source)
XLA Modules:
  0.0 377.6 jit_solution(639883542395501326)
XLA Ops:
  0.7 1.8 pack.1
  2.5 4.1 %collective-permute-start = (bf16[1,4,16,512]{3,2,1,0:T(8,128)(2,1)}, bf16[1,4,16,512]{3,2,1,0:T(8,128)(2,1)S(1)}, u32[]{:S(2)}, u32[]{:S(2)}) collective-permute-start(bf16[1,4,16,512]{3,2,1,0:T(8,128)(2,1)} %bitcast.258), channel_id=1, source_target_pairs={{0,16},{4,20},{8,24},{12,28},{16,0},{20,4},{24,8},{28,12},{1,17},{... | collective-permute-start | bytes 196616 | tf_op jit(solution)/shard_map/ppermute | solution.py:734
  6.9 3.6 collective-permute-done
  10.5 3.5 collective-permute-done.1
  16.4 1.7 collective-permute-start.4
  18.2 1.8 collective-permute-start.5
  20.9 2.8 collective-permute-done.5
  24.5 2.0 collective-permute-start.6
  26.6 1.6 collective-permute-start.7
  28.2 1.6 collective-permute-start.9
  31.8 8.9 %collective-permute-done.8 = bf16[1,5,16,512]{3,2,1,0:T(8,128)(2,1)S(1)} collective-permute-done((bf16[1,5,16,512]{3,2,1,0:T(8,128)(2,1)S(1)}, bf16[1,5,16,512]{3,2,1,0:T(8,128)(2,1)S(1)}, u32[]{:S(2)}, u32[]{:S(2)}) %collective-permute-start.8) | collective-permute-done | bytes 81952 | tf_op jit(solution)/shard_map/ppermute | solution.py:734
  42.4 2.5 collective-permute-start.14
  45.1 1.6 collective-permute-done.15
  46.7 9.6 %collective-permute-done.13 = bf16[2,5,16,512]{3,2,1,0:T(8,128)(2,1)S(1)} collective-permute-done((bf16[2,5,16,512]{3,2,1,0:T(8,128)(2,1)S(1)}, bf16[2,5,16,512]{3,2,1,0:T(8,128)(2,1)S(1)}, u32[]{:S(2)}, u32[]{:S(2)}) %collective-permute-start.13) | collective-permute-done | bytes 163872 | tf_op jit(solution)/shard_map/ppermute | solution.py:734
  58.7 2.2 collective-permute-done.16.refs_2_.refs_16_
  60.9 2.6 first.1
  66.1 2.4 collective-permute-start.20
  70.1 2.3 collective-permute-done.20
  72.4 3.1 collective-permute-done.18
  75.5 2.0 collective-permute-done.21.refs_4_.refs_14_
  79.5 3.0 collective-permute-start.26
  82.6 9.1 %attend_0.1 = (bf16[288,512]{1,0:T(8,128)(2,1)S(1)}, f32[4,576]{1,0:T(4,128)S(1)}, f32[288,512]{1,0:T(8,128)S(1)}, f32[288,512]{1,0:T(8,128)S(1)}, bf16[32,512]{...) custom-call(f32[288,512]{1,0:T(8,128)S(1)} %get-tuple-element.267.refs_0_,, ...), custom_call_target="tpu_custom_call" | custom-call | flops 14300000256 | tf_op jit(solution)/shard_map/attend_0/pallas_call | solution.py:616
  91.6 1.8 collective-permute-start.27
  93.5 3.1 collective-permute-done.27.refs_3_
  98.7 5.5 %collective-permute-done.28.refs_2_ = f32[32,640]{1,0:T(8,128)S(1)} collective-permute-done((f32[32,640]{1,0:T(8,128)S(1)}, f32[32,640]{1,0:T(8,128)S(1)}, u32[]{:S(2)}, u32[]{:S(2)}) %collective-permute-start.28) | collective-permute-done | bytes 81952 | tf_op jit(solution)/shard_map/ppermute | solution.py:635
  105.8 1.6 collective-permute-start.33
  107.4 7.1 %finish_0.1 = (f32[288,512]{1,0:T(8,128)S(1)}, bf16[288,512]{1,0:T(8,128)(2,1)S(1)}, bf16[256,1024]{1,0:T(8,128)(2,1)S(1)}, bf16[32,1024]{1,0:T(8,128)(2,1)S(1)}...) custom-call(f32[288,512]{1,0:T(8,128)S(1)} %get-tuple-element.279.re, ...), custom_call_target="tpu_custom_call" | custom-call | flops 11000000512 | tf_op jit(solution)/shard_map/finish_0/pallas_call | solution.py:616
  119.7 2.6 collective-permute-start.38
  122.3 4.7 %collective-permute-done.38 = bf16[2,4,16,512]{3,2,1,0:T(8,128)(2,1)S(1)} collective-permute-done((bf16[2,4,16,512]{3,2,1,0:T(8,128)(2,1)S(1)}, bf16[2,4,16,512]{3,2,1,0:T(8,128)(2,1)S(1)}, u32[]{:S(2)}, u32[]{:S(2)}) %collective-permute-start.38) | collective-permute-done | bytes 131104 | tf_op jit(solution)/shard_map/ppermute | solution.py:734
  128.9 1.7 collective-permute-done.36
  135.9 9.0 %attend_1.1 = (bf16[288,512]{1,0:T(8,128)(2,1)S(1)}, f32[4,576]{1,0:T(4,128)S(1)}, f32[288,512]{1,0:T(8,128)S(1)}, f32[288,512]{1,0:T(8,128)S(1)}, bf16[32,512]{...) custom-call(f32[288,512]{1,0:T(8,128)S(1)} %get-tuple-element.290.refs_0_,, ...), custom_call_target="tpu_custom_call" | custom-call | flops 14300000256 | tf_op jit(solution)/shard_map/attend_1/pallas_call | solution.py:616
  147.4 2.7 collective-permute-start.47
  150.7 1.6 collective-permute-start.49
  152.4 12.5 %collective-permute-done.49.refs_3_ = f32[32,640]{1,0:T(8,128)S(1)} collective-permute-done((f32[32,640]{1,0:T(8,128)S(1)}, f32[32,640]{1,0:T(8,128)S(1)}, u32[]{:S(2)}, u32[]{:S(2)}) %collective-permute-start.49) | collective-permute-done | bytes 81952 | tf_op jit(solution)/shard_map/ppermute | solution.py:635
  166.6 4.3 %collective-permute-done.50.refs_2_ = f32[32,640]{1,0:T(8,128)S(1)} collective-permute-done((f32[32,640]{1,0:T(8,128)S(1)}, f32[32,640]{1,0:T(8,128)S(1)}, u32[]{:S(2)}, u32[]{:S(2)}) %collective-permute-start.50) | collective-permute-done | bytes 81952 | tf_op jit(solution)/shard_map/ppermute | solution.py:635
  171.0 6.0 %finish_1.1 = (f32[288,512]{1,0:T(8,128)S(1)}, f32[32,512]{1,0:T(8,128)S(1)}, f32[32,512]{1,0:T(8,128)S(1)}, f32[32,512]{1,0:T(8,128)S(1)}, f32[288,512]{1,0:T(8...) custom-call(f32[288,512]{1,0:T(8,128)S(1)} %get-tuple-element.304.re, ...), custom_call_target="tpu_custom_call" | custom-call | flops 11000000512 | tf_op jit(solution)/shard_map/finish_1/pallas_call | solution.py:616
  177.1 11.8 %feed_back_1.1 = (bf16[16,5,16,512]{3,2,1,0:T(8,128)(2,1)S(1)}, bf16[16,5,16,512]{3,2,1,0:T(8,128)(2,1)S(1)}, bf16[16,5,16,512]{3,2,1,0:T(8,128)(2,1)S(1)}, bf16...) custom-call(f32[288,512]{1,0:T(8,128)S(1)} %fusion.2.refs_0_, ...), custom_call_target="tpu_custom_call" | custom-call | flops 12099999744 | tf_op jit(solution)/shard_map/feed_back_1/pallas_call | solution.py:616
  189.9 3.8 collective-permute-done.57.refs_2_
  197.3 4.1 %read_back_1.1 = (bf16[16,5,16,512]{3,2,1,0:T(8,128)(2,1)S(1)}, bf16[16,5,16,512]{3,2,1,0:T(8,128)(2,1)S(1)}, f32[4,512]{1,0:T(4,128)S(1)}, f32[32,512]{1,0:T(8,...) custom-call(bf16[64,512]{1,0:T(8,128)(2,1)S(1)} %get-tuple-element.338.refs_0_, ...), custom_call_target="tpu_custom_call" | custom-call | flops 4400000000 | tf_op jit(solution)/shard_map/read_back_1/pallas_call | solution.py:616
  202.1 3.4 collective-permute-done.62.refs_3_
  205.4 5.8 %collective-permute-done.58 = bf16[8,5,16,512]{3,2,1,0:T(8,128)(2,1)S(1)} collective-permute-done((bf16[8,5,16,512]{3,2,1,0:T(8,128)(2,1)S(1)}, bf16[8,5,16,512]{3,2,1,0:T(8,128)(2,1)S(1)}, u32[]{:S(2)}, u32[]{:S(2)}) %collective-permute-start.58) | collective-permute-done | bytes 655392 | tf_op jit(solution)/shard_map/ppermute | solution.py:734
  213.5 1.6 collective-permute-start.64
  215.1 11.1 %attend_back_1.1 = (bf16[16,5,16,512]{3,2,1,0:T(8,128)(2,1)S(1)}, bf16[16,5,16,512]{3,2,1,0:T(8,128)(2,1)S(1)}, f32[2,512]{1,0:T(2,128)S(1)}, f32[288,512]{1,0:T...) custom-call(f32[288,512]{1,0:T(8,128)S(1)} %get-tuple-element.290.re, ...), custom_call_target="tpu_custom_call" | custom-call | flops 15399999488 | tf_op jit(solution)/shard_map/attend_back_1/pallas_call | solution.py:616
  230.2 2.6 collective-permute-start.68
  233.3 11.8 %collective-permute-done.68 = bf16[2,5,16,512]{3,2,1,0:T(8,128)(2,1)S(1)} collective-permute-done((bf16[2,5,16,512]{3,2,1,0:T(8,128)(2,1)S(1)}, bf16[2,5,16,512]{3,2,1,0:T(8,128)(2,1)S(1)}, u32[]{:S(2)}, u32[]{:S(2)}) %collective-permute-start.68) | collective-permute-done | bytes 163872 | tf_op jit(solution)/shard_map/ppermute | solution.py:734
  245.2 2.6 collective-permute-done.69
  247.9 1.6 collective-permute-start.73
  251.1 2.3 input_back_1.1
  253.5 11.6 %feed_back_0.1 = (bf16[16,5,16,512]{3,2,1,0:T(8,128)(2,1)S(1)}, bf16[16,5,16,512]{3,2,1,0:T(8,128)(2,1)S(1)}, bf16[16,5,16,512]{3,2,1,0:T(8,128)(2,1)S(1)}, bf16...) custom-call(f32[288,512]{1,0:T(8,128)S(1)} %get-tuple-element.383.re, ...), custom_call_target="tpu_custom_call" | custom-call | flops 12099999744 | tf_op jit(solution)/shard_map/feed_back_0/pallas_call | solution.py:616
  268.7 3.4 collective-permute-start.91
  275.5 4.1 %read_back_0.1 = (bf16[16,5,16,512]{3,2,1,0:T(8,128)(2,1)S(1)}, bf16[16,5,16,512]{3,2,1,0:T(8,128)(2,1)S(1)}, f32[4,512]{1,0:T(4,128)S(1)}, f32[32,512]{1,0:T(8,...) custom-call(bf16[64,512]{1,0:T(8,128)(2,1)S(1)} %get-tuple-element.404.refs_0_, ...), custom_call_target="tpu_custom_call" | custom-call | flops 4400000000 | tf_op jit(solution)/shard_map/read_back_0/pallas_call | solution.py:616
  283.6 5.9 %collective-permute-done.80 = bf16[8,5,16,512]{3,2,1,0:T(8,128)(2,1)S(1)} collective-permute-done((bf16[8,5,16,512]{3,2,1,0:T(8,128)(2,1)S(1)}, bf16[8,5,16,512]{3,2,1,0:T(8,128)(2,1)S(1)}, u32[]{:S(2)}, u32[]{:S(2)}) %collective-permute-start.80) | collective-permute-done | bytes 655392 | tf_op jit(solution)/shard_map/ppermute | solution.py:734
  289.4 4.8 %collective-permute-done.81 = bf16[8,5,16,512]{3,2,1,0:T(8,128)(2,1)S(1)} collective-permute-done((bf16[8,5,16,512]{3,2,1,0:T(8,128)(2,1)S(1)}, bf16[8,5,16,512]{3,2,1,0:T(8,128)(2,1)S(1)}, u32[]{:S(2)}, u32[]{:S(2)}) %collective-permute-start.81) | collective-permute-done | bytes 655392 | tf_op jit(solution)/shard_map/ppermute | solution.py:734
  296.0 11.2 %attend_back_0.1 = (bf16[16,3,16,512]{3,2,1,0:T(8,128)(2,1)S(1)}, bf16[16,3,16,512]{3,2,1,0:T(8,128)(2,1)S(1)}, f32[2,512]{1,0:T(2,128)S(1)}, f32[288,512]{1,0:T...) custom-call(f32[288,512]{1,0:T(8,128)S(1)} %get-tuple-element.267.re, ...), custom_call_target="tpu_custom_call" | custom-call | flops 15399999488 | tf_op jit(solution)/shard_map/attend_back_0/pallas_call | solution.py:616
  308.1 2.7 collective-permute-start.93
  314.4 4.4 %collective-permute-done.93 = bf16[2,5,16,512]{3,2,1,0:T(8,128)(2,1)S(1)} collective-permute-done((bf16[2,5,16,512]{3,2,1,0:T(8,128)(2,1)S(1)}, bf16[2,5,16,512]{3,2,1,0:T(8,128)(2,1)S(1)}, u32[]{:S(2)}, u32[]{:S(2)}) %collective-permute-start.93) | collective-permute-done | bytes 163872 | tf_op jit(solution)/shard_map/ppermute | solution.py:734
  318.9 9.8 %collective-permute-done.94 = bf16[2,5,16,512]{3,2,1,0:T(8,128)(2,1)S(1)} collective-permute-done((bf16[2,5,16,512]{3,2,1,0:T(8,128)(2,1)S(1)}, bf16[2,5,16,512]{3,2,1,0:T(8,128)(2,1)S(1)}, u32[]{:S(2)}, u32[]{:S(2)}) %collective-permute-start.94) | collective-permute-done | bytes 163872 | tf_op jit(solution)/shard_map/ppermute | solution.py:734
  332.9 2.5 input_back_0.1
  337.1 4.7 %collective-permute-done.101 = bf16[1,5,16,512]{3,2,1,0:T(8,128)(2,1)S(1)} collective-permute-done((bf16[1,5,16,512]{3,2,1,0:T(8,128)(2,1)S(1)}, bf16[1,5,16,512]{3,2,1,0:T(8,128)(2,1)S(1)}, u32[]{:S(2)}, u32[]{:S(2)}) %collective-permute-start.101) | collective-permute-done | bytes 81952 | tf_op jit(solution)/shard_map/ppermute | solution.py:734
  343.3 3.0 collective-permute-done.105
  351.8 5.8 %collective-permute-done.111 = bf16[1,5,16,512]{3,2,1,0:T(8,128)(2,1)S(1)} collective-permute-done((bf16[1,5,16,512]{3,2,1,0:T(8,128)(2,1)S(1)}, bf16[1,5,16,512]{3,2,1,0:T(8,128)(2,1)S(1)}, u32[]{:S(2)}, u32[]{:S(2)}) %collective-permute-start.111) | collective-permute-done | bytes 81952 | tf_op jit(solution)/shard_map/ppermute | solution.py:734
  359.2 4.4 %collective-permute-done.110 = bf16[2,5,16,512]{3,2,1,0:T(8,128)(2,1)S(1)} collective-permute-done((bf16[2,5,16,512]{3,2,1,0:T(8,128)(2,1)S(1)}, bf16[2,5,16,512]{3,2,1,0:T(8,128)(2,1)S(1)}, u32[]{:S(2)}, u32[]{:S(2)}) %collective-permute-start.110) | collective-permute-done | bytes 163872 | tf_op jit(solution)/shard_map/ppermute | solution.py:734
  364.4 2.5 collective-permute-start.113
  368.8 6.4 %collective-permute-done.115 = bf16[1,5,16,512]{3,2,1,0:T(8,128)(2,1)S(1)} collective-permute-done((bf16[1,5,16,512]{3,2,1,0:T(8,128)(2,1)S(1)}, bf16[1,5,16,512]{3,2,1,0:T(8,128)(2,1)S(1)}, u32[]{:S(2)}, u32[]{:S(2)}) %collective-permute-start.115) | collective-permute-done | bytes 81952 | tf_op jit(solution)/shard_map/ppermute | solution.py:734
  (418 shorter events, 86.5 us)
Async XLA Ops:
  14.2 9.5 %collective-permute-start.2 = (bf16[2,4,16,512]{3,2,1,0:T(8,128)(2,1)S(1)}, bf16[2,4,16,512]{3,2,1,0:T(8,128)(2,1)S(1)}, u32[]{:S(2)}, u32[]{:S(2)}) collective-permute-start(bf16[2,4,16,512]{3,2,1,0:T(8,128)(2,1)S(1)} %pad_maximum_fusion.28), channel_id=1, source_target_pairs={{0,8},{4,12},{8,0},{12,4},{16,24},{20,28},{24,16},{28,20},{1,9},{5... | collective-permute-start | bytes 393224 | tf_op jit(solution)/shard_map/ppermute | solution.py:734
  14.8 9.7 %collective-permute-start.3 = (bf16[2,5,16,512]{3,2,1,0:T(8,128)(2,1)S(1)}, bf16[2,5,16,512]{3,2,1,0:T(8,128)(2,1)S(1)}, u32[]{:S(2)}, u32[]{:S(2)}) collective-permute-start(bf16[2,5,16,512]{3,2,1,0:T(8,128)(2,1)S(1)} %pad_maximum_fusion.23), channel_id=1, source_target_pairs={{0,8},{4,12},{8,0},{12,4},{16,24},{20,28},{24,16},{28,20},{1,9},{5... | collective-permute-start | bytes 491528 | tf_op jit(solution)/shard_map/ppermute | solution.py:734
  24.5 16.2 %collective-permute-start.6 = (bf16[4,4,16,512]{3,2,1,0:T(8,128)(2,1)S(1)}, bf16[4,4,16,512]{3,2,1,0:T(8,128)(2,1)S(1)}, u32[]{:S(2)}, u32[]{:S(2)}) collective-permute-start(bf16[4,4,16,512]{3,2,1,0:T(8,128)(2,1)S(1)} %pad_maximum_fusion.18), channel_id=1, source_target_pairs={{0,2},{1,3},{2,0},{3,1},{4,6},{5,7},{6,4},{7,5},{8,10},{9,11},{10,... | collective-permute-start | bytes 786440 | tf_op jit(solution)/shard_map/ppermute | solution.py:734
  26.6 14.1 %collective-permute-start.7 = (bf16[4,5,16,512]{3,2,1,0:T(8,128)(2,1)S(1)}, bf16[4,5,16,512]{3,2,1,0:T(8,128)(2,1)S(1)}, u32[]{:S(2)}, u32[]{:S(2)}) collective-permute-start(bf16[4,5,16,512]{3,2,1,0:T(8,128)(2,1)S(1)} %pad_maximum_fusion.13), channel_id=1, source_target_pairs={{0,4},{4,0},{8,12},{12,8},{16,20},{20,16},{24,28},{28,24},{1,5},{5... | collective-permute-start | bytes 983048 | tf_op jit(solution)/shard_map/ppermute | solution.py:734
  28.2 12.5 %collective-permute-start.9 = (bf16[2,5,16,512]{3,2,1,0:T(8,128)(2,1)S(1)}, bf16[2,5,16,512]{3,2,1,0:T(8,128)(2,1)S(1)}, u32[]{:S(2)}, u32[]{:S(2)}) collective-permute-start(bf16[2,5,16,512]{3,2,1,0:T(8,128)(2,1)S(1)} %pad_maximum_fusion.24), channel_id=1, source_target_pairs={{0,16},{4,20},{8,24},{12,28},{16,0},{20,4},{24,8},{28,12},{1,17},{... | collective-permute-start | bytes 491528 | tf_op jit(solution)/shard_map/ppermute | solution.py:734
  29.8 10.9 %collective-permute-start.10 = (bf16[2,5,16,512]{3,2,1,0:T(8,128)(2,1)S(1)}, bf16[2,5,16,512]{3,2,1,0:T(8,128)(2,1)S(1)}, u32[]{:S(2)}, u32[]{:S(2)}) collective-permute-start(bf16[2,5,16,512]{3,2,1,0:T(8,128)(2,1)S(1)} %pad_maximum_fusion.25), channel_id=1, source_target_pairs={{0,2},{1,3},{2,0},{3,1},{4,6},{5,7},{6,4},{7,5},{8,10},{9,11},{10,... | collective-permute-start | bytes 491528 | tf_op jit(solution)/shard_map/ppermute | solution.py:734
  30.4 10.3 %collective-permute-start.8 = (bf16[1,5,16,512]{3,2,1,0:T(8,128)(2,1)S(1)}, bf16[1,5,16,512]{3,2,1,0:T(8,128)(2,1)S(1)}, u32[]{:S(2)}, u32[]{:S(2)}) collective-permute-start(bf16[1,5,16,512]{3,2,1,0:T(8,128)(2,1)S(1)} %bitcast.270), channel_id=1, source_target_pairs={{0,16},{4,20},{8,24},{12,28},{16,0},{20,4},{24,8},{28,12},{1,17},{... | collective-permute-start | bytes 245768 | tf_op jit(solution)/shard_map/ppermute | solution.py:734
  40.8 15.5 %collective-permute-start.12 = (bf16[8,5,16,512]{3,2,1,0:T(8,128)(2,1)S(1)}, bf16[8,5,16,512]{3,2,1,0:T(8,128)(2,1)S(1)}, u32[]{:S(2)}, u32[]{:S(2)}) collective-permute-start(bf16[8,5,16,512]{3,2,1,0:T(8,128)(2,1)S(1)} %pad_maximum_fusion.3), channel_id=1, source_target_pairs={{0,2},{1,3},{2,0},{3,1},{4,6},{5,7},{6,4},{7,5},{8,10},{9,11},{10,... | collective-permute-start | bytes 1966088 | tf_op jit(solution)/shard_map/ppermute | solution.py:734
  41.8 14.4 %collective-permute-start.11 = (bf16[8,4,16,512]{3,2,1,0:T(8,128)(2,1)S(1)}, bf16[8,4,16,512]{3,2,1,0:T(8,128)(2,1)S(1)}, u32[]{:S(2)}, u32[]{:S(2)}) collective-permute-start(bf16[8,4,16,512]{3,2,1,0:T(8,128)(2,1)S(1)} %pad_maximum_fusion.8), channel_id=1, source_target_pairs={{0,4},{4,0},{8,12},{12,8},{16,20},{20,16},{24,28},{28,24},{1,5},{5... | collective-permute-start | bytes 1572872 | tf_op jit(solution)/shard_map/ppermute | solution.py:734
  42.4 13.9 %collective-permute-start.14 = (bf16[4,5,16,512]{3,2,1,0:T(8,128)(2,1)S(1)}, bf16[4,5,16,512]{3,2,1,0:T(8,128)(2,1)S(1)}, u32[]{:S(2)}, u32[]{:S(2)}) collective-permute-start(bf16[4,5,16,512]{3,2,1,0:T(8,128)(2,1)S(1)} %pad_maximum_fusion.14), channel_id=1, source_target_pairs={{0,8},{4,12},{8,0},{12,4},{16,24},{20,28},{24,16},{28,20},{1,9},{5... | collective-permute-start | bytes 983048 | tf_op jit(solution)/shard_map/ppermute | solution.py:734
  44.9 11.3 %collective-permute-start.13 = (bf16[2,5,16,512]{3,2,1,0:T(8,128)(2,1)S(1)}, bf16[2,5,16,512]{3,2,1,0:T(8,128)(2,1)S(1)}, u32[]{:S(2)}, u32[]{:S(2)}) collective-permute-start(bf16[2,5,16,512]{3,2,1,0:T(8,128)(2,1)S(1)} %pad_maximum_fusion.26), channel_id=1, source_target_pairs={{0,8},{4,12},{8,0},{12,4},{16,24},{20,28},{24,16},{28,20},{1,9},{5... | collective-permute-start | bytes 491528 | tf_op jit(solution)/shard_map/ppermute | solution.py:734
  57.3 12.9 %collective-permute-start.19 = (bf16[4,5,16,512]{3,2,1,0:T(8,128)(2,1)S(1)}, bf16[4,5,16,512]{3,2,1,0:T(8,128)(2,1)S(1)}, u32[]{:S(2)}, u32[]{:S(2)}) collective-permute-start(bf16[4,5,16,512]{3,2,1,0:T(8,128)(2,1)S(1)} %pad_maximum_fusion.16), channel_id=1, source_target_pairs={{0,4},{4,0},{8,12},{12,8},{16,20},{20,16},{24,28},{28,24},{1,5},{5... | collective-permute-start | bytes 983048 | tf_op jit(solution)/shard_map/ppermute | solution.py:734
  63.5 14.0 %collective-permute-start.21 = (bf16[256,1024]{1,0:T(8,128)(2,1)S(1)}, bf16[256,1024]{1,0:T(8,128)(2,1)S(1)}, u32[]{:S(2)}, u32[]{:S(2)}) collective-permute-start(bf16[256,1024]{1,0:T(8,128)(2,1)S(1)} %get-tuple-element.273.refs_2_.refs_12_), channel_id=1, source_target_pairs={{0,2},{1,3},{2,0},{3,1},{4,6},{5,7},{6,4},{7,5},{8,10},{9,11},{10,... | collective-permute-start | bytes 1572872 | tf_op jit(solution)/shard_map/ppermute | solution.py:635
  64.9 10.7 %collective-permute-start.18 = (bf16[4,5,16,512]{3,2,1,0:T(8,128)(2,1)S(1)}, bf16[4,5,16,512]{3,2,1,0:T(8,128)(2,1)S(1)}, u32[]{:S(2)}, u32[]{:S(2)}) collective-permute-start(bf16[4,5,16,512]{3,2,1,0:T(8,128)(2,1)S(1)} %pad_maximum_fusion.15), channel_id=1, source_target_pairs={{0,4},{4,0},{8,12},{12,8},{16,20},{20,16},{24,28},{28,24},{1,5},{5... | collective-permute-start | bytes 983048 | tf_op jit(solution)/shard_map/ppermute | solution.py:734
  68.6 24.9 %collective-permute-start.25 = (bf16[8,5,16,512]{3,2,1,0:T(8,128)(2,1)S(1)}, bf16[8,5,16,512]{3,2,1,0:T(8,128)(2,1)S(1)}, u32[]{:S(2)}, u32[]{:S(2)}) collective-permute-start(bf16[8,5,16,512]{3,2,1,0:T(8,128)(2,1)S(1)} %pad_maximum_fusion.5), channel_id=1, source_target_pairs={{0,4},{4,0},{8,12},{12,8},{16,20},{20,16},{24,28},{28,24},{1,5},{5... | collective-permute-start | bytes 1966088 | tf_op jit(solution)/shard_map/ppermute | solution.py:734
  78.2 18.5 %collective-permute-start.24 = (bf16[8,5,16,512]{3,2,1,0:T(8,128)(2,1)S(1)}, bf16[8,5,16,512]{3,2,1,0:T(8,128)(2,1)S(1)}, u32[]{:S(2)}, u32[]{:S(2)}) collective-permute-start(bf16[8,5,16,512]{3,2,1,0:T(8,128)(2,1)S(1)} %pad_maximum_fusion.4), channel_id=1, source_target_pairs={{0,2},{1,3},{2,0},{3,1},{4,6},{5,7},{6,4},{7,5},{8,10},{9,11},{10,... | collective-permute-start | bytes 1966088 | tf_op jit(solution)/shard_map/ppermute | solution.py:734
  79.5 17.6 %collective-permute-start.26 = (bf16[8,5,16,512]{3,2,1,0:T(8,128)(2,1)S(1)}, bf16[8,5,16,512]{3,2,1,0:T(8,128)(2,1)S(1)}, u32[]{:S(2)}, u32[]{:S(2)}) collective-permute-start(bf16[8,5,16,512]{3,2,1,0:T(8,128)(2,1)S(1)} %pad_maximum_fusion.6), channel_id=1, source_target_pairs={{0,8},{4,12},{8,0},{12,4},{16,24},{20,28},{24,16},{28,20},{1,9},{5... | collective-permute-start | bytes 1966088 | tf_op jit(solution)/shard_map/ppermute | solution.py:734
  97.3 10.0 %collective-permute-start.31 = (bf16[16,5,16,512]{3,2,1,0:T(8,128)(2,1)S(1)}, bf16[16,5,16,512]{3,2,1,0:T(8,128)(2,1)S(1)}, u32[]{:S(2)}, u32[]{:S(2)}) collective-permute-start(bf16[16,5,16,512]{3,2,1,0:T(8,128)(2,1)S(1)} %constant_dynamic-update-slice_fusion.30.refs_9_.refs_11_), channel_id=1, source_target_pairs={{0,1},{1,0},{2,3},{3,2},{4,5},{5,4},{6,7},{7,6},{8,9},{9,8},{10,11... | collective-permute-start | bytes 3932168 | tf_op jit(solution)/shard_map/ppermute | solution.py:734
  104.2 10.3 %collective-permute-start.34 = (bf16[1,8,16,512]{3,2,1,0:T(8,128)(2,1)S(1)}, bf16[1,8,16,512]{3,2,1,0:T(8,128)(2,1)S(1)}, u32[]{:S(2)}, u32[]{:S(2)}) collective-permute-start(bf16[1,8,16,512]{3,2,1,0:T(8,128)(2,1)S(1)} %bitcast.275), channel_id=1, source_target_pairs={{0,16},{4,20},{8,24},{12,28},{16,0},{20,4},{24,8},{28,12},{1,17},{... | collective-permute-start | bytes 393224 | tf_op jit(solution)/shard_map/ppermute | solution.py:734
  115.1 15.6 %collective-permute-start.36 = (bf16[8,5,16,512]{3,2,1,0:T(8,128)(2,1)S(1)}, bf16[8,5,16,512]{3,2,1,0:T(8,128)(2,1)S(1)}, u32[]{:S(2)}, u32[]{:S(2)}) collective-permute-start(bf16[8,5,16,512]{3,2,1,0:T(8,128)(2,1)S(1)} %pad_maximum_fusion.7), channel_id=1, source_target_pairs={{0,4},{4,0},{8,12},{12,8},{16,20},{20,16},{24,28},{28,24},{1,5},{5... | collective-permute-start | bytes 1966088 | tf_op jit(solution)/shard_map/ppermute | solution.py:734
  116.6 12.3 %collective-permute-start.39 = (bf16[256,1024]{1,0:T(8,128)(2,1)S(1)}, bf16[256,1024]{1,0:T(8,128)(2,1)S(1)}, u32[]{:S(2)}, u32[]{:S(2)}) collective-permute-start(bf16[256,1024]{1,0:T(8,128)(2,1)S(1)} %get-tuple-element.300.refs_2_.refs_12_), channel_id=1, source_target_pairs={{0,2},{1,3},{2,0},{3,1},{4,6},{5,7},{6,4},{7,5},{8,10},{9,11},{10,... | collective-permute-start | bytes 1572872 | tf_op jit(solution)/shard_map/ppermute | solution.py:635
  131.4 13.6 %collective-permute-start.43 = (bf16[4,4,16,512]{3,2,1,0:T(8,128)(2,1)S(1)}, bf16[4,4,16,512]{3,2,1,0:T(8,128)(2,1)S(1)}, u32[]{:S(2)}, u32[]{:S(2)}) collective-permute-start(bf16[4,4,16,512]{3,2,1,0:T(8,128)(2,1)S(1)} %get-tuple-element.516), channel_id=1, source_target_pairs={{0,2},{1,3},{2,0},{3,1},{4,6},{5,7},{6,4},{7,5},{8,10},{9,11},{10,... | collective-permute-start | bytes 786440 | tf_op jit(solution)/shard_map/ppermute | solution.py:734
  132.9 12.8 %collective-permute-start.44 = (bf16[4,4,16,512]{3,2,1,0:T(8,128)(2,1)S(1)}, bf16[4,4,16,512]{3,2,1,0:T(8,128)(2,1)S(1)}, u32[]{:S(2)}, u32[]{:S(2)}) collective-permute-start(bf16[4,4,16,512]{3,2,1,0:T(8,128)(2,1)S(1)} %pad_maximum_fusion.20), channel_id=1, source_target_pairs={{0,2},{1,3},{2,0},{3,1},{4,6},{5,7},{6,4},{7,5},{8,10},{9,11},{10,... | collective-permute-start | bytes 786440 | tf_op jit(solution)/shard_map/ppermute | solution.py:734
  134.5 11.2 %collective-permute-start.45 = (bf16[4,4,16,512]{3,2,1,0:T(8,128)(2,1)S(1)}, bf16[4,4,16,512]{3,2,1,0:T(8,128)(2,1)S(1)}, u32[]{:S(2)}, u32[]{:S(2)}) collective-permute-start(bf16[4,4,16,512]{3,2,1,0:T(8,128)(2,1)S(1)} %get-tuple-element.515), channel_id=1, source_target_pairs={{0,4},{4,0},{8,12},{12,8},{16,20},{20,16},{24,28},{28,24},{1,5},{5... | collective-permute-start | bytes 786440 | tf_op jit(solution)/shard_map/ppermute | solution.py:734
  145.8 19.1 %collective-permute-start.46 = (bf16[8,4,16,512]{3,2,1,0:T(8,128)(2,1)S(1)}, bf16[8,4,16,512]{3,2,1,0:T(8,128)(2,1)S(1)}, u32[]{:S(2)}, u32[]{:S(2)}) collective-permute-start(bf16[8,4,16,512]{3,2,1,0:T(8,128)(2,1)S(1)} %pad_maximum_fusion.10), channel_id=1, source_target_pairs={{0,4},{4,0},{8,12},{12,8},{16,20},{20,16},{24,28},{28,24},{1,5},{5... | collective-permute-start | bytes 1572872 | tf_op jit(solution)/shard_map/ppermute | solution.py:734
  147.4 17.5 %collective-permute-start.47 = (bf16[8,4,16,512]{3,2,1,0:T(8,128)(2,1)S(1)}, bf16[8,4,16,512]{3,2,1,0:T(8,128)(2,1)S(1)}, u32[]{:S(2)}, u32[]{:S(2)}) collective-permute-start(bf16[8,4,16,512]{3,2,1,0:T(8,128)(2,1)S(1)} %pad_maximum_fusion.11), channel_id=1, source_target_pairs={{0,8},{4,12},{8,0},{12,4},{16,24},{20,28},{24,16},{28,20},{1,9},{5... | collective-permute-start | bytes 1572872 | tf_op jit(solution)/shard_map/ppermute | solution.py:734
  150.1 14.8 %collective-permute-start.48 = (bf16[8,4,16,512]{3,2,1,0:T(8,128)(2,1)S(1)}, bf16[8,4,16,512]{3,2,1,0:T(8,128)(2,1)S(1)}, u32[]{:S(2)}, u32[]{:S(2)}) collective-permute-start(bf16[8,4,16,512]{3,2,1,0:T(8,128)(2,1)S(1)} %pad_maximum_fusion.12), channel_id=1, source_target_pairs={{0,2},{1,3},{2,0},{3,1},{4,6},{5,7},{6,4},{7,5},{8,10},{9,11},{10,... | collective-permute-start | bytes 1572872 | tf_op jit(solution)/shard_map/ppermute | solution.py:734
  150.7 14.2 %collective-permute-start.49 = (f32[32,640]{1,0:T(8,128)S(1)}, f32[32,640]{1,0:T(8,128)S(1)}, u32[]{:S(2)}, u32[]{:S(2)}) collective-permute-start(f32[32,640]{1,0:T(8,128)S(1)} %get-tuple-element.312.refs_1_), channel_id=1, source_target_pairs={{0,2},{1,3},{2,0},{3,1},{4,6},{5,7},{6,4},{7,5},{8,10},{9,11},{10,... | collective-permute-start | bytes 245768 | tf_op jit(solution)/shard_map/ppermute | solution.py:635
  194.4 16.8 %collective-permute-start.58 = (bf16[8,5,16,512]{3,2,1,0:T(8,128)(2,1)S(1)}, bf16[8,5,16,512]{3,2,1,0:T(8,128)(2,1)S(1)}, u32[]{:S(2)}, u32[]{:S(2)}) collective-permute-start(bf16[8,5,16,512]{3,2,1,0:T(8,128)(2,1)S(1)} %slice.805), channel_id=1, source_target_pairs={{0,4},{4,0},{8,12},{12,8},{16,20},{20,16},{24,28},{28,24},{1,5},{5... | collective-permute-start | bytes 1966088 | tf_op jit(solution)/shard_map/ppermute | solution.py:734
  195.6 16.6 %collective-permute-start.59 = (bf16[8,5,16,512]{3,2,1,0:T(8,128)(2,1)S(1)}, bf16[8,5,16,512]{3,2,1,0:T(8,128)(2,1)S(1)}, u32[]{:S(2)}, u32[]{:S(2)}) collective-permute-start(bf16[8,5,16,512]{3,2,1,0:T(8,128)(2,1)S(1)} %slice.806), channel_id=1, source_target_pairs={{0,8},{4,12},{8,0},{12,4},{16,24},{20,28},{24,16},{28,20},{1,9},{5... | collective-permute-start | bytes 1966088 | tf_op jit(solution)/shard_map/ppermute | solution.py:734
  212.4 13.9 %collective-permute-start.63 = (bf16[4,5,16,512]{3,2,1,0:T(8,128)(2,1)S(1)}, bf16[4,5,16,512]{3,2,1,0:T(8,128)(2,1)S(1)}, u32[]{:S(2)}, u32[]{:S(2)}) collective-permute-start(bf16[4,5,16,512]{3,2,1,0:T(8,128)(2,1)S(1)} %slice.808), channel_id=1, source_target_pairs={{0,8},{4,12},{8,0},{12,4},{16,24},{20,28},{24,16},{28,20},{1,9},{5... | collective-permute-start | bytes 983048 | tf_op jit(solution)/shard_map/ppermute | solution.py:734
  213.5 12.7 %collective-permute-start.64 = (bf16[4,5,16,512]{3,2,1,0:T(8,128)(2,1)S(1)}, bf16[4,5,16,512]{3,2,1,0:T(8,128)(2,1)S(1)}, u32[]{:S(2)}, u32[]{:S(2)}) collective-permute-start(bf16[4,5,16,512]{3,2,1,0:T(8,128)(2,1)S(1)} %slice.810), channel_id=1, source_target_pairs={{0,4},{4,0},{8,12},{12,8},{16,20},{20,16},{24,28},{28,24},{1,5},{5... | collective-permute-start | bytes 983048 | tf_op jit(solution)/shard_map/ppermute | solution.py:734
  215.1 11.2 %collective-permute-start.65 = (bf16[16,5,16,512]{3,2,1,0:T(8,128)(2,1)S(1)}, bf16[16,5,16,512]{3,2,1,0:T(8,128)(2,1)S(1)}, u32[]{:S(2)}, u32[]{:S(2)}) collective-permute-start(bf16[16,5,16,512]{3,2,1,0:T(8,128)(2,1)S(1)} %get-tuple-element.356), channel_id=1, source_target_pairs={{0,1},{1,0},{2,3},{3,2},{4,5},{5,4},{6,7},{7,6},{8,9},{9,8},{10,11... | collective-permute-start | bytes 3932168 | tf_op jit(solution)/shard_map/ppermute | solution.py:734
  227.4 20.4 %collective-permute-start.70 = (bf16[8,5,16,512]{3,2,1,0:T(8,128)(2,1)S(1)}, bf16[8,5,16,512]{3,2,1,0:T(8,128)(2,1)S(1)}, u32[]{:S(2)}, u32[]{:S(2)}) collective-permute-start(bf16[8,5,16,512]{3,2,1,0:T(8,128)(2,1)S(1)} %slice.815), channel_id=1, source_target_pairs={{0,4},{4,0},{8,12},{12,8},{16,20},{20,16},{24,28},{28,24},{1,5},{5... | collective-permute-start | bytes 1966088 | tf_op jit(solution)/shard_map/ppermute | solution.py:734
  229.4 18.4 %collective-permute-start.72 = (bf16[288,1024]{1,0:T(8,128)(2,1)S(1)}, bf16[288,1024]{1,0:T(8,128)(2,1)S(1)}, u32[]{:S(2)}, u32[]{:S(2)}) collective-permute-start(bf16[288,1024]{1,0:T(8,128)(2,1)S(1)} %add_convert_fusion.17.refs_5_), channel_id=1, source_target_pairs={{0,2},{1,3},{2,0},{3,1},{4,6},{5,7},{6,4},{7,5},{8,10},{9,11},{10,... | collective-permute-start | bytes 1769480 | tf_op jit(solution)/shard_map/ppermute | solution.py:635
  230.2 15.0 %collective-permute-start.68 = (bf16[2,5,16,512]{3,2,1,0:T(8,128)(2,1)S(1)}, bf16[2,5,16,512]{3,2,1,0:T(8,128)(2,1)S(1)}, u32[]{:S(2)}, u32[]{:S(2)}) collective-permute-start(bf16[2,5,16,512]{3,2,1,0:T(8,128)(2,1)S(1)} %slice.812), channel_id=1, source_target_pairs={{0,16},{4,20},{8,24},{12,28},{16,0},{20,4},{24,8},{28,12},{1,17},{... | collective-permute-start | bytes 491528 | tf_op jit(solution)/shard_map/ppermute | solution.py:734
  232.9 14.9 %collective-permute-start.69 = (bf16[2,5,16,512]{3,2,1,0:T(8,128)(2,1)S(1)}, bf16[2,5,16,512]{3,2,1,0:T(8,128)(2,1)S(1)}, u32[]{:S(2)}, u32[]{:S(2)}) collective-permute-start(bf16[2,5,16,512]{3,2,1,0:T(8,128)(2,1)S(1)} %slice.814), channel_id=1, source_target_pairs={{0,16},{4,20},{8,24},{12,28},{16,0},{20,4},{24,8},{28,12},{1,17},{... | collective-permute-start | bytes 491528 | tf_op jit(solution)/shard_map/ppermute | solution.py:734
  247.9 17.2 %collective-permute-start.73 = (bf16[1,5,16,512]{3,2,1,0:T(8,128)(2,1)S(1)}, bf16[1,5,16,512]{3,2,1,0:T(8,128)(2,1)S(1)}, u32[]{:S(2)}, u32[]{:S(2)}) collective-permute-start(bf16[1,5,16,512]{3,2,1,0:T(8,128)(2,1)S(1)} %slice.817), channel_id=1, source_target_pairs={{0,2},{1,3},{2,0},{3,1},{4,6},{5,7},{6,4},{7,5},{8,10},{9,11},{10,... | collective-permute-start | bytes 245768 | tf_op jit(solution)/shard_map/ppermute | solution.py:734
  249.6 15.6 %collective-permute-start.74 = (bf16[1,5,16,512]{3,2,1,0:T(8,128)(2,1)S(1)}, bf16[1,5,16,512]{3,2,1,0:T(8,128)(2,1)S(1)}, u32[]{:S(2)}, u32[]{:S(2)}) collective-permute-start(bf16[1,5,16,512]{3,2,1,0:T(8,128)(2,1)S(1)} %slice.819), channel_id=1, source_target_pairs={{0,2},{1,3},{2,0},{3,1},{4,6},{5,7},{6,4},{7,5},{8,10},{9,11},{10,... | collective-permute-start | bytes 245768 | tf_op jit(solution)/shard_map/ppermute | solution.py:734
  250.4 14.8 %collective-permute-start.75 = (bf16[4,5,16,512]{3,2,1,0:T(8,128)(2,1)S(1)}, bf16[4,5,16,512]{3,2,1,0:T(8,128)(2,1)S(1)}, u32[]{:S(2)}, u32[]{:S(2)}) collective-permute-start(bf16[4,5,16,512]{3,2,1,0:T(8,128)(2,1)S(1)} %slice.821), channel_id=1, source_target_pairs={{0,8},{4,12},{8,0},{12,4},{16,24},{20,28},{24,16},{28,20},{1,9},{5... | collective-permute-start | bytes 983048 | tf_op jit(solution)/shard_map/ppermute | solution.py:734
  253.4 18.8 %collective-permute-start.78 = (bf16[16,5,16,512]{3,2,1,0:T(8,128)(2,1)S(1)}, bf16[16,5,16,512]{3,2,1,0:T(8,128)(2,1)S(1)}, u32[]{:S(2)}, u32[]{:S(2)}) collective-permute-start(bf16[16,5,16,512]{3,2,1,0:T(8,128)(2,1)S(1)} %get-tuple-element.399), channel_id=1, source_target_pairs={{0,1},{1,0},{2,3},{3,2},{4,5},{5,4},{6,7},{7,6},{8,9},{9,8},{10,11... | collective-permute-start | bytes 3932168 | tf_op jit(solution)/shard_map/ppermute | solution.py:734
  268.7 38.5 %collective-permute-start.91 = (bf16[2,5,16,512]{3,2,1,0:T(8,128)(2,1)S(1)}, bf16[2,5,16,512]{3,2,1,0:T(8,128)(2,1)S(1)}, u32[]{:S(2)}, u32[]{:S(2)}) collective-permute-start(bf16[2,5,16,512]{3,2,1,0:T(8,128)(2,1)S(1)} %slice.830), channel_id=1, source_target_pairs={{0,16},{4,20},{8,24},{12,28},{16,0},{20,4},{24,8},{28,12},{1,17},{... | collective-permute-start | bytes 491528 | tf_op jit(solution)/shard_map/ppermute | solution.py:734
  272.8 16.6 %collective-permute-start.80 = (bf16[8,5,16,512]{3,2,1,0:T(8,128)(2,1)S(1)}, bf16[8,5,16,512]{3,2,1,0:T(8,128)(2,1)S(1)}, u32[]{:S(2)}, u32[]{:S(2)}) collective-permute-start(bf16[8,5,16,512]{3,2,1,0:T(8,128)(2,1)S(1)} %slice.822), channel_id=1, source_target_pairs={{0,4},{4,0},{8,12},{12,8},{16,20},{20,16},{24,28},{28,24},{1,5},{5... | collective-permute-start | bytes 1966088 | tf_op jit(solution)/shard_map/ppermute | solution.py:734
  274.5 19.8 %collective-permute-start.81 = (bf16[8,5,16,512]{3,2,1,0:T(8,128)(2,1)S(1)}, bf16[8,5,16,512]{3,2,1,0:T(8,128)(2,1)S(1)}, u32[]{:S(2)}, u32[]{:S(2)}) collective-permute-start(bf16[8,5,16,512]{3,2,1,0:T(8,128)(2,1)S(1)} %slice.823), channel_id=1, source_target_pairs={{0,8},{4,12},{8,0},{12,4},{16,24},{20,28},{24,16},{28,20},{1,9},{5... | collective-permute-start | bytes 1966088 | tf_op jit(solution)/shard_map/ppermute | solution.py:734
  281.7 25.5 %collective-permute-start.90 = (bf16[8,5,16,512]{3,2,1,0:T(8,128)(2,1)S(1)}, bf16[8,5,16,512]{3,2,1,0:T(8,128)(2,1)S(1)}, u32[]{:S(2)}, u32[]{:S(2)}) collective-permute-start(bf16[8,5,16,512]{3,2,1,0:T(8,128)(2,1)S(1)} %slice.828), channel_id=1, source_target_pairs={{0,2},{1,3},{2,0},{3,1},{4,6},{5,7},{6,4},{7,5},{8,10},{9,11},{10,... | collective-permute-start | bytes 1966088 | tf_op jit(solution)/shard_map/ppermute | solution.py:734
  295.1 12.2 %collective-permute-start.87 = (bf16[4,5,16,512]{3,2,1,0:T(8,128)(2,1)S(1)}, bf16[4,5,16,512]{3,2,1,0:T(8,128)(2,1)S(1)}, u32[]{:S(2)}, u32[]{:S(2)}) collective-permute-start(bf16[4,5,16,512]{3,2,1,0:T(8,128)(2,1)S(1)} %slice.825), channel_id=1, source_target_pairs={{0,8},{4,12},{8,0},{12,4},{16,24},{20,28},{24,16},{28,20},{1,9},{5... | collective-permute-start | bytes 983048 | tf_op jit(solution)/shard_map/ppermute | solution.py:734
  295.5 11.8 %collective-permute-start.88 = (bf16[4,5,16,512]{3,2,1,0:T(8,128)(2,1)S(1)}, bf16[4,5,16,512]{3,2,1,0:T(8,128)(2,1)S(1)}, u32[]{:S(2)}, u32[]{:S(2)}) collective-permute-start(bf16[4,5,16,512]{3,2,1,0:T(8,128)(2,1)S(1)} %slice.827), channel_id=1, source_target_pairs={{0,4},{4,0},{8,12},{12,8},{16,20},{20,16},{24,28},{28,24},{1,5},{5... | collective-permute-start | bytes 983048 | tf_op jit(solution)/shard_map/ppermute | solution.py:734
  296.0 11.2 %collective-permute-start.89 = (bf16[16,5,16,512]{3,2,1,0:T(8,128)(2,1)S(1)}, bf16[16,5,16,512]{3,2,1,0:T(8,128)(2,1)S(1)}, u32[]{:S(2)}, u32[]{:S(2)}) collective-permute-start(bf16[16,5,16,512]{3,2,1,0:T(8,128)(2,1)S(1)} %get-tuple-element.431), channel_id=1, source_target_pairs={{0,1},{1,0},{2,3},{3,2},{4,5},{5,4},{6,7},{7,6},{8,9},{9,8},{10,11... | collective-permute-start | bytes 3932168 | tf_op jit(solution)/shard_map/ppermute | solution.py:734
  308.1 10.7 %collective-permute-start.93 = (bf16[2,5,16,512]{3,2,1,0:T(8,128)(2,1)S(1)}, bf16[2,5,16,512]{3,2,1,0:T(8,128)(2,1)S(1)}, u32[]{:S(2)}, u32[]{:S(2)}) collective-permute-start(bf16[2,5,16,512]{3,2,1,0:T(8,128)(2,1)S(1)} %slice.832), channel_id=1, source_target_pairs={{0,16},{4,20},{8,24},{12,28},{16,0},{20,4},{24,8},{28,12},{1,17},{... | collective-permute-start | bytes 491528 | tf_op jit(solution)/shard_map/ppermute | solution.py:734
  311.4 17.9 %collective-permute-start.95 = (bf16[8,5,16,512]{3,2,1,0:T(8,128)(2,1)S(1)}, bf16[8,5,16,512]{3,2,1,0:T(8,128)(2,1)S(1)}, u32[]{:S(2)}, u32[]{:S(2)}) collective-permute-start(bf16[8,5,16,512]{3,2,1,0:T(8,128)(2,1)S(1)} %slice.835), channel_id=1, source_target_pairs={{0,4},{4,0},{8,12},{12,8},{16,20},{20,16},{24,28},{28,24},{1,5},{5... | collective-permute-start | bytes 1966088 | tf_op jit(solution)/shard_map/ppermute | solution.py:734
  312.3 17.0 %collective-permute-start.97 = (bf16[16,3,16,512]{3,2,1,0:T(8,128)(2,1)S(1)}, bf16[16,3,16,512]{3,2,1,0:T(8,128)(2,1)S(1)}, u32[]{:S(2)}, u32[]{:S(2)}) collective-permute-start(bf16[16,3,16,512]{3,2,1,0:T(8,128)(2,1)S(1)} %get-tuple-element.445), channel_id=1, source_target_pairs={{0,1},{1,0},{2,3},{3,2},{4,5},{5,4},{6,7},{7,6},{8,9},{9,8},{10,11... | collective-permute-start | bytes 2359304 | tf_op jit(solution)/shard_map/ppermute | solution.py:734
  312.5 16.8 %collective-permute-start.98 = (bf16[288,1024]{1,0:T(8,128)(2,1)S(1)}, bf16[288,1024]{1,0:T(8,128)(2,1)S(1)}, u32[]{:S(2)}, u32[]{:S(2)}) collective-permute-start(bf16[288,1024]{1,0:T(8,128)(2,1)S(1)} %add_convert_fusion.16.refs_5_), channel_id=1, source_target_pairs={{0,2},{1,3},{2,0},{3,1},{4,6},{5,7},{6,4},{7,5},{8,10},{9,11},{10,... | collective-permute-start | bytes 1769480 | tf_op jit(solution)/shard_map/ppermute | solution.py:635
  314.2 15.1 %collective-permute-start.96 = (bf16[4,5,16,512]{3,2,1,0:T(8,128)(2,1)S(1)}, bf16[4,5,16,512]{3,2,1,0:T(8,128)(2,1)S(1)}, u32[]{:S(2)}, u32[]{:S(2)}) collective-permute-start(bf16[4,5,16,512]{3,2,1,0:T(8,128)(2,1)S(1)} %slice.837), channel_id=1, source_target_pairs={{0,8},{4,12},{8,0},{12,4},{16,24},{20,28},{24,16},{28,20},{1,9},{5... | collective-permute-start | bytes 983048 | tf_op jit(solution)/shard_map/ppermute | solution.py:734
  318.8 9.8 %collective-permute-start.94 = (bf16[2,5,16,512]{3,2,1,0:T(8,128)(2,1)S(1)}, bf16[2,5,16,512]{3,2,1,0:T(8,128)(2,1)S(1)}, u32[]{:S(2)}, u32[]{:S(2)}) collective-permute-start(bf16[2,5,16,512]{3,2,1,0:T(8,128)(2,1)S(1)} %slice.834), channel_id=1, source_target_pairs={{0,16},{4,20},{8,24},{12,28},{16,0},{20,4},{24,8},{28,12},{1,17},{... | collective-permute-start | bytes 491528 | tf_op jit(solution)/shard_map/ppermute | solution.py:734
  329.6 16.7 %collective-permute-start.99 = (bf16[4,5,16,512]{3,2,1,0:T(8,128)(2,1)S(1)}, bf16[4,5,16,512]{3,2,1,0:T(8,128)(2,1)S(1)}, u32[]{:S(2)}, u32[]{:S(2)}) collective-permute-start(bf16[4,5,16,512]{3,2,1,0:T(8,128)(2,1)S(1)} %slice.840), channel_id=1, source_target_pairs={{0,2},{1,3},{2,0},{3,1},{4,6},{5,7},{6,4},{7,5},{8,10},{9,11},{10,... | collective-permute-start | bytes 983048 | tf_op jit(solution)/shard_map/ppermute | solution.py:734
  331.4 14.9 %collective-permute-start.100 = (bf16[8,3,16,512]{3,2,1,0:T(8,128)(2,1)S(1)}, bf16[8,3,16,512]{3,2,1,0:T(8,128)(2,1)S(1)}, u32[]{:S(2)}, u32[]{:S(2)}) collective-permute-start(bf16[8,3,16,512]{3,2,1,0:T(8,128)(2,1)S(1)} %slice.841), channel_id=1, source_target_pairs={{0,4},{4,0},{8,12},{12,8},{16,20},{20,16},{24,28},{28,24},{1,5},{5... | collective-permute-start | bytes 1179656 | tf_op jit(solution)/shard_map/ppermute | solution.py:734
  335.4 10.9 %collective-permute-start.104 = (bf16[16,3,16,512]{3,2,1,0:T(8,128)(2,1)S(1)}, bf16[16,3,16,512]{3,2,1,0:T(8,128)(2,1)S(1)}, u32[]{:S(2)}, u32[]{:S(2)}) collective-permute-start(bf16[16,3,16,512]{3,2,1,0:T(8,128)(2,1)S(1)} %get-tuple-element.465), channel_id=1, source_target_pairs={{0,1},{1,0},{2,3},{3,2},{4,5},{5,4},{6,7},{7,6},{8,9},{9,8},{10,11... | collective-permute-start | bytes 2359304 | tf_op jit(solution)/shard_map/ppermute | solution.py:734
  336.5 9.8 %collective-permute-start.103 = (bf16[2,5,16,512]{3,2,1,0:T(8,128)(2,1)S(1)}, bf16[2,5,16,512]{3,2,1,0:T(8,128)(2,1)S(1)}, u32[]{:S(2)}, u32[]{:S(2)}) collective-permute-start(bf16[2,5,16,512]{3,2,1,0:T(8,128)(2,1)S(1)} %slice.847), channel_id=1, source_target_pairs={{0,4},{4,0},{8,12},{12,8},{16,20},{20,16},{24,28},{28,24},{1,5},{5... | collective-permute-start | bytes 491528 | tf_op jit(solution)/shard_map/ppermute | solution.py:734
  346.7 16.9 %collective-permute-start.106 = (bf16[4,3,16,512]{3,2,1,0:T(8,128)(2,1)S(1)}, bf16[4,3,16,512]{3,2,1,0:T(8,128)(2,1)S(1)}, u32[]{:S(2)}, u32[]{:S(2)}) collective-permute-start(bf16[4,3,16,512]{3,2,1,0:T(8,128)(2,1)S(1)} %get-tuple-element.514), channel_id=1, source_target_pairs={{0,2},{1,3},{2,0},{3,1},{4,6},{5,7},{6,4},{7,5},{8,10},{9,11},{10,... | collective-permute-start | bytes 589832 | tf_op jit(solution)/shard_map/ppermute | solution.py:734
  347.4 16.2 %collective-permute-start.107 = (bf16[4,3,16,512]{3,2,1,0:T(8,128)(2,1)S(1)}, bf16[4,3,16,512]{3,2,1,0:T(8,128)(2,1)S(1)}, u32[]{:S(2)}, u32[]{:S(2)}) collective-permute-start(bf16[4,3,16,512]{3,2,1,0:T(8,128)(2,1)S(1)} %get-tuple-element.513), channel_id=1, source_target_pairs={{0,4},{4,0},{8,12},{12,8},{16,20},{20,16},{24,28},{28,24},{1,5},{5... | collective-permute-start | bytes 589832 | tf_op jit(solution)/shard_map/ppermute | solution.py:734
  348.8 14.7 %collective-permute-start.108 = (bf16[4,3,16,512]{3,2,1,0:T(8,128)(2,1)S(1)}, bf16[4,3,16,512]{3,2,1,0:T(8,128)(2,1)S(1)}, u32[]{:S(2)}, u32[]{:S(2)}) collective-permute-start(bf16[4,3,16,512]{3,2,1,0:T(8,128)(2,1)S(1)} %get-tuple-element.512), channel_id=1, source_target_pairs={{0,6},{1,7},{2,4},{3,5},{4,2},{5,3},{6,0},{7,1},{8,14},{9,15},{10,... | collective-permute-start | bytes 589832 | tf_op jit(solution)/shard_map/ppermute | solution.py:732
  350.4 13.2 %collective-permute-start.109 = (bf16[4,3,16,512]{3,2,1,0:T(8,128)(2,1)S(1)}, bf16[4,3,16,512]{3,2,1,0:T(8,128)(2,1)S(1)}, u32[]{:S(2)}, u32[]{:S(2)}) collective-permute-start(bf16[4,3,16,512]{3,2,1,0:T(8,128)(2,1)S(1)} %slice.855), channel_id=1, source_target_pairs={{0,2},{1,3},{2,0},{3,1},{4,6},{5,7},{6,4},{7,5},{8,10},{9,11},{10,... | collective-permute-start | bytes 589832 | tf_op jit(solution)/shard_map/ppermute | solution.py:734
  363.9 11.3 %collective-permute-start.112 = (bf16[1,6,16,512]{3,2,1,0:T(8,128)(2,1)S(1)}, bf16[1,6,16,512]{3,2,1,0:T(8,128)(2,1)S(1)}, u32[]{:S(2)}, u32[]{:S(2)}) collective-permute-start(bf16[1,6,16,512]{3,2,1,0:T(8,128)(2,1)S(1)} %pad_maximum_fusion.30), channel_id=1, source_target_pairs={{0,16},{4,20},{8,24},{12,28},{16,0},{20,4},{24,8},{28,12},{1,17},{... | collective-permute-start | bytes 294920 | tf_op jit(solution)/shard_map/ppermute | solution.py:734
  364.4 10.8 %collective-permute-start.113 = (bf16[1,6,16,512]{3,2,1,0:T(8,128)(2,1)S(1)}, bf16[1,6,16,512]{3,2,1,0:T(8,128)(2,1)S(1)}, u32[]{:S(2)}, u32[]{:S(2)}) collective-permute-start(bf16[1,6,16,512]{3,2,1,0:T(8,128)(2,1)S(1)} %pad_maximum_fusion.31), channel_id=1, source_target_pairs={{0,8},{4,12},{8,0},{12,4},{16,24},{20,28},{24,16},{28,20},{1,9},{5... | collective-permute-start | bytes 294920 | tf_op jit(solution)/shard_map/ppermute | solution.py:734
  (67 other events, 360.7 us)
